TPU v7x, 32 devices: a whole 2x2x4 slice. The times are simulated.
32 devices in a mesh: shot: 2 (over y), xy: 8 (over z, x), gz: 2 (over core).
Axes of the slice: x: 2, y: 2, z: 4, core: 2. Of those that a mesh axis runs over, the one named last changes fastest.
Arguments:
- wave_p: float32 [256, 8, 640], P(('shot', 'xy'), 'gz'), parts along dimension 0, may hold values from -6 to 6
- wave_q: float32 [256, 8, 640], P(('shot', 'xy'), 'gz'), parts along dimension 0, may hold values from -6 to 6
- prior_p: float32 [256, 8, 640], P(('shot', 'xy'), 'gz'), parts along dimension 0, may hold values from -6 to 6
- prior_q: float32 [256, 8, 640], P(('shot', 'xy'), 'gz'), parts along dimension 0, may hold values from -6 to 6
- courant: bfloat16 [128, 8, 640], P('xy', 'gz'), may hold values from 0.049804688 to 0.19921875
- epsilon: bfloat16 [128, 8, 640], P('xy', 'gz'), may hold values from 0 to 0.3984375
- thomsen_delta: bfloat16 [128, 8, 640], P('xy', 'gz'), may hold values from -0.099609375 to 0.29882812
- tilt_angle: bfloat16 [128, 8, 640], P('xy', 'gz'), may hold values from -3.140625 to 3.140625
- azimuth: bfloat16 [128, 8, 640], P('xy', 'gz'), may hold values from -3.140625 to 3.140625
Outputs:
- next_p: float32 [256, 8, 640], P(('shot', 'xy'), 'gz'), parts along dimension 0
- next_q: float32 [256, 8, 640], P(('shot', 'xy'), 'gz'), parts along dimension 0
- detail_first: float32 [128, 8, 640], P(('shot', 'xy'), 'gz'), parts along dimension 0
- detail_second: float32 [64, 8, 640], P(('shot', 'xy'), 'gz'), parts along dimension 0
- detail_third: float32 [32, 8, 640], P(('shot', 'xy'), 'gz'), parts along dimension 0
- approx_coarse: float32 [32, 8, 640], P(('shot', 'xy'), 'gz'), parts along dimension 0
There are 2 independent parts, one for each index of `shot`. A program takes and returns all parts, laid end to end along the dimension named above; an argument that names none is the same for every part. Nothing has to cross between parts.
All inputs are finite; a program needn't handle non-finite values.
Results may differ from a plain program's by a relative error of at most 0.0003.
Values sent between devices are 32-bit elements; how exact they have to be, the bound alone decides.
No kernel may reach another device: no remote copies, remote signals or barrier semaphores. Data moves between devices by JAX's collectives and lax.ppermute only.
A program may use at most 64 MiB of HBM per device.

v0:
```python
import jax
import jax.numpy as jnp
from jax import lax
from jax.sharding import PartitionSpec as P

SECOND = (-205.0 / 72.0, 8.0 / 5.0, -1.0 / 5.0, 8.0 / 315.0, -1.0 / 560.0)
FIRST = (4.0 / 5.0, -1.0 / 5.0, 4.0 / 105.0, -1.0 / 280.0)
LIFT = (-1.586134342, -0.05298011854, 0.8829110762, 0.4435068522)
ZETA = 1.149604398


def padded_2(value, sides, width):
    for axis, dim in sides:
        size, length = (lax.axis_size(axis), value.shape[dim])
        up = [(i, (i + 1) % size) for i in range(size - 1)]
        down = [(j, i) for i, j in up]
        last = lax.slice_in_dim(value, length - width, length, axis=dim)
        leading = lax.slice_in_dim(value, 0, width, axis=dim)
        before = lax.ppermute(last, axis, up)
        after = lax.ppermute(leading, axis, down)
        value = jnp.concatenate([before, value, after], axis=dim)
    return value


def strip(values, along, offset, length):
    return lax.slice_in_dim(values, offset, offset + length, axis=along)


def first_along(padded, along):
    length = padded.shape[along] - 8
    total = FIRST[0] * (strip(padded, along, 5, length) - strip(padded, along, 3, length))
    for number in range(2, 5):
        total = total + FIRST[number - 1] * (
            strip(padded, along, 4 + number, length) - strip(padded, along, 4 - number, length)
        )
    return total


def second_along(padded, along):
    length = padded.shape[along] - 8
    total = SECOND[0] * strip(padded, along, 4, length)
    for number in range(1, 5):
        total = total + SECOND[number] * (
            strip(padded, along, 4 + number, length) + strip(padded, along, 4 - number, length)
        )
    return total


def trim(values, along):
    return strip(values, along, 4, values.shape[along] - 8)


def derivatives(padded):
    dxx = second_along(trim(trim(padded, 1), 2), 0)
    dyy = second_along(trim(trim(padded, 0), 1), 2)
    dzz = second_along(trim(trim(padded, 0), 2), 1)
    along_x = first_along(padded, 0)
    dxy = first_along(trim(along_x, 1), 2)
    dxz = first_along(trim(along_x, 2), 1)
    dzy = first_along(first_along(trim(padded, 0), 1), 2)
    return (dxx, dyy, dzz, dxy, dzy, dxz)


def advance(
    p_padded,
    q_padded,
    wave_p,
    wave_q,
    prior_p,
    prior_q,
    courant,
    epsilon,
    thomsen_delta,
    tilt_angle,
    azimuth,
):
    tilt = tilt_angle.astype(jnp.float32)
    turn = azimuth.astype(jnp.float32)
    sine_tilt = jnp.sin(tilt)
    cosine_tilt = jnp.cos(tilt)
    sine_turn = jnp.sin(turn)
    cosine_turn = jnp.cos(turn)
    double_tilt = jnp.sin(2.0 * tilt)
    weights = (
        sine_tilt * sine_tilt * cosine_turn * cosine_turn,
        sine_tilt * sine_tilt * sine_turn * sine_turn,
        cosine_tilt * cosine_tilt,
        sine_tilt * sine_tilt * jnp.sin(2.0 * turn),
        double_tilt * sine_turn,
        double_tilt * cosine_turn,
    )

    def rotated(parts):
        total = weights[0] * parts[0]
        for number in range(1, 6):
            total = total + weights[number] * parts[number]
        return total

    p_parts = derivatives(p_padded)
    h_one_p = rotated(p_parts)
    h_two_p = p_parts[0] + p_parts[1] + p_parts[2] - h_one_p
    h_one_q = rotated(derivatives(q_padded))
    root = jnp.sqrt(1.0 + 2.0 * thomsen_delta.astype(jnp.float32))
    speed = courant.astype(jnp.float32)
    stretch = 1.0 + 2.0 * epsilon.astype(jnp.float32)
    next_p = 2.0 * wave_p - prior_p + speed * (stretch * h_two_p + root * h_one_q)
    next_q = 2.0 * wave_q - prior_q + speed * (root * h_two_p + h_one_q)
    return (next_p, next_q)


def lift_steps(evens, odds, ahead, behind):
    odds = odds + LIFT[0] * (evens + ahead(evens))
    evens = evens + LIFT[1] * (odds + behind(odds))
    odds = odds + LIFT[2] * (evens + ahead(evens))
    evens = evens + LIFT[3] * (odds + behind(odds))
    return (evens * ZETA, odds * (1.0 / ZETA))


def lift_last(values):
    half = values.shape[-1] // 2
    split = values.reshape(values.shape[:-1] + (half, 2))
    return lift_steps(
        split[..., 0],
        split[..., 1],
        lambda field: jnp.roll(field, -1, axis=-1),
        lambda field: jnp.roll(field, 1, axis=-1),
    )


def lift_first(values):
    half = values.shape[0] // 2
    split = values.reshape((half, 2) + values.shape[1:])
    return lift_steps(
        split[:, 0],
        split[:, 1],
        lambda field: jnp.roll(field, -1, axis=0),
        lambda field: jnp.roll(field, 1, axis=0),
    )


def transform_last(values):
    details = []
    coarse = values
    for number in range(3):
        coarse, detail = lift_last(coarse)
        details.append(detail)
    return jnp.concatenate(details + [coarse], axis=-1)


def body(wave_p, wave_q, prior_p, prior_q, courant, epsilon, thomsen_delta, tilt_angle, azimuth):
    stacked = jnp.stack([wave_p, wave_q])
    extended = padded_2(stacked, (("xy", 1), ("gz", 2)), 4)
    padded = jnp.pad(extended, ((0, 0), (0, 0), (0, 0), (4, 4)))
    next_p, next_q = advance(
        padded[0],
        padded[1],
        wave_p,
        wave_q,
        prior_p,
        prior_q,
        courant,
        epsilon,
        thomsen_delta,
        tilt_angle,
        azimuth,
    )
    crossline = transform_last(next_p)
    local_rows = crossline.shape[0]
    flattened = crossline.reshape(local_rows, -1)
    columns = lax.all_to_all(flattened, "xy", split_axis=1, concat_axis=0, tiled=True)
    group_size = lax.axis_size("xy")
    column_count = columns.shape[1]
    coarse = columns
    members = []
    for number in range(3):
        coarse, detail = lift_first(coarse)
        members.append(detail)
    members.append(coarse)
    packed = jnp.concatenate(
        [
            member.reshape(group_size, member.shape[0] // group_size, column_count)
            for member in members
        ],
        axis=1,
    )
    packed = packed.reshape(-1, column_count)
    returned = lax.all_to_all(packed, "xy", split_axis=0, concat_axis=1, tiled=True)
    tail_shape = crossline.shape[1:]
    first_rows = local_rows // 2
    second_rows = local_rows // 4
    third_rows = local_rows // 8
    detail_first = returned[0:first_rows].reshape((first_rows,) + tail_shape)
    detail_second = returned[first_rows : first_rows + second_rows].reshape(
        (second_rows,) + tail_shape
    )
    start_third = first_rows + second_rows
    detail_third = returned[start_third : start_third + third_rows].reshape(
        (third_rows,) + tail_shape
    )
    approx_coarse = returned[start_third + third_rows :].reshape((third_rows,) + tail_shape)
    return (next_p, next_q, detail_first, detail_second, detail_third, approx_coarse)


def solution(mesh):
    placed = (
        P(("shot", "xy"), "gz", None),
        P(("shot", "xy"), "gz", None),
        P(("shot", "xy"), "gz", None),
        P(("shot", "xy"), "gz", None),
        P("xy", "gz", None),
        P("xy", "gz", None),
        P("xy", "gz", None),
        P("xy", "gz", None),
        P("xy", "gz", None),
    )
    return jax.shard_map(
        body,
        mesh=mesh,
        in_specs=placed,
        out_specs=(
            P(("shot", "xy"), "gz", None),
            P(("shot", "xy"), "gz", None),
            P(("shot", "xy"), "gz", None),
            P(("shot", "xy"), "gz", None),
            P(("shot", "xy"), "gz", None),
            P(("shot", "xy"), "gz", None),
        ),
        check_vma=False,
    )
```

profile of v0, /device:TPU:0, one launch (start us, length us, event | category | flops | bytes accessed | tf_op | source)
XLA Modules:
  0.0 77.3 jit_solution(3347124975533758275)
XLA Ops:
  0.6 0.9 %pad_maximum_fusion.12 = (f32[2,4,4,640]{3,2,1,0:T(4,128)S(1)}, f32[2,4,4,640]{3,2,1,0:T(4,128)S(1)}) fusion(f32[1,16,4,640]{3,2,1,0:T(4,128)} %bitcast.153, f32[1,16,4,640]{3,2,1,0:T(4,128)} %bitcast.160), kind=kLoop, calls=%fused_computation.287 | loop fusion | flops 40960 | bytes 491520 | tf_op jit(solution)/shard_map/slice | solution.py:17
  1.5 4.8 %collective-permute-start = (f32[2,4,4,640]{3,2,1,0:T(4,128)S(1)}, f32[2,4,4,640]{3,2,1,0:T(4,128)S(1)}, u32[]{:S(2)}, u32[]{:S(2)}) collective-permute-start(f32[2,4,4,640]{3,2,1,0:T(4,128)S(1)} %get-tuple-element.61), channel_id=1, source_target_pairs={{0,2},{2,4},{4,6},{6,8},{8,10},{10,12},{12,14},{1,3},{3,5},{5,7},{... | collective-permute-start | bytes 245768 | tf_op jit(solution)/shard_map/ppermute | solution.py:19
  6.4 1.3 %collective-permute-start.1 = (f32[2,4,4,640]{3,2,1,0:T(4,128)S(1)}, f32[2,4,4,640]{3,2,1,0:T(4,128)S(1)}, u32[]{:S(2)}, u32[]{:S(2)}) collective-permute-start(f32[2,4,4,640]{3,2,1,0:T(4,128)S(1)} %get-tuple-element.62), channel_id=1, source_target_pairs={{2,0},{4,2},{6,4},{8,6},{10,8},{12,10},{14,12},{3,1},{5,3},{7,5},{... | collective-permute-start | bytes 245768 | tf_op jit(solution)/shard_map/ppermute | solution.py:20
  7.7 0.7 collective-permute-done
  8.4 4.3 %collective-permute-done.1 = f32[2,4,4,640]{3,2,1,0:T(4,128)S(1)} collective-permute-done((f32[2,4,4,640]{3,2,1,0:T(4,128)S(1)}, f32[2,4,4,640]{3,2,1,0:T(4,128)S(1)}, u32[]{:S(2)}, u32[]{:S(2)}) %collective-permute-start.1) | collective-permute-done | bytes 81952 | tf_op jit(solution)/shard_map/ppermute | solution.py:20
  12.7 1.1 %pad_maximum_fusion = f32[2,24,4,640]{3,2,1,0:T(4,128)S(1)} fusion(f32[2,4,4,640]{3,2,1,0:T(4,128)S(1)} %collective-permute-done.1, f32[1,16,4,640]{3,2,1,0:T(4,128)} %bitcast.154, f32[1,16,4,640]{3,2,1,0:T(4,128)} %bitcast.161, f32[2,4,4,640]{3,2,1,0:T(4,128)S(1)} %collective-permute-done), kind=kLoop, calls=%fused_computation.36 | loop fusion | flops 368640 | bytes 983040 | tf_op jit(solution)/shard_map/concatenate | solution.py:21
  13.8 1.3 %collective-permute-start.3 = (f32[2,24,4,640]{3,2,1,0:T(4,128)S(1)}, f32[2,24,4,640]{3,2,1,0:T(4,128)S(1)}, u32[]{:S(2)}, u32[]{:S(2)}) collective-permute-start(f32[2,24,4,640]{3,2,1,0:T(4,128)S(1)} %pad_maximum_fusion), channel_id=1, source_target_pairs={{1,0},{3,2},{5,4},{7,6},{9,8},{11,10},{13,12},{15,14},{17,16},{19,... | collective-permute-start | bytes 1474568 | tf_op jit(solution)/shard_map/ppermute | solution.py:20
  15.1 3.1 %collective-permute-start.2 = (f32[2,24,4,640]{3,2,1,0:T(4,128)S(1)}, f32[2,24,4,640]{3,2,1,0:T(4,128)S(1)}, u32[]{:S(2)}, u32[]{:S(2)}) collective-permute-start(f32[2,24,4,640]{3,2,1,0:T(4,128)S(1)} %pad_maximum_fusion), channel_id=1, source_target_pairs={{0,1},{2,3},{4,5},{6,7},{8,9},{10,11},{12,13},{14,15},{16,17},{18,... | collective-permute-start | bytes 1474568 | tf_op jit(solution)/shard_map/ppermute | solution.py:19
  18.2 1.4 %collective-permute-done.2 = f32[2,24,4,640]{3,2,1,0:T(4,128)S(1)} collective-permute-done((f32[2,24,4,640]{3,2,1,0:T(4,128)S(1)}, f32[2,24,4,640]{3,2,1,0:T(4,128)S(1)}, u32[]{:S(2)}, u32[]{:S(2)}) %collective-permute-start.2) | collective-permute-done | bytes 491552 | tf_op jit(solution)/shard_map/ppermute | solution.py:19
  19.6 2.3 %select_maximum_fusion = f32[2,24,12,648]{3,2,1,0:T(8,128)S(1)} fusion(f32[2,24,4,640]{3,2,1,0:T(4,128)S(1)} %collective-permute-done.3, f32[2,24,4,640]{3,2,1,0:T(4,128)S(1)} %collective-permute-done.2, f32[2,4,4,640]{3,2,1,0:T(4,128)S(1)} %collective-permute-done.1, f32[2,4,4,640]{3,2,1,0:T(4,128)S(1)} %collective-permute-done, ...), kind=kLoop, calls=%fused_computation.2 | loop fusion | flops 5225472 | bytes 2967552 | tf_op jit(solution)/shard_map/concatenate | solution.py:21
  22.0 0.2 slice_bitcast_fusion
  22.1 0.6 slice_bitcast_fusion.2
  22.8 0.6 fusion.18
  23.4 0.3 copy-done
  23.9 10.8 %fusion.34 = (f32[16,4,640]{2,1,0:T(4,128)}, f32[16,4,640]{2,1,0:T(4,128)S(1)}, f32[16,4,640]{2,1,0:T(4,128)S(1)}) fusion(bf16[16,4,640]{2,1,0:T(4,128)(2,1)S(1)} %copy-done.3, f32[16,4,640]{2,1,0:T(4,128)S(1)} %copy-done.5, f32[16,4,640]{2,1,0:T(4,128)S(1)} %copy-done, bf16[16,4,640]{2,1,0:T(4,128)(2,1)S(1)} %copy-done.4, ...), kind=kLoop, calls=%fused_computation.73 | loop fusion | flops 7782400 | bytes 17530880 | tf_op jit(solution)/shard_map/add | solution.py:107
  34.8 0.2 fusion.33
  35.0 0.4 copy.333
  35.4 1.0 %fusion.189 = (f32[16,4,320,1]{0,3,2,1:T(1,128)S(1)}, f32[16,4,320,1]{0,3,2,1:T(1,128)S(1)}) fusion(f32[16,4,320,2]{0,3,2,1:T(2,128)S(1)} %bitcast.150), kind=kLoop, calls=%fused_computation.351 | loop fusion | bytes 327680 | tf_op jit(solution)/shard_map/slice | solution.py:123
  36.5 0.3 copy.335
  36.9 0.3 copy.382
  37.6 0.3 copy.344
  37.9 0.3 copy.338
  38.4 0.3 copy.341
  38.8 0.2 copy.347
  39.1 0.3 copy.348
  39.4 0.3 copy.342
  39.6 0.3 copy.343
  39.9 0.3 copy.337
  40.2 0.3 copy.339
  40.5 0.2 copy.345
  40.8 0.3 copy.346
  41.6 0.2 copy.349
  41.8 0.1 copy.358
  42.4 0.2 copy.361
  42.5 0.1 copy.362
  42.7 0.2 copy.356
  43.0 0.2 copy.351
  43.3 0.2 copy.350
  43.6 0.2 copy.359
  45.0 14.0 %all_to_all.29 = f32[16,8,320]{2,0,1:T(8,128)S(1)} all-to-all(f32[16,8,320]{2,0,1:T(8,128)S(1)} %copy.364), channel_id=1, replica_groups=mesh['shot'=2,'xy'=8,'gz'=2] {'xy'}, dimensions={1} | all-to-all | bytes 327680 | tf_op jit(solution)/shard_map/all_to_all | solution.py:170
  59.2 0.5 broadcast.187
  59.8 1.2 %fusion.184 = (f32[64,320]{1,0:T(8,128)S(1)}, f32[64,1,320]{2,1,0:T(1,128)S(1)}, f32[64,320]{1,0:T(8,128)S(1)}, f32[64,1,320]{2,1,0:T(1,128)S(1)}) fusion(f32[]{:T(128)} %broadcast.187, f32[64,2,320]{2,1,0:T(2,128)S(1)} %reshape.155), kind=kLoop, calls=%fused_computation.349 | loop fusion | bytes 491524 | tf_op jit(solution)/shard_map/slice | solution.py:134
  62.4 0.8 %fusion.182 = (f32[16,320]{1,0:T(8,128)S(1)}, f32[16,1,320]{2,1,0:T(1,128)S(1)}, f32[16,320]{1,0:T(8,128)S(1)}, f32[16,1,320]{2,1,0:T(1,128)S(1)}) fusion(f32[]{:T(128)} %broadcast.187, f32[16,2,320]{2,1,0:T(2,128)S(1)} %add_multiply_fusion.2), kind=kLoop, calls=%fused_computation.347 | loop fusion | bytes 122884 | tf_op jit(solution)/shard_map/slice | solution.py:134
  63.7 10.7 %all_to_all.30 = f32[8,16,320]{2,1,0:T(8,128)S(1)} all-to-all(f32[8,16,320]{2,1,0:T(8,128)S(1)} %pad_maximum_fusion.1), channel_id=1, replica_groups=mesh['shot'=2,'xy'=8,'gz'=2] {'xy'}, dimensions={0} | all-to-all | bytes 327680 | tf_op jit(solution)/shard_map/all_to_all | solution.py:187
  74.5 0.7 reshape.157
  75.2 0.7 reshape.156
  75.9 0.7 reshape.159
  76.6 0.7 reshape.158
  (132 shorter events, 5.3 us)
Async XLA Ops:
  1.5 6.9 %collective-permute-start = (f32[2,4,4,640]{3,2,1,0:T(4,128)S(1)}, f32[2,4,4,640]{3,2,1,0:T(4,128)S(1)}, u32[]{:S(2)}, u32[]{:S(2)}) collective-permute-start(f32[2,4,4,640]{3,2,1,0:T(4,128)S(1)} %get-tuple-element.61), channel_id=1, source_target_pairs={{0,2},{2,4},{4,6},{6,8},{8,10},{10,12},{12,14},{1,3},{3,5},{5,7},{... | collective-permute-start | bytes 245768 | tf_op jit(solution)/shard_map/ppermute | solution.py:19
  6.4 6.3 %collective-permute-start.1 = (f32[2,4,4,640]{3,2,1,0:T(4,128)S(1)}, f32[2,4,4,640]{3,2,1,0:T(4,128)S(1)}, u32[]{:S(2)}, u32[]{:S(2)}) collective-permute-start(f32[2,4,4,640]{3,2,1,0:T(4,128)S(1)} %get-tuple-element.62), channel_id=1, source_target_pairs={{2,0},{4,2},{6,4},{8,6},{10,8},{12,10},{14,12},{3,1},{5,3},{7,5},{... | collective-permute-start | bytes 245768 | tf_op jit(solution)/shard_map/ppermute | solution.py:20
  13.8 4.4 %collective-permute-start.3 = (f32[2,24,4,640]{3,2,1,0:T(4,128)S(1)}, f32[2,24,4,640]{3,2,1,0:T(4,128)S(1)}, u32[]{:S(2)}, u32[]{:S(2)}) collective-permute-start(f32[2,24,4,640]{3,2,1,0:T(4,128)S(1)} %pad_maximum_fusion), channel_id=1, source_target_pairs={{1,0},{3,2},{5,4},{7,6},{9,8},{11,10},{13,12},{15,14},{17,16},{19,... | collective-permute-start | bytes 1474568 | tf_op jit(solution)/shard_map/ppermute | solution.py:20
  15.1 4.5 %collective-permute-start.2 = (f32[2,24,4,640]{3,2,1,0:T(4,128)S(1)}, f32[2,24,4,640]{3,2,1,0:T(4,128)S(1)}, u32[]{:S(2)}, u32[]{:S(2)}) collective-permute-start(f32[2,24,4,640]{3,2,1,0:T(4,128)S(1)} %pad_maximum_fusion), channel_id=1, source_target_pairs={{0,1},{2,3},{4,5},{6,7},{8,9},{10,11},{12,13},{14,15},{16,17},{18,... | collective-permute-start | bytes 1474568 | tf_op jit(solution)/shard_map/ppermute | solution.py:19
  22.7 0.9 %copy-start = (f32[16,4,640]{2,1,0:T(4,128)S(1)}, f32[16,4,640]{2,1,0:T(4,128)}, u32[]{:S(2)}) copy-start(f32[16,4,640]{2,1,0:T(4,128)} %param.10) | copy-start | bytes 491524
  22.7 1.0 %copy-start.3 = (bf16[16,4,640]{2,1,0:T(4,128)(2,1)S(1)}, bf16[16,4,640]{2,1,0:T(4,128)(2,1)}, u32[]{:S(2)}) copy-start(bf16[16,4,640]{2,1,0:T(4,128)(2,1)} %param.13) | copy-start | bytes 245764
  22.8 1.0 %copy-start.4 = (bf16[16,4,640]{2,1,0:T(4,128)(2,1)S(1)}, bf16[16,4,640]{2,1,0:T(4,128)(2,1)}, u32[]{:S(2)}) copy-start(bf16[16,4,640]{2,1,0:T(4,128)(2,1)} %param.15) | copy-start | bytes 245764
  22.8 1.0 %copy-start.5 = (f32[16,4,640]{2,1,0:T(4,128)S(1)}, f32[16,4,640]{2,1,0:T(4,128)}, u32[]{:S(2)}) copy-start(f32[16,4,640]{2,1,0:T(4,128)} %param.12) | copy-start | bytes 491524
  22.8 1.1 %copy-start.8 = (bf16[16,4,640]{2,1,0:T(4,128)(2,1)S(1)}, bf16[16,4,640]{2,1,0:T(4,128)(2,1)}, u32[]{:S(2)}) copy-start(bf16[16,4,640]{2,1,0:T(4,128)(2,1)} %param.17) | copy-start | bytes 245764
  22.8 1.1 %copy-start.9 = (bf16[16,4,640]{2,1,0:T(4,128)(2,1)S(1)}, bf16[16,4,640]{2,1,0:T(4,128)(2,1)}, u32[]{:S(2)}) copy-start(bf16[16,4,640]{2,1,0:T(4,128)(2,1)} %param.16) | copy-start | bytes 245764
  23.9 10.8 %copy-start.1 = (f32[16,4,640]{2,1,0:T(4,128)S(1)}, f32[16,4,640]{2,1,0:T(4,128)}, u32[]{:S(2)}) copy-start(f32[16,4,640]{2,1,0:T(4,128)} %param.9) | copy-start | bytes 491524
  23.9 10.8 %copy-start.6 = (f32[16,4,640]{2,1,0:T(4,128)S(1)}, f32[16,4,640]{2,1,0:T(4,128)}, u32[]{:S(2)}) copy-start(f32[16,4,640]{2,1,0:T(4,128)} %param.11) | copy-start | bytes 491524
  23.9 10.8 %copy-start.7 = (bf16[16,4,640]{2,1,0:T(4,128)(2,1)S(1)}, bf16[16,4,640]{2,1,0:T(4,128)(2,1)}, u32[]{:S(2)}) copy-start(bf16[16,4,640]{2,1,0:T(4,128)(2,1)} %param.14) | copy-start | bytes 245764
  35.0 1.8 %copy-start.2 = (f32[16,4,640]{2,1,0:T(4,128)}, f32[16,4,640]{2,1,0:T(4,128)S(1)}, u32[]{:S(2)}) copy-start(f32[16,4,640]{2,1,0:T(4,128)S(1)} %fusion.33) | copy-start | bytes 491524
where the time goes:
time: 77.7 us; the launch traced here: 77.3 us
  blocking collectives  24.8 us (32%)
  other arithmetic  18.6 us (24%)
  local copies, waits for them, and re-layouts  15.5 us (20%)
  starting transfers between devices  10.5 us (14%)
  waiting for transfers between devices  6.47 us (8%)
  between operations  1.52 us (2%)
    all_to_all x1, blocking collectives, body(): lax.all_to_all(flattened, 'xy', split_axis=1, concat_axis=0, tiled=True)  14 us
    add x1, other arithmetic, advance(): next_q = 2.0 * wave_q - prior_q + speed * (root * h_two_p + h_one_q)  10.8 us
    all_to_all x1, blocking collectives, body(): lax.all_to_all(packed, 'xy', split_axis=0, concat_axis=1, tiled=True)  10.7 us
    ppermute x2, starting transfers between devices, padded_2(): before = lax.ppermute(last, axis, up)  7.93 us
    ppermute x2, waiting for transfers between devices, padded_2(): after = lax.ppermute(leading, axis, down)  4.3 us
    concatenate x2, other arithmetic, padded_2(): value = jnp.concatenate([before, value, after], axis=dim)  3.43 us
    ppermute x2, starting transfers between devices, padded_2(): after = lax.ppermute(leading, axis, down)  2.58 us
    ppermute x2, waiting for transfers between devices, padded_2(): before = lax.ppermute(last, axis, up)  2.17 us
  transfers between devices with their start and end apart: 4, of which 3 were waited for; matrix products, arithmetic and copies ran while one was open for 0% of the time, Pallas kernels for 0%

commit v1 on v0

v1 whole, which is shorter than its diff:
```python
import functools

import jax
import jax.numpy as jnp
import numpy as np
from jax import lax
from jax.experimental import pallas as pl
from jax.experimental.pallas import tpu as pltpu
from jax.sharding import PartitionSpec as P

SECOND = (-205.0 / 72.0, 8.0 / 5.0, -1.0 / 5.0, 8.0 / 315.0, -1.0 / 560.0)
FIRST = (4.0 / 5.0, -1.0 / 5.0, 4.0 / 105.0, -1.0 / 280.0)
LIFT = (-1.586134342, -0.05298011854, 0.8829110762, 0.4435068522)
ZETA = 1.149604398
LANES = 128


def lift_level(values):
    even, odd = values[0::2], values[1::2]
    odd = odd + LIFT[0] * (even + np.roll(even, -1, 0))
    even = even + LIFT[1] * (odd + np.roll(odd, 1, 0))
    odd = odd + LIFT[2] * (even + np.roll(even, -1, 0))
    even = even + LIFT[3] * (odd + np.roll(odd, 1, 0))
    return even * ZETA, odd * (1.0 / ZETA)


def three_levels(length):
    coarse, members = np.eye(length), []
    for _ in range(3):
        coarse, detail = lift_level(coarse)
        members.append(detail)
    return members + [coarse]


def split_bf16(matrix):
    high = matrix.astype(jnp.bfloat16)
    low = (matrix - high.astype(np.float64)).astype(jnp.bfloat16)
    return high, low


def inline_blocks(rows):
    bricks, brick = 8, 4
    members = three_levels(rows * bricks)
    wanted = np.concatenate(
        [m[brick * len(m) // bricks : (brick + 1) * len(m) // bricks] for m in members]
    )

    def block(offset):
        return wanted[:, rows * (brick + offset) : rows * (brick + offset + 1)]

    factors = {}
    for offset in (-1, 1, -2, 2):
        left, sizes, right = np.linalg.svd(block(offset))
        rank = int((sizes > 1e-12).sum())
        root = np.sqrt(sizes[:rank])
        factors[offset] = (left[:, :rank] * root, root[:, None] * right[:rank])
    return block(0), factors


def sine_cosine(angle):
    turns = jnp.round(angle * (2.0 / np.pi))
    rest = angle - turns * 1.5703125
    rest = rest - turns * 4.837512969970703125e-4
    rest = rest - turns * 7.549789948768648e-8
    square = rest * rest
    sine = rest + rest * square * (
        -1.6666654611e-1 + square * (8.3321608736e-3 + square * -1.9515295891e-4)
    )
    cosine = (
        1.0
        - 0.5 * square
        + square
        * square
        * (4.166664568298827e-2 + square * (-1.388731625493765e-3 + square * 2.443315711809948e-5))
    )
    quarter = turns.astype(jnp.int32)
    swapped = (quarter & 1) == 1
    out_sine = jnp.where(swapped, cosine, sine)
    out_cosine = jnp.where(swapped, sine, cosine)
    out_sine = jnp.where((quarter & 2) == 2, -out_sine, out_sine)
    out_cosine = jnp.where(((quarter + 1) & 2) == 2, -out_cosine, out_cosine)
    return out_sine, out_cosine


def weights_kernel(
    waves, prior_p, prior_q, courant, epsilon, delta, tilt, azimuth, axis_x, axis_y, axis_z, gain_a, gain_b, base
):
    rows = waves.shape[0]
    top = lax.broadcasted_iota(jnp.int32, waves.shape[1:], 0) < 4

    def swap(value):
        return pltpu.roll(value, 4, 0)

    for x in range(rows):
        angles = jnp.concatenate(
            [tilt[x].astype(jnp.float32), azimuth[x].astype(jnp.float32)], axis=0
        )
        sine, cosine = sine_cosine(angles)
        sine_other, cosine_other = swap(sine), swap(cosine)
        sine_tilt = jnp.where(top, sine, sine_other)
        axis_x[x] = sine_tilt * jnp.where(top, cosine_other, cosine)
        axis_y[x] = sine * sine_other
        axis_z[x] = jnp.where(top, cosine, cosine_other)
        speed = courant[x].astype(jnp.float32)
        root = jnp.sqrt(1.0 + 2.0 * delta[x].astype(jnp.float32))
        stretch = 1.0 + 2.0 * epsilon[x].astype(jnp.float32)
        gain_a[x] = jnp.concatenate([speed * stretch, speed], axis=0)
        across = speed * root
        gain_b[x] = jnp.concatenate([across, across], axis=0)
        base[x] = 2.0 * waves[x] - jnp.concatenate([prior_p[x], prior_q[x]], axis=0)


def shifted(value, width):
    wide = jnp.concatenate(
        [value, jnp.zeros((value.shape[0], LANES), jnp.float32)], axis=1
    )
    total = width + LANES
    ahead = [pltpu.roll(wide, total - k, 1)[:, :width] for k in range(1, 5)]
    behind = [pltpu.roll(wide, k, 1)[:, :width] for k in range(1, 5)]
    return ahead, behind


def first_of(ahead, behind):
    total = FIRST[0] * (ahead[0] - behind[0])
    for k in range(1, 4):
        total = total + FIRST[k] * (ahead[k] - behind[k])
    return total


def second_of(centre, ahead, behind):
    total = SECOND[0] * centre
    for k in range(4):
        total = total + SECOND[k + 1] * (ahead[k] + behind[k])
    return total


def dot3(a_high, a_low, b_high, b_low):
    def dot(a, b):
        return jnp.dot(a, b, preferred_element_type=jnp.float32)

    return dot(a_high, b_high) + (dot(a_low, b_high) + dot(a_high, b_low))


def halves(value):
    high = value.astype(jnp.bfloat16)
    return high, (value - high.astype(jnp.float32)).astype(jnp.bfloat16)


def step_kernel(
    gives,
    waves,
    other,
    left,
    right,
    left_cross,
    right_cross,
    axis_x,
    axis_y,
    axis_z,
    gain_a,
    gain_b,
    base,
    across_high,
    across_low,
    inline_high,
    inline_low,
    next_p,
    next_q,
    mine,
    *rest,
):
    sends, (ext, dz_ext, dzz_ext, pressure) = rest[:-4], rest[-4:]
    rows, _, width = waves.shape
    lower = lax.axis_index("gz") == 0
    sub = lax.broadcasted_iota(jnp.int32, waves.shape[1:], 0)
    layer = sub & 3
    top = sub < 4
    above = jnp.where(lower, 1.0, 0.0)
    below = jnp.where(lower, 0.0, 1.0)

    for x in range(rows + 8):
        if x < 4:
            own, far = left[x], left_cross[x]
        elif x < rows + 4:
            own, far = waves[x - 4], other[x - 4]
        else:
            own, far = right[x - rows - 4], right_cross[x - rows - 4]
        ext[x] = own
        up, down = far * above, far * below
        ahead, behind = [], []
        for k in range(1, 4):
            ahead.append(jnp.where(layer < 4 - k, pltpu.roll(own, 8 - k, 0), pltpu.roll(up, 4 - k, 0)))
            behind.append(jnp.where(layer >= k, pltpu.roll(own, k, 0), pltpu.roll(down, 4 + k, 0)))
        ahead.append(up)
        behind.append(down)
        dz_ext[x] = first_of(ahead, behind)
        if 4 <= x < rows + 4:
            dzz_ext[x - 4] = second_of(own, ahead, behind)

    def row(x, carry):
        centre = ext[x + 4]
        ahead = [ext[x + 4 + k] for k in range(1, 5)]
        behind = [ext[x + 4 - k] for k in range(1, 5)]
        dxx = second_of(centre, ahead, behind)
        dx = first_of(ahead, behind)
        dxz = first_of(
            [dz_ext[x + 4 + k] for k in range(1, 5)], [dz_ext[x + 4 - k] for k in range(1, 5)]
        )
        dyy = second_of(centre, *shifted(centre, width))
        dxy = first_of(*shifted(dx, width))
        dzy = first_of(*shifted(dz_ext[x + 4], width))
        dzz = dzz_ext[x]
        n_x, n_y, n_z = axis_x[x], axis_y[x], axis_z[x]
        h_one = (n_x * n_x) * dxx
        h_one = h_one + (n_y * n_y) * dyy
        h_one = h_one + (n_z * n_z) * dzz
        h_one = h_one + 2.0 * (n_x * n_y * dxy + n_z * (n_y * dzy + n_x * dxz))
        h_two = dxx + dyy + dzz - h_one
        mixed = jnp.where(top, h_two, h_one)
        result = base[x] + gain_a[x] * mixed + gain_b[x] * pltpu.roll(mixed, 4, 0)
        next_p[x] = result[:4]
        next_q[x] = result[4:]
        pressure[x] = result
        return carry

    lax.fori_loop(0, rows, row, 0)

    packed = jnp.concatenate(
        [
            jnp.where(top, pressure[x], pltpu.roll(pressure[x + 1], 4, 0))
            for x in range(0, rows, 2)
        ],
        axis=0,
    )
    crossline = dot3(*halves(packed), across_high[...], across_low[...])
    parts = dot3(inline_high[...], inline_low[...], *halves(crossline))
    mine[...] = parts[: 4 * rows]
    for (start, size), send in zip(gives, sends):
        send[...] = parts[start : start + size]


def finish_kernel(takes, mine, *rest):
    received, outs = rest[:4], rest[4:]
    at = 0
    for out in outs:
        for row in range(out.shape[0]):
            total = mine[4 * at : 4 * at + 4]
            for take, got in zip(takes, received):
                for j in range(take.shape[1]):
                    factor = float(take[at, j])
                    if abs(factor) > 1e-13:
                        total = total + factor * got[4 * j : 4 * j + 4]
            out[row] = total
            at += 1


def body(size, wave_p, wave_q, prior_p, prior_q, courant, epsilon, thomsen_delta, tilt_angle, azimuth):
    rows, layers, width = wave_p.shape
    f32 = jnp.float32
    waves = jnp.concatenate([wave_p, wave_q], axis=1)
    up = [(i, i + 1) for i in range(size - 1)]
    down = [(i + 1, i) for i in range(size - 1)]

    def crossed(pairs):
        return [(2 * i + g, 2 * j + 1 - g) for i, j in pairs for g in range(2)]

    last, leading = waves[rows - 4 :], waves[:4]
    other = lax.ppermute(waves, "gz", [(0, 1), (1, 0)])
    left = lax.ppermute(last, "xy", up)
    right = lax.ppermute(leading, "xy", down)
    left_cross = lax.ppermute(last, ("xy", "gz"), crossed(up))
    right_cross = lax.ppermute(leading, ("xy", "gz"), crossed(down))

    stack = jax.ShapeDtypeStruct((rows, 8, width), f32)
    cells = rows * layers * width
    weights = pl.pallas_call(
        weights_kernel,
        out_shape=[stack] * 6,
        cost_estimate=pl.CostEstimate(flops=100 * cells, bytes_accessed=60 * cells, transcendentals=0),
        name="weights",
    )(waves, prior_p, prior_q, courant, epsilon, thomsen_delta, tilt_angle, azimuth)

    own, factors = inline_blocks(rows)
    offsets = (-1, 1, -2, 2)
    pieces, gives, start = [own], [], rows * 4
    for offset in offsets:
        give = factors[offset][1]
        pad = give.shape[0] % 2
        pieces.append(np.pad(give, ((0, pad), (0, 0))))
        gives.append((start, 4 * (give.shape[0] + pad)))
        start += gives[-1][1]
    inline = np.kron(np.concatenate(pieces), np.eye(4))
    across = np.concatenate(three_levels(width)).T
    vmem = 48 * 1024 * 1024
    results = pl.pallas_call(
        functools.partial(step_kernel, gives),
        out_shape=[
            jax.ShapeDtypeStruct(wave_p.shape, f32),
            jax.ShapeDtypeStruct(wave_p.shape, f32),
            jax.ShapeDtypeStruct((4 * rows, width), f32),
        ]
        + [jax.ShapeDtypeStruct((count, width), f32) for _, count in gives],
        scratch_shapes=[
            pltpu.VMEM((rows + 8, 8, width), f32),
            pltpu.VMEM((rows + 8, 8, width), f32),
            pltpu.VMEM((rows, 8, width), f32),
            pltpu.VMEM((rows, 8, width), f32),
        ],
        compiler_params=pltpu.CompilerParams(vmem_limit_bytes=vmem),
        cost_estimate=pl.CostEstimate(flops=400 * cells, bytes_accessed=100 * cells, transcendentals=0),
        name="step",
    )(
        waves,
        other,
        left,
        right,
        left_cross,
        right_cross,
        *weights,
        *[jnp.asarray(m) for m in split_bf16(across)],
        *[jnp.asarray(m) for m in split_bf16(inline)],
    )
    next_p, next_q, mine = results[:3]
    received = [
        lax.ppermute(send, "xy", [(i, (i - offset) % size) for i in range(size)])
        for offset, send in zip(offsets, results[3:])
    ]
    outs = pl.pallas_call(
        functools.partial(finish_kernel, [factors[offset][0] for offset in offsets]),
        out_shape=[
            jax.ShapeDtypeStruct((count, layers, width), f32)
            for count in (rows // 2, rows // 4, rows // 8, rows // 8)
        ],
        name="finish",
    )(mine, *received)
    return (next_p, next_q, *outs)


def solution(mesh):
    split = P(("shot", "xy"), "gz", None)
    shared = P("xy", "gz", None)
    return jax.shard_map(
        functools.partial(body, mesh.shape["xy"]),
        mesh=mesh,
        in_specs=(split,) * 4 + (shared,) * 5,
        out_specs=(split,) * 6,
        check_vma=False,
    )
```

time: 77.7 us -> 45 us (0.58)
  blocking collectives: 24.8 us -> 0 us
  other arithmetic: 18.6 us -> 1.19 us
  starting transfers between devices: 10.5 us -> 22 us
  Pallas kernels: 0 us -> 10.3 us
  local copies, waits for them, and re-layouts: 15.5 us -> 8.14 us
  waiting for transfers between devices: 6.47 us -> 1.99 us
    all_to_all x2 -> x0, blocking collectives: 24.8 us -> none  [the longest x1 14 us: body(): lax.all_to_all(flattened, 'xy', split_axis=1, concat_axis=0, tiled=True)]
    add x18 -> x0, other arithmetic: 12.4 us -> none  [the longest x1 10.8 us: advance(): next_q = 2.0 * wave_q - prior_q + speed * (root * h_two_p + h_one_q)]
    ppermute x4 -> x9, starting transfers between devices: 10.5 us -> 22 us  [the longest x4 8.55 us: body(): lax.ppermute(send, 'xy', [(i, (i - offset) % size) for i in range(size)])]
    pallas_call x0 -> x3, Pallas kernels: none -> 10.3 us  [the longest x1 5.39 us: body(): pl.pallas_call(functools.partial(step_kernel, gives), out_shape=[jax.Shap...]
    unnamed x23 -> x38, local copies, waits for them, and re-layouts: 0.9 us -> 8.14 us
    slice x50 -> x0, local copies, waits for them, and re-layouts: 5.42 us -> none  [the longest x2 2.03 us: lift_first(): split[:, 0]]
    ppermute x4 -> x9, waiting for transfers between devices: 6.47 us -> 1.99 us  [the longest x4 1.98 us: body(): lax.ppermute(send, 'xy', [(i, (i - offset) % size) for i in range(size)])]
    concatenate x32 -> x0, local copies, waits for them, and re-layouts: 3.91 us -> none  [the longest x8 1.69 us: lift_last(): jnp.roll(field, -1, axis=-1)]
  transfers between devices with their start and end apart: 4 -> 9, of which waited for: 3 -> 1; matrix products, arithmetic and copies ran while one was open for 0% -> 0% of each run, Pallas kernels for 0% -> 7%
where the time goes in v1:
time: 45 us; the launch traced here: 44.5 us
  starting transfers between devices  22 us (49%)
  Pallas kernels  10.3 us (23%)
  local copies, waits for them, and re-layouts  8.14 us (18%)
  waiting for transfers between devices  1.99 us (4%)
  other arithmetic  1.19 us (3%)
  between operations  0.85 us (2%)
    ppermute x4, starting transfers between devices, body(): lax.ppermute(send, 'xy', [(i, (i - offset) % size) for i in range(size)])  8.55 us
    unnamed x38, local copies, waits for them, and re-layouts  8.14 us
    ppermute x1, starting transfers between devices, body(): left_cross = lax.ppermute(last, ('xy', 'gz'), crossed(up))  5.77 us
    pallas_call x1, Pallas kernels, body(): pl.pallas_call(functools.partial(step_kernel, gives), out_shape=[jax.Shap...  5.39 us
    ppermute x1, starting transfers between devices, body(): left = lax.ppermute(last, 'xy', up)  4.59 us
    pallas_call x1, Pallas kernels, body(): pl.pallas_call(weights_kernel, out_shape=[stack] * 6, cost_estimate=pl.Co...  3.08 us
    ppermute x4, waiting for transfers between devices, body(): lax.ppermute(send, 'xy', [(i, (i - offset) % size) for i in range(size)])  1.98 us
    pallas_call x1, Pallas kernels, body(): pl.pallas_call(functools.partial(finish_kernel, [factors[offset][0] for o...  1.8 us
  transfers between devices with their start and end apart: 9, of which 1 were waited for; matrix products, arithmetic and copies ran while one was open for 0% of the time, Pallas kernels for 7%

profile of v1, /device:TPU:0, one launch (start us, length us, event | category | flops | bytes accessed | tf_op | source)
XLA Modules:
  0.0 44.5 jit_solution(10060984712812944446)
XLA Ops:
  0.6 0.0 copy-start.13
  0.6 0.0 copy-start.14
  0.7 0.0 copy-start.3
  0.7 1.2 %pad_maximum_fusion.waves = f32[16,8,640]{2,1,0:T(8,128)S(1)} fusion(f32[16,4,640]{2,1,0:T(4,128)} %param.14, f32[16,4,640]{2,1,0:T(4,128)} %param.13), kind=kLoop, calls=%fused_computation.2 | loop fusion | flops 81920 | bytes 655360 | tf_op jit(solution)/shard_map/concatenate | solution.py:260
  1.8 0.0 copy-start
  1.8 0.0 copy-start.2
  1.8 0.5 %collective-permute-start = (f32[16,8,640]{2,1,0:T(8,128)S(1)}, f32[16,8,640]{2,1,0:T(8,128)S(1)}, u32[]{:S(2)}, u32[]{:S(2)}) collective-permute-start(f32[16,8,640]{2,1,0:T(8,128)S(1)} %pad_maximum_fusion.waves), channel_id=1, source_target_pairs={{0,1},{1,0},{2,3},{3,2},{4,5},{5,4},{6,7},{7,6},{8,9},{9,8},{10,11... | collective-permute-start | bytes 983048 | tf_op jit(solution)/shard_map/ppermute | solution.py:268
  2.4 0.0 copy-done.13
  2.4 0.0 copy-done.14
  2.4 1.3 %collective-permute-start.4 = (f32[4,8,640]{2,1,0:T(8,128)S(1)}, f32[4,8,640]{2,1,0:T(8,128)S(1)}, u32[]{:S(2)}, u32[]{:S(2)}) collective-permute-start(f32[4,8,640]{2,1,0:T(8,128)S(1)} %get-tuple-element.40), channel_id=1, source_target_pairs={{2,1},{3,0},{4,3},{5,2},{6,5},{7,4},{8,7},{9,6},{10,9},{11,8},{12,... | collective-permute-start | bytes 245768 | tf_op jit(solution)/shard_map/ppermute | solution.py:272
  3.7 1.3 %collective-permute-start.2 = (f32[4,8,640]{2,1,0:T(8,128)S(1)}, f32[4,8,640]{2,1,0:T(8,128)S(1)}, u32[]{:S(2)}, u32[]{:S(2)}) collective-permute-start(f32[4,8,640]{2,1,0:T(8,128)S(1)} %get-tuple-element.40), channel_id=1, source_target_pairs={{2,0},{4,2},{6,4},{8,6},{10,8},{12,10},{14,12},{3,1},{5,3},{7,5},{... | collective-permute-start | bytes 245768 | tf_op jit(solution)/shard_map/ppermute | solution.py:270
  5.0 5.8 %collective-permute-start.3 = (f32[4,8,640]{2,1,0:T(8,128)S(1)}, f32[4,8,640]{2,1,0:T(8,128)S(1)}, u32[]{:S(2)}, u32[]{:S(2)}) collective-permute-start(f32[4,8,640]{2,1,0:T(8,128)S(1)} %get-tuple-element.41), channel_id=1, source_target_pairs={{0,3},{1,2},{2,5},{3,4},{4,7},{5,6},{6,9},{7,8},{8,11},{9,10},{10,... | collective-permute-start | bytes 245768 | tf_op jit(solution)/shard_map/ppermute | solution.py:271
  10.8 4.6 %collective-permute-start.1 = (f32[4,8,640]{2,1,0:T(8,128)S(1)}, f32[4,8,640]{2,1,0:T(8,128)S(1)}, u32[]{:S(2)}, u32[]{:S(2)}) collective-permute-start(f32[4,8,640]{2,1,0:T(8,128)S(1)} %get-tuple-element.41), channel_id=1, source_target_pairs={{0,2},{2,4},{4,6},{6,8},{8,10},{10,12},{12,14},{1,3},{3,5},{5,7},{... | collective-permute-start | bytes 245768 | tf_op jit(solution)/shard_map/ppermute | solution.py:269
  15.4 0.0 copy-done
  15.4 0.0 copy-start.11
  15.4 0.0 copy-start.12
  15.4 3.1 %weights.1 = (f32[16,8,640]{2,1,0:T(8,128)}, f32[16,8,640]{2,1,0:T(8,128)}, f32[16,8,640]{2,1,0:T(8,128)}, f32[16,8,640]{2,1,0:T(8,128)}, f32[16,8,640]{2,1,0:T(8,128)}, /*index=5*/f32[16,8,640]{2,1,0:T(8,128)}) custom-call(f32[16,8,640]{2,1,0:T(8,128)} %copy-done, f32[16,4,640]{2,1,0:T(4,128)} %prior_p.1, f32[16,4,640]{2,1,0:T(4,128)} %prior_q.1, ...), custom_call_target="tpu_custom_call" | custom-call | flops 4096000 | bytes 2457600 | tf_op jit(solution)/shard_map/weights/pallas_call | solution.py:276
  18.5 0.0 collective-permute-done.4.right_cross
  18.5 0.0 collective-permute-done.2.right
  18.5 0.0 collective-permute-done.3.left_cross
  18.5 0.0 collective-permute-done.1.left
  18.5 0.0 collective-permute-done.other
  18.5 0.0 copy-done.3
  18.6 0.0 copy-done.2
  18.6 0.0 copy-done.11
  18.6 0.0 copy-done.12
  18.6 1.0 %copy-done.1 = f32[16,8,640]{2,1,0:T(8,128)S(1)} copy-done((f32[16,8,640]{2,1,0:T(8,128)S(1)}, f32[16,8,640]{2,1,0:T(8,128)}, u32[]{:S(2)}) %copy-start.1) | copy-done | bytes 327704
  19.6 1.0 %copy-done.4 = f32[16,8,640]{2,1,0:T(8,128)S(1)} copy-done((f32[16,8,640]{2,1,0:T(8,128)S(1)}, f32[16,8,640]{2,1,0:T(8,128)}, u32[]{:S(2)}) %copy-start.4) | copy-done | bytes 327704
  20.5 1.0 %copy-done.5 = f32[16,8,640]{2,1,0:T(8,128)S(1)} copy-done((f32[16,8,640]{2,1,0:T(8,128)S(1)}, f32[16,8,640]{2,1,0:T(8,128)}, u32[]{:S(2)}) %copy-start.5) | copy-done | bytes 327704
  21.5 1.0 %copy-done.6 = f32[16,8,640]{2,1,0:T(8,128)S(1)} copy-done((f32[16,8,640]{2,1,0:T(8,128)S(1)}, f32[16,8,640]{2,1,0:T(8,128)}, u32[]{:S(2)}) %copy-start.6) | copy-done | bytes 327704
  22.5 1.0 %copy-done.7 = f32[16,8,640]{2,1,0:T(8,128)S(1)} copy-done((f32[16,8,640]{2,1,0:T(8,128)S(1)}, f32[16,8,640]{2,1,0:T(8,128)}, u32[]{:S(2)}) %copy-start.7) | copy-done | bytes 327704
  23.5 1.0 %copy-done.8 = f32[16,8,640]{2,1,0:T(8,128)S(1)} copy-done((f32[16,8,640]{2,1,0:T(8,128)S(1)}, f32[16,8,640]{2,1,0:T(8,128)}, u32[]{:S(2)}) %copy-start.8) | copy-done | bytes 327704
  24.4 1.0 %copy-done.9 = f32[16,8,640]{2,1,0:T(8,128)S(1)} copy-done((f32[16,8,640]{2,1,0:T(8,128)S(1)}, f32[16,8,640]{2,1,0:T(8,128)}, u32[]{:S(2)}) %copy-start.9) | copy-done | bytes 327704
  25.4 5.4 %step.1 = (f32[16,4,640]{2,1,0:T(4,128)}, f32[16,4,640]{2,1,0:T(4,128)}, f32[64,640]{1,0:T(8,128)S(1)}, f32[24,640]{1,0:T(8,128)S(1)}, f32[24,640]{1,0:T(8,128)S...) custom-call(f32[16,8,640]{2,1,0:T(8,128)S(1)} %copy-done.1, f32[16,8,640]{2,1,0:T(8,128)S(1)} %collective-permute-done.other, ...), custom_call_target="tpu_custom_call" | custom-call | flops 16384000 | bytes 4096000 | tf_op jit(solution)/shard_map/step/pallas_call | solution.py:295
  30.8 0.7 %copy-done.10 = f32[64,640]{1,0:T(8,128)} copy-done((f32[64,640]{1,0:T(8,128)}, f32[64,640]{1,0:T(8,128)S(1)}, u32[]{:S(2)}) %copy-start.10) | copy-done | bytes 163864
  31.5 1.7 %collective-permute-start.5 = (f32[24,640]{1,0:T(8,128)S(1)}, f32[24,640]{1,0:T(8,128)S(1)}, u32[]{:S(2)}, u32[]{:S(2)}) collective-permute-start(f32[24,640]{1,0:T(8,128)S(1)} %get-tuple-element.32), channel_id=1, source_target_pairs={{0,2},{2,4},{4,6},{6,8},{8,10},{10,12},{12,14},{14,0},{1,3},{3,5},... | collective-permute-start | bytes 184328 | tf_op jit(solution)/shard_map/ppermute | solution.py:325
  33.2 3.0 %collective-permute-start.6 = (f32[24,640]{1,0:T(8,128)S(1)}, f32[24,640]{1,0:T(8,128)S(1)}, u32[]{:S(2)}, u32[]{:S(2)}) collective-permute-start(f32[24,640]{1,0:T(8,128)S(1)} %get-tuple-element.33), channel_id=1, source_target_pairs={{0,14},{2,0},{4,2},{6,4},{8,6},{10,8},{12,10},{14,12},{1,15},{3,1}... | collective-permute-start | bytes 184328 | tf_op jit(solution)/shard_map/ppermute | solution.py:325
  36.2 1.1 %collective-permute-start.7 = (f32[8,640]{1,0:T(8,128)S(1)}, f32[8,640]{1,0:T(8,128)S(1)}, u32[]{:S(2)}, u32[]{:S(2)}) collective-permute-start(f32[8,640]{1,0:T(8,128)S(1)} %get-tuple-element.34), channel_id=1, source_target_pairs={{0,4},{2,6},{4,8},{6,10},{8,12},{10,14},{12,0},{14,2},{1,5},{3,7},... | collective-permute-start | bytes 61448 | tf_op jit(solution)/shard_map/ppermute | solution.py:325
  37.3 2.7 %collective-permute-start.8 = (f32[8,640]{1,0:T(8,128)S(1)}, f32[8,640]{1,0:T(8,128)S(1)}, u32[]{:S(2)}, u32[]{:S(2)}) collective-permute-start(f32[8,640]{1,0:T(8,128)S(1)} %get-tuple-element.35), channel_id=1, source_target_pairs={{0,12},{2,14},{4,0},{6,2},{8,4},{10,6},{12,8},{14,10},{1,13},{3,15... | collective-permute-start | bytes 61448 | tf_op jit(solution)/shard_map/ppermute | solution.py:325
  40.0 2.0 %collective-permute-done.7.rest_2_ = f32[8,640]{1,0:T(8,128)S(1)} collective-permute-done((f32[8,640]{1,0:T(8,128)S(1)}, f32[8,640]{1,0:T(8,128)S(1)}, u32[]{:S(2)}, u32[]{:S(2)}) %collective-permute-start.7) | collective-permute-done | bytes 20512 | tf_op jit(solution)/shard_map/ppermute | solution.py:325
  42.0 0.0 collective-permute-done.8.rest_3_
  42.0 0.0 collective-permute-done.5.rest_0_
  42.0 0.0 collective-permute-done.6.rest_1_
  42.0 0.6 %copy-done.17 = f32[8,640]{1,0:T(8,128)} copy-done((f32[8,640]{1,0:T(8,128)}, f32[8,640]{1,0:T(8,128)S(1)}, u32[]{:S(2)}) %copy-start.17) | copy-done | bytes 20504
  42.6 0.0 copy-done.18
  42.6 0.0 copy-done.15
  42.6 0.0 copy-done.16
  42.7 1.8 %finish.1 = (f32[8,4,640]{2,1,0:T(4,128)}, f32[4,4,640]{2,1,0:T(4,128)}, f32[2,4,640]{2,1,0:T(4,128)}, f32[2,4,640]{2,1,0:T(4,128)}) custom-call(f32[64,640]{1,0:T(8,128)} %copy-done.10, f32[24,640]{1,0:T(8,128)} %copy-done.15, f32[24,640]{1,0:T(8,128)} %copy-done.16, f32[8,640]{1,0:T(8,128)} %copy-done.17, f32[8,640]{1,0:T(8,128)} %copy-done.18), custom_call_target="tpu_custom_call" | custom-call | tf_op jit(solution)/shard_map/finish/pallas_call | solution.py:328
  (13 shorter events, 0.1 us)
Async XLA Ops:
  0.6 1.7 %copy-start.13 = (f32[16,4,640]{2,1,0:T(4,128)S(1)}, f32[16,4,640]{2,1,0:T(4,128)}, u32[]{:S(2)}) copy-start(f32[16,4,640]{2,1,0:T(4,128)} %param.14) | copy-start | bytes 491524
  0.6 1.7 %copy-start.14 = (f32[16,4,640]{2,1,0:T(4,128)S(1)}, f32[16,4,640]{2,1,0:T(4,128)}, u32[]{:S(2)}) copy-start(f32[16,4,640]{2,1,0:T(4,128)} %param.13) | copy-start | bytes 491524
  0.7 17.9 %copy-start.3 = (bf16[640,640]{1,0:T(8,128)(2,1)S(1)}, bf16[640,640]{1,0:T(8,128)(2,1)}, u32[]{:S(2)}) copy-start(bf16[640,640]{1,0:T(8,128)(2,1)} %constant.8.clone.across_high) | copy-start | bytes 2457604
  1.8 13.6 %copy-start = (f32[16,8,640]{2,1,0:T(8,128)}, f32[16,8,640]{2,1,0:T(8,128)S(1)}, u32[]{:S(2)}) copy-start(f32[16,8,640]{2,1,0:T(8,128)S(1)} %pad_maximum_fusion.waves) | copy-start | bytes 983044
  1.8 16.7 %copy-start.2 = (bf16[640,640]{1,0:T(8,128)(2,1)S(1)}, bf16[640,640]{1,0:T(8,128)(2,1)}, u32[]{:S(2)}) copy-start(bf16[640,640]{1,0:T(8,128)(2,1)} %constant.9.clone.across_low) | copy-start | bytes 2457604
  1.8 16.7 %collective-permute-start = (f32[16,8,640]{2,1,0:T(8,128)S(1)}, f32[16,8,640]{2,1,0:T(8,128)S(1)}, u32[]{:S(2)}, u32[]{:S(2)}) collective-permute-start(f32[16,8,640]{2,1,0:T(8,128)S(1)} %pad_maximum_fusion.waves), channel_id=1, source_target_pairs={{0,1},{1,0},{2,3},{3,2},{4,5},{5,4},{6,7},{7,6},{8,9},{9,8},{10,11... | collective-permute-start | bytes 983048 | tf_op jit(solution)/shard_map/ppermute | solution.py:268
  2.4 16.1 %collective-permute-start.4 = (f32[4,8,640]{2,1,0:T(8,128)S(1)}, f32[4,8,640]{2,1,0:T(8,128)S(1)}, u32[]{:S(2)}, u32[]{:S(2)}) collective-permute-start(f32[4,8,640]{2,1,0:T(8,128)S(1)} %get-tuple-element.40), channel_id=1, source_target_pairs={{2,1},{3,0},{4,3},{5,2},{6,5},{7,4},{8,7},{9,6},{10,9},{11,8},{12,... | collective-permute-start | bytes 245768 | tf_op jit(solution)/shard_map/ppermute | solution.py:272
  3.7 14.8 %collective-permute-start.2 = (f32[4,8,640]{2,1,0:T(8,128)S(1)}, f32[4,8,640]{2,1,0:T(8,128)S(1)}, u32[]{:S(2)}, u32[]{:S(2)}) collective-permute-start(f32[4,8,640]{2,1,0:T(8,128)S(1)} %get-tuple-element.40), channel_id=1, source_target_pairs={{2,0},{4,2},{6,4},{8,6},{10,8},{12,10},{14,12},{3,1},{5,3},{7,5},{... | collective-permute-start | bytes 245768 | tf_op jit(solution)/shard_map/ppermute | solution.py:270
  5.0 13.5 %collective-permute-start.3 = (f32[4,8,640]{2,1,0:T(8,128)S(1)}, f32[4,8,640]{2,1,0:T(8,128)S(1)}, u32[]{:S(2)}, u32[]{:S(2)}) collective-permute-start(f32[4,8,640]{2,1,0:T(8,128)S(1)} %get-tuple-element.41), channel_id=1, source_target_pairs={{0,3},{1,2},{2,5},{3,4},{4,7},{5,6},{6,9},{7,8},{8,11},{9,10},{10,... | collective-permute-start | bytes 245768 | tf_op jit(solution)/shard_map/ppermute | solution.py:271
  10.8 7.7 %collective-permute-start.1 = (f32[4,8,640]{2,1,0:T(8,128)S(1)}, f32[4,8,640]{2,1,0:T(8,128)S(1)}, u32[]{:S(2)}, u32[]{:S(2)}) collective-permute-start(f32[4,8,640]{2,1,0:T(8,128)S(1)} %get-tuple-element.41), channel_id=1, source_target_pairs={{0,2},{2,4},{4,6},{6,8},{8,10},{10,12},{12,14},{1,3},{3,5},{5,7},{... | collective-permute-start | bytes 245768 | tf_op jit(solution)/shard_map/ppermute | solution.py:269
  15.4 3.2 %copy-start.11 = (bf16[128,64]{1,0:T(8,128)(2,1)S(1)}, bf16[128,64]{1,0:T(8,128)(2,1)}, u32[]{:S(2)}) copy-start(bf16[128,64]{1,0:T(8,128)(2,1)} %constant.11.clone.inline_low) | copy-start | bytes 49156
  15.4 3.2 %copy-start.12 = (bf16[128,64]{1,0:T(8,128)(2,1)S(1)}, bf16[128,64]{1,0:T(8,128)(2,1)}, u32[]{:S(2)}) copy-start(bf16[128,64]{1,0:T(8,128)(2,1)} %constant.10.clone.inline_high) | copy-start | bytes 49156
  18.6 1.0 %copy-start.1 = (f32[16,8,640]{2,1,0:T(8,128)S(1)}, f32[16,8,640]{2,1,0:T(8,128)}, u32[]{:S(2)}) copy-start(f32[16,8,640]{2,1,0:T(8,128)} %copy-done) | copy-start | bytes 983044
  19.6 1.0 %copy-start.4 = (f32[16,8,640]{2,1,0:T(8,128)S(1)}, f32[16,8,640]{2,1,0:T(8,128)}, u32[]{:S(2)}) copy-start(f32[16,8,640]{2,1,0:T(8,128)} %get-tuple-element.23.axis_x) | copy-start | bytes 983044
  20.5 1.0 %copy-start.5 = (f32[16,8,640]{2,1,0:T(8,128)S(1)}, f32[16,8,640]{2,1,0:T(8,128)}, u32[]{:S(2)}) copy-start(f32[16,8,640]{2,1,0:T(8,128)} %get-tuple-element.24.axis_y) | copy-start | bytes 983044
  21.5 1.0 %copy-start.6 = (f32[16,8,640]{2,1,0:T(8,128)S(1)}, f32[16,8,640]{2,1,0:T(8,128)}, u32[]{:S(2)}) copy-start(f32[16,8,640]{2,1,0:T(8,128)} %get-tuple-element.25.axis_z) | copy-start | bytes 983044
  22.5 1.0 %copy-start.7 = (f32[16,8,640]{2,1,0:T(8,128)S(1)}, f32[16,8,640]{2,1,0:T(8,128)}, u32[]{:S(2)}) copy-start(f32[16,8,640]{2,1,0:T(8,128)} %get-tuple-element.26.gain_a) | copy-start | bytes 983044
  23.5 1.0 %copy-start.8 = (f32[16,8,640]{2,1,0:T(8,128)S(1)}, f32[16,8,640]{2,1,0:T(8,128)}, u32[]{:S(2)}) copy-start(f32[16,8,640]{2,1,0:T(8,128)} %get-tuple-element.27.gain_b) | copy-start | bytes 983044
  24.4 1.0 %copy-start.9 = (f32[16,8,640]{2,1,0:T(8,128)S(1)}, f32[16,8,640]{2,1,0:T(8,128)}, u32[]{:S(2)}) copy-start(f32[16,8,640]{2,1,0:T(8,128)} %get-tuple-element.28.base) | copy-start | bytes 983044
  30.8 0.7 %copy-start.10 = (f32[64,640]{1,0:T(8,128)}, f32[64,640]{1,0:T(8,128)S(1)}, u32[]{:S(2)}) copy-start(f32[64,640]{1,0:T(8,128)S(1)} %get-tuple-element.31.mine) | copy-start | bytes 491524
  31.5 10.5 %collective-permute-start.5 = (f32[24,640]{1,0:T(8,128)S(1)}, f32[24,640]{1,0:T(8,128)S(1)}, u32[]{:S(2)}, u32[]{:S(2)}) collective-permute-start(f32[24,640]{1,0:T(8,128)S(1)} %get-tuple-element.32), channel_id=1, source_target_pairs={{0,2},{2,4},{4,6},{6,8},{8,10},{10,12},{12,14},{14,0},{1,3},{3,5},... | collective-permute-start | bytes 184328 | tf_op jit(solution)/shard_map/ppermute | solution.py:325
  33.2 8.8 %collective-permute-start.6 = (f32[24,640]{1,0:T(8,128)S(1)}, f32[24,640]{1,0:T(8,128)S(1)}, u32[]{:S(2)}, u32[]{:S(2)}) collective-permute-start(f32[24,640]{1,0:T(8,128)S(1)} %get-tuple-element.33), channel_id=1, source_target_pairs={{0,14},{2,0},{4,2},{6,4},{8,6},{10,8},{12,10},{14,12},{1,15},{3,1}... | collective-permute-start | bytes 184328 | tf_op jit(solution)/shard_map/ppermute | solution.py:325
  36.2 5.8 %collective-permute-start.7 = (f32[8,640]{1,0:T(8,128)S(1)}, f32[8,640]{1,0:T(8,128)S(1)}, u32[]{:S(2)}, u32[]{:S(2)}) collective-permute-start(f32[8,640]{1,0:T(8,128)S(1)} %get-tuple-element.34), channel_id=1, source_target_pairs={{0,4},{2,6},{4,8},{6,10},{8,12},{10,14},{12,0},{14,2},{1,5},{3,7},... | collective-permute-start | bytes 61448 | tf_op jit(solution)/shard_map/ppermute | solution.py:325
  37.3 4.7 %collective-permute-start.8 = (f32[8,640]{1,0:T(8,128)S(1)}, f32[8,640]{1,0:T(8,128)S(1)}, u32[]{:S(2)}, u32[]{:S(2)}) collective-permute-start(f32[8,640]{1,0:T(8,128)S(1)} %get-tuple-element.35), channel_id=1, source_target_pairs={{0,12},{2,14},{4,0},{6,2},{8,4},{10,6},{12,8},{14,10},{1,13},{3,15... | collective-permute-start | bytes 61448 | tf_op jit(solution)/shard_map/ppermute | solution.py:325
  42.0 0.6 %copy-start.17 = (f32[8,640]{1,0:T(8,128)}, f32[8,640]{1,0:T(8,128)S(1)}, u32[]{:S(2)}) copy-start(f32[8,640]{1,0:T(8,128)S(1)} %collective-permute-done.7.rest_2_) | copy-start | bytes 61444
  42.0 0.6 %copy-start.18 = (f32[8,640]{1,0:T(8,128)}, f32[8,640]{1,0:T(8,128)S(1)}, u32[]{:S(2)}) copy-start(f32[8,640]{1,0:T(8,128)S(1)} %collective-permute-done.8.rest_3_) | copy-start | bytes 61444
  42.0 0.6 %copy-start.15 = (f32[24,640]{1,0:T(8,128)}, f32[24,640]{1,0:T(8,128)S(1)}, u32[]{:S(2)}) copy-start(f32[24,640]{1,0:T(8,128)S(1)} %collective-permute-done.5.rest_0_) | copy-start | bytes 184324
  42.0 0.6 %copy-start.16 = (f32[24,640]{1,0:T(8,128)}, f32[24,640]{1,0:T(8,128)S(1)}, u32[]{:S(2)}) copy-start(f32[24,640]{1,0:T(8,128)S(1)} %collective-permute-done.6.rest_1_) | copy-start | bytes 184324

commit v2 on v1

--- a/solution.py
+++ b/solution.py
@@ -150,10 +150,8 @@
     gives,
     waves,
     other,
-    left,
-    right,
-    left_cross,
-    right_cross,
+    edges,
+    edges_other,
     axis_x,
     axis_y,
     axis_z,
@@ -180,11 +178,11 @@
 
     for x in range(rows + 8):
         if x < 4:
-            own, far = left[x], left_cross[x]
+            own, far = edges[x], edges_other[x]
         elif x < rows + 4:
             own, far = waves[x - 4], other[x - 4]
         else:
-            own, far = right[x - rows - 4], right_cross[x - rows - 4]
+            own, far = edges[x - rows], edges_other[x - rows]
         ext[x] = own
         up, down = far * above, far * below
         ahead, behind = [], []
@@ -261,22 +259,21 @@
     up = [(i, i + 1) for i in range(size - 1)]
     down = [(i + 1, i) for i in range(size - 1)]
 
-    def crossed(pairs):
-        return [(2 * i + g, 2 * j + 1 - g) for i, j in pairs for g in range(2)]
-
     last, leading = waves[rows - 4 :], waves[:4]
     other = lax.ppermute(waves, "gz", [(0, 1), (1, 0)])
     left = lax.ppermute(last, "xy", up)
     right = lax.ppermute(leading, "xy", down)
-    left_cross = lax.ppermute(last, ("xy", "gz"), crossed(up))
-    right_cross = lax.ppermute(leading, ("xy", "gz"), crossed(down))
+    edges = jnp.concatenate([left, right], axis=0)
+    edges_other = lax.ppermute(edges, "gz", [(0, 1), (1, 0)])
 
     stack = jax.ShapeDtypeStruct((rows, 8, width), f32)
     cells = rows * layers * width
+    params = pltpu.CompilerParams(vmem_limit_bytes=16 * 1024 * 1024)
     weights = pl.pallas_call(
         weights_kernel,
         out_shape=[stack] * 6,
         cost_estimate=pl.CostEstimate(flops=100 * cells, bytes_accessed=60 * cells, transcendentals=0),
+        compiler_params=params,
         name="weights",
     )(waves, prior_p, prior_q, courant, epsilon, thomsen_delta, tilt_angle, azimuth)
 
@@ -291,7 +288,6 @@
         start += gives[-1][1]
     inline = np.kron(np.concatenate(pieces), np.eye(4))
     across = np.concatenate(three_levels(width)).T
-    vmem = 48 * 1024 * 1024
     results = pl.pallas_call(
         functools.partial(step_kernel, gives),
         out_shape=[
@@ -306,16 +302,14 @@
             pltpu.VMEM((rows, 8, width), f32),
             pltpu.VMEM((rows, 8, width), f32),
         ],
-        compiler_params=pltpu.CompilerParams(vmem_limit_bytes=vmem),
+        compiler_params=params,
         cost_estimate=pl.CostEstimate(flops=400 * cells, bytes_accessed=100 * cells, transcendentals=0),
         name="step",
     )(
         waves,
         other,
-        left,
-        right,
-        left_cross,
-        right_cross,
+        edges,
+        edges_other,
         *weights,
         *[jnp.asarray(m) for m in split_bf16(across)],
         *[jnp.asarray(m) for m in split_bf16(inline)],
@@ -331,6 +325,7 @@
             jax.ShapeDtypeStruct((count, layers, width), f32)
             for count in (rows // 2, rows // 4, rows // 8, rows // 8)
         ],
+        compiler_params=params,
         name="finish",
     )(mine, *received)
     return (next_p, next_q, *outs)

time: 45 us -> 30.9 us (0.69)
  local copies, waits for them, and re-layouts: 8.14 us -> 0.08 us
  starting transfers between devices: 22 us -> 16.3 us
  Pallas kernels: 10.3 us -> 6.94 us
  waiting for transfers between devices: 1.99 us -> 4.39 us
  other arithmetic: 1.19 us -> 2.1 us
    unnamed x38 -> x23, local copies, waits for them, and re-layouts: 8.14 us -> 0.07 us
    ppermute x2 -> x1, starting transfers between devices: 7.06 us -> 0.07 us  [body(): edges_other = lax.ppermute(edges, 'gz', [(0, 1), (1, 0)])]
    pallas_call x1, Pallas kernels: 3.08 us -> 0.71 us  [body(): pl.pallas_call(weights_kernel, out_shape=[stack] * 6, cost_estimate=pl.Co...]
    ppermute x1, waiting for transfers between devices: 0.01 us -> 1.26 us  [body(): left = lax.ppermute(last, 'xy', up)]
    ppermute x1, starting transfers between devices: 4.59 us -> 5.61 us  [body(): left = lax.ppermute(last, 'xy', up)]
    pallas_call x1, Pallas kernels: 1.8 us -> 0.83 us  [body(): pl.pallas_call(functools.partial(finish_kernel, [factors[offset][0] for o...]
    concatenate x2, other arithmetic: 1.19 us -> 2.1 us  [body(): waves = jnp.concatenate([wave_p, wave_q], axis=1)]
    ppermute x4, starting transfers between devices: 8.55 us -> 9.3 us  [body(): lax.ppermute(send, 'xy', [(i, (i - offset) % size) for i in range(size)])]
  transfers between devices with their start and end apart: 9 -> 8, of which waited for: 1 -> 3; matrix products, arithmetic and copies ran while one was open for 0% -> 4% of each run, Pallas kernels for 7% -> 2%
where the time goes in v2:
time: 30.9 us; the launch traced here: 30.7 us
  starting transfers between devices  16.3 us (53%)
  Pallas kernels  6.94 us (22%)
  waiting for transfers between devices  4.39 us (14%)
  other arithmetic  2.1 us (7%)
  between operations  0.86 us (3%)
    ppermute x4, starting transfers between devices, body(): lax.ppermute(send, 'xy', [(i, (i - offset) % size) for i in range(size)])  9.3 us
    ppermute x1, starting transfers between devices, body(): left = lax.ppermute(last, 'xy', up)  5.61 us
    pallas_call x1, Pallas kernels, body(): pl.pallas_call(functools.partial(step_kernel, gives), out_shape=[jax.Shap...  5.4 us
    ppermute x4, waiting for transfers between devices, body(): lax.ppermute(send, 'xy', [(i, (i - offset) % size) for i in range(size)])  2.55 us
    concatenate x2, other arithmetic, body(): waves = jnp.concatenate([wave_p, wave_q], axis=1)  2.1 us
    ppermute x1, starting transfers between devices, body(): right = lax.ppermute(leading, 'xy', down)  1.29 us
    ppermute x1, waiting for transfers between devices, body(): left = lax.ppermute(last, 'xy', up)  1.26 us
    pallas_call x1, Pallas kernels, body(): pl.pallas_call(functools.partial(finish_kernel, [factors[offset][0] for o...  0.83 us
  transfers between devices with their start and end apart: 8, of which 3 were waited for; matrix products, arithmetic and copies ran while one was open for 4% of the time, Pallas kernels for 2%

profile of v2, /device:TPU:0, one launch (start us, length us, event | category | flops | bytes accessed | tf_op | source)
XLA Modules:
  0.0 30.7 jit_solution(16259980362740235470)
XLA Ops:
  0.6 0.0 copy-start.4
  0.6 0.0 copy-start.5
  0.7 0.0 copy-start.6
  0.7 0.0 copy-start.7
  0.7 0.0 copy-start.8
  0.7 1.0 %fusion.1 = (f32[4,8,640]{2,1,0:T(8,128)S(1)}, f32[4,8,640]{2,1,0:T(8,128)S(1)}) fusion(f32[16,4,640]{2,1,0:T(4,128)} %param.13, f32[16,4,640]{2,1,0:T(4,128)} %param.14), kind=kLoop, calls=%fused_computation.6 | loop fusion | flops 40960 | bytes 491520 | tf_op jit(solution)/shard_map/concatenate | solution.py:258
  1.6 1.3 %collective-permute-start.2 = (f32[4,8,640]{2,1,0:T(8,128)S(1)}, f32[4,8,640]{2,1,0:T(8,128)S(1)}, u32[]{:S(2)}, u32[]{:S(2)}) collective-permute-start(f32[4,8,640]{2,1,0:T(8,128)S(1)} %get-tuple-element.40), channel_id=1, source_target_pairs={{2,0},{4,2},{6,4},{8,6},{10,8},{12,10},{14,12},{3,1},{5,3},{7,5},{... | collective-permute-start | bytes 245768 | tf_op jit(solution)/shard_map/ppermute | solution.py:265
  2.9 0.0 copy-start.2
  3.0 0.0 copy-start.3
  3.0 5.6 %collective-permute-start.1 = (f32[4,8,640]{2,1,0:T(8,128)S(1)}, f32[4,8,640]{2,1,0:T(8,128)S(1)}, u32[]{:S(2)}, u32[]{:S(2)}) collective-permute-start(f32[4,8,640]{2,1,0:T(8,128)S(1)} %get-tuple-element.41), channel_id=1, source_target_pairs={{0,2},{2,4},{4,6},{6,8},{8,10},{10,12},{12,14},{1,3},{3,5},{5,7},{... | collective-permute-start | bytes 245768 | tf_op jit(solution)/shard_map/ppermute | solution.py:264
  8.6 0.0 copy-start.1
  8.6 1.1 %pad_maximum_fusion.waves = f32[16,8,640]{2,1,0:T(8,128)S(1)} fusion(f32[16,4,640]{2,1,0:T(4,128)} %param.14, f32[16,4,640]{2,1,0:T(4,128)} %param.13), kind=kLoop, calls=%fused_computation.2 | loop fusion | flops 81920 | bytes 655360 | tf_op jit(solution)/shard_map/concatenate | solution.py:258
  9.7 0.0 copy-start
  9.7 0.1 collective-permute-start
  9.8 1.3 %collective-permute-done.1 = f32[4,8,640]{2,1,0:T(8,128)S(1)} collective-permute-done((f32[4,8,640]{2,1,0:T(8,128)S(1)}, f32[4,8,640]{2,1,0:T(8,128)S(1)}, u32[]{:S(2)}, u32[]{:S(2)}) %collective-permute-start.1) | collective-permute-done | bytes 81952 | tf_op jit(solution)/shard_map/ppermute | solution.py:264
  11.1 0.0 collective-permute-done.2
  11.1 0.1 collective-permute-start.3
  11.2 0.0 copy-done.4
  11.2 0.0 copy-done.5
  11.2 0.0 copy-done.6
  11.2 0.0 copy-done.7
  11.2 0.0 copy-done.8
  11.2 0.0 copy-done.2
  11.3 0.0 copy-done.3
  11.3 0.0 copy-start.9
  11.3 0.0 copy-start.10
  11.3 0.7 %weights.1 = (f32[16,8,640]{2,1,0:T(8,128)S(1)}, f32[16,8,640]{2,1,0:T(8,128)S(1)}, f32[16,8,640]{2,1,0:T(8,128)S(1)}, f32[16,8,640]{2,1,0:T(8,128)S(1)}, f32[16...) custom-call(f32[16,8,640]{2,1,0:T(8,128)S(1)} %pad_maximum_fusion.waves, f32[16,4,640]{2,1,0:T(4,128)S(1)} %copy-done.2, ...), custom_call_target="tpu_custom_call" | custom-call | flops 4096000 | bytes 2457600 | tf_op jit(solution)/shard_map/weights/pallas_call | solution.py:272
  12.0 0.6 %collective-permute-done.3.edges_other = f32[8,8,640]{2,1,0:T(8,128)S(1)} collective-permute-done((f32[8,8,640]{2,1,0:T(8,128)S(1)}, f32[8,8,640]{2,1,0:T(8,128)S(1)}, u32[]{:S(2)}, u32[]{:S(2)}) %collective-permute-start.3) | collective-permute-done | bytes 163872 | tf_op jit(solution)/shard_map/ppermute | solution.py:267
  12.6 0.0 collective-permute-done.other
  12.6 0.0 copy-done.1
  12.6 0.0 copy-done
  12.6 0.0 copy-done.9
  12.6 0.0 copy-done.10
  12.6 5.4 %step.1 = (f32[16,4,640]{2,1,0:T(4,128)}, f32[16,4,640]{2,1,0:T(4,128)}, f32[64,640]{1,0:T(8,128)S(1)}, f32[24,640]{1,0:T(8,128)S(1)}, f32[24,640]{1,0:T(8,128)S...) custom-call(f32[16,8,640]{2,1,0:T(8,128)S(1)} %pad_maximum_fusion.waves, f32[16,8,640]{2,1,0:T(8,128)S(1)} %collective-permute-done.other, ...), custom_call_target="tpu_custom_call" | custom-call | flops 16384000 | bytes 4096000 | tf_op jit(solution)/shard_map/step/pallas_call | solution.py:291
  18.0 2.5 %collective-permute-start.4 = (f32[24,640]{1,0:T(8,128)S(1)}, f32[24,640]{1,0:T(8,128)S(1)}, u32[]{:S(2)}, u32[]{:S(2)}) collective-permute-start(f32[24,640]{1,0:T(8,128)S(1)} %get-tuple-element.32), channel_id=1, source_target_pairs={{0,2},{2,4},{4,6},{6,8},{8,10},{10,12},{12,14},{14,0},{1,3},{3,5},... | collective-permute-start | bytes 184328 | tf_op jit(solution)/shard_map/ppermute | solution.py:319
  20.5 3.0 %collective-permute-start.5 = (f32[24,640]{1,0:T(8,128)S(1)}, f32[24,640]{1,0:T(8,128)S(1)}, u32[]{:S(2)}, u32[]{:S(2)}) collective-permute-start(f32[24,640]{1,0:T(8,128)S(1)} %get-tuple-element.33), channel_id=1, source_target_pairs={{0,14},{2,0},{4,2},{6,4},{8,6},{10,8},{12,10},{14,12},{1,15},{3,1}... | collective-permute-start | bytes 184328 | tf_op jit(solution)/shard_map/ppermute | solution.py:319
  23.5 1.7 %collective-permute-start.6 = (f32[8,640]{1,0:T(8,128)S(1)}, f32[8,640]{1,0:T(8,128)S(1)}, u32[]{:S(2)}, u32[]{:S(2)}) collective-permute-start(f32[8,640]{1,0:T(8,128)S(1)} %get-tuple-element.34), channel_id=1, source_target_pairs={{0,4},{2,6},{4,8},{6,10},{8,12},{10,14},{12,0},{14,2},{1,5},{3,7},... | collective-permute-start | bytes 61448 | tf_op jit(solution)/shard_map/ppermute | solution.py:319
  25.2 2.1 %collective-permute-start.7 = (f32[8,640]{1,0:T(8,128)S(1)}, f32[8,640]{1,0:T(8,128)S(1)}, u32[]{:S(2)}, u32[]{:S(2)}) collective-permute-start(f32[8,640]{1,0:T(8,128)S(1)} %get-tuple-element.35), channel_id=1, source_target_pairs={{0,12},{2,14},{4,0},{6,2},{8,4},{10,6},{12,8},{14,10},{1,13},{3,15... | collective-permute-start | bytes 61448 | tf_op jit(solution)/shard_map/ppermute | solution.py:319
  27.3 2.5 %collective-permute-done.6.rest_2_ = f32[8,640]{1,0:T(8,128)S(1)} collective-permute-done((f32[8,640]{1,0:T(8,128)S(1)}, f32[8,640]{1,0:T(8,128)S(1)}, u32[]{:S(2)}, u32[]{:S(2)}) %collective-permute-start.6) | collective-permute-done | bytes 20512 | tf_op jit(solution)/shard_map/ppermute | solution.py:319
  29.9 0.0 collective-permute-done.7.rest_3_
  29.9 0.0 collective-permute-done.4.rest_0_
  29.9 0.0 collective-permute-done.5.rest_1_
  29.9 0.8 %finish.1 = (f32[8,4,640]{2,1,0:T(4,128)}, f32[4,4,640]{2,1,0:T(4,128)}, f32[2,4,640]{2,1,0:T(4,128)}, f32[2,4,640]{2,1,0:T(4,128)}) custom-call(f32[64,640]{1,0:T(8,128)S(1)} %get-tuple-element.31.mine, f32[24,640]{1,0:T(8,128)S(1)} %collective-permute-done.4.rest_0_, f32[24,640]{1,0:T(8,128)S(1)} %collective-permute-done.5.rest_1_, ...), custom_call_target="tpu_custom_call" | custom-call | tf_op jit(solution)/shard_map/finish/pallas_call | solution.py:322
  (2 shorter events, 0.0 us)
Async XLA Ops:
  0.6 10.6 %copy-start.4 = (bf16[16,4,640]{2,1,0:T(4,128)(2,1)S(1)}, bf16[16,4,640]{2,1,0:T(4,128)(2,1)}, u32[]{:S(2)}) copy-start(bf16[16,4,640]{2,1,0:T(4,128)(2,1)} %courant.1) | copy-start | bytes 245764
  0.6 10.6 %copy-start.5 = (bf16[16,4,640]{2,1,0:T(4,128)(2,1)S(1)}, bf16[16,4,640]{2,1,0:T(4,128)(2,1)}, u32[]{:S(2)}) copy-start(bf16[16,4,640]{2,1,0:T(4,128)(2,1)} %epsilon.1) | copy-start | bytes 245764
  0.7 10.6 %copy-start.6 = (bf16[16,4,640]{2,1,0:T(4,128)(2,1)S(1)}, bf16[16,4,640]{2,1,0:T(4,128)(2,1)}, u32[]{:S(2)}) copy-start(bf16[16,4,640]{2,1,0:T(4,128)(2,1)} %delta.1) | copy-start | bytes 245764
  0.7 10.6 %copy-start.7 = (bf16[16,4,640]{2,1,0:T(4,128)(2,1)S(1)}, bf16[16,4,640]{2,1,0:T(4,128)(2,1)}, u32[]{:S(2)}) copy-start(bf16[16,4,640]{2,1,0:T(4,128)(2,1)} %tilt.1) | copy-start | bytes 245764
  0.7 10.6 %copy-start.8 = (bf16[16,4,640]{2,1,0:T(4,128)(2,1)S(1)}, bf16[16,4,640]{2,1,0:T(4,128)(2,1)}, u32[]{:S(2)}) copy-start(bf16[16,4,640]{2,1,0:T(4,128)(2,1)} %azimuth.1) | copy-start | bytes 245764
  1.6 9.5 %collective-permute-start.2 = (f32[4,8,640]{2,1,0:T(8,128)S(1)}, f32[4,8,640]{2,1,0:T(8,128)S(1)}, u32[]{:S(2)}, u32[]{:S(2)}) collective-permute-start(f32[4,8,640]{2,1,0:T(8,128)S(1)} %get-tuple-element.40), channel_id=1, source_target_pairs={{2,0},{4,2},{6,4},{8,6},{10,8},{12,10},{14,12},{3,1},{5,3},{7,5},{... | collective-permute-start | bytes 245768 | tf_op jit(solution)/shard_map/ppermute | solution.py:265
  2.9 8.3 %copy-start.2 = (f32[16,4,640]{2,1,0:T(4,128)S(1)}, f32[16,4,640]{2,1,0:T(4,128)}, u32[]{:S(2)}) copy-start(f32[16,4,640]{2,1,0:T(4,128)} %prior_p.1) | copy-start | bytes 491524
  3.0 8.3 %copy-start.3 = (f32[16,4,640]{2,1,0:T(4,128)S(1)}, f32[16,4,640]{2,1,0:T(4,128)}, u32[]{:S(2)}) copy-start(f32[16,4,640]{2,1,0:T(4,128)} %prior_q.1) | copy-start | bytes 491524
  3.0 8.1 %collective-permute-start.1 = (f32[4,8,640]{2,1,0:T(8,128)S(1)}, f32[4,8,640]{2,1,0:T(8,128)S(1)}, u32[]{:S(2)}, u32[]{:S(2)}) collective-permute-start(f32[4,8,640]{2,1,0:T(8,128)S(1)} %get-tuple-element.41), channel_id=1, source_target_pairs={{0,2},{2,4},{4,6},{6,8},{8,10},{10,12},{12,14},{1,3},{3,5},{5,7},{... | collective-permute-start | bytes 245768 | tf_op jit(solution)/shard_map/ppermute | solution.py:264
  8.6 4.0 %copy-start.1 = (bf16[640,640]{1,0:T(8,128)(2,1)S(1)}, bf16[640,640]{1,0:T(8,128)(2,1)}, u32[]{:S(2)}) copy-start(bf16[640,640]{1,0:T(8,128)(2,1)} %constant.8.clone.across_high) | copy-start | bytes 2457604
  9.7 2.9 %copy-start = (bf16[640,640]{1,0:T(8,128)(2,1)S(1)}, bf16[640,640]{1,0:T(8,128)(2,1)}, u32[]{:S(2)}) copy-start(bf16[640,640]{1,0:T(8,128)(2,1)} %constant.9.clone.across_low) | copy-start | bytes 2457604
  9.7 2.8 %collective-permute-start = (f32[16,8,640]{2,1,0:T(8,128)S(1)}, f32[16,8,640]{2,1,0:T(8,128)S(1)}, u32[]{:S(2)}, u32[]{:S(2)}) collective-permute-start(f32[16,8,640]{2,1,0:T(8,128)S(1)} %pad_maximum_fusion.waves), channel_id=1, source_target_pairs={{0,1},{1,0},{2,3},{3,2},{4,5},{5,4},{6,7},{7,6},{8,9},{9,8},{10,11... | collective-permute-start | bytes 983048 | tf_op jit(solution)/shard_map/ppermute | solution.py:263
  11.1 1.5 %collective-permute-start.3 = (f32[8,8,640]{2,1,0:T(8,128)S(1)}, f32[8,8,640]{2,1,0:T(8,128)S(1)}, u32[]{:S(2)}, u32[]{:S(2)}) collective-permute-start(f32[8,8,640]{2,1,0:T(8,128)S(1)} %constant_dynamic-update-slice_fusion.edges), channel_id=1, source_target_pairs={{0,1},{1,0},{2,3},{3,2},{4,5},{5,4},{6,7},{7,6},{8,9},{9,8},{10,11... | collective-permute-start | bytes 491528 | tf_op jit(solution)/shard_map/ppermute | solution.py:267
  11.3 1.3 %copy-start.9 = (bf16[128,64]{1,0:T(8,128)(2,1)S(1)}, bf16[128,64]{1,0:T(8,128)(2,1)}, u32[]{:S(2)}) copy-start(bf16[128,64]{1,0:T(8,128)(2,1)} %constant.11.clone.inline_low) | copy-start | bytes 49156
  11.3 1.3 %copy-start.10 = (bf16[128,64]{1,0:T(8,128)(2,1)S(1)}, bf16[128,64]{1,0:T(8,128)(2,1)}, u32[]{:S(2)}) copy-start(bf16[128,64]{1,0:T(8,128)(2,1)} %constant.10.clone.inline_high) | copy-start | bytes 49156
  18.0 11.9 %collective-permute-start.4 = (f32[24,640]{1,0:T(8,128)S(1)}, f32[24,640]{1,0:T(8,128)S(1)}, u32[]{:S(2)}, u32[]{:S(2)}) collective-permute-start(f32[24,640]{1,0:T(8,128)S(1)} %get-tuple-element.32), channel_id=1, source_target_pairs={{0,2},{2,4},{4,6},{6,8},{8,10},{10,12},{12,14},{14,0},{1,3},{3,5},... | collective-permute-start | bytes 184328 | tf_op jit(solution)/shard_map/ppermute | solution.py:319
  20.5 9.4 %collective-permute-start.5 = (f32[24,640]{1,0:T(8,128)S(1)}, f32[24,640]{1,0:T(8,128)S(1)}, u32[]{:S(2)}, u32[]{:S(2)}) collective-permute-start(f32[24,640]{1,0:T(8,128)S(1)} %get-tuple-element.33), channel_id=1, source_target_pairs={{0,14},{2,0},{4,2},{6,4},{8,6},{10,8},{12,10},{14,12},{1,15},{3,1}... | collective-permute-start | bytes 184328 | tf_op jit(solution)/shard_map/ppermute | solution.py:319
  23.5 6.4 %collective-permute-start.6 = (f32[8,640]{1,0:T(8,128)S(1)}, f32[8,640]{1,0:T(8,128)S(1)}, u32[]{:S(2)}, u32[]{:S(2)}) collective-permute-start(f32[8,640]{1,0:T(8,128)S(1)} %get-tuple-element.34), channel_id=1, source_target_pairs={{0,4},{2,6},{4,8},{6,10},{8,12},{10,14},{12,0},{14,2},{1,5},{3,7},... | collective-permute-start | bytes 61448 | tf_op jit(solution)/shard_map/ppermute | solution.py:319
  25.2 4.7 %collective-permute-start.7 = (f32[8,640]{1,0:T(8,128)S(1)}, f32[8,640]{1,0:T(8,128)S(1)}, u32[]{:S(2)}, u32[]{:S(2)}) collective-permute-start(f32[8,640]{1,0:T(8,128)S(1)} %get-tuple-element.35), channel_id=1, source_target_pairs={{0,12},{2,14},{4,0},{6,2},{8,4},{10,6},{12,8},{14,10},{1,13},{3,15... | collective-permute-start | bytes 61448 | tf_op jit(solution)/shard_map/ppermute | solution.py:319

commit v3 on v2

--- a/solution.py
+++ b/solution.py
@@ -147,6 +147,7 @@
 
 
 def step_kernel(
+    size,
     gives,
     waves,
     other,
@@ -170,6 +171,11 @@
     sends, (ext, dz_ext, dzz_ext, pressure) = rest[:-4], rest[-4:]
     rows, _, width = waves.shape
     lower = lax.axis_index("gz") == 0
+    place = lax.axis_index("xy")
+    even, early = place % 2 == 0, place % 4 < 2
+    left_at, right_at = jnp.where(even, 4, 0), jnp.where(even, 0, 4)
+    left_in = jnp.where(place > 0, 1.0, 0.0)
+    right_in = jnp.where(place < size - 1, 1.0, 0.0)
     sub = lax.broadcasted_iota(jnp.int32, waves.shape[1:], 0)
     layer = sub & 3
     top = sub < 4
@@ -178,11 +184,12 @@
 
     for x in range(rows + 8):
         if x < 4:
-            own, far = edges[x], edges_other[x]
+            own, far = edges[left_at + x] * left_in, edges_other[left_at + x] * left_in
         elif x < rows + 4:
             own, far = waves[x - 4], other[x - 4]
         else:
-            own, far = edges[x - rows], edges_other[x - rows]
+            at = right_at + x - rows - 4
+            own, far = edges[at] * right_in, edges_other[at] * right_in
         ext[x] = own
         up, down = far * above, far * below
         ahead, behind = [], []
@@ -233,12 +240,26 @@
     crossline = dot3(*halves(packed), across_high[...], across_low[...])
     parts = dot3(inline_high[...], inline_low[...], *halves(crossline))
     mine[...] = parts[: 4 * rows]
-    for (start, size), send in zip(gives, sends):
-        send[...] = parts[start : start + size]
+    to_next, to_previous, to_second_next, to_second_previous = (
+        parts[start : start + count] for start, count in gives
+    )
+    sends[0][...] = jnp.where(even, to_previous, to_next)
+    sends[1][...] = jnp.where(even, to_next, to_previous)
+    sends[2][...] = jnp.where(early, to_second_previous, to_second_next)
+    sends[3][...] = jnp.where(early, to_second_next, to_second_previous)
 
 
 def finish_kernel(takes, mine, *rest):
-    received, outs = rest[:4], rest[4:]
+    outer, inner, outer_second, inner_second = (ref[...] for ref in rest[:4])
+    outs = rest[4:]
+    place = lax.axis_index("xy")
+    even, early = place % 2 == 0, place % 4 < 2
+    received = (
+        jnp.where(even, outer, inner),
+        jnp.where(even, inner, outer),
+        jnp.where(early, outer_second, inner_second),
+        jnp.where(early, inner_second, outer_second),
+    )
     at = 0
     for out in outs:
         for row in range(out.shape[0]):
@@ -252,18 +273,34 @@
             at += 1
 
 
+def pair_swaps(size):
+    one = [1 if i % 2 == 0 else -1 for i in range(size)]
+    two = [2 if i % 4 < 2 else -2 for i in range(size)]
+    return [
+        [(i, (i - one[i]) % size) for i in range(size)],
+        [(i, i + one[i]) for i in range(size)],
+        [(i, (i - two[i]) % size) for i in range(size)],
+        [(i, i + two[i]) for i in range(size)],
+    ]
+
+
 def body(size, wave_p, wave_q, prior_p, prior_q, courant, epsilon, thomsen_delta, tilt_angle, azimuth):
     rows, layers, width = wave_p.shape
     f32 = jnp.float32
     waves = jnp.concatenate([wave_p, wave_q], axis=1)
-    up = [(i, i + 1) for i in range(size - 1)]
-    down = [(i + 1, i) for i in range(size - 1)]
-
-    last, leading = waves[rows - 4 :], waves[:4]
+    even = lax.axis_index("xy") % 2 == 0
+    pairs = pair_swaps(size)
+
+    def stacked(start):
+        stop = start + 4
+        return jnp.concatenate([wave_p[start:stop], wave_q[start:stop]], axis=1)
+
+    last, leading = stacked(rows - 4), stacked(0)
+    open_outer = [(i, i) if abs(i - j) > 1 else (i, j) for i, j in pairs[0]]
+    outer = lax.ppermute(jnp.where(even, leading, last), "xy", open_outer)
+    inner = lax.ppermute(jnp.where(even, last, leading), "xy", pairs[1])
+    edges = jnp.concatenate([inner, outer], axis=0)
     other = lax.ppermute(waves, "gz", [(0, 1), (1, 0)])
-    left = lax.ppermute(last, "xy", up)
-    right = lax.ppermute(leading, "xy", down)
-    edges = jnp.concatenate([left, right], axis=0)
     edges_other = lax.ppermute(edges, "gz", [(0, 1), (1, 0)])
 
     stack = jax.ShapeDtypeStruct((rows, 8, width), f32)
@@ -289,7 +326,7 @@
     inline = np.kron(np.concatenate(pieces), np.eye(4))
     across = np.concatenate(three_levels(width)).T
     results = pl.pallas_call(
-        functools.partial(step_kernel, gives),
+        functools.partial(step_kernel, size, gives),
         out_shape=[
             jax.ShapeDtypeStruct(wave_p.shape, f32),
             jax.ShapeDtypeStruct(wave_p.shape, f32),
@@ -315,10 +352,7 @@
         *[jnp.asarray(m) for m in split_bf16(inline)],
     )
     next_p, next_q, mine = results[:3]
-    received = [
-        lax.ppermute(send, "xy", [(i, (i - offset) % size) for i in range(size)])
-        for offset, send in zip(offsets, results[3:])
-    ]
+    received = [lax.ppermute(send, "xy", pair) for send, pair in zip(results[3:], pairs)]
     outs = pl.pallas_call(
         functools.partial(finish_kernel, [factors[offset][0] for offset in offsets]),
         out_shape=[

time: 30.9 us -> 28.8 us (0.932)
  starting transfers between devices: 16.3 us -> 13.9 us
  other arithmetic: 2.1 us -> 1.1 us
  local copies, waits for them, and re-layouts: 0.08 us -> 1 us
  waiting for transfers between devices: 4.39 us -> 4.79 us
    ppermute x6, starting transfers between devices: 16.2 us -> 13.8 us  [the longest x4 7.18 us: body(): lax.ppermute(send, 'xy', pair)]
    concatenate x2 -> x1, other arithmetic: 2.1 us -> 1.06 us  [body(): waves = jnp.concatenate([wave_p, wave_q], axis=1)]
    slice x0 -> x1, local copies, waits for them, and re-layouts: none -> 0.91 us  [stacked(): return jnp.concatenate([wave_p[start:stop], wave_q[start:stop]], axis=1)]
    ppermute x6, waiting for transfers between devices: 3.82 us -> 4.19 us  [the longest x4 2.66 us: body(): lax.ppermute(send, 'xy', pair)]
  transfers between devices with their start and end apart: 8 -> 8, of which waited for: 3 -> 4; matrix products, arithmetic and copies ran while one was open for 4% -> 4% of each run, Pallas kernels for 2% -> 2%
where the time goes in v3:
time: 28.8 us; the launch traced here: 28.6 us
  starting transfers between devices  13.9 us (48%)
  Pallas kernels  6.95 us (24%)
  waiting for transfers between devices  4.79 us (17%)
  other arithmetic  1.1 us (4%)
  local copies, waits for them, and re-layouts  1 us (3%)
  between operations  0.87 us (3%)
    ppermute x4, starting transfers between devices, body(): lax.ppermute(send, 'xy', pair)  7.18 us
    ppermute x1, starting transfers between devices, body(): inner = lax.ppermute(jnp.where(even, last, leading), 'xy', pairs[1])  5.79 us
    pallas_call x1, Pallas kernels, body(): pl.pallas_call(functools.partial(step_kernel, size, gives), out_shape=[ja...  5.42 us
    ppermute x4, waiting for transfers between devices, body(): lax.ppermute(send, 'xy', pair)  2.66 us
    ppermute x1, waiting for transfers between devices, body(): inner = lax.ppermute(jnp.where(even, last, leading), 'xy', pairs[1])  1.54 us
    concatenate x1, other arithmetic, body(): waves = jnp.concatenate([wave_p, wave_q], axis=1)  1.06 us
    slice x1, local copies, waits for them, and re-layouts, stacked(): return jnp.concatenate([wave_p[start:stop], wave_q[start:stop]], axis=1)  0.91 us
    pallas_call x1, Pallas kernels, body(): pl.pallas_call(functools.partial(finish_kernel, [factors[offset][0] for o...  0.82 us
  transfers between devices with their start and end apart: 8, of which 4 were waited for; matrix products, arithmetic and copies ran while one was open for 4% of the time, Pallas kernels for 2%

profile of v3, /device:TPU:0, one launch (start us, length us, event | category | flops | bytes accessed | tf_op | source)
XLA Modules:
  0.0 28.6 jit_solution(11497696700824802429)
XLA Ops:
  0.6 0.0 copy-start.11
  0.7 0.0 copy-start.9
  0.7 0.0 copy-start.10
  0.7 0.9 %fusion.2 = (f32[4,4,640]{2,1,0:T(4,128)S(1)}, f32[4,4,640]{2,1,0:T(4,128)S(1)}, f32[4,4,640]{2,1,0:T(4,128)S(1)}, f32[4,4,640]{2,1,0:T(4,128)S(1)}) fusion(f32[16,4,640]{2,1,0:T(4,128)} %param.13, f32[16,4,640]{2,1,0:T(4,128)} %param.14), kind=kLoop, calls=%fused_computation.7 | loop fusion | bytes 327680 | tf_op jit(solution)/shard_map/slice | solution.py:296
  1.6 0.0 copy-start.4
  1.6 0.0 copy-start.5
  1.6 0.0 copy-start.6
  1.6 0.0 copy-start.7
  1.6 0.0 copy-start.8
  1.7 0.8 %collective-permute-start.2 = (f32[4,8,640]{2,1,0:T(8,128)S(1)}, f32[4,8,640]{2,1,0:T(8,128)S(1)}, u32[]{:S(2)}, u32[]{:S(2)}) collective-permute-start(f32[4,8,640]{2,1,0:T(8,128)S(1)} %get-tuple-element.40), channel_id=1, source_target_pairs={{0,0},{2,4},{4,2},{6,8},{8,6},{10,12},{12,10},{14,14},{1,1},{3,5},... | collective-permute-start | bytes 245768 | tf_op jit(solution)/shard_map/ppermute | solution.py:300
  2.5 0.0 copy-start.2
  2.5 0.0 copy-start.3
  2.5 5.8 %collective-permute-start.1 = (f32[4,8,640]{2,1,0:T(8,128)S(1)}, f32[4,8,640]{2,1,0:T(8,128)S(1)}, u32[]{:S(2)}, u32[]{:S(2)}) collective-permute-start(f32[4,8,640]{2,1,0:T(8,128)S(1)} %get-tuple-element.41), channel_id=1, source_target_pairs={{0,2},{2,0},{4,6},{6,4},{8,10},{10,8},{12,14},{14,12},{1,3},{3,1},... | collective-permute-start | bytes 245768 | tf_op jit(solution)/shard_map/ppermute | solution.py:301
  8.3 0.0 copy-done.11
  8.3 0.0 copy-start.1
  8.3 1.1 %pad_maximum_fusion.waves = f32[16,8,640]{2,1,0:T(8,128)S(1)} fusion(f32[16,4,640]{2,1,0:T(4,128)S(1)} %copy-done.11, f32[16,4,640]{2,1,0:T(4,128)} %param.13), kind=kLoop, calls=%fused_computation | loop fusion | flops 81920 | bytes 655360 | tf_op jit(solution)/shard_map/concatenate | solution.py:290
  9.4 0.0 copy-start
  9.4 0.1 collective-permute-start
  9.5 1.5 %collective-permute-done.1 = f32[4,8,640]{2,1,0:T(8,128)S(1)} collective-permute-done((f32[4,8,640]{2,1,0:T(8,128)S(1)}, f32[4,8,640]{2,1,0:T(8,128)S(1)}, u32[]{:S(2)}, u32[]{:S(2)}) %collective-permute-start.1) | collective-permute-done | bytes 81952 | tf_op jit(solution)/shard_map/ppermute | solution.py:301
  11.0 0.0 collective-permute-done.2
  11.1 0.1 collective-permute-start.3
  11.1 0.0 copy-done.4
  11.1 0.0 copy-done.5
  11.2 0.0 copy-done.6
  11.2 0.0 copy-done.7
  11.2 0.0 copy-done.8
  11.2 0.0 copy-done.2
  11.2 0.0 copy-done.3
  11.2 0.7 %weights.1 = (f32[16,8,640]{2,1,0:T(8,128)S(1)}, f32[16,8,640]{2,1,0:T(8,128)S(1)}, f32[16,8,640]{2,1,0:T(8,128)S(1)}, f32[16,8,640]{2,1,0:T(8,128)S(1)}, f32[16...) custom-call(f32[16,8,640]{2,1,0:T(8,128)S(1)} %pad_maximum_fusion.waves, f32[16,4,640]{2,1,0:T(4,128)S(1)} %copy-done.2, ...), custom_call_target="tpu_custom_call" | custom-call | flops 4096000 | bytes 2457600 | tf_op jit(solution)/shard_map/weights/pallas_call | solution.py:309
  11.9 0.6 %collective-permute-done.3.edges_other = f32[8,8,640]{2,1,0:T(8,128)S(1)} collective-permute-done((f32[8,8,640]{2,1,0:T(8,128)S(1)}, f32[8,8,640]{2,1,0:T(8,128)S(1)}, u32[]{:S(2)}, u32[]{:S(2)}) %collective-permute-start.3) | collective-permute-done | bytes 163872 | tf_op jit(solution)/shard_map/ppermute | solution.py:304
  12.5 0.0 collective-permute-done.other
  12.5 0.0 copy-done.9
  12.5 0.0 copy-done.10
  12.5 0.0 copy-done.1
  12.5 0.0 copy-done
  12.5 5.4 %step.1 = (f32[16,4,640]{2,1,0:T(4,128)}, f32[16,4,640]{2,1,0:T(4,128)}, f32[64,640]{1,0:T(8,128)S(1)}, f32[24,640]{1,0:T(8,128)S(1)}, f32[24,640]{1,0:T(8,128)S...) custom-call(f32[16,8,640]{2,1,0:T(8,128)S(1)} %pad_maximum_fusion.waves, f32[16,8,640]{2,1,0:T(8,128)S(1)} %collective-permute-done.other, ...), custom_call_target="tpu_custom_call" | custom-call | flops 16384000 | bytes 4096000 | tf_op jit(solution)/shard_map/step/pallas_call | solution.py:328
  18.0 3.6 %collective-permute-start.4 = (f32[24,640]{1,0:T(8,128)S(1)}, f32[24,640]{1,0:T(8,128)S(1)}, u32[]{:S(2)}, u32[]{:S(2)}) collective-permute-start(f32[24,640]{1,0:T(8,128)S(1)} %get-tuple-element.32), channel_id=1, source_target_pairs={{0,14},{2,4},{4,2},{6,8},{8,6},{10,12},{12,10},{14,0},{1,15},{3,5}... | collective-permute-start | bytes 184328 | tf_op jit(solution)/shard_map/ppermute | solution.py:355
  21.5 0.5 %collective-permute-start.5 = (f32[24,640]{1,0:T(8,128)S(1)}, f32[24,640]{1,0:T(8,128)S(1)}, u32[]{:S(2)}, u32[]{:S(2)}) collective-permute-start(f32[24,640]{1,0:T(8,128)S(1)} %get-tuple-element.33), channel_id=1, source_target_pairs={{0,2},{2,0},{4,6},{6,4},{8,10},{10,8},{12,14},{14,12},{1,3},{3,1},... | collective-permute-start | bytes 184328 | tf_op jit(solution)/shard_map/ppermute | solution.py:355
  22.0 1.9 %collective-permute-start.6 = (f32[8,640]{1,0:T(8,128)S(1)}, f32[8,640]{1,0:T(8,128)S(1)}, u32[]{:S(2)}, u32[]{:S(2)}) collective-permute-start(f32[8,640]{1,0:T(8,128)S(1)} %get-tuple-element.34), channel_id=1, source_target_pairs={{0,12},{2,14},{4,8},{6,10},{8,4},{10,6},{12,0},{14,2},{1,13},{3,15... | collective-permute-start | bytes 61448 | tf_op jit(solution)/shard_map/ppermute | solution.py:355
  23.9 1.2 %collective-permute-start.7 = (f32[8,640]{1,0:T(8,128)S(1)}, f32[8,640]{1,0:T(8,128)S(1)}, u32[]{:S(2)}, u32[]{:S(2)}) collective-permute-start(f32[8,640]{1,0:T(8,128)S(1)} %get-tuple-element.35), channel_id=1, source_target_pairs={{0,4},{2,6},{4,0},{6,2},{8,12},{10,14},{12,8},{14,10},{1,5},{3,7},... | collective-permute-start | bytes 61448 | tf_op jit(solution)/shard_map/ppermute | solution.py:355
  25.1 2.4 %collective-permute-done.6.rest_2_ = f32[8,640]{1,0:T(8,128)S(1)} collective-permute-done((f32[8,640]{1,0:T(8,128)S(1)}, f32[8,640]{1,0:T(8,128)S(1)}, u32[]{:S(2)}, u32[]{:S(2)}) %collective-permute-start.6) | collective-permute-done | bytes 20512 | tf_op jit(solution)/shard_map/ppermute | solution.py:355
  27.6 0.2 collective-permute-done.7.rest_3_
  27.8 0.0 collective-permute-done.4.rest_0_
  27.8 0.0 collective-permute-done.5.rest_1_
  27.8 0.8 %finish.1 = (f32[8,4,640]{2,1,0:T(4,128)}, f32[4,4,640]{2,1,0:T(4,128)}, f32[2,4,640]{2,1,0:T(4,128)}, f32[2,4,640]{2,1,0:T(4,128)}) custom-call(f32[64,640]{1,0:T(8,128)S(1)} %get-tuple-element.31.mine, f32[24,640]{1,0:T(8,128)S(1)} %collective-permute-done.4.rest_0_, f32[24,640]{1,0:T(8,128)S(1)} %collective-permute-done.5.rest_1_, ...), custom_call_target="tpu_custom_call" | custom-call | tf_op jit(solution)/shard_map/finish/pallas_call | solution.py:356
  (3 shorter events, 0.1 us)
Async XLA Ops:
  0.6 7.7 %copy-start.11 = (f32[16,4,640]{2,1,0:T(4,128)S(1)}, f32[16,4,640]{2,1,0:T(4,128)}, u32[]{:S(2)}) copy-start(f32[16,4,640]{2,1,0:T(4,128)} %param.14) | copy-start | bytes 491524
  0.7 11.9 %copy-start.9 = (bf16[128,64]{1,0:T(8,128)(2,1)S(1)}, bf16[128,64]{1,0:T(8,128)(2,1)}, u32[]{:S(2)}) copy-start(bf16[128,64]{1,0:T(8,128)(2,1)} %constant.31.clone.inline_low) | copy-start | bytes 49156
  0.7 11.9 %copy-start.10 = (bf16[128,64]{1,0:T(8,128)(2,1)S(1)}, bf16[128,64]{1,0:T(8,128)(2,1)}, u32[]{:S(2)}) copy-start(bf16[128,64]{1,0:T(8,128)(2,1)} %constant.30.clone.inline_high) | copy-start | bytes 49156
  1.6 9.5 %copy-start.4 = (bf16[16,4,640]{2,1,0:T(4,128)(2,1)S(1)}, bf16[16,4,640]{2,1,0:T(4,128)(2,1)}, u32[]{:S(2)}) copy-start(bf16[16,4,640]{2,1,0:T(4,128)(2,1)} %courant.1) | copy-start | bytes 245764
  1.6 9.5 %copy-start.5 = (bf16[16,4,640]{2,1,0:T(4,128)(2,1)S(1)}, bf16[16,4,640]{2,1,0:T(4,128)(2,1)}, u32[]{:S(2)}) copy-start(bf16[16,4,640]{2,1,0:T(4,128)(2,1)} %epsilon.1) | copy-start | bytes 245764
  1.6 9.5 %copy-start.6 = (bf16[16,4,640]{2,1,0:T(4,128)(2,1)S(1)}, bf16[16,4,640]{2,1,0:T(4,128)(2,1)}, u32[]{:S(2)}) copy-start(bf16[16,4,640]{2,1,0:T(4,128)(2,1)} %delta.1) | copy-start | bytes 245764
  1.6 9.5 %copy-start.7 = (bf16[16,4,640]{2,1,0:T(4,128)(2,1)S(1)}, bf16[16,4,640]{2,1,0:T(4,128)(2,1)}, u32[]{:S(2)}) copy-start(bf16[16,4,640]{2,1,0:T(4,128)(2,1)} %tilt.1) | copy-start | bytes 245764
  1.6 9.5 %copy-start.8 = (bf16[16,4,640]{2,1,0:T(4,128)(2,1)S(1)}, bf16[16,4,640]{2,1,0:T(4,128)(2,1)}, u32[]{:S(2)}) copy-start(bf16[16,4,640]{2,1,0:T(4,128)(2,1)} %azimuth.1) | copy-start | bytes 245764
  1.7 9.3 %collective-permute-start.2 = (f32[4,8,640]{2,1,0:T(8,128)S(1)}, f32[4,8,640]{2,1,0:T(8,128)S(1)}, u32[]{:S(2)}, u32[]{:S(2)}) collective-permute-start(f32[4,8,640]{2,1,0:T(8,128)S(1)} %get-tuple-element.40), channel_id=1, source_target_pairs={{0,0},{2,4},{4,2},{6,8},{8,6},{10,12},{12,10},{14,14},{1,1},{3,5},... | collective-permute-start | bytes 245768 | tf_op jit(solution)/shard_map/ppermute | solution.py:300
  2.5 8.7 %copy-start.2 = (f32[16,4,640]{2,1,0:T(4,128)S(1)}, f32[16,4,640]{2,1,0:T(4,128)}, u32[]{:S(2)}) copy-start(f32[16,4,640]{2,1,0:T(4,128)} %prior_p.1) | copy-start | bytes 491524
  2.5 8.7 %copy-start.3 = (f32[16,4,640]{2,1,0:T(4,128)S(1)}, f32[16,4,640]{2,1,0:T(4,128)}, u32[]{:S(2)}) copy-start(f32[16,4,640]{2,1,0:T(4,128)} %prior_q.1) | copy-start | bytes 491524
  2.5 8.5 %collective-permute-start.1 = (f32[4,8,640]{2,1,0:T(8,128)S(1)}, f32[4,8,640]{2,1,0:T(8,128)S(1)}, u32[]{:S(2)}, u32[]{:S(2)}) collective-permute-start(f32[4,8,640]{2,1,0:T(8,128)S(1)} %get-tuple-element.41), channel_id=1, source_target_pairs={{0,2},{2,0},{4,6},{6,4},{8,10},{10,8},{12,14},{14,12},{1,3},{3,1},... | collective-permute-start | bytes 245768 | tf_op jit(solution)/shard_map/ppermute | solution.py:301
  8.3 4.2 %copy-start.1 = (bf16[640,640]{1,0:T(8,128)(2,1)S(1)}, bf16[640,640]{1,0:T(8,128)(2,1)}, u32[]{:S(2)}) copy-start(bf16[640,640]{1,0:T(8,128)(2,1)} %constant.28.clone.across_high) | copy-start | bytes 2457604
  9.4 3.1 %copy-start = (bf16[640,640]{1,0:T(8,128)(2,1)S(1)}, bf16[640,640]{1,0:T(8,128)(2,1)}, u32[]{:S(2)}) copy-start(bf16[640,640]{1,0:T(8,128)(2,1)} %constant.29.clone.across_low) | copy-start | bytes 2457604
  9.4 3.1 %collective-permute-start = (f32[16,8,640]{2,1,0:T(8,128)S(1)}, f32[16,8,640]{2,1,0:T(8,128)S(1)}, u32[]{:S(2)}, u32[]{:S(2)}) collective-permute-start(f32[16,8,640]{2,1,0:T(8,128)S(1)} %pad_maximum_fusion.waves), channel_id=1, source_target_pairs={{0,1},{1,0},{2,3},{3,2},{4,5},{5,4},{6,7},{7,6},{8,9},{9,8},{10,11... | collective-permute-start | bytes 983048 | tf_op jit(solution)/shard_map/ppermute | solution.py:303
  11.1 1.5 %collective-permute-start.3 = (f32[8,8,640]{2,1,0:T(8,128)S(1)}, f32[8,8,640]{2,1,0:T(8,128)S(1)}, u32[]{:S(2)}, u32[]{:S(2)}) collective-permute-start(f32[8,8,640]{2,1,0:T(8,128)S(1)} %constant_dynamic-update-slice_fusion.edges), channel_id=1, source_target_pairs={{0,1},{1,0},{2,3},{3,2},{4,5},{5,4},{6,7},{7,6},{8,9},{9,8},{10,11... | collective-permute-start | bytes 491528 | tf_op jit(solution)/shard_map/ppermute | solution.py:304
  18.0 9.8 %collective-permute-start.4 = (f32[24,640]{1,0:T(8,128)S(1)}, f32[24,640]{1,0:T(8,128)S(1)}, u32[]{:S(2)}, u32[]{:S(2)}) collective-permute-start(f32[24,640]{1,0:T(8,128)S(1)} %get-tuple-element.32), channel_id=1, source_target_pairs={{0,14},{2,4},{4,2},{6,8},{8,6},{10,12},{12,10},{14,0},{1,15},{3,5}... | collective-permute-start | bytes 184328 | tf_op jit(solution)/shard_map/ppermute | solution.py:355
  21.5 6.3 %collective-permute-start.5 = (f32[24,640]{1,0:T(8,128)S(1)}, f32[24,640]{1,0:T(8,128)S(1)}, u32[]{:S(2)}, u32[]{:S(2)}) collective-permute-start(f32[24,640]{1,0:T(8,128)S(1)} %get-tuple-element.33), channel_id=1, source_target_pairs={{0,2},{2,0},{4,6},{6,4},{8,10},{10,8},{12,14},{14,12},{1,3},{3,1},... | collective-permute-start | bytes 184328 | tf_op jit(solution)/shard_map/ppermute | solution.py:355
  22.0 5.6 %collective-permute-start.6 = (f32[8,640]{1,0:T(8,128)S(1)}, f32[8,640]{1,0:T(8,128)S(1)}, u32[]{:S(2)}, u32[]{:S(2)}) collective-permute-start(f32[8,640]{1,0:T(8,128)S(1)} %get-tuple-element.34), channel_id=1, source_target_pairs={{0,12},{2,14},{4,8},{6,10},{8,4},{10,6},{12,0},{14,2},{1,13},{3,15... | collective-permute-start | bytes 61448 | tf_op jit(solution)/shard_map/ppermute | solution.py:355
  23.9 3.9 %collective-permute-start.7 = (f32[8,640]{1,0:T(8,128)S(1)}, f32[8,640]{1,0:T(8,128)S(1)}, u32[]{:S(2)}, u32[]{:S(2)}) collective-permute-start(f32[8,640]{1,0:T(8,128)S(1)} %get-tuple-element.35), channel_id=1, source_target_pairs={{0,4},{2,6},{4,0},{6,2},{8,12},{10,14},{12,8},{14,10},{1,5},{3,7},... | collective-permute-start | bytes 61448 | tf_op jit(solution)/shard_map/ppermute | solution.py:355

commit v4 on v3

--- a/solution.py
+++ b/solution.py
@@ -138,21 +138,60 @@
     def dot(a, b):
         return jnp.dot(a, b, preferred_element_type=jnp.float32)
 
-    return dot(a_high, b_high) + (dot(a_low, b_high) + dot(a_high, b_low))
+    rows = a_high.shape[0]
+    both = dot(jnp.concatenate([a_high, a_low], axis=0), b_high)
+    return both[:rows] + (both[rows:] + dot(a_high, b_low))
 
 
 def halves(value):
     high = value.astype(jnp.bfloat16)
     return high, (value - high.astype(jnp.float32)).astype(jnp.bfloat16)
+
+
+def depth_neighbours(own, far, lower):
+    layer = lax.broadcasted_iota(jnp.int32, own.shape, 0) & 3
+    up = far * jnp.where(lower, 1.0, 0.0)
+    down = far * jnp.where(lower, 0.0, 1.0)
+    ahead, behind = [], []
+    for k in range(1, 4):
+        ahead.append(jnp.where(layer < 4 - k, pltpu.roll(own, 8 - k, 0), pltpu.roll(up, 4 - k, 0)))
+        behind.append(jnp.where(layer >= k, pltpu.roll(own, k, 0), pltpu.roll(down, 4 + k, 0)))
+    return ahead + [up], behind + [down]
+
+
+def depth_kernel(waves, other, dz, dzz):
+    lower = lax.axis_index("gz") == 0
+    for x in range(waves.shape[0]):
+        own = waves[x]
+        ahead, behind = depth_neighbours(own, other[x], lower)
+        dz[x] = first_of(ahead, behind)
+        dzz[x] = second_of(own, ahead, behind)
+
+
+def cross_kernel(waves, dz, dzz, axis_y, axis_z, h_part, sum_part):
+    rows, _, width = waves.shape
+
+    def row(x, carry):
+        centre = waves[x]
+        dyy = second_of(centre, *shifted(centre, width))
+        dzy = first_of(*shifted(dz[x], width))
+        n_y, n_z = axis_y[x], axis_z[x]
+        h_part[x] = (n_y * n_y) * dyy + n_z * (n_z * dzz[x] + 2.0 * n_y * dzy)
+        sum_part[x] = dyy + dzz[x]
+        return carry
+
+    lax.fori_loop(0, rows, row, 0, unroll=4)
 
 
 def step_kernel(
     size,
     gives,
     waves,
-    other,
     edges,
     edges_other,
+    dz,
+    h_part,
+    sum_part,
     axis_x,
     axis_y,
     axis_z,
@@ -163,12 +202,11 @@
     across_low,
     inline_high,
     inline_low,
-    next_p,
-    next_q,
-    mine,
+    pressure,
+    crossline,
     *rest,
 ):
-    sends, (ext, dz_ext, dzz_ext, pressure) = rest[:-4], rest[-4:]
+    sends, (ext, dz_ext) = rest[:-2], rest[-2:]
     rows, _, width = waves.shape
     lower = lax.axis_index("gz") == 0
     place = lax.axis_index("xy")
@@ -176,59 +214,33 @@
     left_at, right_at = jnp.where(even, 4, 0), jnp.where(even, 0, 4)
     left_in = jnp.where(place > 0, 1.0, 0.0)
     right_in = jnp.where(place < size - 1, 1.0, 0.0)
-    sub = lax.broadcasted_iota(jnp.int32, waves.shape[1:], 0)
-    layer = sub & 3
-    top = sub < 4
-    above = jnp.where(lower, 1.0, 0.0)
-    below = jnp.where(lower, 0.0, 1.0)
-
-    for x in range(rows + 8):
-        if x < 4:
-            own, far = edges[left_at + x] * left_in, edges_other[left_at + x] * left_in
-        elif x < rows + 4:
-            own, far = waves[x - 4], other[x - 4]
-        else:
-            at = right_at + x - rows - 4
-            own, far = edges[at] * right_in, edges_other[at] * right_in
-        ext[x] = own
-        up, down = far * above, far * below
-        ahead, behind = [], []
-        for k in range(1, 4):
-            ahead.append(jnp.where(layer < 4 - k, pltpu.roll(own, 8 - k, 0), pltpu.roll(up, 4 - k, 0)))
-            behind.append(jnp.where(layer >= k, pltpu.roll(own, k, 0), pltpu.roll(down, 4 + k, 0)))
-        ahead.append(up)
-        behind.append(down)
-        dz_ext[x] = first_of(ahead, behind)
-        if 4 <= x < rows + 4:
-            dzz_ext[x - 4] = second_of(own, ahead, behind)
+    top = lax.broadcasted_iota(jnp.int32, waves.shape[1:], 0) < 4
+
+    for x in range(4):
+        for at, inside, to in ((left_at, left_in, x), (right_at, right_in, rows + 4 + x)):
+            own, far = edges[at + x] * inside, edges_other[at + x] * inside
+            ext[to] = own
+            dz_ext[to] = first_of(*depth_neighbours(own, far, lower))
+    for x in range(rows):
+        ext[x + 4] = waves[x]
+        dz_ext[x + 4] = dz[x]
 
     def row(x, carry):
-        centre = ext[x + 4]
         ahead = [ext[x + 4 + k] for k in range(1, 5)]
         behind = [ext[x + 4 - k] for k in range(1, 5)]
-        dxx = second_of(centre, ahead, behind)
-        dx = first_of(ahead, behind)
+        dxx = second_of(ext[x + 4], ahead, behind)
+        dxy = first_of(*shifted(first_of(ahead, behind), width))
         dxz = first_of(
             [dz_ext[x + 4 + k] for k in range(1, 5)], [dz_ext[x + 4 - k] for k in range(1, 5)]
         )
-        dyy = second_of(centre, *shifted(centre, width))
-        dxy = first_of(*shifted(dx, width))
-        dzy = first_of(*shifted(dz_ext[x + 4], width))
-        dzz = dzz_ext[x]
-        n_x, n_y, n_z = axis_x[x], axis_y[x], axis_z[x]
-        h_one = (n_x * n_x) * dxx
-        h_one = h_one + (n_y * n_y) * dyy
-        h_one = h_one + (n_z * n_z) * dzz
-        h_one = h_one + 2.0 * (n_x * n_y * dxy + n_z * (n_y * dzy + n_x * dxz))
-        h_two = dxx + dyy + dzz - h_one
+        n_x = axis_x[x]
+        h_one = h_part[x] + n_x * (n_x * dxx + 2.0 * (axis_y[x] * dxy + axis_z[x] * dxz))
+        h_two = dxx + sum_part[x] - h_one
         mixed = jnp.where(top, h_two, h_one)
-        result = base[x] + gain_a[x] * mixed + gain_b[x] * pltpu.roll(mixed, 4, 0)
-        next_p[x] = result[:4]
-        next_q[x] = result[4:]
-        pressure[x] = result
+        pressure[x] = base[x] + gain_a[x] * mixed + gain_b[x] * pltpu.roll(mixed, 4, 0)
         return carry
 
-    lax.fori_loop(0, rows, row, 0)
+    lax.fori_loop(0, rows, row, 0, unroll=4)
 
     packed = jnp.concatenate(
         [
@@ -237,9 +249,9 @@
         ],
         axis=0,
     )
-    crossline = dot3(*halves(packed), across_high[...], across_low[...])
-    parts = dot3(inline_high[...], inline_low[...], *halves(crossline))
-    mine[...] = parts[: 4 * rows]
+    transformed = dot3(*halves(packed), across_high[...], across_low[...])
+    crossline[...] = transformed
+    parts = dot3(inline_high[...], inline_low[...], *halves(transformed))
     to_next, to_previous, to_second_next, to_second_previous = (
         parts[start : start + count] for start, count in gives
     )
@@ -247,6 +259,13 @@
     sends[1][...] = jnp.where(even, to_next, to_previous)
     sends[2][...] = jnp.where(early, to_second_previous, to_second_next)
     sends[3][...] = jnp.where(early, to_second_next, to_second_previous)
+
+
+def own_kernel(pressure, crossline, own_high, own_low, next_p, next_q, mine):
+    for x in range(pressure.shape[0]):
+        next_p[x] = pressure[x, :4]
+        next_q[x] = pressure[x, 4:]
+    mine[...] = dot3(own_high[...], own_low[...], *halves(crossline[...]))
 
 
 def finish_kernel(takes, mine, *rest):
@@ -287,80 +306,81 @@
 def body(size, wave_p, wave_q, prior_p, prior_q, courant, epsilon, thomsen_delta, tilt_angle, azimuth):
     rows, layers, width = wave_p.shape
     f32 = jnp.float32
-    waves = jnp.concatenate([wave_p, wave_q], axis=1)
     even = lax.axis_index("xy") % 2 == 0
     pairs = pair_swaps(size)
-
-    def stacked(start):
-        stop = start + 4
-        return jnp.concatenate([wave_p[start:stop], wave_q[start:stop]], axis=1)
-
-    last, leading = stacked(rows - 4), stacked(0)
-    open_outer = [(i, i) if abs(i - j) > 1 else (i, j) for i, j in pairs[0]]
-    outer = lax.ppermute(jnp.where(even, leading, last), "xy", open_outer)
+    cores = [(0, 1), (1, 0)]
+    waves = lax.optimization_barrier(jnp.concatenate([wave_p, wave_q], axis=1))
+    leading, last = waves[:4], waves[rows - 4 :]
+    open_outer = [
+        (2 * i + g, 2 * i + 1 - g) if abs(i - j) > 1 else (2 * i + g, 2 * j + g)
+        for i, j in pairs[0]
+        for g in range(2)
+    ]
+    outer = lax.ppermute(jnp.where(even, leading, last), ("xy", "gz"), open_outer)
     inner = lax.ppermute(jnp.where(even, last, leading), "xy", pairs[1])
-    edges = jnp.concatenate([inner, outer], axis=0)
-    other = lax.ppermute(waves, "gz", [(0, 1), (1, 0)])
-    edges_other = lax.ppermute(edges, "gz", [(0, 1), (1, 0)])
+    other = lax.ppermute(waves, "gz", cores)
 
     stack = jax.ShapeDtypeStruct((rows, 8, width), f32)
     cells = rows * layers * width
     params = pltpu.CompilerParams(vmem_limit_bytes=16 * 1024 * 1024)
-    weights = pl.pallas_call(
-        weights_kernel,
-        out_shape=[stack] * 6,
-        cost_estimate=pl.CostEstimate(flops=100 * cells, bytes_accessed=60 * cells, transcendentals=0),
-        compiler_params=params,
-        name="weights",
-    )(waves, prior_p, prior_q, courant, epsilon, thomsen_delta, tilt_angle, azimuth)
+
+    def kernel(function, out_shape, work, name, scratch_shapes=()):
+        cost = pl.CostEstimate(flops=work * cells, bytes_accessed=40 * cells, transcendentals=0)
+        return pl.pallas_call(
+            function,
+            out_shape=out_shape,
+            scratch_shapes=scratch_shapes,
+            compiler_params=params,
+            cost_estimate=cost,
+            name=name,
+        )
+
+    axis_x, axis_y, axis_z, *gains = kernel(weights_kernel, [stack] * 6, 100, "weights")(
+        waves, prior_p, prior_q, courant, epsilon, thomsen_delta, tilt_angle, azimuth
+    )
+    dz, dzz = kernel(depth_kernel, [stack] * 2, 100, "depth")(waves, other)
+    outer, inner, dz, axis_x = lax.optimization_barrier((outer, inner, dz, axis_x))
+    edges = jnp.concatenate([inner, outer], axis=0)
+    edges_other = lax.ppermute(edges, "gz", cores)
+    h_part, sum_part = kernel(cross_kernel, [stack] * 2, 100, "cross")(waves, dz, dzz, axis_y, axis_z)
 
     own, factors = inline_blocks(rows)
     offsets = (-1, 1, -2, 2)
-    pieces, gives, start = [own], [], rows * 4
+    pieces, gives, start = [], [], 0
     for offset in offsets:
         give = factors[offset][1]
         pad = give.shape[0] % 2
         pieces.append(np.pad(give, ((0, pad), (0, 0))))
         gives.append((start, 4 * (give.shape[0] + pad)))
         start += gives[-1][1]
-    inline = np.kron(np.concatenate(pieces), np.eye(4))
-    across = np.concatenate(three_levels(width)).T
-    results = pl.pallas_call(
+
+    def parts(matrix):
+        return [jnp.asarray(part) for part in split_bf16(matrix)]
+
+    across = parts(np.concatenate(three_levels(width)).T)
+    inline = parts(np.kron(np.concatenate(pieces), np.eye(4)))
+    inline_own = parts(np.kron(own, np.eye(4)))
+    flat = jax.ShapeDtypeStruct((layers * rows, width), f32)
+    pressure, crossline, *sends = kernel(
         functools.partial(step_kernel, size, gives),
-        out_shape=[
-            jax.ShapeDtypeStruct(wave_p.shape, f32),
-            jax.ShapeDtypeStruct(wave_p.shape, f32),
-            jax.ShapeDtypeStruct((4 * rows, width), f32),
-        ]
-        + [jax.ShapeDtypeStruct((count, width), f32) for _, count in gives],
-        scratch_shapes=[
-            pltpu.VMEM((rows + 8, 8, width), f32),
-            pltpu.VMEM((rows + 8, 8, width), f32),
-            pltpu.VMEM((rows, 8, width), f32),
-            pltpu.VMEM((rows, 8, width), f32),
-        ],
-        compiler_params=params,
-        cost_estimate=pl.CostEstimate(flops=400 * cells, bytes_accessed=100 * cells, transcendentals=0),
-        name="step",
-    )(
-        waves,
-        other,
-        edges,
-        edges_other,
-        *weights,
-        *[jnp.asarray(m) for m in split_bf16(across)],
-        *[jnp.asarray(m) for m in split_bf16(inline)],
-    )
-    next_p, next_q, mine = results[:3]
-    received = [lax.ppermute(send, "xy", pair) for send, pair in zip(results[3:], pairs)]
-    outs = pl.pallas_call(
+        [stack, flat] + [jax.ShapeDtypeStruct((count, width), f32) for _, count in gives],
+        400,
+        "step",
+        [pltpu.VMEM((rows + 8, 8, width), f32)] * 2,
+    )(waves, edges, edges_other, dz, h_part, sum_part, axis_x, axis_y, axis_z, *gains, *across, *inline)
+    received = [lax.ppermute(send, "xy", pair) for send, pair in zip(sends, pairs)]
+    grid = jax.ShapeDtypeStruct(wave_p.shape, f32)
+    next_p, next_q, mine = kernel(own_kernel, [grid, grid, flat], 100, "own")(
+        pressure, crossline, *inline_own
+    )
+    outs = kernel(
         functools.partial(finish_kernel, [factors[offset][0] for offset in offsets]),
-        out_shape=[
+        [
             jax.ShapeDtypeStruct((count, layers, width), f32)
             for count in (rows // 2, rows // 4, rows // 8, rows // 8)
         ],
-        compiler_params=params,
-        name="finish",
+        20,
+        "finish",
     )(mine, *received)
     return (next_p, next_q, *outs)
 

time: 28.8 us -> 23.9 us (0.83)
  starting transfers between devices: 13.9 us -> 11 us
  local copies, waits for them, and re-layouts: 1 us -> 0.08 us
  Pallas kernels: 6.95 us -> 6.42 us
  waiting for transfers between devices: 4.79 us -> 4.31 us
    ppermute x1, starting transfers between devices: 5.79 us -> 2.6 us  [body(): inner = lax.ppermute(jnp.where(even, last, leading), 'xy', pairs[1])]
    ppermute x1, waiting for transfers between devices: 1.54 us -> 2.65 us  [body(): inner = lax.ppermute(jnp.where(even, last, leading), 'xy', pairs[1])]
    ppermute x4, waiting for transfers between devices: 2.66 us -> 1.65 us  [body(): lax.ppermute(send, 'xy', pair)]
    slice x1 -> x0, local copies, waits for them, and re-layouts: 0.91 us -> none  [stacked(): return jnp.concatenate([wave_p[start:stop], wave_q[start:stop]], axis=1)]
    ppermute x3, waiting for transfers between devices: 0.6 us -> 0.01 us  [the longest x1 0.01 us: body(): lax.ppermute(jnp.where(even, leading, last), ('xy', 'gz'), open_outer)]
    pallas_call x3 -> x6, Pallas kernels: 6.95 us -> 6.42 us  [the longest x1 1.92 us: body(): kernel(functools.partial(step_kernel, size, gives), [stack, flat] + [jax....]
    ppermute x4, starting transfers between devices: 7.18 us -> 7.59 us  [body(): lax.ppermute(send, 'xy', pair)]
  transfers between devices with their start and end apart: 8 -> 8, of which waited for: 4 -> 2; matrix products, arithmetic and copies ran while one was open for 4% -> 0% of each run, Pallas kernels for 2% -> 15%
where the time goes in v4:
time: 23.9 us; the launch traced here: 23.8 us
  starting transfers between devices  11 us (46%)
  Pallas kernels  6.42 us (27%)
  waiting for transfers between devices  4.31 us (18%)
  other arithmetic  1.15 us (5%)
  between operations  0.86 us (4%)
    ppermute x4, starting transfers between devices, body(): lax.ppermute(send, 'xy', pair)  7.59 us
    ppermute x1, waiting for transfers between devices, body(): inner = lax.ppermute(jnp.where(even, last, leading), 'xy', pairs[1])  2.65 us
    ppermute x1, starting transfers between devices, body(): inner = lax.ppermute(jnp.where(even, last, leading), 'xy', pairs[1])  2.6 us
    pallas_call x1, Pallas kernels, body(): kernel(functools.partial(step_kernel, size, gives), [stack, flat] + [jax....  1.92 us
    pallas_call x1, Pallas kernels, body(): kernel(cross_kernel, [stack] * 2, 100, 'cross')  1.68 us
    ppermute x4, waiting for transfers between devices, body(): lax.ppermute(send, 'xy', pair)  1.65 us
    concatenate x1, other arithmetic, body(): waves = lax.optimization_barrier(jnp.concatenate([wave_p, wave_q], axis=1))  1.13 us
    pallas_call x1, Pallas kernels, body(): kernel(functools.partial(finish_kernel, [factors[offset][0] for offset in...  0.82 us
  transfers between devices with their start and end apart: 8, of which 2 were waited for; matrix products, arithmetic and copies ran while one was open for 0% of the time, Pallas kernels for 15%

profile of v4, /device:TPU:0, one launch (start us, length us, event | category | flops | bytes accessed | tf_op | source)
XLA Modules:
  0.0 23.8 jit_solution(8126727503075221648)
XLA Ops:
  0.6 0.0 copy-start.4
  0.6 0.0 copy-start.5
  0.7 0.0 copy-start.6
  0.7 0.0 copy-start.7
  0.7 0.0 copy-start.8
  0.7 1.1 %pad_maximum_fusion.waves = f32[16,8,640]{2,1,0:T(8,128)S(1)} fusion(f32[16,4,640]{2,1,0:T(4,128)} %param.16, f32[16,4,640]{2,1,0:T(4,128)} %param.15), kind=kLoop, calls=%fused_computation | loop fusion | flops 81920 | bytes 655360 | tf_op jit(solution)/shard_map/concatenate | solution.py:312
  1.8 0.5 %collective-permute-start.2 = (f32[16,8,640]{2,1,0:T(8,128)S(1)}, f32[16,8,640]{2,1,0:T(8,128)S(1)}, u32[]{:S(2)}, u32[]{:S(2)}) collective-permute-start(f32[16,8,640]{2,1,0:T(8,128)S(1)} %pad_maximum_fusion.waves), channel_id=1, source_target_pairs={{0,1},{1,0},{2,3},{3,2},{4,5},{5,4},{6,7},{7,6},{8,9},{9,8},{10,11... | collective-permute-start | bytes 983048 | tf_op jit(solution)/shard_map/ppermute | solution.py:321
  2.3 0.0 copy-start.2
  2.4 2.6 %collective-permute-start.1 = (f32[4,8,640]{2,1,0:T(8,128)S(1)}, f32[4,8,640]{2,1,0:T(8,128)S(1)}, u32[]{:S(2)}, u32[]{:S(2)}) collective-permute-start(f32[4,8,640]{2,1,0:T(8,128)S(1)} %get-tuple-element.60), channel_id=1, source_target_pairs={{0,2},{2,0},{4,6},{6,4},{8,10},{10,8},{12,14},{14,12},{1,3},{3,1},... | collective-permute-start | bytes 245768 | tf_op jit(solution)/shard_map/ppermute | solution.py:320
  5.0 0.2 collective-permute-start
  5.1 0.0 copy-done.4
  5.1 0.0 copy-done.5
  5.1 0.0 copy-done.6
  5.2 0.0 copy-done.7
  5.2 0.0 copy-done.8
  5.2 0.0 copy-done.2
  5.2 0.0 copy-done.3
  5.2 0.7 %weights.1 = (f32[16,8,640]{2,1,0:T(8,128)S(1)}, f32[16,8,640]{2,1,0:T(8,128)S(1)}, f32[16,8,640]{2,1,0:T(8,128)S(1)}, f32[16,8,640]{2,1,0:T(8,128)S(1)}, f32[16...) custom-call(f32[16,8,640]{2,1,0:T(8,128)S(1)} %pad_maximum_fusion.waves, f32[16,4,640]{2,1,0:T(4,128)S(1)} %copy-done.2, ...), custom_call_target="tpu_custom_call" | custom-call | flops 4096000 | bytes 1638400 | tf_op jit(solution)/shard_map/weights/pallas_call | solution.py:338
  5.9 0.0 collective-permute-done.2.other
  5.9 0.5 %depth.1 = (f32[16,8,640]{2,1,0:T(8,128)S(1)}, f32[16,8,640]{2,1,0:T(8,128)S(1)}) custom-call(f32[16,8,640]{2,1,0:T(8,128)S(1)} %pad_maximum_fusion.waves, f32[16,8,640]{2,1,0:T(8,128)S(1)} %collective-permute-done.2.other), custom_call_target="tpu_custom_call" | custom-call | flops 4096000 | bytes 1638400 | tf_op jit(solution)/shard_map/depth/pallas_call | solution.py:341
  6.4 2.6 %collective-permute-done.1 = f32[4,8,640]{2,1,0:T(8,128)S(1)} collective-permute-done((f32[4,8,640]{2,1,0:T(8,128)S(1)}, f32[4,8,640]{2,1,0:T(8,128)S(1)}, u32[]{:S(2)}, u32[]{:S(2)}) %collective-permute-start.1) | collective-permute-done | bytes 81952 | tf_op jit(solution)/shard_map/ppermute | solution.py:320
  9.0 0.0 collective-permute-done
  9.1 0.0 copy-start.9
  9.1 0.0 copy-start.10
  9.1 0.1 collective-permute-start.3
  9.2 0.0 copy-start
  9.2 0.0 copy-start.1
  9.2 1.7 %cross.1 = (f32[16,8,640]{2,1,0:T(8,128)S(1)}, f32[16,8,640]{2,1,0:T(8,128)S(1)}) custom-call(f32[16,8,640]{2,1,0:T(8,128)S(1)} %pad_maximum_fusion.waves, f32[16,8,640]{2,1,0:T(8,128)S(1)} %get-tuple-element.37.dz, f32[16,8,640]{2,1,0:T(8,128)S(1)} %get-tuple-element.38.dzz, f32[16,8,640]{2,1,0:T(8,128)S(1)} %get-tuple-element.39.axis_y, ...), custom_call_target="tpu_custom_call" | custom-call | flops 4096000 | bytes 1638400 | tf_op jit(solution)/shard_map/cross/pallas_call | solution.py:345
  10.9 0.0 collective-permute-done.3.edges_other
  10.9 0.0 copy-done.9
  10.9 0.0 copy-done.10
  10.9 0.0 copy-done
  10.9 0.0 copy-done.1
  10.9 0.0 copy-start.11
  11.0 0.0 copy-start.12
  11.0 1.9 %step.1 = (f32[16,8,640]{2,1,0:T(8,128)S(1)}, f32[64,640]{1,0:T(8,128)S(1)}, f32[24,640]{1,0:T(8,128)S(1)}, f32[24,640]{1,0:T(8,128)S(1)}, f32[8,640]{1,0:T(8,128)S(1)}, /*index=5*/f32[8,640]{1,0:T(8,128)S(1)}) custom-call(f32[16,8,640]{2,1,0:T(8,128)S(1)} %pad_maximum_fusion.waves, f32[8,8,640]{2,1,0:T(8,128)S(1)} %constant_dynamic-update-slice_fusion.edges, ...), custom_call_target="tpu_custom_call" | custom-call | flops 16384000 | bytes 1638400 | tf_op jit(solution)/shard_map/step/pallas_call | solution.py:364
  12.9 3.8 %collective-permute-start.4 = (f32[24,640]{1,0:T(8,128)S(1)}, f32[24,640]{1,0:T(8,128)S(1)}, u32[]{:S(2)}, u32[]{:S(2)}) collective-permute-start(f32[24,640]{1,0:T(8,128)S(1)} %get-tuple-element.52), channel_id=1, source_target_pairs={{0,14},{2,4},{4,2},{6,8},{8,6},{10,12},{12,10},{14,0},{1,15},{3,5}... | collective-permute-start | bytes 184328 | tf_op jit(solution)/shard_map/ppermute | solution.py:371
  16.7 0.6 %collective-permute-start.5 = (f32[24,640]{1,0:T(8,128)S(1)}, f32[24,640]{1,0:T(8,128)S(1)}, u32[]{:S(2)}, u32[]{:S(2)}) collective-permute-start(f32[24,640]{1,0:T(8,128)S(1)} %get-tuple-element.53), channel_id=1, source_target_pairs={{0,2},{2,0},{4,6},{6,4},{8,10},{10,8},{12,14},{14,12},{1,3},{3,1},... | collective-permute-start | bytes 184328 | tf_op jit(solution)/shard_map/ppermute | solution.py:371
  17.3 1.6 %collective-permute-start.6 = (f32[8,640]{1,0:T(8,128)S(1)}, f32[8,640]{1,0:T(8,128)S(1)}, u32[]{:S(2)}, u32[]{:S(2)}) collective-permute-start(f32[8,640]{1,0:T(8,128)S(1)} %get-tuple-element.54), channel_id=1, source_target_pairs={{0,12},{2,14},{4,8},{6,10},{8,4},{10,6},{12,0},{14,2},{1,13},{3,15... | collective-permute-start | bytes 61448 | tf_op jit(solution)/shard_map/ppermute | solution.py:371
  18.9 1.5 %collective-permute-start.7 = (f32[8,640]{1,0:T(8,128)S(1)}, f32[8,640]{1,0:T(8,128)S(1)}, u32[]{:S(2)}, u32[]{:S(2)}) collective-permute-start(f32[8,640]{1,0:T(8,128)S(1)} %get-tuple-element.55), channel_id=1, source_target_pairs={{0,4},{2,6},{4,0},{6,2},{8,12},{10,14},{12,8},{14,10},{1,5},{3,7},... | collective-permute-start | bytes 61448 | tf_op jit(solution)/shard_map/ppermute | solution.py:371
  20.5 0.0 copy-done.11
  20.5 0.0 copy-done.12
  20.5 0.8 %own.1 = (f32[16,4,640]{2,1,0:T(4,128)}, f32[16,4,640]{2,1,0:T(4,128)}, f32[64,640]{1,0:T(8,128)S(1)}) custom-call(f32[16,8,640]{2,1,0:T(8,128)S(1)} %get-tuple-element.47.pressure, f32[64,640]{1,0:T(8,128)S(1)} %get-tuple-element.48.crossline, bf16[64,64]{1,0:T(8,128)(2,1)S(1)} %copy-done.12, bf16[64,64]{1,0:T(8,128)(2,1)S(1)} %copy-done.11), custom_call_target="tpu_custom_call" | custom-call | flops 4096000 | bytes 1638400 | tf_op jit(solution)/shard_map/own/pallas_call | solution.py:373
  21.3 1.6 %collective-permute-done.6.rest_2_ = f32[8,640]{1,0:T(8,128)S(1)} collective-permute-done((f32[8,640]{1,0:T(8,128)S(1)}, f32[8,640]{1,0:T(8,128)S(1)}, u32[]{:S(2)}, u32[]{:S(2)}) %collective-permute-start.6) | collective-permute-done | bytes 20512 | tf_op jit(solution)/shard_map/ppermute | solution.py:371
  22.9 0.0 collective-permute-done.7.rest_3_
  23.0 0.0 collective-permute-done.4.rest_0_
  23.0 0.0 collective-permute-done.5.rest_1_
  23.0 0.8 %finish.1 = (f32[8,4,640]{2,1,0:T(4,128)}, f32[4,4,640]{2,1,0:T(4,128)}, f32[2,4,640]{2,1,0:T(4,128)}, f32[2,4,640]{2,1,0:T(4,128)}) custom-call(f32[64,640]{1,0:T(8,128)S(1)} %get-tuple-element.51.mine, f32[24,640]{1,0:T(8,128)S(1)} %collective-permute-done.4.rest_0_, f32[24,640]{1,0:T(8,128)S(1)} %collective-permute-done.5.rest_1_, ...), custom_call_target="tpu_custom_call" | custom-call | flops 819200 | bytes 1638400 | tf_op jit(solution)/shard_map/finish/pallas_call | solution.py:376
  (4 shorter events, 0.0 us)
Async XLA Ops:
  0.6 4.5 %copy-start.4 = (bf16[16,4,640]{2,1,0:T(4,128)(2,1)S(1)}, bf16[16,4,640]{2,1,0:T(4,128)(2,1)}, u32[]{:S(2)}) copy-start(bf16[16,4,640]{2,1,0:T(4,128)(2,1)} %courant.1) | copy-start | bytes 245764
  0.6 4.5 %copy-start.5 = (bf16[16,4,640]{2,1,0:T(4,128)(2,1)S(1)}, bf16[16,4,640]{2,1,0:T(4,128)(2,1)}, u32[]{:S(2)}) copy-start(bf16[16,4,640]{2,1,0:T(4,128)(2,1)} %epsilon.1) | copy-start | bytes 245764
  0.7 4.5 %copy-start.6 = (bf16[16,4,640]{2,1,0:T(4,128)(2,1)S(1)}, bf16[16,4,640]{2,1,0:T(4,128)(2,1)}, u32[]{:S(2)}) copy-start(bf16[16,4,640]{2,1,0:T(4,128)(2,1)} %delta.1) | copy-start | bytes 245764
  0.7 4.5 %copy-start.7 = (bf16[16,4,640]{2,1,0:T(4,128)(2,1)S(1)}, bf16[16,4,640]{2,1,0:T(4,128)(2,1)}, u32[]{:S(2)}) copy-start(bf16[16,4,640]{2,1,0:T(4,128)(2,1)} %tilt.1) | copy-start | bytes 245764
  0.7 4.5 %copy-start.8 = (bf16[16,4,640]{2,1,0:T(4,128)(2,1)S(1)}, bf16[16,4,640]{2,1,0:T(4,128)(2,1)}, u32[]{:S(2)}) copy-start(bf16[16,4,640]{2,1,0:T(4,128)(2,1)} %azimuth.1) | copy-start | bytes 245764
  1.8 4.1 %collective-permute-start.2 = (f32[16,8,640]{2,1,0:T(8,128)S(1)}, f32[16,8,640]{2,1,0:T(8,128)S(1)}, u32[]{:S(2)}, u32[]{:S(2)}) collective-permute-start(f32[16,8,640]{2,1,0:T(8,128)S(1)} %pad_maximum_fusion.waves), channel_id=1, source_target_pairs={{0,1},{1,0},{2,3},{3,2},{4,5},{5,4},{6,7},{7,6},{8,9},{9,8},{10,11... | collective-permute-start | bytes 983048 | tf_op jit(solution)/shard_map/ppermute | solution.py:321
  2.3 2.8 %copy-start.2 = (f32[16,4,640]{2,1,0:T(4,128)S(1)}, f32[16,4,640]{2,1,0:T(4,128)}, u32[]{:S(2)}) copy-start(f32[16,4,640]{2,1,0:T(4,128)} %prior_p.1) | copy-start | bytes 491524
  2.3 2.8 %copy-start.3 = (f32[16,4,640]{2,1,0:T(4,128)S(1)}, f32[16,4,640]{2,1,0:T(4,128)}, u32[]{:S(2)}) copy-start(f32[16,4,640]{2,1,0:T(4,128)} %prior_q.1) | copy-start | bytes 491524
  2.4 6.7 %collective-permute-start.1 = (f32[4,8,640]{2,1,0:T(8,128)S(1)}, f32[4,8,640]{2,1,0:T(8,128)S(1)}, u32[]{:S(2)}, u32[]{:S(2)}) collective-permute-start(f32[4,8,640]{2,1,0:T(8,128)S(1)} %get-tuple-element.60), channel_id=1, source_target_pairs={{0,2},{2,0},{4,6},{6,4},{8,10},{10,8},{12,14},{14,12},{1,3},{3,1},... | collective-permute-start | bytes 245768 | tf_op jit(solution)/shard_map/ppermute | solution.py:320
  5.0 4.1 %collective-permute-start = (f32[4,8,640]{2,1,0:T(8,128)S(1)}, f32[4,8,640]{2,1,0:T(8,128)S(1)}, u32[]{:S(2)}, u32[]{:S(2)}) collective-permute-start(f32[4,8,640]{2,1,0:T(8,128)S(1)} %get-tuple-element.61), channel_id=1, source_target_pairs={{0,1},{1,0},{2,4},{3,5},{4,2},{5,3},{6,8},{7,9},{8,6},{9,7},{10,12... | collective-permute-start | bytes 245768 | tf_op jit(solution)/shard_map/ppermute | solution.py:319
  9.1 1.8 %copy-start.9 = (bf16[64,64]{1,0:T(8,128)(2,1)S(1)}, bf16[64,64]{1,0:T(8,128)(2,1)}, u32[]{:S(2)}) copy-start(bf16[64,64]{1,0:T(8,128)(2,1)} %constant.35.clone.inline_low) | copy-start | bytes 24580
  9.1 1.8 %copy-start.10 = (bf16[64,64]{1,0:T(8,128)(2,1)S(1)}, bf16[64,64]{1,0:T(8,128)(2,1)}, u32[]{:S(2)}) copy-start(bf16[64,64]{1,0:T(8,128)(2,1)} %constant.34.clone.inline_high) | copy-start | bytes 24580
  9.1 1.8 %collective-permute-start.3 = (f32[8,8,640]{2,1,0:T(8,128)S(1)}, f32[8,8,640]{2,1,0:T(8,128)S(1)}, u32[]{:S(2)}, u32[]{:S(2)}) collective-permute-start(f32[8,8,640]{2,1,0:T(8,128)S(1)} %constant_dynamic-update-slice_fusion.edges), channel_id=1, source_target_pairs={{0,1},{1,0},{2,3},{3,2},{4,5},{5,4},{6,7},{7,6},{8,9},{9,8},{10,11... | collective-permute-start | bytes 491528 | tf_op jit(solution)/shard_map/ppermute | solution.py:344
  9.2 1.7 %copy-start = (bf16[640,640]{1,0:T(8,128)(2,1)S(1)}, bf16[640,640]{1,0:T(8,128)(2,1)}, u32[]{:S(2)}) copy-start(bf16[640,640]{1,0:T(8,128)(2,1)} %constant.33.clone.across_low) | copy-start | bytes 2457604
  9.2 1.7 %copy-start.1 = (bf16[640,640]{1,0:T(8,128)(2,1)S(1)}, bf16[640,640]{1,0:T(8,128)(2,1)}, u32[]{:S(2)}) copy-start(bf16[640,640]{1,0:T(8,128)(2,1)} %constant.32.clone.across_high) | copy-start | bytes 2457604
  10.9 9.5 %copy-start.11 = (bf16[64,64]{1,0:T(8,128)(2,1)S(1)}, bf16[64,64]{1,0:T(8,128)(2,1)}, u32[]{:S(2)}) copy-start(bf16[64,64]{1,0:T(8,128)(2,1)} %constant.37.clone.own_low) | copy-start | bytes 24580
  11.0 9.5 %copy-start.12 = (bf16[64,64]{1,0:T(8,128)(2,1)S(1)}, bf16[64,64]{1,0:T(8,128)(2,1)}, u32[]{:S(2)}) copy-start(bf16[64,64]{1,0:T(8,128)(2,1)} %constant.36.clone.own_high) | copy-start | bytes 24580
  12.9 10.1 %collective-permute-start.4 = (f32[24,640]{1,0:T(8,128)S(1)}, f32[24,640]{1,0:T(8,128)S(1)}, u32[]{:S(2)}, u32[]{:S(2)}) collective-permute-start(f32[24,640]{1,0:T(8,128)S(1)} %get-tuple-element.52), channel_id=1, source_target_pairs={{0,14},{2,4},{4,2},{6,8},{8,6},{10,12},{12,10},{14,0},{1,15},{3,5}... | collective-permute-start | bytes 184328 | tf_op jit(solution)/shard_map/ppermute | solution.py:371
  16.7 6.2 %collective-permute-start.5 = (f32[24,640]{1,0:T(8,128)S(1)}, f32[24,640]{1,0:T(8,128)S(1)}, u32[]{:S(2)}, u32[]{:S(2)}) collective-permute-start(f32[24,640]{1,0:T(8,128)S(1)} %get-tuple-element.53), channel_id=1, source_target_pairs={{0,2},{2,0},{4,6},{6,4},{8,10},{10,8},{12,14},{14,12},{1,3},{3,1},... | collective-permute-start | bytes 184328 | tf_op jit(solution)/shard_map/ppermute | solution.py:371
  17.3 5.6 %collective-permute-start.6 = (f32[8,640]{1,0:T(8,128)S(1)}, f32[8,640]{1,0:T(8,128)S(1)}, u32[]{:S(2)}, u32[]{:S(2)}) collective-permute-start(f32[8,640]{1,0:T(8,128)S(1)} %get-tuple-element.54), channel_id=1, source_target_pairs={{0,12},{2,14},{4,8},{6,10},{8,4},{10,6},{12,0},{14,2},{1,13},{3,15... | collective-permute-start | bytes 61448 | tf_op jit(solution)/shard_map/ppermute | solution.py:371
  18.9 4.0 %collective-permute-start.7 = (f32[8,640]{1,0:T(8,128)S(1)}, f32[8,640]{1,0:T(8,128)S(1)}, u32[]{:S(2)}, u32[]{:S(2)}) collective-permute-start(f32[8,640]{1,0:T(8,128)S(1)} %get-tuple-element.55), channel_id=1, source_target_pairs={{0,4},{2,6},{4,0},{6,2},{8,12},{10,14},{12,8},{14,10},{1,5},{3,7},... | collective-permute-start | bytes 61448 | tf_op jit(solution)/shard_map/ppermute | solution.py:371

commit v5 on v4

--- a/solution.py
+++ b/solution.py
@@ -183,17 +183,46 @@
     lax.fori_loop(0, rows, row, 0, unroll=4)
 
 
+def halo_places(size, rows):
+    place = lax.axis_index("xy")
+    even = place % 2 == 0
+    left_at, right_at = jnp.where(even, 4, 0), jnp.where(even, 0, 4)
+    left_in = jnp.where(place > 0, 1.0, 0.0)
+    right_in = jnp.where(place < size - 1, 1.0, 0.0)
+    for x in range(4):
+        yield left_at + x, x, left_in
+        yield right_at + x, rows + 4 + x, right_in
+
+
+def inline_kernel(size, waves, edges, axis_x, axis_y, h_part, sum_part, h_more, sum_all, ext):
+    rows, _, width = waves.shape
+    for at, to, inside in halo_places(size, rows):
+        ext[to] = edges[at] * inside
+    for x in range(rows):
+        ext[x + 4] = waves[x]
+
+    def row(x, carry):
+        ahead = [ext[x + 4 + k] for k in range(1, 5)]
+        behind = [ext[x + 4 - k] for k in range(1, 5)]
+        dxx = second_of(ext[x + 4], ahead, behind)
+        dxy = first_of(*shifted(first_of(ahead, behind), width))
+        n_x = axis_x[x]
+        h_more[x] = h_part[x] + n_x * (n_x * dxx + 2.0 * (axis_y[x] * dxy))
+        sum_all[x] = sum_part[x] + dxx
+        return carry
+
+    lax.fori_loop(0, rows, row, 0, unroll=4)
+
+
 def step_kernel(
     size,
     gives,
-    waves,
     edges,
     edges_other,
     dz,
-    h_part,
-    sum_part,
+    h_more,
+    sum_all,
     axis_x,
-    axis_y,
     axis_z,
     gain_a,
     gain_b,
@@ -206,41 +235,27 @@
     crossline,
     *rest,
 ):
-    sends, (ext, dz_ext) = rest[:-2], rest[-2:]
-    rows, _, width = waves.shape
+    sends, dz_ext = rest[:-1], rest[-1]
+    rows, _, width = dz.shape
     lower = lax.axis_index("gz") == 0
     place = lax.axis_index("xy")
     even, early = place % 2 == 0, place % 4 < 2
-    left_at, right_at = jnp.where(even, 4, 0), jnp.where(even, 0, 4)
-    left_in = jnp.where(place > 0, 1.0, 0.0)
-    right_in = jnp.where(place < size - 1, 1.0, 0.0)
-    top = lax.broadcasted_iota(jnp.int32, waves.shape[1:], 0) < 4
-
-    for x in range(4):
-        for at, inside, to in ((left_at, left_in, x), (right_at, right_in, rows + 4 + x)):
-            own, far = edges[at + x] * inside, edges_other[at + x] * inside
-            ext[to] = own
-            dz_ext[to] = first_of(*depth_neighbours(own, far, lower))
+    top = lax.broadcasted_iota(jnp.int32, dz.shape[1:], 0) < 4
+
+    for at, to, inside in halo_places(size, rows):
+        own, far = edges[at] * inside, edges_other[at] * inside
+        dz_ext[to] = first_of(*depth_neighbours(own, far, lower))
     for x in range(rows):
-        ext[x + 4] = waves[x]
         dz_ext[x + 4] = dz[x]
 
-    def row(x, carry):
-        ahead = [ext[x + 4 + k] for k in range(1, 5)]
-        behind = [ext[x + 4 - k] for k in range(1, 5)]
-        dxx = second_of(ext[x + 4], ahead, behind)
-        dxy = first_of(*shifted(first_of(ahead, behind), width))
+    for x in range(rows):
         dxz = first_of(
             [dz_ext[x + 4 + k] for k in range(1, 5)], [dz_ext[x + 4 - k] for k in range(1, 5)]
         )
-        n_x = axis_x[x]
-        h_one = h_part[x] + n_x * (n_x * dxx + 2.0 * (axis_y[x] * dxy + axis_z[x] * dxz))
-        h_two = dxx + sum_part[x] - h_one
+        h_one = h_more[x] + 2.0 * (axis_x[x] * axis_z[x] * dxz)
+        h_two = sum_all[x] - h_one
         mixed = jnp.where(top, h_two, h_one)
         pressure[x] = base[x] + gain_a[x] * mixed + gain_b[x] * pltpu.roll(mixed, 4, 0)
-        return carry
-
-    lax.fori_loop(0, rows, row, 0, unroll=4)
 
     packed = jnp.concatenate(
         [
@@ -257,8 +272,8 @@
     )
     sends[0][...] = jnp.where(even, to_previous, to_next)
     sends[1][...] = jnp.where(even, to_next, to_previous)
-    sends[2][...] = jnp.where(early, to_second_previous, to_second_next)
-    sends[3][...] = jnp.where(early, to_second_next, to_second_previous)
+    sends[2][...] = jnp.where(early, to_second_next, to_second_previous)
+    sends[3][...] = jnp.where(early, to_second_previous, to_second_next)
 
 
 def own_kernel(pressure, crossline, own_high, own_low, next_p, next_q, mine):
@@ -269,7 +284,7 @@
 
 
 def finish_kernel(takes, mine, *rest):
-    outer, inner, outer_second, inner_second = (ref[...] for ref in rest[:4])
+    outer, inner, inner_second, outer_second = (ref[...] for ref in rest[:4])
     outs = rest[4:]
     place = lax.axis_index("xy")
     even, early = place % 2 == 0, place % 4 < 2
@@ -298,8 +313,8 @@
     return [
         [(i, (i - one[i]) % size) for i in range(size)],
         [(i, i + one[i]) for i in range(size)],
+        [(i, i + two[i]) for i in range(size)],
         [(i, (i - two[i]) % size) for i in range(size)],
-        [(i, i + two[i]) for i in range(size)],
     ]
 
 
@@ -339,10 +354,17 @@
         waves, prior_p, prior_q, courant, epsilon, thomsen_delta, tilt_angle, azimuth
     )
     dz, dzz = kernel(depth_kernel, [stack] * 2, 100, "depth")(waves, other)
-    outer, inner, dz, axis_x = lax.optimization_barrier((outer, inner, dz, axis_x))
+    h_part, sum_part = kernel(cross_kernel, [stack] * 2, 100, "cross")(waves, dz, dzz, axis_y, axis_z)
+    outer, inner, h_part, sum_part = lax.optimization_barrier((outer, inner, h_part, sum_part))
     edges = jnp.concatenate([inner, outer], axis=0)
     edges_other = lax.ppermute(edges, "gz", cores)
-    h_part, sum_part = kernel(cross_kernel, [stack] * 2, 100, "cross")(waves, dz, dzz, axis_y, axis_z)
+    h_more, sum_all = kernel(
+        functools.partial(inline_kernel, size),
+        [stack] * 2,
+        100,
+        "inline",
+        [pltpu.VMEM((rows + 8, 8, width), f32)],
+    )(waves, edges, axis_x, axis_y, h_part, sum_part)
 
     own, factors = inline_blocks(rows)
     offsets = (-1, 1, -2, 2)
@@ -366,8 +388,8 @@
         [stack, flat] + [jax.ShapeDtypeStruct((count, width), f32) for _, count in gives],
         400,
         "step",
-        [pltpu.VMEM((rows + 8, 8, width), f32)] * 2,
-    )(waves, edges, edges_other, dz, h_part, sum_part, axis_x, axis_y, axis_z, *gains, *across, *inline)
+        [pltpu.VMEM((rows + 8, 8, width), f32)],
+    )(edges, edges_other, dz, h_more, sum_all, axis_x, axis_z, *gains, *across, *inline)
     received = [lax.ppermute(send, "xy", pair) for send, pair in zip(sends, pairs)]
     grid = jax.ShapeDtypeStruct(wave_p.shape, f32)
     next_p, next_q, mine = kernel(own_kernel, [grid, grid, flat], 100, "own")(

time: 23.9 us -> 24.2 us (1.013)
  starting transfers between devices: 11 us -> 11.9 us
  waiting for transfers between devices: 4.31 us -> 3.48 us
    ppermute x1, waiting for transfers between devices: 2.65 us -> 0.96 us  [body(): inner = lax.ppermute(jnp.where(even, last, leading), 'xy', pairs[1])]
    pallas_call x0 -> x1, Pallas kernels: none -> 1.09 us  [body(): kernel(functools.partial(inline_kernel, size), [stack] * 2, 100, 'inline'...]
    pallas_call x1, Pallas kernels: 1.92 us -> 1 us  [body(): kernel(functools.partial(step_kernel, size, gives), [stack, flat] + [jax....]
    ppermute x4, starting transfers between devices: 7.59 us -> 8.49 us  [body(): lax.ppermute(send, 'xy', pair)]
    ppermute x4, waiting for transfers between devices: 1.65 us -> 2.28 us  [body(): lax.ppermute(send, 'xy', pair)]
  transfers between devices with their start and end apart: 8 -> 8, of which waited for: 2 -> 3; matrix products, arithmetic and copies ran while one was open for 0% -> 0% of each run, Pallas kernels for 15% -> 20%
where the time goes in v5:
time: 24.2 us; the launch traced here: 24 us
  starting transfers between devices  11.9 us (49%)
  Pallas kernels  6.59 us (27%)
  waiting for transfers between devices  3.48 us (14%)
  other arithmetic  1.15 us (5%)
  between operations  0.83 us (3%)
    ppermute x4, starting transfers between devices, body(): lax.ppermute(send, 'xy', pair)  8.49 us
    ppermute x1, starting transfers between devices, body(): inner = lax.ppermute(jnp.where(even, last, leading), 'xy', pairs[1])  2.6 us
    ppermute x4, waiting for transfers between devices, body(): lax.ppermute(send, 'xy', pair)  2.28 us
    pallas_call x1, Pallas kernels, body(): kernel(cross_kernel, [stack] * 2, 100, 'cross')  1.68 us
    concatenate x1, other arithmetic, body(): waves = lax.optimization_barrier(jnp.concatenate([wave_p, wave_q], axis=1))  1.13 us
    pallas_call x1, Pallas kernels, body(): kernel(functools.partial(inline_kernel, size), [stack] * 2, 100, 'inline'...  1.09 us
    pallas_call x1, Pallas kernels, body(): kernel(functools.partial(step_kernel, size, gives), [stack, flat] + [jax....  1 us
    ppermute x1, waiting for transfers between devices, body(): inner = lax.ppermute(jnp.where(even, last, leading), 'xy', pairs[1])  0.96 us
  transfers between devices with their start and end apart: 8, of which 3 were waited for; matrix products, arithmetic and copies ran while one was open for 0% of the time, Pallas kernels for 20%

profile of v5, /device:TPU:0, one launch (start us, length us, event | category | flops | bytes accessed | tf_op | source)
XLA Modules:
  0.0 24.0 jit_solution(14384168037037495501)
XLA Ops:
  0.6 0.0 copy-start.4
  0.6 0.0 copy-start.5
  0.7 0.0 copy-start.6
  0.7 0.0 copy-start.7
  0.7 0.0 copy-start.8
  0.7 1.1 %pad_maximum_fusion.waves = f32[16,8,640]{2,1,0:T(8,128)S(1)} fusion(f32[16,4,640]{2,1,0:T(4,128)} %param.16, f32[16,4,640]{2,1,0:T(4,128)} %param.15), kind=kLoop, calls=%fused_computation | loop fusion | flops 81920 | bytes 655360 | tf_op jit(solution)/shard_map/concatenate | solution.py:327
  1.8 0.5 %collective-permute-start.2 = (f32[16,8,640]{2,1,0:T(8,128)S(1)}, f32[16,8,640]{2,1,0:T(8,128)S(1)}, u32[]{:S(2)}, u32[]{:S(2)}) collective-permute-start(f32[16,8,640]{2,1,0:T(8,128)S(1)} %pad_maximum_fusion.waves), channel_id=1, source_target_pairs={{0,1},{1,0},{2,3},{3,2},{4,5},{5,4},{6,7},{7,6},{8,9},{9,8},{10,11... | collective-permute-start | bytes 983048 | tf_op jit(solution)/shard_map/ppermute | solution.py:336
  2.4 2.6 %collective-permute-start.1 = (f32[4,8,640]{2,1,0:T(8,128)S(1)}, f32[4,8,640]{2,1,0:T(8,128)S(1)}, u32[]{:S(2)}, u32[]{:S(2)}) collective-permute-start(f32[4,8,640]{2,1,0:T(8,128)S(1)} %get-tuple-element.64), channel_id=1, source_target_pairs={{0,2},{2,0},{4,6},{6,4},{8,10},{10,8},{12,14},{14,12},{1,3},{3,1},... | collective-permute-start | bytes 245768 | tf_op jit(solution)/shard_map/ppermute | solution.py:335
  5.0 0.2 collective-permute-start
  5.1 0.0 copy-done.4
  5.1 0.0 copy-done.5
  5.1 0.0 copy-done.6
  5.2 0.0 copy-done.7
  5.2 0.0 copy-done.8
  5.2 0.0 copy-done.2
  5.2 0.0 copy-done.3
  5.2 0.7 %weights.1 = (f32[16,8,640]{2,1,0:T(8,128)S(1)}, f32[16,8,640]{2,1,0:T(8,128)S(1)}, f32[16,8,640]{2,1,0:T(8,128)S(1)}, f32[16,8,640]{2,1,0:T(8,128)S(1)}, f32[16...) custom-call(f32[16,8,640]{2,1,0:T(8,128)S(1)} %pad_maximum_fusion.waves, f32[16,4,640]{2,1,0:T(4,128)S(1)} %copy-done.2, ...), custom_call_target="tpu_custom_call" | custom-call | flops 4096000 | bytes 1638400 | tf_op jit(solution)/shard_map/weights/pallas_call | solution.py:353
  5.9 0.0 collective-permute-done.2.other
  5.9 0.5 %depth.1 = (f32[16,8,640]{2,1,0:T(8,128)S(1)}, f32[16,8,640]{2,1,0:T(8,128)S(1)}) custom-call(f32[16,8,640]{2,1,0:T(8,128)S(1)} %pad_maximum_fusion.waves, f32[16,8,640]{2,1,0:T(8,128)S(1)} %collective-permute-done.2.other), custom_call_target="tpu_custom_call" | custom-call | flops 4096000 | bytes 1638400 | tf_op jit(solution)/shard_map/depth/pallas_call | solution.py:356
  6.4 1.7 %cross.1 = (f32[16,8,640]{2,1,0:T(8,128)S(1)}, f32[16,8,640]{2,1,0:T(8,128)S(1)}) custom-call(f32[16,8,640]{2,1,0:T(8,128)S(1)} %pad_maximum_fusion.waves, f32[16,8,640]{2,1,0:T(8,128)S(1)} %get-tuple-element.35.dz, f32[16,8,640]{2,1,0:T(8,128)S(1)} %get-tuple-element.36.dzz, f32[16,8,640]{2,1,0:T(8,128)S(1)} %get-tuple-element.37.axis_y, ...), custom_call_target="tpu_custom_call" | custom-call | flops 4096000 | bytes 1638400 | tf_op jit(solution)/shard_map/cross/pallas_call | solution.py:357
  8.1 1.0 %collective-permute-done.1 = f32[4,8,640]{2,1,0:T(8,128)S(1)} collective-permute-done((f32[4,8,640]{2,1,0:T(8,128)S(1)}, f32[4,8,640]{2,1,0:T(8,128)S(1)}, u32[]{:S(2)}, u32[]{:S(2)}) %collective-permute-start.1) | collective-permute-done | bytes 81952 | tf_op jit(solution)/shard_map/ppermute | solution.py:335
  9.0 0.0 collective-permute-done
  9.1 0.1 collective-permute-start.3
  9.2 0.0 copy-start
  9.2 0.0 copy-start.1
  9.2 0.0 copy-start.9
  9.2 0.0 copy-start.10
  9.2 1.1 %inline.1 = (f32[16,8,640]{2,1,0:T(8,128)S(1)}, f32[16,8,640]{2,1,0:T(8,128)S(1)}) custom-call(f32[16,8,640]{2,1,0:T(8,128)S(1)} %pad_maximum_fusion.waves, f32[8,8,640]{2,1,0:T(8,128)S(1)} %constant_dynamic-update-slice_fusion.edges, f32[16,8,640]{2,1,0:T(8,128)S(1)} %get-tuple-element.43.axis_x, f32[16,8,640]{2,1,0:T(8,128)S(1)} %get-tuple-element.37.axis_y, ...), custom_call_target="tpu_custom_call" | custom-call | flops 4096000 | bytes 1638400 | tf_op jit(solution)/shard_map/inline/pallas_call | solution.py:361
  10.3 0.2 collective-permute-done.3.edges_other
  10.5 0.0 copy-done
  10.5 0.0 copy-done.1
  10.6 0.0 copy-done.9
  10.6 0.0 copy-done.10
  10.6 0.0 copy-start.11
  10.6 0.0 copy-start.12
  10.6 1.0 %step.1 = (f32[16,8,640]{2,1,0:T(8,128)S(1)}, f32[64,640]{1,0:T(8,128)S(1)}, f32[24,640]{1,0:T(8,128)S(1)}, f32[24,640]{1,0:T(8,128)S(1)}, f32[8,640]{1,0:T(8,128)S(1)}, /*index=5*/f32[8,640]{1,0:T(8,128)S(1)}) custom-call(f32[8,8,640]{2,1,0:T(8,128)S(1)} %constant_dynamic-update-slice_fusion.edges, f32[8,8,640]{2,1,0:T(8,128)S(1)} %collective-permute-done.3.edges_other, ...), custom_call_target="tpu_custom_call" | custom-call | flops 16384000 | bytes 1638400 | tf_op jit(solution)/shard_map/step/pallas_call | solution.py:386
  11.6 3.8 %collective-permute-start.4 = (f32[24,640]{1,0:T(8,128)S(1)}, f32[24,640]{1,0:T(8,128)S(1)}, u32[]{:S(2)}, u32[]{:S(2)}) collective-permute-start(f32[24,640]{1,0:T(8,128)S(1)} %get-tuple-element.56), channel_id=1, source_target_pairs={{0,14},{2,4},{4,2},{6,8},{8,6},{10,12},{12,10},{14,0},{1,15},{3,5}... | collective-permute-start | bytes 184328 | tf_op jit(solution)/shard_map/ppermute | solution.py:393
  15.4 0.6 %collective-permute-start.5 = (f32[24,640]{1,0:T(8,128)S(1)}, f32[24,640]{1,0:T(8,128)S(1)}, u32[]{:S(2)}, u32[]{:S(2)}) collective-permute-start(f32[24,640]{1,0:T(8,128)S(1)} %get-tuple-element.57), channel_id=1, source_target_pairs={{0,2},{2,0},{4,6},{6,4},{8,10},{10,8},{12,14},{14,12},{1,3},{3,1},... | collective-permute-start | bytes 184328 | tf_op jit(solution)/shard_map/ppermute | solution.py:393
  16.0 1.6 %collective-permute-start.6 = (f32[8,640]{1,0:T(8,128)S(1)}, f32[8,640]{1,0:T(8,128)S(1)}, u32[]{:S(2)}, u32[]{:S(2)}) collective-permute-start(f32[8,640]{1,0:T(8,128)S(1)} %get-tuple-element.58), channel_id=1, source_target_pairs={{0,4},{2,6},{4,0},{6,2},{8,12},{10,14},{12,8},{14,10},{1,5},{3,7},... | collective-permute-start | bytes 61448 | tf_op jit(solution)/shard_map/ppermute | solution.py:393
  17.6 2.5 %collective-permute-start.7 = (f32[8,640]{1,0:T(8,128)S(1)}, f32[8,640]{1,0:T(8,128)S(1)}, u32[]{:S(2)}, u32[]{:S(2)}) collective-permute-start(f32[8,640]{1,0:T(8,128)S(1)} %get-tuple-element.59), channel_id=1, source_target_pairs={{0,12},{2,14},{4,8},{6,10},{8,4},{10,6},{12,0},{14,2},{1,13},{3,15... | collective-permute-start | bytes 61448 | tf_op jit(solution)/shard_map/ppermute | solution.py:393
  20.1 0.0 copy-done.11
  20.1 0.0 copy-done.12
  20.1 0.8 %own.1 = (f32[16,4,640]{2,1,0:T(4,128)}, f32[16,4,640]{2,1,0:T(4,128)}, f32[64,640]{1,0:T(8,128)S(1)}) custom-call(f32[16,8,640]{2,1,0:T(8,128)S(1)} %get-tuple-element.51.pressure, f32[64,640]{1,0:T(8,128)S(1)} %get-tuple-element.52.crossline, bf16[64,64]{1,0:T(8,128)(2,1)S(1)} %copy-done.12, bf16[64,64]{1,0:T(8,128)(2,1)S(1)} %copy-done.11), custom_call_target="tpu_custom_call" | custom-call | flops 4096000 | bytes 1638400 | tf_op jit(solution)/shard_map/own/pallas_call | solution.py:395
  20.9 0.0 collective-permute-done.6.rest_2_
  20.9 2.3 %collective-permute-done.7.rest_3_ = f32[8,640]{1,0:T(8,128)S(1)} collective-permute-done((f32[8,640]{1,0:T(8,128)S(1)}, f32[8,640]{1,0:T(8,128)S(1)}, u32[]{:S(2)}, u32[]{:S(2)}) %collective-permute-start.7) | collective-permute-done | bytes 20512 | tf_op jit(solution)/shard_map/ppermute | solution.py:393
  23.2 0.0 collective-permute-done.4.rest_0_
  23.2 0.0 collective-permute-done.5.rest_1_
  23.2 0.8 %finish.1 = (f32[8,4,640]{2,1,0:T(4,128)}, f32[4,4,640]{2,1,0:T(4,128)}, f32[2,4,640]{2,1,0:T(4,128)}, f32[2,4,640]{2,1,0:T(4,128)}) custom-call(f32[64,640]{1,0:T(8,128)S(1)} %get-tuple-element.55.mine, f32[24,640]{1,0:T(8,128)S(1)} %collective-permute-done.4.rest_0_, f32[24,640]{1,0:T(8,128)S(1)} %collective-permute-done.5.rest_1_, ...), custom_call_target="tpu_custom_call" | custom-call | flops 819200 | bytes 1638400 | tf_op jit(solution)/shard_map/finish/pallas_call | solution.py:398
  (5 shorter events, 0.0 us)
Async XLA Ops:
  0.6 4.5 %copy-start.4 = (bf16[16,4,640]{2,1,0:T(4,128)(2,1)S(1)}, bf16[16,4,640]{2,1,0:T(4,128)(2,1)}, u32[]{:S(2)}) copy-start(bf16[16,4,640]{2,1,0:T(4,128)(2,1)} %courant.1) | copy-start | bytes 245764
  0.6 4.5 %copy-start.5 = (bf16[16,4,640]{2,1,0:T(4,128)(2,1)S(1)}, bf16[16,4,640]{2,1,0:T(4,128)(2,1)}, u32[]{:S(2)}) copy-start(bf16[16,4,640]{2,1,0:T(4,128)(2,1)} %epsilon.1) | copy-start | bytes 245764
  0.7 4.5 %copy-start.6 = (bf16[16,4,640]{2,1,0:T(4,128)(2,1)S(1)}, bf16[16,4,640]{2,1,0:T(4,128)(2,1)}, u32[]{:S(2)}) copy-start(bf16[16,4,640]{2,1,0:T(4,128)(2,1)} %delta.1) | copy-start | bytes 245764
  0.7 4.5 %copy-start.7 = (bf16[16,4,640]{2,1,0:T(4,128)(2,1)S(1)}, bf16[16,4,640]{2,1,0:T(4,128)(2,1)}, u32[]{:S(2)}) copy-start(bf16[16,4,640]{2,1,0:T(4,128)(2,1)} %tilt.1) | copy-start | bytes 245764
  0.7 4.5 %copy-start.8 = (bf16[16,4,640]{2,1,0:T(4,128)(2,1)S(1)}, bf16[16,4,640]{2,1,0:T(4,128)(2,1)}, u32[]{:S(2)}) copy-start(bf16[16,4,640]{2,1,0:T(4,128)(2,1)} %azimuth.1) | copy-start | bytes 245764
  1.8 4.1 %collective-permute-start.2 = (f32[16,8,640]{2,1,0:T(8,128)S(1)}, f32[16,8,640]{2,1,0:T(8,128)S(1)}, u32[]{:S(2)}, u32[]{:S(2)}) collective-permute-start(f32[16,8,640]{2,1,0:T(8,128)S(1)} %pad_maximum_fusion.waves), channel_id=1, source_target_pairs={{0,1},{1,0},{2,3},{3,2},{4,5},{5,4},{6,7},{7,6},{8,9},{9,8},{10,11... | collective-permute-start | bytes 983048 | tf_op jit(solution)/shard_map/ppermute | solution.py:336
  2.3 2.8 %copy-start.2 = (f32[16,4,640]{2,1,0:T(4,128)S(1)}, f32[16,4,640]{2,1,0:T(4,128)}, u32[]{:S(2)}) copy-start(f32[16,4,640]{2,1,0:T(4,128)} %prior_p.1) | copy-start | bytes 491524
  2.3 2.8 %copy-start.3 = (f32[16,4,640]{2,1,0:T(4,128)S(1)}, f32[16,4,640]{2,1,0:T(4,128)}, u32[]{:S(2)}) copy-start(f32[16,4,640]{2,1,0:T(4,128)} %prior_q.1) | copy-start | bytes 491524
  2.4 6.7 %collective-permute-start.1 = (f32[4,8,640]{2,1,0:T(8,128)S(1)}, f32[4,8,640]{2,1,0:T(8,128)S(1)}, u32[]{:S(2)}, u32[]{:S(2)}) collective-permute-start(f32[4,8,640]{2,1,0:T(8,128)S(1)} %get-tuple-element.64), channel_id=1, source_target_pairs={{0,2},{2,0},{4,6},{6,4},{8,10},{10,8},{12,14},{14,12},{1,3},{3,1},... | collective-permute-start | bytes 245768 | tf_op jit(solution)/shard_map/ppermute | solution.py:335
  5.0 4.1 %collective-permute-start = (f32[4,8,640]{2,1,0:T(8,128)S(1)}, f32[4,8,640]{2,1,0:T(8,128)S(1)}, u32[]{:S(2)}, u32[]{:S(2)}) collective-permute-start(f32[4,8,640]{2,1,0:T(8,128)S(1)} %get-tuple-element.65), channel_id=1, source_target_pairs={{0,1},{1,0},{2,4},{3,5},{4,2},{5,3},{6,8},{7,9},{8,6},{9,7},{10,12... | collective-permute-start | bytes 245768 | tf_op jit(solution)/shard_map/ppermute | solution.py:334
  9.1 1.5 %collective-permute-start.3 = (f32[8,8,640]{2,1,0:T(8,128)S(1)}, f32[8,8,640]{2,1,0:T(8,128)S(1)}, u32[]{:S(2)}, u32[]{:S(2)}) collective-permute-start(f32[8,8,640]{2,1,0:T(8,128)S(1)} %constant_dynamic-update-slice_fusion.edges), channel_id=1, source_target_pairs={{0,1},{1,0},{2,3},{3,2},{4,5},{5,4},{6,7},{7,6},{8,9},{9,8},{10,11... | collective-permute-start | bytes 491528 | tf_op jit(solution)/shard_map/ppermute | solution.py:360
  9.2 1.4 %copy-start = (bf16[640,640]{1,0:T(8,128)(2,1)S(1)}, bf16[640,640]{1,0:T(8,128)(2,1)}, u32[]{:S(2)}) copy-start(bf16[640,640]{1,0:T(8,128)(2,1)} %constant.33.clone.across_low) | copy-start | bytes 2457604
  9.2 1.4 %copy-start.1 = (bf16[640,640]{1,0:T(8,128)(2,1)S(1)}, bf16[640,640]{1,0:T(8,128)(2,1)}, u32[]{:S(2)}) copy-start(bf16[640,640]{1,0:T(8,128)(2,1)} %constant.32.clone.across_high) | copy-start | bytes 2457604
  9.2 1.4 %copy-start.9 = (bf16[64,64]{1,0:T(8,128)(2,1)S(1)}, bf16[64,64]{1,0:T(8,128)(2,1)}, u32[]{:S(2)}) copy-start(bf16[64,64]{1,0:T(8,128)(2,1)} %constant.35.clone.inline_low) | copy-start | bytes 24580
  9.2 1.4 %copy-start.10 = (bf16[64,64]{1,0:T(8,128)(2,1)S(1)}, bf16[64,64]{1,0:T(8,128)(2,1)}, u32[]{:S(2)}) copy-start(bf16[64,64]{1,0:T(8,128)(2,1)} %constant.34.clone.inline_high) | copy-start | bytes 24580
  10.6 9.5 %copy-start.11 = (bf16[64,64]{1,0:T(8,128)(2,1)S(1)}, bf16[64,64]{1,0:T(8,128)(2,1)}, u32[]{:S(2)}) copy-start(bf16[64,64]{1,0:T(8,128)(2,1)} %constant.37.clone.own_low) | copy-start | bytes 24580
  10.6 9.5 %copy-start.12 = (bf16[64,64]{1,0:T(8,128)(2,1)S(1)}, bf16[64,64]{1,0:T(8,128)(2,1)}, u32[]{:S(2)}) copy-start(bf16[64,64]{1,0:T(8,128)(2,1)} %constant.36.clone.own_high) | copy-start | bytes 24580
  11.6 11.6 %collective-permute-start.4 = (f32[24,640]{1,0:T(8,128)S(1)}, f32[24,640]{1,0:T(8,128)S(1)}, u32[]{:S(2)}, u32[]{:S(2)}) collective-permute-start(f32[24,640]{1,0:T(8,128)S(1)} %get-tuple-element.56), channel_id=1, source_target_pairs={{0,14},{2,4},{4,2},{6,8},{8,6},{10,12},{12,10},{14,0},{1,15},{3,5}... | collective-permute-start | bytes 184328 | tf_op jit(solution)/shard_map/ppermute | solution.py:393
  15.4 7.8 %collective-permute-start.5 = (f32[24,640]{1,0:T(8,128)S(1)}, f32[24,640]{1,0:T(8,128)S(1)}, u32[]{:S(2)}, u32[]{:S(2)}) collective-permute-start(f32[24,640]{1,0:T(8,128)S(1)} %get-tuple-element.57), channel_id=1, source_target_pairs={{0,2},{2,0},{4,6},{6,4},{8,10},{10,8},{12,14},{14,12},{1,3},{3,1},... | collective-permute-start | bytes 184328 | tf_op jit(solution)/shard_map/ppermute | solution.py:393
  16.0 4.9 %collective-permute-start.6 = (f32[8,640]{1,0:T(8,128)S(1)}, f32[8,640]{1,0:T(8,128)S(1)}, u32[]{:S(2)}, u32[]{:S(2)}) collective-permute-start(f32[8,640]{1,0:T(8,128)S(1)} %get-tuple-element.58), channel_id=1, source_target_pairs={{0,4},{2,6},{4,0},{6,2},{8,12},{10,14},{12,8},{14,10},{1,5},{3,7},... | collective-permute-start | bytes 61448 | tf_op jit(solution)/shard_map/ppermute | solution.py:393
  17.6 5.6 %collective-permute-start.7 = (f32[8,640]{1,0:T(8,128)S(1)}, f32[8,640]{1,0:T(8,128)S(1)}, u32[]{:S(2)}, u32[]{:S(2)}) collective-permute-start(f32[8,640]{1,0:T(8,128)S(1)} %get-tuple-element.59), channel_id=1, source_target_pairs={{0,12},{2,14},{4,8},{6,10},{8,4},{10,6},{12,0},{14,2},{1,13},{3,15... | collective-permute-start | bytes 61448 | tf_op jit(solution)/shard_map/ppermute | solution.py:393

commit v6 on v4

--- a/solution.py
+++ b/solution.py
@@ -13,6 +13,7 @@
 LIFT = (-1.586134342, -0.05298011854, 0.8829110762, 0.4435068522)
 ZETA = 1.149604398
 LANES = 128
+SCALE_FIRST, SCALE_SECOND = 840.0, 5040.0
 
 
 def lift_level(values):
@@ -30,6 +31,14 @@
         coarse, detail = lift_level(coarse)
         members.append(detail)
     return members + [coarse]
+
+
+def band(width, taps, sign, scale):
+    matrix = np.zeros((width, width))
+    for k, tap in enumerate(taps, 1):
+        value = float(np.round(tap * scale))
+        matrix += value * np.eye(width, k=-k) + sign * value * np.eye(width, k=k)
+    return jnp.asarray(matrix.astype(jnp.bfloat16))
 
 
 def split_bf16(matrix):
@@ -110,16 +119,6 @@
         base[x] = 2.0 * waves[x] - jnp.concatenate([prior_p[x], prior_q[x]], axis=0)
 
 
-def shifted(value, width):
-    wide = jnp.concatenate(
-        [value, jnp.zeros((value.shape[0], LANES), jnp.float32)], axis=1
-    )
-    total = width + LANES
-    ahead = [pltpu.roll(wide, total - k, 1)[:, :width] for k in range(1, 5)]
-    behind = [pltpu.roll(wide, k, 1)[:, :width] for k in range(1, 5)]
-    return ahead, behind
-
-
 def first_of(ahead, behind):
     total = FIRST[0] * (ahead[0] - behind[0])
     for k in range(1, 4):
@@ -159,41 +158,105 @@
     return ahead + [up], behind + [down]
 
 
-def depth_kernel(waves, other, dz, dzz):
+def across(parts, taps):
+    width = parts.shape[1]
+    blocks = []
+    for start in range(0, width, 2 * LANES):
+        stop = min(start + 2 * LANES, width)
+        low, high = max(start - LANES, 0), min(stop + LANES, width)
+        blocks.append(
+            jnp.dot(
+                parts[:, low:high], taps[low:high, start:stop], preferred_element_type=jnp.float32
+            )
+        )
+    return jnp.concatenate(blocks, axis=1)
+
+
+def joined(parts, rows):
+    return parts[:rows] + parts[rows:]
+
+
+def interior_kernel(
+    waves, other, axis_x, axis_y, axis_z, taps_first, taps_second, h_own, sum_own, dz, dzz, dy, dyy, dzy
+):
+    rows, sub, width = waves.shape
+    flat = rows * sub
     lower = lax.axis_index("gz") == 0
-    for x in range(waves.shape[0]):
+    for x in range(rows):
         own = waves[x]
         ahead, behind = depth_neighbours(own, other[x], lower)
         dz[x] = first_of(ahead, behind)
         dzz[x] = second_of(own, ahead, behind)
-
-
-def cross_kernel(waves, dz, dzz, axis_y, axis_z, h_part, sum_part):
-    rows, _, width = waves.shape
-
-    def row(x, carry):
+    field = jnp.concatenate(halves(waves[...].reshape(flat, width)), axis=0)
+    slope = jnp.concatenate(halves(dz[...].reshape(flat, width)), axis=0)
+    dyy[...] = joined(across(field, taps_second), flat).reshape(waves.shape)
+    dy[...] = joined(across(field, taps_first), flat).reshape(waves.shape)
+    dzy[...] = joined(across(slope, taps_first), flat).reshape(waves.shape)
+    for x in range(rows):
         centre = waves[x]
-        dyy = second_of(centre, *shifted(centre, width))
-        dzy = first_of(*shifted(dz[x], width))
-        n_y, n_z = axis_y[x], axis_z[x]
-        h_part[x] = (n_y * n_y) * dyy + n_z * (n_z * dzz[x] + 2.0 * n_y * dzy)
-        sum_part[x] = dyy + dzz[x]
-        return carry
-
-    lax.fori_loop(0, rows, row, 0, unroll=4)
+        dxx = SECOND[0] * centre
+        dxy = jnp.zeros_like(centre)
+        dxz = jnp.zeros_like(centre)
+        for k in range(1, 5):
+            for step in (k, -k):
+                if 0 <= x + step < rows:
+                    weight = FIRST[k - 1] if step > 0 else -FIRST[k - 1]
+                    dxx = dxx + SECOND[k] * waves[x + step]
+                    dxy = dxy + (weight / SCALE_FIRST) * dy[x + step]
+                    dxz = dxz + weight * dz[x + step]
+        cross = SECOND[0] * centre + (1.0 / SCALE_SECOND) * dyy[x]
+        n_x, n_y, n_z = axis_x[x], axis_y[x], axis_z[x]
+        h_one = n_x * (n_x * dxx + 2.0 * (n_y * dxy + n_z * dxz))
+        h_one = h_one + n_y * (n_y * cross + (2.0 / SCALE_FIRST) * (n_z * dzy[x]))
+        h_own[x] = h_one + n_z * (n_z * dzz[x])
+        sum_own[x] = dxx + cross + dzz[x]
+
+
+def halo_rows(size, edges):
+    place = lax.axis_index("xy")
+    even = place % 2 == 0
+    left_at, right_at = jnp.where(even, 4, 0), jnp.where(even, 0, 4)
+    left_in = jnp.where(place > 0, 1.0, 0.0)
+    right_in = jnp.where(place < size - 1, 1.0, 0.0)
+    before = [edges[left_at + x] * left_in for x in range(4)]
+    return before + [edges[right_at + x] * right_in for x in range(4)]
+
+
+def reach(values, row, coefficients, sign):
+    total = None
+    for k in range(1, 5):
+        at = row + 4 - k if row < 4 else row + k - 4
+        if (row < 4 and 0 <= at < 4) or (row >= 4 and 4 <= at < 8):
+            term = (coefficients[k - 1] * (sign if row < 4 else 1.0)) * values[at]
+            total = term if total is None else total + term
+    return total
+
+
+def halo_kernel(size, edges, axis_x, axis_y, h_own, sum_own, taps_first, h_edge, sum_edge):
+    rows, sub, width = h_own.shape
+    values = halo_rows(size, edges)
+    parts = jnp.concatenate(halves(jnp.concatenate(values, axis=0)), axis=0)
+    slopes = joined(across(parts, taps_first), 8 * sub)
+    slopes = [slopes[sub * x : sub * x + sub] for x in range(8)]
+    for row in range(8):
+        x = row if row < 4 else rows - 8 + row
+        dxx = reach(values, row, SECOND[1:], 1.0)
+        dxy = reach(slopes, row, [c / SCALE_FIRST for c in FIRST], -1.0)
+        n_x = axis_x[x]
+        h_edge[row] = h_own[x] + n_x * (n_x * dxx + 2.0 * (axis_y[x] * dxy))
+        sum_edge[row] = sum_own[x] + dxx
 
 
 def step_kernel(
     size,
     gives,
-    waves,
     edges,
     edges_other,
-    dz,
-    h_part,
-    sum_part,
+    h_own,
+    sum_own,
+    h_edge,
+    sum_edge,
     axis_x,
-    axis_y,
     axis_z,
     gain_a,
     gain_b,
@@ -204,43 +267,27 @@
     inline_low,
     pressure,
     crossline,
-    *rest,
+    *sends,
 ):
-    sends, (ext, dz_ext) = rest[:-2], rest[-2:]
-    rows, _, width = waves.shape
+    rows, sub, width = h_own.shape
     lower = lax.axis_index("gz") == 0
     place = lax.axis_index("xy")
     even, early = place % 2 == 0, place % 4 < 2
-    left_at, right_at = jnp.where(even, 4, 0), jnp.where(even, 0, 4)
-    left_in = jnp.where(place > 0, 1.0, 0.0)
-    right_in = jnp.where(place < size - 1, 1.0, 0.0)
-    top = lax.broadcasted_iota(jnp.int32, waves.shape[1:], 0) < 4
-
-    for x in range(4):
-        for at, inside, to in ((left_at, left_in, x), (right_at, right_in, rows + 4 + x)):
-            own, far = edges[at + x] * inside, edges_other[at + x] * inside
-            ext[to] = own
-            dz_ext[to] = first_of(*depth_neighbours(own, far, lower))
+    top = lax.broadcasted_iota(jnp.int32, (sub, width), 0) < 4
+
+    slopes = [
+        first_of(*depth_neighbours(own, far, lower))
+        for own, far in zip(halo_rows(size, edges), halo_rows(size, edges_other))
+    ]
     for x in range(rows):
-        ext[x + 4] = waves[x]
-        dz_ext[x + 4] = dz[x]
-
-    def row(x, carry):
-        ahead = [ext[x + 4 + k] for k in range(1, 5)]
-        behind = [ext[x + 4 - k] for k in range(1, 5)]
-        dxx = second_of(ext[x + 4], ahead, behind)
-        dxy = first_of(*shifted(first_of(ahead, behind), width))
-        dxz = first_of(
-            [dz_ext[x + 4 + k] for k in range(1, 5)], [dz_ext[x + 4 - k] for k in range(1, 5)]
-        )
-        n_x = axis_x[x]
-        h_one = h_part[x] + n_x * (n_x * dxx + 2.0 * (axis_y[x] * dxy + axis_z[x] * dxz))
-        h_two = dxx + sum_part[x] - h_one
-        mixed = jnp.where(top, h_two, h_one)
+        row = x if x < 4 else x - rows + 8
+        if 4 <= x < rows - 4:
+            h_one, total = h_own[x], sum_own[x]
+        else:
+            dxz = reach(slopes, row, FIRST, -1.0)
+            h_one, total = h_edge[row] + 2.0 * (axis_x[x] * axis_z[x] * dxz), sum_edge[row]
+        mixed = jnp.where(top, total - h_one, h_one)
         pressure[x] = base[x] + gain_a[x] * mixed + gain_b[x] * pltpu.roll(mixed, 4, 0)
-        return carry
-
-    lax.fori_loop(0, rows, row, 0, unroll=4)
 
     packed = jnp.concatenate(
         [
@@ -316,9 +363,9 @@
         for i, j in pairs[0]
         for g in range(2)
     ]
+    other = lax.ppermute(waves, "gz", cores)
+    inner = lax.ppermute(jnp.where(even, last, leading), "xy", pairs[1])
     outer = lax.ppermute(jnp.where(even, leading, last), ("xy", "gz"), open_outer)
-    inner = lax.ppermute(jnp.where(even, last, leading), "xy", pairs[1])
-    other = lax.ppermute(waves, "gz", cores)
 
     stack = jax.ShapeDtypeStruct((rows, 8, width), f32)
     cells = rows * layers * width
@@ -338,11 +385,19 @@
     axis_x, axis_y, axis_z, *gains = kernel(weights_kernel, [stack] * 6, 100, "weights")(
         waves, prior_p, prior_q, courant, epsilon, thomsen_delta, tilt_angle, azimuth
     )
-    dz, dzz = kernel(depth_kernel, [stack] * 2, 100, "depth")(waves, other)
-    outer, inner, dz, axis_x = lax.optimization_barrier((outer, inner, dz, axis_x))
+    taps_first = band(width, FIRST, -1.0, SCALE_FIRST)
+    taps_second = band(width, SECOND[1:], 1.0, SCALE_SECOND)
+    work = pltpu.VMEM((rows, 8, width), f32)
+    h_own, sum_own = kernel(interior_kernel, [stack] * 2, 100, "interior", [work] * 5)(
+        waves, other, axis_x, axis_y, axis_z, taps_first, taps_second
+    )
+    outer, inner, h_own, sum_own = lax.optimization_barrier((outer, inner, h_own, sum_own))
     edges = jnp.concatenate([inner, outer], axis=0)
     edges_other = lax.ppermute(edges, "gz", cores)
-    h_part, sum_part = kernel(cross_kernel, [stack] * 2, 100, "cross")(waves, dz, dzz, axis_y, axis_z)
+    edge = jax.ShapeDtypeStruct((8, 8, width), f32)
+    h_edge, sum_edge = kernel(functools.partial(halo_kernel, size), [edge] * 2, 100, "halo")(
+        edges, axis_x, axis_y, h_own, sum_own, taps_first
+    )
 
     own, factors = inline_blocks(rows)
     offsets = (-1, 1, -2, 2)
@@ -357,7 +412,6 @@
     def parts(matrix):
         return [jnp.asarray(part) for part in split_bf16(matrix)]
 
-    across = parts(np.concatenate(three_levels(width)).T)
     inline = parts(np.kron(np.concatenate(pieces), np.eye(4)))
     inline_own = parts(np.kron(own, np.eye(4)))
     flat = jax.ShapeDtypeStruct((layers * rows, width), f32)
@@ -366,8 +420,19 @@
         [stack, flat] + [jax.ShapeDtypeStruct((count, width), f32) for _, count in gives],
         400,
         "step",
-        [pltpu.VMEM((rows + 8, 8, width), f32)] * 2,
-    )(waves, edges, edges_other, dz, h_part, sum_part, axis_x, axis_y, axis_z, *gains, *across, *inline)
+    )(
+        edges,
+        edges_other,
+        h_own,
+        sum_own,
+        h_edge,
+        sum_edge,
+        axis_x,
+        axis_z,
+        *gains,
+        *parts(np.concatenate(three_levels(width)).T),
+        *inline,
+    )
     received = [lax.ppermute(send, "xy", pair) for send, pair in zip(sends, pairs)]
     grid = jax.ShapeDtypeStruct(wave_p.shape, f32)
     next_p, next_q, mine = kernel(own_kernel, [grid, grid, flat], 100, "own")(

time: 23.9 us -> 26.5 us (1.11)
  local copies, waits for them, and re-layouts: 0.08 us -> 5.42 us
  Pallas kernels: 6.42 us -> 4.91 us
  starting transfers between devices: 11 us -> 10.2 us
  waiting for transfers between devices: 4.31 us -> 3.7 us
    unnamed x27 -> x31, local copies, waits for them, and re-layouts: 0.08 us -> 5.41 us
    ppermute x1, waiting for transfers between devices: 2.65 us -> 0.01 us  [body(): inner = lax.ppermute(jnp.where(even, last, leading), 'xy', pairs[1])]
    ppermute x4, waiting for transfers between devices: 1.65 us -> 2.87 us  [body(): lax.ppermute(send, 'xy', pair)]
    ppermute x4, starting transfers between devices: 7.59 us -> 6.48 us  [body(): lax.ppermute(send, 'xy', pair)]
    pallas_call x1, Pallas kernels: 1.92 us -> 0.92 us  [body(): kernel(functools.partial(step_kernel, size, gives), [stack, flat] + [jax....]
    ppermute x1, waiting for transfers between devices: 0.01 us -> 0.82 us  [body(): edges_other = lax.ppermute(edges, 'gz', cores)]
    pallas_call x2, Pallas kernels: 2.15 us -> 1.65 us  [the longest x1 1.4 us: body(): kernel(interior_kernel, [stack] * 2, 100, 'interior', [work] * 5)]
    ppermute x1, starting transfers between devices: 0.07 us -> 0.38 us  [body(): edges_other = lax.ppermute(edges, 'gz', cores)]
  transfers between devices with their start and end apart: 8 -> 8, of which waited for: 2 -> 3; matrix products, arithmetic and copies ran while one was open for 0% -> 0% of each run, Pallas kernels for 15% -> 12%
where the time goes in v6:
time: 26.5 us; the launch traced here: 26.1 us
  starting transfers between devices  10.2 us (38%)
  local copies, waits for them, and re-layouts  5.42 us (20%)
  Pallas kernels  4.91 us (19%)
  waiting for transfers between devices  3.7 us (14%)
  other arithmetic  1.16 us (4%)
  between operations  0.8 us (3%)
    ppermute x4, starting transfers between devices, body(): lax.ppermute(send, 'xy', pair)  6.48 us
    unnamed x31, local copies, waits for them, and re-layouts  5.41 us
    ppermute x4, waiting for transfers between devices, body(): lax.ppermute(send, 'xy', pair)  2.87 us
    ppermute x1, starting transfers between devices, body(): inner = lax.ppermute(jnp.where(even, last, leading), 'xy', pairs[1])  2.58 us
    pallas_call x1, Pallas kernels, body(): kernel(interior_kernel, [stack] * 2, 100, 'interior', [work] * 5)  1.4 us
    concatenate x1, other arithmetic, body(): waves = lax.optimization_barrier(jnp.concatenate([wave_p, wave_q], axis=1))  1.15 us
    pallas_call x1, Pallas kernels, body(): kernel(functools.partial(step_kernel, size, gives), [stack, flat] + [jax....  0.92 us
    ppermute x1, waiting for transfers between devices, body(): edges_other = lax.ppermute(edges, 'gz', cores)  0.82 us
  transfers between devices with their start and end apart: 8, of which 3 were waited for; matrix products, arithmetic and copies ran while one was open for 0% of the time, Pallas kernels for 12%

profile of v6, /device:TPU:0, one launch (start us, length us, event | category | flops | bytes accessed | tf_op | source)
XLA Modules:
  0.0 26.1 jit_solution(4434348200380581710)
XLA Ops:
  0.6 0.0 copy-start.4
  0.6 0.0 copy-start.3
  0.7 1.1 %pad_maximum_fusion.waves = f32[16,8,640]{2,1,0:T(8,128)S(1)} fusion(f32[16,4,640]{2,1,0:T(4,128)} %param.18, f32[16,4,640]{2,1,0:T(4,128)} %param.17), kind=kLoop, calls=%fused_computation | loop fusion | flops 81920 | bytes 655360 | tf_op jit(solution)/shard_map/concatenate | solution.py:359
  1.8 0.0 copy-start
  1.8 0.5 %collective-permute-start.2 = (f32[16,8,640]{2,1,0:T(8,128)S(1)}, f32[16,8,640]{2,1,0:T(8,128)S(1)}, u32[]{:S(2)}, u32[]{:S(2)}) collective-permute-start(f32[16,8,640]{2,1,0:T(8,128)S(1)} %pad_maximum_fusion.waves), channel_id=1, source_target_pairs={{0,1},{1,0},{2,3},{3,2},{4,5},{5,4},{6,7},{7,6},{8,9},{9,8},{10,11... | collective-permute-start | bytes 983048 | tf_op jit(solution)/shard_map/ppermute | solution.py:366
  2.4 2.6 %collective-permute-start.1 = (f32[4,8,640]{2,1,0:T(8,128)S(1)}, f32[4,8,640]{2,1,0:T(8,128)S(1)}, u32[]{:S(2)}, u32[]{:S(2)}) collective-permute-start(f32[4,8,640]{2,1,0:T(8,128)S(1)} %get-tuple-element.60), channel_id=1, source_target_pairs={{0,2},{2,0},{4,6},{6,4},{8,10},{10,8},{12,14},{14,12},{1,3},{3,1},... | collective-permute-start | bytes 245768 | tf_op jit(solution)/shard_map/ppermute | solution.py:367
  4.9 0.2 collective-permute-start
  5.1 0.0 copy-done.4
  5.1 0.0 copy-start.5
  5.1 0.9 %copy-done.5 = f32[16,4,640]{2,1,0:T(4,128)S(1)} copy-done((f32[16,4,640]{2,1,0:T(4,128)S(1)}, f32[16,4,640]{2,1,0:T(4,128)}, u32[]{:S(2)}) %copy-start.5) | copy-done | bytes 163864
  6.1 0.0 copy-start.6
  6.1 0.9 %copy-done.6 = bf16[16,4,640]{2,1,0:T(4,128)(2,1)S(1)} copy-done((bf16[16,4,640]{2,1,0:T(4,128)(2,1)S(1)}, bf16[16,4,640]{2,1,0:T(4,128)(2,1)}, u32[]{:S(2)}) %copy-start.6) | copy-done | bytes 81944
  6.9 0.0 copy-start.7
  6.9 0.9 %copy-done.7 = bf16[16,4,640]{2,1,0:T(4,128)(2,1)S(1)} copy-done((bf16[16,4,640]{2,1,0:T(4,128)(2,1)S(1)}, bf16[16,4,640]{2,1,0:T(4,128)(2,1)}, u32[]{:S(2)}) %copy-start.7) | copy-done | bytes 81944
  7.8 0.9 %copy-done.8 = bf16[16,4,640]{2,1,0:T(4,128)(2,1)S(1)} copy-done((bf16[16,4,640]{2,1,0:T(4,128)(2,1)S(1)}, bf16[16,4,640]{2,1,0:T(4,128)(2,1)}, u32[]{:S(2)}) %copy-start.8) | copy-done | bytes 81944
  8.7 0.9 %copy-done.9 = bf16[16,4,640]{2,1,0:T(4,128)(2,1)S(1)} copy-done((bf16[16,4,640]{2,1,0:T(4,128)(2,1)S(1)}, bf16[16,4,640]{2,1,0:T(4,128)(2,1)}, u32[]{:S(2)}) %copy-start.9) | copy-done | bytes 81944
  9.6 0.9 %copy-done.10 = bf16[16,4,640]{2,1,0:T(4,128)(2,1)S(1)} copy-done((bf16[16,4,640]{2,1,0:T(4,128)(2,1)S(1)}, bf16[16,4,640]{2,1,0:T(4,128)(2,1)}, u32[]{:S(2)}) %copy-start.10) | copy-done | bytes 81944
  10.5 0.7 %weights.1 = (f32[16,8,640]{2,1,0:T(8,128)S(1)}, f32[16,8,640]{2,1,0:T(8,128)S(1)}, f32[16,8,640]{2,1,0:T(8,128)S(1)}, f32[16,8,640]{2,1,0:T(8,128)S(1)}, f32[16...) custom-call(f32[16,8,640]{2,1,0:T(8,128)S(1)} %pad_maximum_fusion.waves, f32[16,4,640]{2,1,0:T(4,128)S(1)} %copy-done.4, ...), custom_call_target="tpu_custom_call" | custom-call | flops 4096000 | bytes 1638400 | tf_op jit(solution)/shard_map/weights/pallas_call | solution.py:385
  11.2 0.0 collective-permute-done.2.other
  11.2 0.0 copy-done.3
  11.2 0.0 copy-done
  11.2 1.4 %interior.1 = (f32[16,8,640]{2,1,0:T(8,128)S(1)}, f32[16,8,640]{2,1,0:T(8,128)S(1)}) custom-call(f32[16,8,640]{2,1,0:T(8,128)S(1)} %pad_maximum_fusion.waves, f32[16,8,640]{2,1,0:T(8,128)S(1)} %collective-permute-done.2.other, f32[16,8,640]{2,1,0:T(8,128)S(1)} %get-tuple-element.33.axis_x, f32[16,8,640]{2,1,0:T(8,128)S(1)} %get-tuple-element.34.axis_y, ...), custom_call_target="tpu_custom_call" | custom-call | flops 4096000 | bytes 1638400 | tf_op jit(solution)/shard_map/interior/pallas_call | solution.py:391
  12.6 0.0 collective-permute-done.1
  12.6 0.0 collective-permute-done
  12.7 0.0 copy-start.1
  12.7 0.0 copy-start.2
  12.7 0.4 %collective-permute-start.3 = (f32[8,8,640]{2,1,0:T(8,128)S(1)}, f32[8,8,640]{2,1,0:T(8,128)S(1)}, u32[]{:S(2)}, u32[]{:S(2)}) collective-permute-start(f32[8,8,640]{2,1,0:T(8,128)S(1)} %constant_dynamic-update-slice_fusion.edges), channel_id=1, source_target_pairs={{0,1},{1,0},{2,3},{3,2},{4,5},{5,4},{6,7},{7,6},{8,9},{9,8},{10,11... | collective-permute-start | bytes 491528 | tf_op jit(solution)/shard_map/ppermute | solution.py:396
  13.1 0.3 halo.1
  13.4 0.8 %collective-permute-done.3.edges_other = f32[8,8,640]{2,1,0:T(8,128)S(1)} collective-permute-done((f32[8,8,640]{2,1,0:T(8,128)S(1)}, f32[8,8,640]{2,1,0:T(8,128)S(1)}, u32[]{:S(2)}, u32[]{:S(2)}) %collective-permute-start.3) | collective-permute-done | bytes 163872 | tf_op jit(solution)/shard_map/ppermute | solution.py:396
  14.2 0.0 copy-done.1
  14.2 0.0 copy-done.2
  14.2 0.0 copy-done.11
  14.2 0.0 copy-done.12
  14.2 0.0 copy-start.13
  14.2 0.0 copy-start.14
  14.2 0.9 %step.1 = (f32[16,8,640]{2,1,0:T(8,128)S(1)}, f32[64,640]{1,0:T(8,128)S(1)}, f32[24,640]{1,0:T(8,128)S(1)}, f32[24,640]{1,0:T(8,128)S(1)}, f32[8,640]{1,0:T(8,128)S(1)}, /*index=5*/f32[8,640]{1,0:T(8,128)S(1)}) custom-call(f32[8,8,640]{2,1,0:T(8,128)S(1)} %constant_dynamic-update-slice_fusion.edges, f32[8,8,640]{2,1,0:T(8,128)S(1)} %collective-permute-done.3.edges_other, ...), custom_call_target="tpu_custom_call" | custom-call | flops 16384000 | bytes 1638400 | tf_op jit(solution)/shard_map/step/pallas_call | solution.py:418
  15.1 3.6 %collective-permute-start.4 = (f32[24,640]{1,0:T(8,128)S(1)}, f32[24,640]{1,0:T(8,128)S(1)}, u32[]{:S(2)}, u32[]{:S(2)}) collective-permute-start(f32[24,640]{1,0:T(8,128)S(1)} %get-tuple-element.52), channel_id=1, source_target_pairs={{0,14},{2,4},{4,2},{6,8},{8,6},{10,12},{12,10},{14,0},{1,15},{3,5}... | collective-permute-start | bytes 184328 | tf_op jit(solution)/shard_map/ppermute | solution.py:436
  18.8 0.0 collective-permute-start.5
  18.8 2.7 %collective-permute-start.6 = (f32[8,640]{1,0:T(8,128)S(1)}, f32[8,640]{1,0:T(8,128)S(1)}, u32[]{:S(2)}, u32[]{:S(2)}) collective-permute-start(f32[8,640]{1,0:T(8,128)S(1)} %get-tuple-element.54), channel_id=1, source_target_pairs={{0,12},{2,14},{4,8},{6,10},{8,4},{10,6},{12,0},{14,2},{1,13},{3,15... | collective-permute-start | bytes 61448 | tf_op jit(solution)/shard_map/ppermute | solution.py:436
  21.5 0.1 collective-permute-start.7
  21.6 0.0 copy-done.13
  21.6 0.0 copy-done.14
  21.6 0.8 %own.1 = (f32[16,4,640]{2,1,0:T(4,128)}, f32[16,4,640]{2,1,0:T(4,128)}, f32[64,640]{1,0:T(8,128)S(1)}) custom-call(f32[16,8,640]{2,1,0:T(8,128)S(1)} %get-tuple-element.47.pressure, f32[64,640]{1,0:T(8,128)S(1)} %get-tuple-element.48.crossline, bf16[64,64]{1,0:T(8,128)(2,1)S(1)} %copy-done.14, bf16[64,64]{1,0:T(8,128)(2,1)S(1)} %copy-done.13), custom_call_target="tpu_custom_call" | custom-call | flops 4096000 | bytes 1638400 | tf_op jit(solution)/shard_map/own/pallas_call | solution.py:438
  22.4 1.9 %collective-permute-done.6.rest_2_ = f32[8,640]{1,0:T(8,128)S(1)} collective-permute-done((f32[8,640]{1,0:T(8,128)S(1)}, f32[8,640]{1,0:T(8,128)S(1)}, u32[]{:S(2)}, u32[]{:S(2)}) %collective-permute-start.6) | collective-permute-done | bytes 20512 | tf_op jit(solution)/shard_map/ppermute | solution.py:436
  24.4 0.9 %collective-permute-done.7.rest_3_ = f32[8,640]{1,0:T(8,128)S(1)} collective-permute-done((f32[8,640]{1,0:T(8,128)S(1)}, f32[8,640]{1,0:T(8,128)S(1)}, u32[]{:S(2)}, u32[]{:S(2)}) %collective-permute-start.7) | collective-permute-done | bytes 20512 | tf_op jit(solution)/shard_map/ppermute | solution.py:436
  25.3 0.0 collective-permute-done.4.rest_0_
  25.3 0.0 collective-permute-done.5.rest_1_
  25.3 0.8 %finish.1 = (f32[8,4,640]{2,1,0:T(4,128)}, f32[4,4,640]{2,1,0:T(4,128)}, f32[2,4,640]{2,1,0:T(4,128)}, f32[2,4,640]{2,1,0:T(4,128)}) custom-call(f32[64,640]{1,0:T(8,128)S(1)} %get-tuple-element.51.mine, f32[24,640]{1,0:T(8,128)S(1)} %collective-permute-done.4.rest_0_, f32[24,640]{1,0:T(8,128)S(1)} %collective-permute-done.5.rest_1_, ...), custom_call_target="tpu_custom_call" | custom-call | flops 819200 | bytes 1638400 | tf_op jit(solution)/shard_map/finish/pallas_call | solution.py:441
  (8 shorter events, 0.0 us)
Async XLA Ops:
  0.6 4.5 %copy-start.4 = (f32[16,4,640]{2,1,0:T(4,128)S(1)}, f32[16,4,640]{2,1,0:T(4,128)}, u32[]{:S(2)}) copy-start(f32[16,4,640]{2,1,0:T(4,128)} %prior_p.1) | copy-start | bytes 491524
  0.6 10.6 %copy-start.3 = (bf16[640,640]{1,0:T(8,128)(2,1)S(1)}, bf16[640,640]{1,0:T(8,128)(2,1)}, u32[]{:S(2)}) copy-start(bf16[640,640]{1,0:T(8,128)(2,1)} %constant.37.clone.taps_second) | copy-start | bytes 2457604
  1.8 9.4 %copy-start = (bf16[640,640]{1,0:T(8,128)(2,1)S(1)}, bf16[640,640]{1,0:T(8,128)(2,1)}, u32[]{:S(2)}) copy-start(bf16[640,640]{1,0:T(8,128)(2,1)} %constant.36.clone.taps_first) | copy-start | bytes 2457604
  1.8 9.4 %collective-permute-start.2 = (f32[16,8,640]{2,1,0:T(8,128)S(1)}, f32[16,8,640]{2,1,0:T(8,128)S(1)}, u32[]{:S(2)}, u32[]{:S(2)}) collective-permute-start(f32[16,8,640]{2,1,0:T(8,128)S(1)} %pad_maximum_fusion.waves), channel_id=1, source_target_pairs={{0,1},{1,0},{2,3},{3,2},{4,5},{5,4},{6,7},{7,6},{8,9},{9,8},{10,11... | collective-permute-start | bytes 983048 | tf_op jit(solution)/shard_map/ppermute | solution.py:366
  2.4 10.3 %collective-permute-start.1 = (f32[4,8,640]{2,1,0:T(8,128)S(1)}, f32[4,8,640]{2,1,0:T(8,128)S(1)}, u32[]{:S(2)}, u32[]{:S(2)}) collective-permute-start(f32[4,8,640]{2,1,0:T(8,128)S(1)} %get-tuple-element.60), channel_id=1, source_target_pairs={{0,2},{2,0},{4,6},{6,4},{8,10},{10,8},{12,14},{14,12},{1,3},{3,1},... | collective-permute-start | bytes 245768 | tf_op jit(solution)/shard_map/ppermute | solution.py:367
  4.9 7.7 %collective-permute-start = (f32[4,8,640]{2,1,0:T(8,128)S(1)}, f32[4,8,640]{2,1,0:T(8,128)S(1)}, u32[]{:S(2)}, u32[]{:S(2)}) collective-permute-start(f32[4,8,640]{2,1,0:T(8,128)S(1)} %get-tuple-element.61), channel_id=1, source_target_pairs={{0,1},{1,0},{2,4},{3,5},{4,2},{5,3},{6,8},{7,9},{8,6},{9,7},{10,12... | collective-permute-start | bytes 245768 | tf_op jit(solution)/shard_map/ppermute | solution.py:368
  5.1 0.9 %copy-start.5 = (f32[16,4,640]{2,1,0:T(4,128)S(1)}, f32[16,4,640]{2,1,0:T(4,128)}, u32[]{:S(2)}) copy-start(f32[16,4,640]{2,1,0:T(4,128)} %prior_q.1) | copy-start | bytes 491524
  6.1 0.9 %copy-start.6 = (bf16[16,4,640]{2,1,0:T(4,128)(2,1)S(1)}, bf16[16,4,640]{2,1,0:T(4,128)(2,1)}, u32[]{:S(2)}) copy-start(bf16[16,4,640]{2,1,0:T(4,128)(2,1)} %courant.1) | copy-start | bytes 245764
  6.9 0.9 %copy-start.7 = (bf16[16,4,640]{2,1,0:T(4,128)(2,1)S(1)}, bf16[16,4,640]{2,1,0:T(4,128)(2,1)}, u32[]{:S(2)}) copy-start(bf16[16,4,640]{2,1,0:T(4,128)(2,1)} %epsilon.1) | copy-start | bytes 245764
  7.8 0.9 %copy-start.8 = (bf16[16,4,640]{2,1,0:T(4,128)(2,1)S(1)}, bf16[16,4,640]{2,1,0:T(4,128)(2,1)}, u32[]{:S(2)}) copy-start(bf16[16,4,640]{2,1,0:T(4,128)(2,1)} %delta.1) | copy-start | bytes 245764
  8.7 0.9 %copy-start.9 = (bf16[16,4,640]{2,1,0:T(4,128)(2,1)S(1)}, bf16[16,4,640]{2,1,0:T(4,128)(2,1)}, u32[]{:S(2)}) copy-start(bf16[16,4,640]{2,1,0:T(4,128)(2,1)} %tilt.1) | copy-start | bytes 245764
  9.6 0.9 %copy-start.10 = (bf16[16,4,640]{2,1,0:T(4,128)(2,1)S(1)}, bf16[16,4,640]{2,1,0:T(4,128)(2,1)}, u32[]{:S(2)}) copy-start(bf16[16,4,640]{2,1,0:T(4,128)(2,1)} %azimuth.1) | copy-start | bytes 245764
  12.7 1.5 %copy-start.1 = (bf16[640,640]{1,0:T(8,128)(2,1)S(1)}, bf16[640,640]{1,0:T(8,128)(2,1)}, u32[]{:S(2)}) copy-start(bf16[640,640]{1,0:T(8,128)(2,1)} %constant.43.clone.across_low) | copy-start | bytes 2457604
  12.7 1.5 %copy-start.2 = (bf16[640,640]{1,0:T(8,128)(2,1)S(1)}, bf16[640,640]{1,0:T(8,128)(2,1)}, u32[]{:S(2)}) copy-start(bf16[640,640]{1,0:T(8,128)(2,1)} %constant.42.clone.across_high) | copy-start | bytes 2457604
  12.7 1.5 %collective-permute-start.3 = (f32[8,8,640]{2,1,0:T(8,128)S(1)}, f32[8,8,640]{2,1,0:T(8,128)S(1)}, u32[]{:S(2)}, u32[]{:S(2)}) collective-permute-start(f32[8,8,640]{2,1,0:T(8,128)S(1)} %constant_dynamic-update-slice_fusion.edges), channel_id=1, source_target_pairs={{0,1},{1,0},{2,3},{3,2},{4,5},{5,4},{6,7},{7,6},{8,9},{9,8},{10,11... | collective-permute-start | bytes 491528 | tf_op jit(solution)/shard_map/ppermute | solution.py:396
  13.1 1.1 %copy-start.11 = (bf16[64,64]{1,0:T(8,128)(2,1)S(1)}, bf16[64,64]{1,0:T(8,128)(2,1)}, u32[]{:S(2)}) copy-start(bf16[64,64]{1,0:T(8,128)(2,1)} %constant.39.clone.inline_low) | copy-start | bytes 24580
  13.1 1.1 %copy-start.12 = (bf16[64,64]{1,0:T(8,128)(2,1)S(1)}, bf16[64,64]{1,0:T(8,128)(2,1)}, u32[]{:S(2)}) copy-start(bf16[64,64]{1,0:T(8,128)(2,1)} %constant.38.clone.inline_high) | copy-start | bytes 24580
  14.2 7.4 %copy-start.13 = (bf16[64,64]{1,0:T(8,128)(2,1)S(1)}, bf16[64,64]{1,0:T(8,128)(2,1)}, u32[]{:S(2)}) copy-start(bf16[64,64]{1,0:T(8,128)(2,1)} %constant.41.clone.own_low) | copy-start | bytes 24580
  14.2 7.4 %copy-start.14 = (bf16[64,64]{1,0:T(8,128)(2,1)S(1)}, bf16[64,64]{1,0:T(8,128)(2,1)}, u32[]{:S(2)}) copy-start(bf16[64,64]{1,0:T(8,128)(2,1)} %constant.40.clone.own_high) | copy-start | bytes 24580
  15.1 10.2 %collective-permute-start.4 = (f32[24,640]{1,0:T(8,128)S(1)}, f32[24,640]{1,0:T(8,128)S(1)}, u32[]{:S(2)}, u32[]{:S(2)}) collective-permute-start(f32[24,640]{1,0:T(8,128)S(1)} %get-tuple-element.52), channel_id=1, source_target_pairs={{0,14},{2,4},{4,2},{6,8},{8,6},{10,12},{12,10},{14,0},{1,15},{3,5}... | collective-permute-start | bytes 184328 | tf_op jit(solution)/shard_map/ppermute | solution.py:436
  18.8 6.5 %collective-permute-start.5 = (f32[24,640]{1,0:T(8,128)S(1)}, f32[24,640]{1,0:T(8,128)S(1)}, u32[]{:S(2)}, u32[]{:S(2)}) collective-permute-start(f32[24,640]{1,0:T(8,128)S(1)} %get-tuple-element.53), channel_id=1, source_target_pairs={{0,2},{2,0},{4,6},{6,4},{8,10},{10,8},{12,14},{14,12},{1,3},{3,1},... | collective-permute-start | bytes 184328 | tf_op jit(solution)/shard_map/ppermute | solution.py:436
  18.8 5.6 %collective-permute-start.6 = (f32[8,640]{1,0:T(8,128)S(1)}, f32[8,640]{1,0:T(8,128)S(1)}, u32[]{:S(2)}, u32[]{:S(2)}) collective-permute-start(f32[8,640]{1,0:T(8,128)S(1)} %get-tuple-element.54), channel_id=1, source_target_pairs={{0,12},{2,14},{4,8},{6,10},{8,4},{10,6},{12,0},{14,2},{1,13},{3,15... | collective-permute-start | bytes 61448 | tf_op jit(solution)/shard_map/ppermute | solution.py:436
  21.5 3.8 %collective-permute-start.7 = (f32[8,640]{1,0:T(8,128)S(1)}, f32[8,640]{1,0:T(8,128)S(1)}, u32[]{:S(2)}, u32[]{:S(2)}) collective-permute-start(f32[8,640]{1,0:T(8,128)S(1)} %get-tuple-element.55), channel_id=1, source_target_pairs={{0,4},{2,6},{4,0},{6,2},{8,12},{10,14},{12,8},{14,10},{1,5},{3,7},... | collective-permute-start | bytes 61448 | tf_op jit(solution)/shard_map/ppermute | solution.py:436

commit v7 on v6

--- a/solution.py
+++ b/solution.py
@@ -33,11 +33,12 @@
     return members + [coarse]
 
 
-def band(width, taps, sign, scale):
-    matrix = np.zeros((width, width))
+def band(taps, sign, scale):
+    offset = np.arange(4 * LANES)[:, None] - LANES - np.arange(2 * LANES)[None]
+    matrix = np.zeros(offset.shape)
     for k, tap in enumerate(taps, 1):
         value = float(np.round(tap * scale))
-        matrix += value * np.eye(width, k=-k) + sign * value * np.eye(width, k=k)
+        matrix += value * (offset == k) + sign * value * (offset == -k)
     return jnp.asarray(matrix.astype(jnp.bfloat16))
 
 
@@ -89,6 +90,26 @@
     out_sine = jnp.where((quarter & 2) == 2, -out_sine, out_sine)
     out_cosine = jnp.where(((quarter + 1) & 2) == 2, -out_cosine, out_cosine)
     return out_sine, out_cosine
+
+
+def load_kernel(wave_p, wave_q, *rest):
+    count = (len(rest) - 4) // 2
+    sources, waves, targets = rest[:count], rest[count], rest[count + 1 : 2 * count + 1]
+    field_p, field_q, arrived = rest[2 * count + 1 :]
+    copies = [
+        pltpu.make_async_copy(source, target, arrived.at[k])
+        for k, (source, target) in enumerate(
+            zip((wave_p, wave_q) + sources, (field_p, field_q) + targets)
+        )
+    ]
+    for copy in copies:
+        copy.start()
+    for copy in copies[:2]:
+        copy.wait()
+    for x in range(waves.shape[0]):
+        waves[x] = jnp.concatenate([field_p[x], field_q[x]], axis=0)
+    for copy in copies[2:]:
+        copy.wait()
 
 
 def weights_kernel(
@@ -163,12 +184,10 @@
     blocks = []
     for start in range(0, width, 2 * LANES):
         stop = min(start + 2 * LANES, width)
-        low, high = max(start - LANES, 0), min(stop + LANES, width)
-        blocks.append(
-            jnp.dot(
-                parts[:, low:high], taps[low:high, start:stop], preferred_element_type=jnp.float32
-            )
-        )
+        first = start - LANES
+        low, high = max(first, 0), min(stop + LANES, width)
+        block = taps[low - first : high - first, : stop - start]
+        blocks.append(jnp.dot(parts[:, low:high], block, preferred_element_type=jnp.float32))
     return jnp.concatenate(blocks, axis=1)
 
 
@@ -356,7 +375,33 @@
     even = lax.axis_index("xy") % 2 == 0
     pairs = pair_swaps(size)
     cores = [(0, 1), (1, 0)]
-    waves = lax.optimization_barrier(jnp.concatenate([wave_p, wave_q], axis=1))
+    stack = jax.ShapeDtypeStruct((rows, 8, width), f32)
+    cells = rows * layers * width
+    params = pltpu.CompilerParams(vmem_limit_bytes=16 * 1024 * 1024)
+
+    def kernel(function, out_shape, work, name, scratch_shapes=(), **specs):
+        cost = pl.CostEstimate(flops=work * cells, bytes_accessed=40 * cells, transcendentals=0)
+        return pl.pallas_call(
+            function,
+            out_shape=out_shape,
+            scratch_shapes=scratch_shapes,
+            compiler_params=params,
+            cost_estimate=cost,
+            name=name,
+            **specs,
+        )
+
+    others = (prior_p, prior_q, courant, epsilon, thomsen_delta, tilt_angle, azimuth)
+    field = pltpu.VMEM(wave_p.shape, f32)
+    waves, *others = kernel(
+        load_kernel,
+        [stack] + [jax.ShapeDtypeStruct(array.shape, array.dtype) for array in others],
+        10,
+        "load",
+        [field, field, pltpu.SemaphoreType.DMA((2 + len(others),))],
+        in_specs=[pl.BlockSpec(memory_space=pltpu.HBM)] * (2 + len(others)),
+        out_specs=[pl.BlockSpec(memory_space=pltpu.VMEM)] * (1 + len(others)),
+    )(wave_p, wave_q, *others)
     leading, last = waves[:4], waves[rows - 4 :]
     open_outer = [
         (2 * i + g, 2 * i + 1 - g) if abs(i - j) > 1 else (2 * i + g, 2 * j + g)
@@ -367,26 +412,11 @@
     inner = lax.ppermute(jnp.where(even, last, leading), "xy", pairs[1])
     outer = lax.ppermute(jnp.where(even, leading, last), ("xy", "gz"), open_outer)
 
-    stack = jax.ShapeDtypeStruct((rows, 8, width), f32)
-    cells = rows * layers * width
-    params = pltpu.CompilerParams(vmem_limit_bytes=16 * 1024 * 1024)
-
-    def kernel(function, out_shape, work, name, scratch_shapes=()):
-        cost = pl.CostEstimate(flops=work * cells, bytes_accessed=40 * cells, transcendentals=0)
-        return pl.pallas_call(
-            function,
-            out_shape=out_shape,
-            scratch_shapes=scratch_shapes,
-            compiler_params=params,
-            cost_estimate=cost,
-            name=name,
-        )
-
     axis_x, axis_y, axis_z, *gains = kernel(weights_kernel, [stack] * 6, 100, "weights")(
-        waves, prior_p, prior_q, courant, epsilon, thomsen_delta, tilt_angle, azimuth
-    )
-    taps_first = band(width, FIRST, -1.0, SCALE_FIRST)
-    taps_second = band(width, SECOND[1:], 1.0, SCALE_SECOND)
+        waves, *others
+    )
+    taps_first = band(FIRST, -1.0, SCALE_FIRST)
+    taps_second = band(SECOND[1:], 1.0, SCALE_SECOND)
     work = pltpu.VMEM((rows, 8, width), f32)
     h_own, sum_own = kernel(interior_kernel, [stack] * 2, 100, "interior", [work] * 5)(
         waves, other, axis_x, axis_y, axis_z, taps_first, taps_second

time: 26.5 us -> 31.2 us (1.18)
  local copies, waits for them, and re-layouts: 5.42 us -> 8.45 us
  Pallas kernels: 4.91 us -> 6.41 us
  other arithmetic: 1.16 us -> 0.01 us
  starting transfers between devices: 10.2 us -> 11 us
  waiting for transfers between devices: 3.7 us -> 4.21 us
    unnamed x31 -> x35, local copies, waits for them, and re-layouts: 5.41 us -> 8.44 us
    pallas_call x1 -> x2, Pallas kernels: 0.71 us -> 2.21 us  [the longest x1 1.51 us: body(): kernel(load_kernel, [stack] + [jax.ShapeDtypeStruct(array.shape, array.dt...]
    ppermute x1, waiting for transfers between devices: 0.01 us -> 1.48 us  [body(): inner = lax.ppermute(jnp.where(even, last, leading), 'xy', pairs[1])]
    ppermute x4, waiting for transfers between devices: 2.87 us -> 1.63 us  [body(): lax.ppermute(send, 'xy', pair)]
    concatenate x1 -> x0, other arithmetic: 1.15 us -> none  [body(): waves = lax.optimization_barrier(jnp.concatenate([wave_p, wave_q], axis=1))]
    ppermute x4, starting transfers between devices: 6.48 us -> 7.59 us  [body(): lax.ppermute(send, 'xy', pair)]
  transfers between devices with their start and end apart: 8 -> 8, of which waited for: 3 -> 3; matrix products, arithmetic and copies ran while one was open for 0% -> 0% of each run, Pallas kernels for 12% -> 10%
where the time goes in v7:
time: 31.2 us; the launch traced here: 30.8 us
  starting transfers between devices  11 us (35%)
  local copies, waits for them, and re-layouts  8.45 us (27%)
  Pallas kernels  6.41 us (21%)
  waiting for transfers between devices  4.21 us (13%)
  between operations  0.79 us (3%)
    unnamed x35, local copies, waits for them, and re-layouts  8.44 us
    ppermute x4, starting transfers between devices, body(): lax.ppermute(send, 'xy', pair)  7.59 us
    ppermute x1, starting transfers between devices, body(): inner = lax.ppermute(jnp.where(even, last, leading), 'xy', pairs[1])  2.58 us
    ppermute x4, waiting for transfers between devices, body(): lax.ppermute(send, 'xy', pair)  1.63 us
    pallas_call x1, Pallas kernels, body(): kernel(load_kernel, [stack] + [jax.ShapeDtypeStruct(array.shape, array.dt...  1.51 us
    ppermute x1, waiting for transfers between devices, body(): inner = lax.ppermute(jnp.where(even, last, leading), 'xy', pairs[1])  1.48 us
    pallas_call x1, Pallas kernels, body(): kernel(interior_kernel, [stack] * 2, 100, 'interior', [work] * 5)  1.39 us
    ppermute x1, waiting for transfers between devices, body(): edges_other = lax.ppermute(edges, 'gz', cores)  1.09 us
  transfers between devices with their start and end apart: 8, of which 3 were waited for; matrix products, arithmetic and copies ran while one was open for 0% of the time, Pallas kernels for 10%

profile of v7, /device:TPU:0, one launch (start us, length us, event | category | flops | bytes accessed | tf_op | source)
XLA Modules:
  0.0 30.8 jit_solution(1488478470850064145)
XLA Ops:
  0.6 0.0 copy-start.4
  0.6 0.9 %copy-done.4 = f32[16,4,640]{2,1,0:T(4,128)S(1)} copy-done((f32[16,4,640]{2,1,0:T(4,128)S(1)}, f32[16,4,640]{2,1,0:T(4,128)}, u32[]{:S(2)}) %copy-start.4) | copy-done | bytes 163864
  1.6 0.0 copy-start.5
  1.6 0.9 %copy-done.5 = f32[16,4,640]{2,1,0:T(4,128)S(1)} copy-done((f32[16,4,640]{2,1,0:T(4,128)S(1)}, f32[16,4,640]{2,1,0:T(4,128)}, u32[]{:S(2)}) %copy-start.5) | copy-done | bytes 163864
  2.5 0.9 %copy-done.6 = f32[16,4,640]{2,1,0:T(4,128)S(1)} copy-done((f32[16,4,640]{2,1,0:T(4,128)S(1)}, f32[16,4,640]{2,1,0:T(4,128)}, u32[]{:S(2)}) %copy-start.6) | copy-done | bytes 163864
  3.4 0.9 %copy-done.7 = f32[16,4,640]{2,1,0:T(4,128)S(1)} copy-done((f32[16,4,640]{2,1,0:T(4,128)S(1)}, f32[16,4,640]{2,1,0:T(4,128)}, u32[]{:S(2)}) %copy-start.7) | copy-done | bytes 163864
  4.3 0.9 %copy-done.8 = bf16[16,4,640]{2,1,0:T(4,128)(2,1)S(1)} copy-done((bf16[16,4,640]{2,1,0:T(4,128)(2,1)S(1)}, bf16[16,4,640]{2,1,0:T(4,128)(2,1)}, u32[]{:S(2)}) %copy-start.8) | copy-done | bytes 81944
  5.2 0.9 %copy-done.9 = bf16[16,4,640]{2,1,0:T(4,128)(2,1)S(1)} copy-done((bf16[16,4,640]{2,1,0:T(4,128)(2,1)S(1)}, bf16[16,4,640]{2,1,0:T(4,128)(2,1)}, u32[]{:S(2)}) %copy-start.9) | copy-done | bytes 81944
  6.1 0.9 %copy-done.10 = bf16[16,4,640]{2,1,0:T(4,128)(2,1)S(1)} copy-done((bf16[16,4,640]{2,1,0:T(4,128)(2,1)S(1)}, bf16[16,4,640]{2,1,0:T(4,128)(2,1)}, u32[]{:S(2)}) %copy-start.10) | copy-done | bytes 81944
  7.0 0.9 %copy-done.11 = bf16[16,4,640]{2,1,0:T(4,128)(2,1)S(1)} copy-done((bf16[16,4,640]{2,1,0:T(4,128)(2,1)S(1)}, bf16[16,4,640]{2,1,0:T(4,128)(2,1)}, u32[]{:S(2)}) %copy-start.11) | copy-done | bytes 81944
  7.9 0.9 %copy-done.12 = bf16[16,4,640]{2,1,0:T(4,128)(2,1)S(1)} copy-done((bf16[16,4,640]{2,1,0:T(4,128)(2,1)S(1)}, bf16[16,4,640]{2,1,0:T(4,128)(2,1)}, u32[]{:S(2)}) %copy-start.12) | copy-done | bytes 81944
  8.7 1.5 %load.1 = (f32[16,8,640]{2,1,0:T(8,128)S(1)}, f32[16,4,640]{2,1,0:T(4,128)S(1)}, f32[16,4,640]{2,1,0:T(4,128)S(1)}, bf16[16,4,640]{2,1,0:T(4,128)(2,1)S(1)}, bf1...) custom-call(f32[16,4,640]{2,1,0:T(4,128)S(1)} %copy-done.4, ...), custom_call_target="tpu_custom_call" | custom-call | flops 409600 | bytes 1638400 | tf_op jit(solution)/shard_map/load/pallas_call | solution.py:396
  10.3 0.5 %collective-permute-start.2 = (f32[16,8,640]{2,1,0:T(8,128)S(1)}, f32[16,8,640]{2,1,0:T(8,128)S(1)}, u32[]{:S(2)}, u32[]{:S(2)}) collective-permute-start(f32[16,8,640]{2,1,0:T(8,128)S(1)} %get-tuple-element.41.waves), channel_id=1, source_target_pairs={{0,1},{1,0},{2,3},{3,2},{4,5},{5,4},{6,7},{7,6},{8,9},{9,8},{10,11... | collective-permute-start | bytes 983048 | tf_op jit(solution)/shard_map/ppermute | solution.py:411
  10.8 2.6 %collective-permute-start.1 = (f32[4,8,640]{2,1,0:T(8,128)S(1)}, f32[4,8,640]{2,1,0:T(8,128)S(1)}, u32[]{:S(2)}, u32[]{:S(2)}) collective-permute-start(f32[4,8,640]{2,1,0:T(8,128)S(1)} %get-tuple-element.76), channel_id=1, source_target_pairs={{0,2},{2,0},{4,6},{6,4},{8,10},{10,8},{12,14},{14,12},{1,3},{3,1},... | collective-permute-start | bytes 245768 | tf_op jit(solution)/shard_map/ppermute | solution.py:412
  13.4 0.2 collective-permute-start
  13.6 0.7 %weights.1 = (f32[16,8,640]{2,1,0:T(8,128)S(1)}, f32[16,8,640]{2,1,0:T(8,128)S(1)}, f32[16,8,640]{2,1,0:T(8,128)S(1)}, f32[16,8,640]{2,1,0:T(8,128)S(1)}, f32[16...) custom-call(f32[16,8,640]{2,1,0:T(8,128)S(1)} %get-tuple-element.41.waves, f32[16,4,640]{2,1,0:T(4,128)S(1)} %get-tuple-element.42.prior_p, ...), custom_call_target="tpu_custom_call" | custom-call | flops 4096000 | bytes 1638400 | tf_op jit(solution)/shard_map/weights/pallas_call | solution.py:415
  14.3 0.0 collective-permute-done.2.other
  14.3 0.2 copy-done
  14.5 0.1 copy-done.3
  14.6 1.4 %interior.1 = (f32[16,8,640]{2,1,0:T(8,128)S(1)}, f32[16,8,640]{2,1,0:T(8,128)S(1)}) custom-call(f32[16,8,640]{2,1,0:T(8,128)S(1)} %get-tuple-element.41.waves, f32[16,8,640]{2,1,0:T(8,128)S(1)} %collective-permute-done.2.other, f32[16,8,640]{2,1,0:T(8,128)S(1)} %get-tuple-element.49.axis_x, f32[16,8,640]{2,1,0:T(8,128)S(1)} %get-tuple-element.50.axis_y, ...), custom_call_target="tpu_custom_call" | custom-call | flops 4096000 | bytes 1638400 | tf_op jit(solution)/shard_map/interior/pallas_call | solution.py:421
  16.0 1.5 %collective-permute-done.1 = f32[4,8,640]{2,1,0:T(8,128)S(1)} collective-permute-done((f32[4,8,640]{2,1,0:T(8,128)S(1)}, f32[4,8,640]{2,1,0:T(8,128)S(1)}, u32[]{:S(2)}, u32[]{:S(2)}) %collective-permute-start.1) | collective-permute-done | bytes 81952 | tf_op jit(solution)/shard_map/ppermute | solution.py:412
  17.5 0.0 collective-permute-done
  17.5 0.0 copy-start.1
  17.5 0.0 copy-start.2
  17.5 0.1 collective-permute-start.3
  17.6 0.0 copy-start.13
  17.6 0.0 copy-start.14
  17.6 0.3 halo.1
  17.9 1.1 %collective-permute-done.3.edges_other = f32[8,8,640]{2,1,0:T(8,128)S(1)} collective-permute-done((f32[8,8,640]{2,1,0:T(8,128)S(1)}, f32[8,8,640]{2,1,0:T(8,128)S(1)}, u32[]{:S(2)}, u32[]{:S(2)}) %collective-permute-start.3) | collective-permute-done | bytes 163872 | tf_op jit(solution)/shard_map/ppermute | solution.py:426
  19.0 0.0 copy-done.1
  19.0 0.0 copy-done.2
  19.0 0.0 copy-done.13
  19.0 0.0 copy-done.14
  19.0 0.0 copy-start.15
  19.0 0.0 copy-start.16
  19.0 0.9 %step.1 = (f32[16,8,640]{2,1,0:T(8,128)S(1)}, f32[64,640]{1,0:T(8,128)S(1)}, f32[24,640]{1,0:T(8,128)S(1)}, f32[24,640]{1,0:T(8,128)S(1)}, f32[8,640]{1,0:T(8,128)S(1)}, /*index=5*/f32[8,640]{1,0:T(8,128)S(1)}) custom-call(f32[8,8,640]{2,1,0:T(8,128)S(1)} %constant_dynamic-update-slice_fusion.edges, f32[8,8,640]{2,1,0:T(8,128)S(1)} %collective-permute-done.3.edges_other, ...), custom_call_target="tpu_custom_call" | custom-call | flops 16384000 | bytes 1638400 | tf_op jit(solution)/shard_map/step/pallas_call | solution.py:448
  20.0 3.8 %collective-permute-start.4 = (f32[24,640]{1,0:T(8,128)S(1)}, f32[24,640]{1,0:T(8,128)S(1)}, u32[]{:S(2)}, u32[]{:S(2)}) collective-permute-start(f32[24,640]{1,0:T(8,128)S(1)} %get-tuple-element.68), channel_id=1, source_target_pairs={{0,14},{2,4},{4,2},{6,8},{8,6},{10,12},{12,10},{14,0},{1,15},{3,5}... | collective-permute-start | bytes 184328 | tf_op jit(solution)/shard_map/ppermute | solution.py:466
  23.8 0.6 %collective-permute-start.5 = (f32[24,640]{1,0:T(8,128)S(1)}, f32[24,640]{1,0:T(8,128)S(1)}, u32[]{:S(2)}, u32[]{:S(2)}) collective-permute-start(f32[24,640]{1,0:T(8,128)S(1)} %get-tuple-element.69), channel_id=1, source_target_pairs={{0,2},{2,0},{4,6},{6,4},{8,10},{10,8},{12,14},{14,12},{1,3},{3,1},... | collective-permute-start | bytes 184328 | tf_op jit(solution)/shard_map/ppermute | solution.py:466
  24.4 1.6 %collective-permute-start.6 = (f32[8,640]{1,0:T(8,128)S(1)}, f32[8,640]{1,0:T(8,128)S(1)}, u32[]{:S(2)}, u32[]{:S(2)}) collective-permute-start(f32[8,640]{1,0:T(8,128)S(1)} %get-tuple-element.70), channel_id=1, source_target_pairs={{0,12},{2,14},{4,8},{6,10},{8,4},{10,6},{12,0},{14,2},{1,13},{3,15... | collective-permute-start | bytes 61448 | tf_op jit(solution)/shard_map/ppermute | solution.py:466
  26.0 1.6 %collective-permute-start.7 = (f32[8,640]{1,0:T(8,128)S(1)}, f32[8,640]{1,0:T(8,128)S(1)}, u32[]{:S(2)}, u32[]{:S(2)}) collective-permute-start(f32[8,640]{1,0:T(8,128)S(1)} %get-tuple-element.71), channel_id=1, source_target_pairs={{0,4},{2,6},{4,0},{6,2},{8,12},{10,14},{12,8},{14,10},{1,5},{3,7},... | collective-permute-start | bytes 61448 | tf_op jit(solution)/shard_map/ppermute | solution.py:466
  27.5 0.0 copy-done.15
  27.5 0.0 copy-done.16
  27.5 0.8 %own.1 = (f32[16,4,640]{2,1,0:T(4,128)}, f32[16,4,640]{2,1,0:T(4,128)}, f32[64,640]{1,0:T(8,128)S(1)}) custom-call(f32[16,8,640]{2,1,0:T(8,128)S(1)} %get-tuple-element.63.pressure, f32[64,640]{1,0:T(8,128)S(1)} %get-tuple-element.64.crossline, bf16[64,64]{1,0:T(8,128)(2,1)S(1)} %copy-done.16, bf16[64,64]{1,0:T(8,128)(2,1)S(1)} %copy-done.15), custom_call_target="tpu_custom_call" | custom-call | flops 4096000 | bytes 1638400 | tf_op jit(solution)/shard_map/own/pallas_call | solution.py:468
  28.4 1.6 %collective-permute-done.6.rest_2_ = f32[8,640]{1,0:T(8,128)S(1)} collective-permute-done((f32[8,640]{1,0:T(8,128)S(1)}, f32[8,640]{1,0:T(8,128)S(1)}, u32[]{:S(2)}, u32[]{:S(2)}) %collective-permute-start.6) | collective-permute-done | bytes 20512 | tf_op jit(solution)/shard_map/ppermute | solution.py:466
  30.0 0.0 collective-permute-done.7.rest_3_
  30.0 0.0 collective-permute-done.4.rest_0_
  30.0 0.0 collective-permute-done.5.rest_1_
  30.0 0.8 %finish.1 = (f32[8,4,640]{2,1,0:T(4,128)}, f32[4,4,640]{2,1,0:T(4,128)}, f32[2,4,640]{2,1,0:T(4,128)}, f32[2,4,640]{2,1,0:T(4,128)}) custom-call(f32[64,640]{1,0:T(8,128)S(1)} %get-tuple-element.67.mine, f32[24,640]{1,0:T(8,128)S(1)} %collective-permute-done.4.rest_0_, f32[24,640]{1,0:T(8,128)S(1)} %collective-permute-done.5.rest_1_, ...), custom_call_target="tpu_custom_call" | custom-call | flops 819200 | bytes 1638400 | tf_op jit(solution)/shard_map/finish/pallas_call | solution.py:471
  (12 shorter events, 0.0 us)
Async XLA Ops:
  0.6 0.9 %copy-start.4 = (f32[16,4,640]{2,1,0:T(4,128)S(1)}, f32[16,4,640]{2,1,0:T(4,128)}, u32[]{:S(2)}) copy-start(f32[16,4,640]{2,1,0:T(4,128)} %wave_p.1) | copy-start | bytes 491524
  1.6 0.9 %copy-start.5 = (f32[16,4,640]{2,1,0:T(4,128)S(1)}, f32[16,4,640]{2,1,0:T(4,128)}, u32[]{:S(2)}) copy-start(f32[16,4,640]{2,1,0:T(4,128)} %wave_q.1) | copy-start | bytes 491524
  2.5 0.9 %copy-start.6 = (f32[16,4,640]{2,1,0:T(4,128)S(1)}, f32[16,4,640]{2,1,0:T(4,128)}, u32[]{:S(2)}) copy-start(f32[16,4,640]{2,1,0:T(4,128)} %rest_0_.1) | copy-start | bytes 491524
  3.4 0.9 %copy-start.7 = (f32[16,4,640]{2,1,0:T(4,128)S(1)}, f32[16,4,640]{2,1,0:T(4,128)}, u32[]{:S(2)}) copy-start(f32[16,4,640]{2,1,0:T(4,128)} %rest_1_.1) | copy-start | bytes 491524
  4.3 0.9 %copy-start.8 = (bf16[16,4,640]{2,1,0:T(4,128)(2,1)S(1)}, bf16[16,4,640]{2,1,0:T(4,128)(2,1)}, u32[]{:S(2)}) copy-start(bf16[16,4,640]{2,1,0:T(4,128)(2,1)} %rest_2_.1) | copy-start | bytes 245764
  5.2 0.9 %copy-start.9 = (bf16[16,4,640]{2,1,0:T(4,128)(2,1)S(1)}, bf16[16,4,640]{2,1,0:T(4,128)(2,1)}, u32[]{:S(2)}) copy-start(bf16[16,4,640]{2,1,0:T(4,128)(2,1)} %rest_3_.1) | copy-start | bytes 245764
  6.1 0.9 %copy-start.10 = (bf16[16,4,640]{2,1,0:T(4,128)(2,1)S(1)}, bf16[16,4,640]{2,1,0:T(4,128)(2,1)}, u32[]{:S(2)}) copy-start(bf16[16,4,640]{2,1,0:T(4,128)(2,1)} %rest_4_.1) | copy-start | bytes 245764
  7.0 0.9 %copy-start.11 = (bf16[16,4,640]{2,1,0:T(4,128)(2,1)S(1)}, bf16[16,4,640]{2,1,0:T(4,128)(2,1)}, u32[]{:S(2)}) copy-start(bf16[16,4,640]{2,1,0:T(4,128)(2,1)} %rest_5_.1) | copy-start | bytes 245764
  7.9 0.9 %copy-start.12 = (bf16[16,4,640]{2,1,0:T(4,128)(2,1)S(1)}, bf16[16,4,640]{2,1,0:T(4,128)(2,1)}, u32[]{:S(2)}) copy-start(bf16[16,4,640]{2,1,0:T(4,128)(2,1)} %rest_6_.1) | copy-start | bytes 245764
  10.3 4.0 %collective-permute-start.2 = (f32[16,8,640]{2,1,0:T(8,128)S(1)}, f32[16,8,640]{2,1,0:T(8,128)S(1)}, u32[]{:S(2)}, u32[]{:S(2)}) collective-permute-start(f32[16,8,640]{2,1,0:T(8,128)S(1)} %get-tuple-element.41.waves), channel_id=1, source_target_pairs={{0,1},{1,0},{2,3},{3,2},{4,5},{5,4},{6,7},{7,6},{8,9},{9,8},{10,11... | collective-permute-start | bytes 983048 | tf_op jit(solution)/shard_map/ppermute | solution.py:411
  10.8 6.7 %collective-permute-start.1 = (f32[4,8,640]{2,1,0:T(8,128)S(1)}, f32[4,8,640]{2,1,0:T(8,128)S(1)}, u32[]{:S(2)}, u32[]{:S(2)}) collective-permute-start(f32[4,8,640]{2,1,0:T(8,128)S(1)} %get-tuple-element.76), channel_id=1, source_target_pairs={{0,2},{2,0},{4,6},{6,4},{8,10},{10,8},{12,14},{14,12},{1,3},{3,1},... | collective-permute-start | bytes 245768 | tf_op jit(solution)/shard_map/ppermute | solution.py:412
  13.4 4.1 %collective-permute-start = (f32[4,8,640]{2,1,0:T(8,128)S(1)}, f32[4,8,640]{2,1,0:T(8,128)S(1)}, u32[]{:S(2)}, u32[]{:S(2)}) collective-permute-start(f32[4,8,640]{2,1,0:T(8,128)S(1)} %get-tuple-element.77), channel_id=1, source_target_pairs={{0,1},{1,0},{2,4},{3,5},{4,2},{5,3},{6,8},{7,9},{8,6},{9,7},{10,12... | collective-permute-start | bytes 245768 | tf_op jit(solution)/shard_map/ppermute | solution.py:413
  13.6 0.9 %copy-start = (bf16[512,256]{1,0:T(8,128)(2,1)S(1)}, bf16[512,256]{1,0:T(8,128)(2,1)}, u32[]{:S(2)}) copy-start(bf16[512,256]{1,0:T(8,128)(2,1)} %constant.36.clone.taps_first) | copy-start | bytes 786436
  13.6 1.0 %copy-start.3 = (bf16[512,256]{1,0:T(8,128)(2,1)S(1)}, bf16[512,256]{1,0:T(8,128)(2,1)}, u32[]{:S(2)}) copy-start(bf16[512,256]{1,0:T(8,128)(2,1)} %constant.37.clone.taps_second) | copy-start | bytes 786436
  17.5 1.5 %copy-start.1 = (bf16[640,640]{1,0:T(8,128)(2,1)S(1)}, bf16[640,640]{1,0:T(8,128)(2,1)}, u32[]{:S(2)}) copy-start(bf16[640,640]{1,0:T(8,128)(2,1)} %constant.43.clone.across_low) | copy-start | bytes 2457604
  17.5 1.5 %copy-start.2 = (bf16[640,640]{1,0:T(8,128)(2,1)S(1)}, bf16[640,640]{1,0:T(8,128)(2,1)}, u32[]{:S(2)}) copy-start(bf16[640,640]{1,0:T(8,128)(2,1)} %constant.42.clone.across_high) | copy-start | bytes 2457604
  17.5 1.5 %collective-permute-start.3 = (f32[8,8,640]{2,1,0:T(8,128)S(1)}, f32[8,8,640]{2,1,0:T(8,128)S(1)}, u32[]{:S(2)}, u32[]{:S(2)}) collective-permute-start(f32[8,8,640]{2,1,0:T(8,128)S(1)} %constant_dynamic-update-slice_fusion.edges), channel_id=1, source_target_pairs={{0,1},{1,0},{2,3},{3,2},{4,5},{5,4},{6,7},{7,6},{8,9},{9,8},{10,11... | collective-permute-start | bytes 491528 | tf_op jit(solution)/shard_map/ppermute | solution.py:426
  17.6 1.4 %copy-start.13 = (bf16[64,64]{1,0:T(8,128)(2,1)S(1)}, bf16[64,64]{1,0:T(8,128)(2,1)}, u32[]{:S(2)}) copy-start(bf16[64,64]{1,0:T(8,128)(2,1)} %constant.39.clone.inline_low) | copy-start | bytes 24580
  17.6 1.4 %copy-start.14 = (bf16[64,64]{1,0:T(8,128)(2,1)S(1)}, bf16[64,64]{1,0:T(8,128)(2,1)}, u32[]{:S(2)}) copy-start(bf16[64,64]{1,0:T(8,128)(2,1)} %constant.38.clone.inline_high) | copy-start | bytes 24580
  19.0 8.5 %copy-start.15 = (bf16[64,64]{1,0:T(8,128)(2,1)S(1)}, bf16[64,64]{1,0:T(8,128)(2,1)}, u32[]{:S(2)}) copy-start(bf16[64,64]{1,0:T(8,128)(2,1)} %constant.41.clone.own_low) | copy-start | bytes 24580
  19.0 8.5 %copy-start.16 = (bf16[64,64]{1,0:T(8,128)(2,1)S(1)}, bf16[64,64]{1,0:T(8,128)(2,1)}, u32[]{:S(2)}) copy-start(bf16[64,64]{1,0:T(8,128)(2,1)} %constant.40.clone.own_high) | copy-start | bytes 24580
  20.0 10.0 %collective-permute-start.4 = (f32[24,640]{1,0:T(8,128)S(1)}, f32[24,640]{1,0:T(8,128)S(1)}, u32[]{:S(2)}, u32[]{:S(2)}) collective-permute-start(f32[24,640]{1,0:T(8,128)S(1)} %get-tuple-element.68), channel_id=1, source_target_pairs={{0,14},{2,4},{4,2},{6,8},{8,6},{10,12},{12,10},{14,0},{1,15},{3,5}... | collective-permute-start | bytes 184328 | tf_op jit(solution)/shard_map/ppermute | solution.py:466
  23.8 6.2 %collective-permute-start.5 = (f32[24,640]{1,0:T(8,128)S(1)}, f32[24,640]{1,0:T(8,128)S(1)}, u32[]{:S(2)}, u32[]{:S(2)}) collective-permute-start(f32[24,640]{1,0:T(8,128)S(1)} %get-tuple-element.69), channel_id=1, source_target_pairs={{0,2},{2,0},{4,6},{6,4},{8,10},{10,8},{12,14},{14,12},{1,3},{3,1},... | collective-permute-start | bytes 184328 | tf_op jit(solution)/shard_map/ppermute | solution.py:466
  24.4 5.6 %collective-permute-start.6 = (f32[8,640]{1,0:T(8,128)S(1)}, f32[8,640]{1,0:T(8,128)S(1)}, u32[]{:S(2)}, u32[]{:S(2)}) collective-permute-start(f32[8,640]{1,0:T(8,128)S(1)} %get-tuple-element.70), channel_id=1, source_target_pairs={{0,12},{2,14},{4,8},{6,10},{8,4},{10,6},{12,0},{14,2},{1,13},{3,15... | collective-permute-start | bytes 61448 | tf_op jit(solution)/shard_map/ppermute | solution.py:466
  26.0 4.0 %collective-permute-start.7 = (f32[8,640]{1,0:T(8,128)S(1)}, f32[8,640]{1,0:T(8,128)S(1)}, u32[]{:S(2)}, u32[]{:S(2)}) collective-permute-start(f32[8,640]{1,0:T(8,128)S(1)} %get-tuple-element.71), channel_id=1, source_target_pairs={{0,4},{2,6},{4,0},{6,2},{8,12},{10,14},{12,8},{14,10},{1,5},{3,7},... | collective-permute-start | bytes 61448 | tf_op jit(solution)/shard_map/ppermute | solution.py:466

commit v8 on v6

--- a/solution.py
+++ b/solution.py
@@ -31,14 +31,6 @@
         coarse, detail = lift_level(coarse)
         members.append(detail)
     return members + [coarse]
-
-
-def band(width, taps, sign, scale):
-    matrix = np.zeros((width, width))
-    for k, tap in enumerate(taps, 1):
-        value = float(np.round(tap * scale))
-        matrix += value * np.eye(width, k=-k) + sign * value * np.eye(width, k=k)
-    return jnp.asarray(matrix.astype(jnp.bfloat16))
 
 
 def split_bf16(matrix):
@@ -91,10 +83,38 @@
     return out_sine, out_cosine
 
 
+def band(shape, taps, sign, scale):
+    offset = lax.broadcasted_iota(jnp.int32, shape, 0) - LANES
+    offset = offset - lax.broadcasted_iota(jnp.int32, shape, 1)
+    values = jnp.zeros(shape, jnp.float32)
+    for k, tap in enumerate(taps, 1):
+        values = jnp.where(jnp.abs(offset) == k, float(np.round(tap * scale)), values)
+    if sign < 0:
+        values = jnp.where(offset < 0, -values, values)
+    return values.astype(jnp.bfloat16)
+
+
 def weights_kernel(
-    waves, prior_p, prior_q, courant, epsilon, delta, tilt, azimuth, axis_x, axis_y, axis_z, gain_a, gain_b, base
+    waves,
+    prior_p,
+    prior_q,
+    courant,
+    epsilon,
+    delta,
+    tilt,
+    azimuth,
+    axis_x,
+    axis_y,
+    axis_z,
+    gain_a,
+    gain_b,
+    base,
+    taps_first,
+    taps_second,
 ):
     rows = waves.shape[0]
+    taps_first[...] = band(taps_first.shape, FIRST, -1.0, SCALE_FIRST)
+    taps_second[...] = band(taps_second.shape, SECOND[1:], 1.0, SCALE_SECOND)
     top = lax.broadcasted_iota(jnp.int32, waves.shape[1:], 0) < 4
 
     def swap(value):
@@ -163,12 +183,10 @@
     blocks = []
     for start in range(0, width, 2 * LANES):
         stop = min(start + 2 * LANES, width)
-        low, high = max(start - LANES, 0), min(stop + LANES, width)
-        blocks.append(
-            jnp.dot(
-                parts[:, low:high], taps[low:high, start:stop], preferred_element_type=jnp.float32
-            )
-        )
+        first = start - LANES
+        low, high = max(first, 0), min(stop + LANES, width)
+        block = taps[low - first : high - first, : stop - start]
+        blocks.append(jnp.dot(parts[:, low:high], block, preferred_element_type=jnp.float32))
     return jnp.concatenate(blocks, axis=1)
 
 
@@ -215,7 +233,7 @@
 def halo_rows(size, edges):
     place = lax.axis_index("xy")
     even = place % 2 == 0
-    left_at, right_at = jnp.where(even, 4, 0), jnp.where(even, 0, 4)
+    left_at, right_at = jnp.where(even, 0, 4), jnp.where(even, 4, 0)
     left_in = jnp.where(place > 0, 1.0, 0.0)
     right_in = jnp.where(place < size - 1, 1.0, 0.0)
     before = [edges[left_at + x] * left_in for x in range(4)]
@@ -356,6 +374,21 @@
     even = lax.axis_index("xy") % 2 == 0
     pairs = pair_swaps(size)
     cores = [(0, 1), (1, 0)]
+    stack = jax.ShapeDtypeStruct((rows, 8, width), f32)
+    cells = rows * layers * width
+    params = pltpu.CompilerParams(vmem_limit_bytes=16 * 1024 * 1024)
+
+    def kernel(function, out_shape, work, name, scratch_shapes=()):
+        cost = pl.CostEstimate(flops=work * cells, bytes_accessed=40 * cells, transcendentals=0)
+        return pl.pallas_call(
+            function,
+            out_shape=out_shape,
+            scratch_shapes=scratch_shapes,
+            compiler_params=params,
+            cost_estimate=cost,
+            name=name,
+        )
+
     waves = lax.optimization_barrier(jnp.concatenate([wave_p, wave_q], axis=1))
     leading, last = waves[:4], waves[rows - 4 :]
     open_outer = [
@@ -367,32 +400,16 @@
     inner = lax.ppermute(jnp.where(even, last, leading), "xy", pairs[1])
     outer = lax.ppermute(jnp.where(even, leading, last), ("xy", "gz"), open_outer)
 
-    stack = jax.ShapeDtypeStruct((rows, 8, width), f32)
-    cells = rows * layers * width
-    params = pltpu.CompilerParams(vmem_limit_bytes=16 * 1024 * 1024)
-
-    def kernel(function, out_shape, work, name, scratch_shapes=()):
-        cost = pl.CostEstimate(flops=work * cells, bytes_accessed=40 * cells, transcendentals=0)
-        return pl.pallas_call(
-            function,
-            out_shape=out_shape,
-            scratch_shapes=scratch_shapes,
-            compiler_params=params,
-            cost_estimate=cost,
-            name=name,
-        )
-
-    axis_x, axis_y, axis_z, *gains = kernel(weights_kernel, [stack] * 6, 100, "weights")(
-        waves, prior_p, prior_q, courant, epsilon, thomsen_delta, tilt_angle, azimuth
-    )
-    taps_first = band(width, FIRST, -1.0, SCALE_FIRST)
-    taps_second = band(width, SECOND[1:], 1.0, SCALE_SECOND)
+    taps = jax.ShapeDtypeStruct((4 * LANES, 2 * LANES), jnp.bfloat16)
+    axis_x, axis_y, axis_z, *gains, taps_first, taps_second = kernel(
+        weights_kernel, [stack] * 6 + [taps] * 2, 100, "weights"
+    )(waves, prior_p, prior_q, courant, epsilon, thomsen_delta, tilt_angle, azimuth)
     work = pltpu.VMEM((rows, 8, width), f32)
     h_own, sum_own = kernel(interior_kernel, [stack] * 2, 100, "interior", [work] * 5)(
         waves, other, axis_x, axis_y, axis_z, taps_first, taps_second
     )
     outer, inner, h_own, sum_own = lax.optimization_barrier((outer, inner, h_own, sum_own))
-    edges = jnp.concatenate([inner, outer], axis=0)
+    edges = jnp.concatenate([outer, inner], axis=0)
     edges_other = lax.ppermute(edges, "gz", cores)
     edge = jax.ShapeDtypeStruct((8, 8, width), f32)
     h_edge, sum_edge = kernel(functools.partial(halo_kernel, size), [edge] * 2, 100, "halo")(

time: 26.5 us -> 22.5 us (0.85); the launches traced: 26.1 us -> 22.4 us
  local copies, waits for them, and re-layouts: 5.42 us -> 0.08 us
  starting transfers between devices: 10.2 us -> 11 us
  waiting for transfers between devices: 3.7 us -> 4.22 us
    unnamed x31 -> x27, local copies, waits for them, and re-layouts: 5.41 us -> 0.08 us
    ppermute x1, waiting for transfers between devices: 0.01 us -> 1.49 us  [body(): inner = lax.ppermute(jnp.where(even, last, leading), 'xy', pairs[1])]
    ppermute x4, waiting for transfers between devices: 2.87 us -> 1.63 us  [body(): lax.ppermute(send, 'xy', pair)]
    ppermute x4, starting transfers between devices: 6.48 us -> 7.59 us  [body(): lax.ppermute(send, 'xy', pair)]
    ppermute x1, starting transfers between devices: 0.38 us -> 0.07 us  [body(): edges_other = lax.ppermute(edges, 'gz', cores)]
    ppermute x1, waiting for transfers between devices: 0.82 us -> 1.09 us  [body(): edges_other = lax.ppermute(edges, 'gz', cores)]
  transfers between devices with their start and end apart: 8 -> 8, of which waited for: 3 -> 3; matrix products, arithmetic and copies ran while one was open for 0% -> 0% of each run, Pallas kernels for 12% -> 15%
where the time goes in v8:
time: 22.5 us; the launch traced here: 22.4 us
  starting transfers between devices  11 us (49%)
  Pallas kernels  5.16 us (23%)
  waiting for transfers between devices  4.22 us (19%)
  other arithmetic  1.15 us (5%)
  between operations  0.83 us (4%)
    ppermute x4, starting transfers between devices, body(): lax.ppermute(send, 'xy', pair)  7.59 us
    ppermute x1, starting transfers between devices, body(): inner = lax.ppermute(jnp.where(even, last, leading), 'xy', pairs[1])  2.6 us
    ppermute x4, waiting for transfers between devices, body(): lax.ppermute(send, 'xy', pair)  1.63 us
    ppermute x1, waiting for transfers between devices, body(): inner = lax.ppermute(jnp.where(even, last, leading), 'xy', pairs[1])  1.49 us
    pallas_call x1, Pallas kernels, body(): kernel(interior_kernel, [stack] * 2, 100, 'interior', [work] * 5)  1.4 us
    concatenate x1, other arithmetic, body(): waves = lax.optimization_barrier(jnp.concatenate([wave_p, wave_q], axis=1))  1.13 us
    ppermute x1, waiting for transfers between devices, body(): edges_other = lax.ppermute(edges, 'gz', cores)  1.09 us
    pallas_call x1, Pallas kernels, body(): kernel(weights_kernel, [stack] * 6 + [taps] * 2, 100, 'weights')  0.95 us
  transfers between devices with their start and end apart: 8, of which 3 were waited for; matrix products, arithmetic and copies ran while one was open for 0% of the time, Pallas kernels for 15%

profile of v8, /device:TPU:0, one launch (start us, length us, event | category | flops | bytes accessed | tf_op | source)
XLA Modules:
  0.0 22.4 jit_solution(17361984142049702171)
XLA Ops:
  0.6 0.0 copy-start.4
  0.6 0.0 copy-start.5
  0.7 0.0 copy-start.6
  0.7 0.0 copy-start.7
  0.7 0.0 copy-start.8
  0.7 1.1 %pad_maximum_fusion.waves = f32[16,8,640]{2,1,0:T(8,128)S(1)} fusion(f32[16,4,640]{2,1,0:T(4,128)} %param.16, f32[16,4,640]{2,1,0:T(4,128)} %param.15), kind=kLoop, calls=%fused_computation | loop fusion | flops 81920 | bytes 655360 | tf_op jit(solution)/shard_map/concatenate | solution.py:392
  1.8 0.5 %collective-permute-start.2 = (f32[16,8,640]{2,1,0:T(8,128)S(1)}, f32[16,8,640]{2,1,0:T(8,128)S(1)}, u32[]{:S(2)}, u32[]{:S(2)}) collective-permute-start(f32[16,8,640]{2,1,0:T(8,128)S(1)} %pad_maximum_fusion.waves), channel_id=1, source_target_pairs={{0,1},{1,0},{2,3},{3,2},{4,5},{5,4},{6,7},{7,6},{8,9},{9,8},{10,11... | collective-permute-start | bytes 983048 | tf_op jit(solution)/shard_map/ppermute | solution.py:399
  2.3 0.0 copy-start.2
  2.4 2.6 %collective-permute-start.1 = (f32[4,8,640]{2,1,0:T(8,128)S(1)}, f32[4,8,640]{2,1,0:T(8,128)S(1)}, u32[]{:S(2)}, u32[]{:S(2)}) collective-permute-start(f32[4,8,640]{2,1,0:T(8,128)S(1)} %get-tuple-element.64), channel_id=1, source_target_pairs={{0,2},{2,0},{4,6},{6,4},{8,10},{10,8},{12,14},{14,12},{1,3},{3,1},... | collective-permute-start | bytes 245768 | tf_op jit(solution)/shard_map/ppermute | solution.py:400
  5.0 0.2 collective-permute-start
  5.1 0.0 copy-done.4
  5.1 0.0 copy-done.5
  5.1 0.0 copy-done.6
  5.2 0.0 copy-done.7
  5.2 0.0 copy-done.8
  5.2 0.0 copy-done.2
  5.2 0.0 copy-done.3
  5.2 1.0 %weights.1 = (f32[16,8,640]{2,1,0:T(8,128)S(1)}, f32[16,8,640]{2,1,0:T(8,128)S(1)}, f32[16,8,640]{2,1,0:T(8,128)S(1)}, f32[16,8,640]{2,1,0:T(8,128)S(1)}, f32[16...) custom-call(f32[16,8,640]{2,1,0:T(8,128)S(1)} %pad_maximum_fusion.wa, ...), custom_call_target="tpu_custom_call" | custom-call | flops 4096000 | bytes 1638400 | tf_op jit(solution)/shard_map/weights/pallas_call | solution.py:404
  6.1 0.0 collective-permute-done.2.other
  6.2 1.4 %interior.1 = (f32[16,8,640]{2,1,0:T(8,128)S(1)}, f32[16,8,640]{2,1,0:T(8,128)S(1)}) custom-call(f32[16,8,640]{2,1,0:T(8,128)S(1)} %pad_maximum_fusion.waves, f32[16,8,640]{2,1,0:T(8,128)S(1)} %collective-permute-done.2.other, f32[16,8,640]{2,1,0:T(8,128)S(1)} %get-tuple-element.35.axis_x, f32[16,8,640]{2,1,0:T(8,128)S(1)} %get-tuple-element.36.axis_y, ...), custom_call_target="tpu_custom_call" | custom-call | flops 4096000 | bytes 1638400 | tf_op jit(solution)/shard_map/interior/pallas_call | solution.py:408
  7.6 1.5 %collective-permute-done.1 = f32[4,8,640]{2,1,0:T(8,128)S(1)} collective-permute-done((f32[4,8,640]{2,1,0:T(8,128)S(1)}, f32[4,8,640]{2,1,0:T(8,128)S(1)}, u32[]{:S(2)}, u32[]{:S(2)}) %collective-permute-start.1) | collective-permute-done | bytes 81952 | tf_op jit(solution)/shard_map/ppermute | solution.py:400
  9.0 0.0 collective-permute-done
  9.1 0.0 copy-start
  9.1 0.0 copy-start.1
  9.1 0.1 collective-permute-start.3
  9.2 0.0 copy-start.9
  9.2 0.0 copy-start.10
  9.2 0.3 %halo.1 = (f32[8,8,640]{2,1,0:T(8,128)S(1)}, f32[8,8,640]{2,1,0:T(8,128)S(1)}) custom-call(f32[8,8,640]{2,1,0:T(8,128)S(1)} %constant_dynamic-update-slice_fusion.edges, f32[16,8,640]{2,1,0:T(8,128)S(1)} %get-tuple-element.35.axis_x, f32[16,8,640]{2,1,0:T(8,128)S(1)} %get-tuple-element.36.axis_y, f32[16,8,640]{2,1,0:T(8,128)S(1)} %get-tuple-element.44.h_own, ...), custom_call_target="tpu_custom_call" | custom-call | flops 4096000 | bytes 1638400 | tf_op jit(solution)/shard_map/halo/pallas_call | solution.py:415
  9.5 1.1 %collective-permute-done.3.edges_other = f32[8,8,640]{2,1,0:T(8,128)S(1)} collective-permute-done((f32[8,8,640]{2,1,0:T(8,128)S(1)}, f32[8,8,640]{2,1,0:T(8,128)S(1)}, u32[]{:S(2)}, u32[]{:S(2)}) %collective-permute-start.3) | collective-permute-done | bytes 163872 | tf_op jit(solution)/shard_map/ppermute | solution.py:413
  10.6 0.0 copy-done
  10.6 0.0 copy-done.1
  10.6 0.0 copy-done.9
  10.6 0.0 copy-done.10
  10.6 0.0 copy-start.11
  10.6 0.0 copy-start.12
  10.6 0.9 %step.1 = (f32[16,8,640]{2,1,0:T(8,128)S(1)}, f32[64,640]{1,0:T(8,128)S(1)}, f32[24,640]{1,0:T(8,128)S(1)}, f32[24,640]{1,0:T(8,128)S(1)}, f32[8,640]{1,0:T(8,128)S(1)}, /*index=5*/f32[8,640]{1,0:T(8,128)S(1)}) custom-call(f32[8,8,640]{2,1,0:T(8,128)S(1)} %constant_dynamic-update-slice_fusion.edges, f32[8,8,640]{2,1,0:T(8,128)S(1)} %collective-permute-done.3.edges_other, ...), custom_call_target="tpu_custom_call" | custom-call | flops 16384000 | bytes 1638400 | tf_op jit(solution)/shard_map/step/pallas_call | solution.py:435
  11.5 3.8 %collective-permute-start.4 = (f32[24,640]{1,0:T(8,128)S(1)}, f32[24,640]{1,0:T(8,128)S(1)}, u32[]{:S(2)}, u32[]{:S(2)}) collective-permute-start(f32[24,640]{1,0:T(8,128)S(1)} %get-tuple-element.56), channel_id=1, source_target_pairs={{0,14},{2,4},{4,2},{6,8},{8,6},{10,12},{12,10},{14,0},{1,15},{3,5}... | collective-permute-start | bytes 184328 | tf_op jit(solution)/shard_map/ppermute | solution.py:453
  15.4 0.6 %collective-permute-start.5 = (f32[24,640]{1,0:T(8,128)S(1)}, f32[24,640]{1,0:T(8,128)S(1)}, u32[]{:S(2)}, u32[]{:S(2)}) collective-permute-start(f32[24,640]{1,0:T(8,128)S(1)} %get-tuple-element.57), channel_id=1, source_target_pairs={{0,2},{2,0},{4,6},{6,4},{8,10},{10,8},{12,14},{14,12},{1,3},{3,1},... | collective-permute-start | bytes 184328 | tf_op jit(solution)/shard_map/ppermute | solution.py:453
  16.0 1.6 %collective-permute-start.6 = (f32[8,640]{1,0:T(8,128)S(1)}, f32[8,640]{1,0:T(8,128)S(1)}, u32[]{:S(2)}, u32[]{:S(2)}) collective-permute-start(f32[8,640]{1,0:T(8,128)S(1)} %get-tuple-element.58), channel_id=1, source_target_pairs={{0,12},{2,14},{4,8},{6,10},{8,4},{10,6},{12,0},{14,2},{1,13},{3,15... | collective-permute-start | bytes 61448 | tf_op jit(solution)/shard_map/ppermute | solution.py:453
  17.6 1.6 %collective-permute-start.7 = (f32[8,640]{1,0:T(8,128)S(1)}, f32[8,640]{1,0:T(8,128)S(1)}, u32[]{:S(2)}, u32[]{:S(2)}) collective-permute-start(f32[8,640]{1,0:T(8,128)S(1)} %get-tuple-element.59), channel_id=1, source_target_pairs={{0,4},{2,6},{4,0},{6,2},{8,12},{10,14},{12,8},{14,10},{1,5},{3,7},... | collective-permute-start | bytes 61448 | tf_op jit(solution)/shard_map/ppermute | solution.py:453
  19.1 0.0 copy-done.11
  19.1 0.0 copy-done.12
  19.1 0.8 %own.1 = (f32[16,4,640]{2,1,0:T(4,128)}, f32[16,4,640]{2,1,0:T(4,128)}, f32[64,640]{1,0:T(8,128)S(1)}) custom-call(f32[16,8,640]{2,1,0:T(8,128)S(1)} %get-tuple-element.51.pressure, f32[64,640]{1,0:T(8,128)S(1)} %get-tuple-element.52.crossline, bf16[64,64]{1,0:T(8,128)(2,1)S(1)} %copy-done.12, bf16[64,64]{1,0:T(8,128)(2,1)S(1)} %copy-done.11), custom_call_target="tpu_custom_call" | custom-call | flops 4096000 | bytes 1638400 | tf_op jit(solution)/shard_map/own/pallas_call | solution.py:455
  19.9 1.6 %collective-permute-done.6.rest_2_ = f32[8,640]{1,0:T(8,128)S(1)} collective-permute-done((f32[8,640]{1,0:T(8,128)S(1)}, f32[8,640]{1,0:T(8,128)S(1)}, u32[]{:S(2)}, u32[]{:S(2)}) %collective-permute-start.6) | collective-permute-done | bytes 20512 | tf_op jit(solution)/shard_map/ppermute | solution.py:453
  21.6 0.0 collective-permute-done.7.rest_3_
  21.6 0.0 collective-permute-done.4.rest_0_
  21.6 0.0 collective-permute-done.5.rest_1_
  21.6 0.8 %finish.1 = (f32[8,4,640]{2,1,0:T(4,128)}, f32[4,4,640]{2,1,0:T(4,128)}, f32[2,4,640]{2,1,0:T(4,128)}, f32[2,4,640]{2,1,0:T(4,128)}) custom-call(f32[64,640]{1,0:T(8,128)S(1)} %get-tuple-element.55.mine, f32[24,640]{1,0:T(8,128)S(1)} %collective-permute-done.4.rest_0_, f32[24,640]{1,0:T(8,128)S(1)} %collective-permute-done.5.rest_1_, ...), custom_call_target="tpu_custom_call" | custom-call | flops 819200 | bytes 1638400 | tf_op jit(solution)/shard_map/finish/pallas_call | solution.py:458
  (4 shorter events, 0.0 us)
Async XLA Ops:
  0.6 4.5 %copy-start.4 = (bf16[16,4,640]{2,1,0:T(4,128)(2,1)S(1)}, bf16[16,4,640]{2,1,0:T(4,128)(2,1)}, u32[]{:S(2)}) copy-start(bf16[16,4,640]{2,1,0:T(4,128)(2,1)} %courant.1) | copy-start | bytes 245764
  0.6 4.5 %copy-start.5 = (bf16[16,4,640]{2,1,0:T(4,128)(2,1)S(1)}, bf16[16,4,640]{2,1,0:T(4,128)(2,1)}, u32[]{:S(2)}) copy-start(bf16[16,4,640]{2,1,0:T(4,128)(2,1)} %epsilon.1) | copy-start | bytes 245764
  0.7 4.5 %copy-start.6 = (bf16[16,4,640]{2,1,0:T(4,128)(2,1)S(1)}, bf16[16,4,640]{2,1,0:T(4,128)(2,1)}, u32[]{:S(2)}) copy-start(bf16[16,4,640]{2,1,0:T(4,128)(2,1)} %delta.1) | copy-start | bytes 245764
  0.7 4.5 %copy-start.7 = (bf16[16,4,640]{2,1,0:T(4,128)(2,1)S(1)}, bf16[16,4,640]{2,1,0:T(4,128)(2,1)}, u32[]{:S(2)}) copy-start(bf16[16,4,640]{2,1,0:T(4,128)(2,1)} %tilt.1) | copy-start | bytes 245764
  0.7 4.5 %copy-start.8 = (bf16[16,4,640]{2,1,0:T(4,128)(2,1)S(1)}, bf16[16,4,640]{2,1,0:T(4,128)(2,1)}, u32[]{:S(2)}) copy-start(bf16[16,4,640]{2,1,0:T(4,128)(2,1)} %azimuth.1) | copy-start | bytes 245764
  1.8 4.3 %collective-permute-start.2 = (f32[16,8,640]{2,1,0:T(8,128)S(1)}, f32[16,8,640]{2,1,0:T(8,128)S(1)}, u32[]{:S(2)}, u32[]{:S(2)}) collective-permute-start(f32[16,8,640]{2,1,0:T(8,128)S(1)} %pad_maximum_fusion.waves), channel_id=1, source_target_pairs={{0,1},{1,0},{2,3},{3,2},{4,5},{5,4},{6,7},{7,6},{8,9},{9,8},{10,11... | collective-permute-start | bytes 983048 | tf_op jit(solution)/shard_map/ppermute | solution.py:399
  2.3 2.8 %copy-start.2 = (f32[16,4,640]{2,1,0:T(4,128)S(1)}, f32[16,4,640]{2,1,0:T(4,128)}, u32[]{:S(2)}) copy-start(f32[16,4,640]{2,1,0:T(4,128)} %prior_p.1) | copy-start | bytes 491524
  2.3 2.8 %copy-start.3 = (f32[16,4,640]{2,1,0:T(4,128)S(1)}, f32[16,4,640]{2,1,0:T(4,128)}, u32[]{:S(2)}) copy-start(f32[16,4,640]{2,1,0:T(4,128)} %prior_q.1) | copy-start | bytes 491524
  2.4 6.7 %collective-permute-start.1 = (f32[4,8,640]{2,1,0:T(8,128)S(1)}, f32[4,8,640]{2,1,0:T(8,128)S(1)}, u32[]{:S(2)}, u32[]{:S(2)}) collective-permute-start(f32[4,8,640]{2,1,0:T(8,128)S(1)} %get-tuple-element.64), channel_id=1, source_target_pairs={{0,2},{2,0},{4,6},{6,4},{8,10},{10,8},{12,14},{14,12},{1,3},{3,1},... | collective-permute-start | bytes 245768 | tf_op jit(solution)/shard_map/ppermute | solution.py:400
  5.0 4.1 %collective-permute-start = (f32[4,8,640]{2,1,0:T(8,128)S(1)}, f32[4,8,640]{2,1,0:T(8,128)S(1)}, u32[]{:S(2)}, u32[]{:S(2)}) collective-permute-start(f32[4,8,640]{2,1,0:T(8,128)S(1)} %get-tuple-element.65), channel_id=1, source_target_pairs={{0,1},{1,0},{2,4},{3,5},{4,2},{5,3},{6,8},{7,9},{8,6},{9,7},{10,12... | collective-permute-start | bytes 245768 | tf_op jit(solution)/shard_map/ppermute | solution.py:401
  9.1 1.5 %copy-start = (bf16[640,640]{1,0:T(8,128)(2,1)S(1)}, bf16[640,640]{1,0:T(8,128)(2,1)}, u32[]{:S(2)}) copy-start(bf16[640,640]{1,0:T(8,128)(2,1)} %constant.37.clone.across_low) | copy-start | bytes 2457604
  9.1 1.5 %copy-start.1 = (bf16[640,640]{1,0:T(8,128)(2,1)S(1)}, bf16[640,640]{1,0:T(8,128)(2,1)}, u32[]{:S(2)}) copy-start(bf16[640,640]{1,0:T(8,128)(2,1)} %constant.36.clone.across_high) | copy-start | bytes 2457604
  9.1 1.5 %collective-permute-start.3 = (f32[8,8,640]{2,1,0:T(8,128)S(1)}, f32[8,8,640]{2,1,0:T(8,128)S(1)}, u32[]{:S(2)}, u32[]{:S(2)}) collective-permute-start(f32[8,8,640]{2,1,0:T(8,128)S(1)} %constant_dynamic-update-slice_fusion.edges), channel_id=1, source_target_pairs={{0,1},{1,0},{2,3},{3,2},{4,5},{5,4},{6,7},{7,6},{8,9},{9,8},{10,11... | collective-permute-start | bytes 491528 | tf_op jit(solution)/shard_map/ppermute | solution.py:413
  9.2 1.4 %copy-start.9 = (bf16[64,64]{1,0:T(8,128)(2,1)S(1)}, bf16[64,64]{1,0:T(8,128)(2,1)}, u32[]{:S(2)}) copy-start(bf16[64,64]{1,0:T(8,128)(2,1)} %constant.33.clone.inline_low) | copy-start | bytes 24580
  9.2 1.4 %copy-start.10 = (bf16[64,64]{1,0:T(8,128)(2,1)S(1)}, bf16[64,64]{1,0:T(8,128)(2,1)}, u32[]{:S(2)}) copy-start(bf16[64,64]{1,0:T(8,128)(2,1)} %constant.32.clone.inline_high) | copy-start | bytes 24580
  10.6 8.5 %copy-start.11 = (bf16[64,64]{1,0:T(8,128)(2,1)S(1)}, bf16[64,64]{1,0:T(8,128)(2,1)}, u32[]{:S(2)}) copy-start(bf16[64,64]{1,0:T(8,128)(2,1)} %constant.35.clone.own_low) | copy-start | bytes 24580
  10.6 8.5 %copy-start.12 = (bf16[64,64]{1,0:T(8,128)(2,1)S(1)}, bf16[64,64]{1,0:T(8,128)(2,1)}, u32[]{:S(2)}) copy-start(bf16[64,64]{1,0:T(8,128)(2,1)} %constant.34.clone.own_high) | copy-start | bytes 24580
  11.5 10.0 %collective-permute-start.4 = (f32[24,640]{1,0:T(8,128)S(1)}, f32[24,640]{1,0:T(8,128)S(1)}, u32[]{:S(2)}, u32[]{:S(2)}) collective-permute-start(f32[24,640]{1,0:T(8,128)S(1)} %get-tuple-element.56), channel_id=1, source_target_pairs={{0,14},{2,4},{4,2},{6,8},{8,6},{10,12},{12,10},{14,0},{1,15},{3,5}... | collective-permute-start | bytes 184328 | tf_op jit(solution)/shard_map/ppermute | solution.py:453
  15.4 6.2 %collective-permute-start.5 = (f32[24,640]{1,0:T(8,128)S(1)}, f32[24,640]{1,0:T(8,128)S(1)}, u32[]{:S(2)}, u32[]{:S(2)}) collective-permute-start(f32[24,640]{1,0:T(8,128)S(1)} %get-tuple-element.57), channel_id=1, source_target_pairs={{0,2},{2,0},{4,6},{6,4},{8,10},{10,8},{12,14},{14,12},{1,3},{3,1},... | collective-permute-start | bytes 184328 | tf_op jit(solution)/shard_map/ppermute | solution.py:453
  16.0 5.6 %collective-permute-start.6 = (f32[8,640]{1,0:T(8,128)S(1)}, f32[8,640]{1,0:T(8,128)S(1)}, u32[]{:S(2)}, u32[]{:S(2)}) collective-permute-start(f32[8,640]{1,0:T(8,128)S(1)} %get-tuple-element.58), channel_id=1, source_target_pairs={{0,12},{2,14},{4,8},{6,10},{8,4},{10,6},{12,0},{14,2},{1,13},{3,15... | collective-permute-start | bytes 61448 | tf_op jit(solution)/shard_map/ppermute | solution.py:453
  17.6 4.0 %collective-permute-start.7 = (f32[8,640]{1,0:T(8,128)S(1)}, f32[8,640]{1,0:T(8,128)S(1)}, u32[]{:S(2)}, u32[]{:S(2)}) collective-permute-start(f32[8,640]{1,0:T(8,128)S(1)} %get-tuple-element.59), channel_id=1, source_target_pairs={{0,4},{2,6},{4,0},{6,2},{8,12},{10,14},{12,8},{14,10},{1,5},{3,7},... | collective-permute-start | bytes 61448 | tf_op jit(solution)/shard_map/ppermute | solution.py:453

commit v9 on v8

--- a/solution.py
+++ b/solution.py
@@ -408,7 +408,7 @@
     h_own, sum_own = kernel(interior_kernel, [stack] * 2, 100, "interior", [work] * 5)(
         waves, other, axis_x, axis_y, axis_z, taps_first, taps_second
     )
-    outer, inner, h_own, sum_own = lax.optimization_barrier((outer, inner, h_own, sum_own))
+    h_own, sum_own, inner, outer = lax.optimization_barrier((h_own, sum_own, inner, outer))
     edges = jnp.concatenate([outer, inner], axis=0)
     edges_other = lax.ppermute(edges, "gz", cores)
     edge = jax.ShapeDtypeStruct((8, 8, width), f32)

time: 22.5 us -> 22.5 us (level)
  no operation moved by 1% of the time
where the time goes in v9:
time: 22.5 us; the launch traced here: 22.4 us
  starting transfers between devices  11 us (49%)
  Pallas kernels  5.16 us (23%)
  waiting for transfers between devices  4.22 us (19%)
  other arithmetic  1.15 us (5%)
  between operations  0.83 us (4%)
    ppermute x4, starting transfers between devices, body(): lax.ppermute(send, 'xy', pair)  7.59 us
    ppermute x1, starting transfers between devices, body(): inner = lax.ppermute(jnp.where(even, last, leading), 'xy', pairs[1])  2.6 us
    ppermute x4, waiting for transfers between devices, body(): lax.ppermute(send, 'xy', pair)  1.63 us
    ppermute x1, waiting for transfers between devices, body(): inner = lax.ppermute(jnp.where(even, last, leading), 'xy', pairs[1])  1.49 us
    pallas_call x1, Pallas kernels, body(): kernel(interior_kernel, [stack] * 2, 100, 'interior', [work] * 5)  1.4 us
    concatenate x1, other arithmetic, body(): waves = lax.optimization_barrier(jnp.concatenate([wave_p, wave_q], axis=1))  1.13 us
    ppermute x1, waiting for transfers between devices, body(): edges_other = lax.ppermute(edges, 'gz', cores)  1.09 us
    pallas_call x1, Pallas kernels, body(): kernel(weights_kernel, [stack] * 6 + [taps] * 2, 100, 'weights')  0.95 us
  transfers between devices with their start and end apart: 8, of which 3 were waited for; matrix products, arithmetic and copies ran while one was open for 0% of the time, Pallas kernels for 15%

profile of v9, /device:TPU:0, one launch (start us, length us, event | category | flops | bytes accessed | tf_op | source)
XLA Modules:
  0.0 22.4 jit_solution(3826497646213126885)
XLA Ops:
  0.6 0.0 copy-start.4
  0.6 0.0 copy-start.5
  0.7 0.0 copy-start.6
  0.7 0.0 copy-start.7
  0.7 0.0 copy-start.8
  0.7 1.1 %pad_maximum_fusion.waves = f32[16,8,640]{2,1,0:T(8,128)S(1)} fusion(f32[16,4,640]{2,1,0:T(4,128)} %param.16, f32[16,4,640]{2,1,0:T(4,128)} %param.15), kind=kLoop, calls=%fused_computation | loop fusion | flops 81920 | bytes 655360 | tf_op jit(solution)/shard_map/concatenate | solution.py:392
  1.8 0.5 %collective-permute-start = (f32[16,8,640]{2,1,0:T(8,128)S(1)}, f32[16,8,640]{2,1,0:T(8,128)S(1)}, u32[]{:S(2)}, u32[]{:S(2)}) collective-permute-start(f32[16,8,640]{2,1,0:T(8,128)S(1)} %pad_maximum_fusion.waves), channel_id=1, source_target_pairs={{0,1},{1,0},{2,3},{3,2},{4,5},{5,4},{6,7},{7,6},{8,9},{9,8},{10,11... | collective-permute-start | bytes 983048 | tf_op jit(solution)/shard_map/ppermute | solution.py:399
  2.3 0.0 copy-start.2
  2.4 2.6 %collective-permute-start.1 = (f32[4,8,640]{2,1,0:T(8,128)S(1)}, f32[4,8,640]{2,1,0:T(8,128)S(1)}, u32[]{:S(2)}, u32[]{:S(2)}) collective-permute-start(f32[4,8,640]{2,1,0:T(8,128)S(1)} %get-tuple-element.65), channel_id=1, source_target_pairs={{0,2},{2,0},{4,6},{6,4},{8,10},{10,8},{12,14},{14,12},{1,3},{3,1},... | collective-permute-start | bytes 245768 | tf_op jit(solution)/shard_map/ppermute | solution.py:400
  5.0 0.2 collective-permute-start.2
  5.1 0.0 copy-done.4
  5.1 0.0 copy-done.5
  5.1 0.0 copy-done.6
  5.2 0.0 copy-done.7
  5.2 0.0 copy-done.8
  5.2 0.0 copy-done.2
  5.2 0.0 copy-done.3
  5.2 1.0 %weights.1 = (f32[16,8,640]{2,1,0:T(8,128)S(1)}, f32[16,8,640]{2,1,0:T(8,128)S(1)}, f32[16,8,640]{2,1,0:T(8,128)S(1)}, f32[16,8,640]{2,1,0:T(8,128)S(1)}, f32[16...) custom-call(f32[16,8,640]{2,1,0:T(8,128)S(1)} %pad_maximum_fusion.wa, ...), custom_call_target="tpu_custom_call" | custom-call | flops 4096000 | bytes 1638400 | tf_op jit(solution)/shard_map/weights/pallas_call | solution.py:404
  6.1 0.0 collective-permute-done.other
  6.2 1.4 %interior.1 = (f32[16,8,640]{2,1,0:T(8,128)S(1)}, f32[16,8,640]{2,1,0:T(8,128)S(1)}) custom-call(f32[16,8,640]{2,1,0:T(8,128)S(1)} %pad_maximum_fusion.waves, f32[16,8,640]{2,1,0:T(8,128)S(1)} %collective-permute-done.other, f32[16,8,640]{2,1,0:T(8,128)S(1)} %get-tuple-element.35.axis_x, f32[16,8,640]{2,1,0:T(8,128)S(1)} %get-tuple-element.36.axis_y, ...), custom_call_target="tpu_custom_call" | custom-call | flops 4096000 | bytes 1638400 | tf_op jit(solution)/shard_map/interior/pallas_call | solution.py:408
  7.6 1.5 %collective-permute-done.1 = f32[4,8,640]{2,1,0:T(8,128)S(1)} collective-permute-done((f32[4,8,640]{2,1,0:T(8,128)S(1)}, f32[4,8,640]{2,1,0:T(8,128)S(1)}, u32[]{:S(2)}, u32[]{:S(2)}) %collective-permute-start.1) | collective-permute-done | bytes 81952 | tf_op jit(solution)/shard_map/ppermute | solution.py:400
  9.0 0.0 collective-permute-done.2
  9.1 0.0 copy-start
  9.1 0.0 copy-start.1
  9.1 0.1 collective-permute-start.3
  9.2 0.0 copy-start.9
  9.2 0.0 copy-start.10
  9.2 0.3 %halo.1 = (f32[8,8,640]{2,1,0:T(8,128)S(1)}, f32[8,8,640]{2,1,0:T(8,128)S(1)}) custom-call(f32[8,8,640]{2,1,0:T(8,128)S(1)} %constant_dynamic-update-slice_fusion.edges, f32[16,8,640]{2,1,0:T(8,128)S(1)} %get-tuple-element.35.axis_x, f32[16,8,640]{2,1,0:T(8,128)S(1)} %get-tuple-element.36.axis_y, f32[16,8,640]{2,1,0:T(8,128)S(1)} %get-tuple-element.44.h_own, ...), custom_call_target="tpu_custom_call" | custom-call | flops 4096000 | bytes 1638400 | tf_op jit(solution)/shard_map/halo/pallas_call | solution.py:415
  9.5 1.1 %collective-permute-done.3.edges_other = f32[8,8,640]{2,1,0:T(8,128)S(1)} collective-permute-done((f32[8,8,640]{2,1,0:T(8,128)S(1)}, f32[8,8,640]{2,1,0:T(8,128)S(1)}, u32[]{:S(2)}, u32[]{:S(2)}) %collective-permute-start.3) | collective-permute-done | bytes 163872 | tf_op jit(solution)/shard_map/ppermute | solution.py:413
  10.6 0.0 copy-done
  10.6 0.0 copy-done.1
  10.6 0.0 copy-done.9
  10.6 0.0 copy-done.10
  10.6 0.0 copy-start.11
  10.6 0.0 copy-start.12
  10.6 0.9 %step.1 = (f32[16,8,640]{2,1,0:T(8,128)S(1)}, f32[64,640]{1,0:T(8,128)S(1)}, f32[24,640]{1,0:T(8,128)S(1)}, f32[24,640]{1,0:T(8,128)S(1)}, f32[8,640]{1,0:T(8,128)S(1)}, /*index=5*/f32[8,640]{1,0:T(8,128)S(1)}) custom-call(f32[8,8,640]{2,1,0:T(8,128)S(1)} %constant_dynamic-update-slice_fusion.edges, f32[8,8,640]{2,1,0:T(8,128)S(1)} %collective-permute-done.3.edges_other, ...), custom_call_target="tpu_custom_call" | custom-call | flops 16384000 | bytes 1638400 | tf_op jit(solution)/shard_map/step/pallas_call | solution.py:435
  11.5 3.8 %collective-permute-start.4 = (f32[24,640]{1,0:T(8,128)S(1)}, f32[24,640]{1,0:T(8,128)S(1)}, u32[]{:S(2)}, u32[]{:S(2)}) collective-permute-start(f32[24,640]{1,0:T(8,128)S(1)} %get-tuple-element.56), channel_id=1, source_target_pairs={{0,14},{2,4},{4,2},{6,8},{8,6},{10,12},{12,10},{14,0},{1,15},{3,5}... | collective-permute-start | bytes 184328 | tf_op jit(solution)/shard_map/ppermute | solution.py:453
  15.4 0.6 %collective-permute-start.5 = (f32[24,640]{1,0:T(8,128)S(1)}, f32[24,640]{1,0:T(8,128)S(1)}, u32[]{:S(2)}, u32[]{:S(2)}) collective-permute-start(f32[24,640]{1,0:T(8,128)S(1)} %get-tuple-element.57), channel_id=1, source_target_pairs={{0,2},{2,0},{4,6},{6,4},{8,10},{10,8},{12,14},{14,12},{1,3},{3,1},... | collective-permute-start | bytes 184328 | tf_op jit(solution)/shard_map/ppermute | solution.py:453
  16.0 1.6 %collective-permute-start.6 = (f32[8,640]{1,0:T(8,128)S(1)}, f32[8,640]{1,0:T(8,128)S(1)}, u32[]{:S(2)}, u32[]{:S(2)}) collective-permute-start(f32[8,640]{1,0:T(8,128)S(1)} %get-tuple-element.58), channel_id=1, source_target_pairs={{0,12},{2,14},{4,8},{6,10},{8,4},{10,6},{12,0},{14,2},{1,13},{3,15... | collective-permute-start | bytes 61448 | tf_op jit(solution)/shard_map/ppermute | solution.py:453
  17.6 1.6 %collective-permute-start.7 = (f32[8,640]{1,0:T(8,128)S(1)}, f32[8,640]{1,0:T(8,128)S(1)}, u32[]{:S(2)}, u32[]{:S(2)}) collective-permute-start(f32[8,640]{1,0:T(8,128)S(1)} %get-tuple-element.59), channel_id=1, source_target_pairs={{0,4},{2,6},{4,0},{6,2},{8,12},{10,14},{12,8},{14,10},{1,5},{3,7},... | collective-permute-start | bytes 61448 | tf_op jit(solution)/shard_map/ppermute | solution.py:453
  19.1 0.0 copy-done.11
  19.1 0.0 copy-done.12
  19.1 0.8 %own.1 = (f32[16,4,640]{2,1,0:T(4,128)}, f32[16,4,640]{2,1,0:T(4,128)}, f32[64,640]{1,0:T(8,128)S(1)}) custom-call(f32[16,8,640]{2,1,0:T(8,128)S(1)} %get-tuple-element.51.pressure, f32[64,640]{1,0:T(8,128)S(1)} %get-tuple-element.52.crossline, bf16[64,64]{1,0:T(8,128)(2,1)S(1)} %copy-done.11, bf16[64,64]{1,0:T(8,128)(2,1)S(1)} %copy-done.12), custom_call_target="tpu_custom_call" | custom-call | flops 4096000 | bytes 1638400 | tf_op jit(solution)/shard_map/own/pallas_call | solution.py:455
  19.9 1.6 %collective-permute-done.6.rest_2_ = f32[8,640]{1,0:T(8,128)S(1)} collective-permute-done((f32[8,640]{1,0:T(8,128)S(1)}, f32[8,640]{1,0:T(8,128)S(1)}, u32[]{:S(2)}, u32[]{:S(2)}) %collective-permute-start.6) | collective-permute-done | bytes 20512 | tf_op jit(solution)/shard_map/ppermute | solution.py:453
  21.6 0.0 collective-permute-done.7.rest_3_
  21.6 0.0 collective-permute-done.4.rest_0_
  21.6 0.0 collective-permute-done.5.rest_1_
  21.6 0.8 %finish.1 = (f32[8,4,640]{2,1,0:T(4,128)}, f32[4,4,640]{2,1,0:T(4,128)}, f32[2,4,640]{2,1,0:T(4,128)}, f32[2,4,640]{2,1,0:T(4,128)}) custom-call(f32[64,640]{1,0:T(8,128)S(1)} %get-tuple-element.55.mine, f32[24,640]{1,0:T(8,128)S(1)} %collective-permute-done.4.rest_0_, f32[24,640]{1,0:T(8,128)S(1)} %collective-permute-done.5.rest_1_, ...), custom_call_target="tpu_custom_call" | custom-call | flops 819200 | bytes 1638400 | tf_op jit(solution)/shard_map/finish/pallas_call | solution.py:458
  (4 shorter events, 0.0 us)
Async XLA Ops:
  0.6 4.5 %copy-start.4 = (bf16[16,4,640]{2,1,0:T(4,128)(2,1)S(1)}, bf16[16,4,640]{2,1,0:T(4,128)(2,1)}, u32[]{:S(2)}) copy-start(bf16[16,4,640]{2,1,0:T(4,128)(2,1)} %courant.1) | copy-start | bytes 245764
  0.6 4.5 %copy-start.5 = (bf16[16,4,640]{2,1,0:T(4,128)(2,1)S(1)}, bf16[16,4,640]{2,1,0:T(4,128)(2,1)}, u32[]{:S(2)}) copy-start(bf16[16,4,640]{2,1,0:T(4,128)(2,1)} %epsilon.1) | copy-start | bytes 245764
  0.7 4.5 %copy-start.6 = (bf16[16,4,640]{2,1,0:T(4,128)(2,1)S(1)}, bf16[16,4,640]{2,1,0:T(4,128)(2,1)}, u32[]{:S(2)}) copy-start(bf16[16,4,640]{2,1,0:T(4,128)(2,1)} %delta.1) | copy-start | bytes 245764
  0.7 4.5 %copy-start.7 = (bf16[16,4,640]{2,1,0:T(4,128)(2,1)S(1)}, bf16[16,4,640]{2,1,0:T(4,128)(2,1)}, u32[]{:S(2)}) copy-start(bf16[16,4,640]{2,1,0:T(4,128)(2,1)} %tilt.1) | copy-start | bytes 245764
  0.7 4.5 %copy-start.8 = (bf16[16,4,640]{2,1,0:T(4,128)(2,1)S(1)}, bf16[16,4,640]{2,1,0:T(4,128)(2,1)}, u32[]{:S(2)}) copy-start(bf16[16,4,640]{2,1,0:T(4,128)(2,1)} %azimuth.1) | copy-start | bytes 245764
  1.8 4.3 %collective-permute-start = (f32[16,8,640]{2,1,0:T(8,128)S(1)}, f32[16,8,640]{2,1,0:T(8,128)S(1)}, u32[]{:S(2)}, u32[]{:S(2)}) collective-permute-start(f32[16,8,640]{2,1,0:T(8,128)S(1)} %pad_maximum_fusion.waves), channel_id=1, source_target_pairs={{0,1},{1,0},{2,3},{3,2},{4,5},{5,4},{6,7},{7,6},{8,9},{9,8},{10,11... | collective-permute-start | bytes 983048 | tf_op jit(solution)/shard_map/ppermute | solution.py:399
  2.3 2.8 %copy-start.2 = (f32[16,4,640]{2,1,0:T(4,128)S(1)}, f32[16,4,640]{2,1,0:T(4,128)}, u32[]{:S(2)}) copy-start(f32[16,4,640]{2,1,0:T(4,128)} %prior_p.1) | copy-start | bytes 491524
  2.3 2.8 %copy-start.3 = (f32[16,4,640]{2,1,0:T(4,128)S(1)}, f32[16,4,640]{2,1,0:T(4,128)}, u32[]{:S(2)}) copy-start(f32[16,4,640]{2,1,0:T(4,128)} %prior_q.1) | copy-start | bytes 491524
  2.4 6.7 %collective-permute-start.1 = (f32[4,8,640]{2,1,0:T(8,128)S(1)}, f32[4,8,640]{2,1,0:T(8,128)S(1)}, u32[]{:S(2)}, u32[]{:S(2)}) collective-permute-start(f32[4,8,640]{2,1,0:T(8,128)S(1)} %get-tuple-element.65), channel_id=1, source_target_pairs={{0,2},{2,0},{4,6},{6,4},{8,10},{10,8},{12,14},{14,12},{1,3},{3,1},... | collective-permute-start | bytes 245768 | tf_op jit(solution)/shard_map/ppermute | solution.py:400
  5.0 4.1 %collective-permute-start.2 = (f32[4,8,640]{2,1,0:T(8,128)S(1)}, f32[4,8,640]{2,1,0:T(8,128)S(1)}, u32[]{:S(2)}, u32[]{:S(2)}) collective-permute-start(f32[4,8,640]{2,1,0:T(8,128)S(1)} %get-tuple-element.64), channel_id=1, source_target_pairs={{0,1},{1,0},{2,4},{3,5},{4,2},{5,3},{6,8},{7,9},{8,6},{9,7},{10,12... | collective-permute-start | bytes 245768 | tf_op jit(solution)/shard_map/ppermute | solution.py:401
  9.1 1.5 %copy-start = (bf16[640,640]{1,0:T(8,128)(2,1)S(1)}, bf16[640,640]{1,0:T(8,128)(2,1)}, u32[]{:S(2)}) copy-start(bf16[640,640]{1,0:T(8,128)(2,1)} %constant.36.clone.across_high) | copy-start | bytes 2457604
  9.1 1.5 %copy-start.1 = (bf16[640,640]{1,0:T(8,128)(2,1)S(1)}, bf16[640,640]{1,0:T(8,128)(2,1)}, u32[]{:S(2)}) copy-start(bf16[640,640]{1,0:T(8,128)(2,1)} %constant.37.clone.across_low) | copy-start | bytes 2457604
  9.1 1.5 %collective-permute-start.3 = (f32[8,8,640]{2,1,0:T(8,128)S(1)}, f32[8,8,640]{2,1,0:T(8,128)S(1)}, u32[]{:S(2)}, u32[]{:S(2)}) collective-permute-start(f32[8,8,640]{2,1,0:T(8,128)S(1)} %constant_dynamic-update-slice_fusion.edges), channel_id=1, source_target_pairs={{0,1},{1,0},{2,3},{3,2},{4,5},{5,4},{6,7},{7,6},{8,9},{9,8},{10,11... | collective-permute-start | bytes 491528 | tf_op jit(solution)/shard_map/ppermute | solution.py:413
  9.2 1.4 %copy-start.9 = (bf16[64,64]{1,0:T(8,128)(2,1)S(1)}, bf16[64,64]{1,0:T(8,128)(2,1)}, u32[]{:S(2)}) copy-start(bf16[64,64]{1,0:T(8,128)(2,1)} %constant.32.clone.inline_high) | copy-start | bytes 24580
  9.2 1.4 %copy-start.10 = (bf16[64,64]{1,0:T(8,128)(2,1)S(1)}, bf16[64,64]{1,0:T(8,128)(2,1)}, u32[]{:S(2)}) copy-start(bf16[64,64]{1,0:T(8,128)(2,1)} %constant.33.clone.inline_low) | copy-start | bytes 24580
  10.6 8.5 %copy-start.11 = (bf16[64,64]{1,0:T(8,128)(2,1)S(1)}, bf16[64,64]{1,0:T(8,128)(2,1)}, u32[]{:S(2)}) copy-start(bf16[64,64]{1,0:T(8,128)(2,1)} %constant.34.clone.own_high) | copy-start | bytes 24580
  10.6 8.5 %copy-start.12 = (bf16[64,64]{1,0:T(8,128)(2,1)S(1)}, bf16[64,64]{1,0:T(8,128)(2,1)}, u32[]{:S(2)}) copy-start(bf16[64,64]{1,0:T(8,128)(2,1)} %constant.35.clone.own_low) | copy-start | bytes 24580
  11.5 10.0 %collective-permute-start.4 = (f32[24,640]{1,0:T(8,128)S(1)}, f32[24,640]{1,0:T(8,128)S(1)}, u32[]{:S(2)}, u32[]{:S(2)}) collective-permute-start(f32[24,640]{1,0:T(8,128)S(1)} %get-tuple-element.56), channel_id=1, source_target_pairs={{0,14},{2,4},{4,2},{6,8},{8,6},{10,12},{12,10},{14,0},{1,15},{3,5}... | collective-permute-start | bytes 184328 | tf_op jit(solution)/shard_map/ppermute | solution.py:453
  15.4 6.2 %collective-permute-start.5 = (f32[24,640]{1,0:T(8,128)S(1)}, f32[24,640]{1,0:T(8,128)S(1)}, u32[]{:S(2)}, u32[]{:S(2)}) collective-permute-start(f32[24,640]{1,0:T(8,128)S(1)} %get-tuple-element.57), channel_id=1, source_target_pairs={{0,2},{2,0},{4,6},{6,4},{8,10},{10,8},{12,14},{14,12},{1,3},{3,1},... | collective-permute-start | bytes 184328 | tf_op jit(solution)/shard_map/ppermute | solution.py:453
  16.0 5.6 %collective-permute-start.6 = (f32[8,640]{1,0:T(8,128)S(1)}, f32[8,640]{1,0:T(8,128)S(1)}, u32[]{:S(2)}, u32[]{:S(2)}) collective-permute-start(f32[8,640]{1,0:T(8,128)S(1)} %get-tuple-element.58), channel_id=1, source_target_pairs={{0,12},{2,14},{4,8},{6,10},{8,4},{10,6},{12,0},{14,2},{1,13},{3,15... | collective-permute-start | bytes 61448 | tf_op jit(solution)/shard_map/ppermute | solution.py:453
  17.6 4.0 %collective-permute-start.7 = (f32[8,640]{1,0:T(8,128)S(1)}, f32[8,640]{1,0:T(8,128)S(1)}, u32[]{:S(2)}, u32[]{:S(2)}) collective-permute-start(f32[8,640]{1,0:T(8,128)S(1)} %get-tuple-element.59), channel_id=1, source_target_pairs={{0,4},{2,6},{4,0},{6,2},{8,12},{10,14},{12,8},{14,10},{1,5},{3,7},... | collective-permute-start | bytes 61448 | tf_op jit(solution)/shard_map/ppermute | solution.py:453

commit v10 on v9

--- a/solution.py
+++ b/solution.py
@@ -194,8 +194,63 @@
     return parts[:rows] + parts[rows:]
 
 
-def interior_kernel(
-    waves, other, axis_x, axis_y, axis_z, taps_first, taps_second, h_own, sum_own, dz, dzz, dy, dyy, dzy
+def interior_kernel(waves, axis_x, axis_y, taps_first, taps_second, h_part, sum_part, dy, dyy):
+    rows, sub, width = waves.shape
+    flat = rows * sub
+    field = jnp.concatenate(halves(waves[...].reshape(flat, width)), axis=0)
+    dyy[...] = joined(across(field, taps_second), flat).reshape(waves.shape)
+    dy[...] = joined(across(field, taps_first), flat).reshape(waves.shape)
+    for x in range(rows):
+        dxx = SECOND[0] * waves[x]
+        cross = dxx + (1.0 / SCALE_SECOND) * dyy[x]
+        dxy = jnp.zeros_like(dxx)
+        for k in range(1, 5):
+            for step in (k, -k):
+                if 0 <= x + step < rows:
+                    weight = FIRST[k - 1] if step > 0 else -FIRST[k - 1]
+                    dxx = dxx + SECOND[k] * waves[x + step]
+                    dxy = dxy + (weight / SCALE_FIRST) * dy[x + step]
+        n_x, n_y = axis_x[x], axis_y[x]
+        h_part[x] = n_x * (n_x * dxx + 2.0 * (n_y * dxy)) + n_y * (n_y * cross)
+        sum_part[x] = dxx + cross
+
+
+def halo_rows(size, edges):
+    place = lax.axis_index("xy")
+    even = place % 2 == 0
+    left_at, right_at = jnp.where(even, 0, 4), jnp.where(even, 4, 0)
+    left_in = jnp.where(place > 0, 1.0, 0.0)
+    right_in = jnp.where(place < size - 1, 1.0, 0.0)
+    before = [edges[left_at + x] * left_in for x in range(4)]
+    return before + [edges[right_at + x] * right_in for x in range(4)]
+
+
+def reach(values, row, coefficients, sign):
+    total = None
+    for k in range(1, 5):
+        at = row + 4 - k if row < 4 else row + k - 4
+        if (row < 4 and 0 <= at < 4) or (row >= 4 and 4 <= at < 8):
+            term = (coefficients[k - 1] * (sign if row < 4 else 1.0)) * values[at]
+            total = term if total is None else total + term
+    return total
+
+
+def depth_kernel(
+    size,
+    waves,
+    other,
+    edges,
+    axis_x,
+    axis_y,
+    axis_z,
+    h_part,
+    sum_part,
+    taps_first,
+    h_own,
+    sum_own,
+    dz,
+    dzz,
+    dzy,
 ):
     rows, sub, width = waves.shape
     flat = rows * sub
@@ -205,64 +260,31 @@
         ahead, behind = depth_neighbours(own, other[x], lower)
         dz[x] = first_of(ahead, behind)
         dzz[x] = second_of(own, ahead, behind)
-    field = jnp.concatenate(halves(waves[...].reshape(flat, width)), axis=0)
     slope = jnp.concatenate(halves(dz[...].reshape(flat, width)), axis=0)
-    dyy[...] = joined(across(field, taps_second), flat).reshape(waves.shape)
-    dy[...] = joined(across(field, taps_first), flat).reshape(waves.shape)
     dzy[...] = joined(across(slope, taps_first), flat).reshape(waves.shape)
+    values = halo_rows(size, edges)
+    parts = jnp.concatenate(halves(jnp.concatenate(values, axis=0)), axis=0)
+    slopes = joined(across(parts, taps_first), 8 * sub)
+    slopes = [slopes[sub * x : sub * x + sub] for x in range(8)]
     for x in range(rows):
-        centre = waves[x]
-        dxx = SECOND[0] * centre
-        dxy = jnp.zeros_like(centre)
-        dxz = jnp.zeros_like(centre)
+        n_x, n_y, n_z = axis_x[x], axis_y[x], axis_z[x]
+        dxz = jnp.zeros_like(n_x)
         for k in range(1, 5):
             for step in (k, -k):
                 if 0 <= x + step < rows:
                     weight = FIRST[k - 1] if step > 0 else -FIRST[k - 1]
-                    dxx = dxx + SECOND[k] * waves[x + step]
-                    dxy = dxy + (weight / SCALE_FIRST) * dy[x + step]
                     dxz = dxz + weight * dz[x + step]
-        cross = SECOND[0] * centre + (1.0 / SCALE_SECOND) * dyy[x]
-        n_x, n_y, n_z = axis_x[x], axis_y[x], axis_z[x]
-        h_one = n_x * (n_x * dxx + 2.0 * (n_y * dxy + n_z * dxz))
-        h_one = h_one + n_y * (n_y * cross + (2.0 / SCALE_FIRST) * (n_z * dzy[x]))
-        h_own[x] = h_one + n_z * (n_z * dzz[x])
-        sum_own[x] = dxx + cross + dzz[x]
-
-
-def halo_rows(size, edges):
-    place = lax.axis_index("xy")
-    even = place % 2 == 0
-    left_at, right_at = jnp.where(even, 0, 4), jnp.where(even, 4, 0)
-    left_in = jnp.where(place > 0, 1.0, 0.0)
-    right_in = jnp.where(place < size - 1, 1.0, 0.0)
-    before = [edges[left_at + x] * left_in for x in range(4)]
-    return before + [edges[right_at + x] * right_in for x in range(4)]
-
-
-def reach(values, row, coefficients, sign):
-    total = None
-    for k in range(1, 5):
-        at = row + 4 - k if row < 4 else row + k - 4
-        if (row < 4 and 0 <= at < 4) or (row >= 4 and 4 <= at < 8):
-            term = (coefficients[k - 1] * (sign if row < 4 else 1.0)) * values[at]
-            total = term if total is None else total + term
-    return total
-
-
-def halo_kernel(size, edges, axis_x, axis_y, h_own, sum_own, taps_first, h_edge, sum_edge):
-    rows, sub, width = h_own.shape
-    values = halo_rows(size, edges)
-    parts = jnp.concatenate(halves(jnp.concatenate(values, axis=0)), axis=0)
-    slopes = joined(across(parts, taps_first), 8 * sub)
-    slopes = [slopes[sub * x : sub * x + sub] for x in range(8)]
-    for row in range(8):
-        x = row if row < 4 else rows - 8 + row
-        dxx = reach(values, row, SECOND[1:], 1.0)
-        dxy = reach(slopes, row, [c / SCALE_FIRST for c in FIRST], -1.0)
-        n_x = axis_x[x]
-        h_edge[row] = h_own[x] + n_x * (n_x * dxx + 2.0 * (axis_y[x] * dxy))
-        sum_edge[row] = sum_own[x] + dxx
+        mixed = n_x * dxz + (1.0 / SCALE_FIRST) * (n_y * dzy[x])
+        h_one = h_part[x] + n_z * (n_z * dzz[x] + 2.0 * mixed)
+        total = sum_part[x] + dzz[x]
+        if x < 4 or x >= rows - 4:
+            row = x if x < 4 else x - rows + 8
+            dxx = reach(values, row, SECOND[1:], 1.0)
+            dxy = reach(slopes, row, [c / SCALE_FIRST for c in FIRST], -1.0)
+            h_one = h_one + n_x * (n_x * dxx + 2.0 * (n_y * dxy))
+            total = total + dxx
+        h_own[x] = h_one
+        sum_own[x] = total
 
 
 def step_kernel(
@@ -272,8 +294,6 @@
     edges_other,
     h_own,
     sum_own,
-    h_edge,
-    sum_edge,
     axis_x,
     axis_z,
     gain_a,
@@ -298,13 +318,11 @@
         for own, far in zip(halo_rows(size, edges), halo_rows(size, edges_other))
     ]
     for x in range(rows):
-        row = x if x < 4 else x - rows + 8
-        if 4 <= x < rows - 4:
-            h_one, total = h_own[x], sum_own[x]
-        else:
-            dxz = reach(slopes, row, FIRST, -1.0)
-            h_one, total = h_edge[row] + 2.0 * (axis_x[x] * axis_z[x] * dxz), sum_edge[row]
-        mixed = jnp.where(top, total - h_one, h_one)
+        h_one = h_own[x]
+        if x < 4 or x >= rows - 4:
+            dxz = reach(slopes, x if x < 4 else x - rows + 8, FIRST, -1.0)
+            h_one = h_one + 2.0 * (axis_x[x] * axis_z[x] * dxz)
+        mixed = jnp.where(top, sum_own[x] - h_one, h_one)
         pressure[x] = base[x] + gain_a[x] * mixed + gain_b[x] * pltpu.roll(mixed, 4, 0)
 
     packed = jnp.concatenate(
@@ -396,24 +414,25 @@
         for i, j in pairs[0]
         for g in range(2)
     ]
-    other = lax.ppermute(waves, "gz", cores)
-    inner = lax.ppermute(jnp.where(even, last, leading), "xy", pairs[1])
-    outer = lax.ppermute(jnp.where(even, leading, last), ("xy", "gz"), open_outer)
+    to_inner, to_outer = jnp.where(even, last, leading), jnp.where(even, leading, last)
+    to_inner, to_outer, fields = lax.optimization_barrier((to_inner, to_outer, waves))
+    outer = lax.ppermute(to_outer, ("xy", "gz"), open_outer)
+    inner = lax.ppermute(to_inner, "xy", pairs[1])
+    other = lax.ppermute(fields, "gz", cores)
 
     taps = jax.ShapeDtypeStruct((4 * LANES, 2 * LANES), jnp.bfloat16)
     axis_x, axis_y, axis_z, *gains, taps_first, taps_second = kernel(
         weights_kernel, [stack] * 6 + [taps] * 2, 100, "weights"
     )(waves, prior_p, prior_q, courant, epsilon, thomsen_delta, tilt_angle, azimuth)
     work = pltpu.VMEM((rows, 8, width), f32)
-    h_own, sum_own = kernel(interior_kernel, [stack] * 2, 100, "interior", [work] * 5)(
-        waves, other, axis_x, axis_y, axis_z, taps_first, taps_second
-    )
-    h_own, sum_own, inner, outer = lax.optimization_barrier((h_own, sum_own, inner, outer))
-    edges = jnp.concatenate([outer, inner], axis=0)
+    h_part, sum_part = kernel(interior_kernel, [stack] * 2, 100, "interior", [work] * 2)(
+        waves, axis_x, axis_y, taps_first, taps_second
+    )
+    h_part, outer, inner = lax.optimization_barrier((h_part, outer, inner))
+    edges, other = lax.optimization_barrier((jnp.concatenate([outer, inner], axis=0), other))
     edges_other = lax.ppermute(edges, "gz", cores)
-    edge = jax.ShapeDtypeStruct((8, 8, width), f32)
-    h_edge, sum_edge = kernel(functools.partial(halo_kernel, size), [edge] * 2, 100, "halo")(
-        edges, axis_x, axis_y, h_own, sum_own, taps_first
+    h_own, sum_own = kernel(functools.partial(depth_kernel, size), [stack] * 2, 100, "depth", [work] * 3)(
+        waves, other, edges, axis_x, axis_y, axis_z, h_part, sum_part, taps_first
     )
 
     own, factors = inline_blocks(rows)
@@ -442,8 +461,6 @@
         edges_other,
         h_own,
         sum_own,
-        h_edge,
-        sum_edge,
         axis_x,
         axis_z,
         *gains,

time: 22.5 us -> 23.3 us (1.036)
  starting transfers between devices: 11 us -> 12 us
  waiting for transfers between devices: 4.22 us -> 3.95 us
    ppermute x3, starting transfers between devices: 3.3 us -> 4.63 us  [the longest x1 4.03 us: body(): inner = lax.ppermute(to_inner, 'xy', pairs[1])]
    ppermute x1, waiting for transfers between devices: 1.09 us -> 0.36 us  [body(): edges_other = lax.ppermute(edges, 'gz', cores)]
    ppermute x4, starting transfers between devices: 7.59 us -> 7.25 us  [body(): lax.ppermute(send, 'xy', pair)]
    ppermute x3, waiting for transfers between devices: 1.49 us -> 1.76 us  [the longest x1 1.75 us: body(): inner = lax.ppermute(to_inner, 'xy', pairs[1])]
  transfers between devices with their start and end apart: 8 -> 8, of which waited for: 3 -> 4; matrix products, arithmetic and copies ran while one was open for 0% -> 0% of each run, Pallas kernels for 15% -> 15%
where the time goes in v10:
time: 23.3 us; the launch traced here: 23.1 us
  starting transfers between devices  12 us (52%)
  Pallas kernels  5.11 us (22%)
  waiting for transfers between devices  3.95 us (17%)
  other arithmetic  1.16 us (5%)
  between operations  0.83 us (4%)
    ppermute x4, starting transfers between devices, body(): lax.ppermute(send, 'xy', pair)  7.25 us
    ppermute x1, starting transfers between devices, body(): inner = lax.ppermute(to_inner, 'xy', pairs[1])  4.03 us
    ppermute x4, waiting for transfers between devices, body(): lax.ppermute(send, 'xy', pair)  1.83 us
    ppermute x1, waiting for transfers between devices, body(): inner = lax.ppermute(to_inner, 'xy', pairs[1])  1.75 us
    concatenate x1, other arithmetic, body(): waves = lax.optimization_barrier(jnp.concatenate([wave_p, wave_q], axis=1))  1.13 us
    pallas_call x1, Pallas kernels, body(): kernel(functools.partial(depth_kernel, size), [stack] * 2, 100, 'depth',...  0.96 us
    pallas_call x1, Pallas kernels, body(): kernel(weights_kernel, [stack] * 6 + [taps] * 2, 100, 'weights')  0.95 us
    pallas_call x1, Pallas kernels, body(): kernel(functools.partial(step_kernel, size, gives), [stack, flat] + [jax....  0.9 us
  transfers between devices with their start and end apart: 8, of which 4 were waited for; matrix products, arithmetic and copies ran while one was open for 0% of the time, Pallas kernels for 15%

profile of v10, /device:TPU:0, one launch (start us, length us, event | category | flops | bytes accessed | tf_op | source)
XLA Modules:
  0.0 23.1 jit_solution(14283281053896405899)
XLA Ops:
  0.6 0.0 copy-start.4
  0.7 0.0 copy-start.5
  0.7 0.0 copy-start.6
  0.7 0.0 copy-start.7
  0.7 0.0 copy-start.8
  0.7 1.1 %pad_maximum_fusion.waves = f32[16,8,640]{2,1,0:T(8,128)S(1)} fusion(f32[16,4,640]{2,1,0:T(4,128)} %param.16, f32[16,4,640]{2,1,0:T(4,128)} %param.15), kind=kLoop, calls=%fused_computation | loop fusion | flops 81920 | bytes 655360 | tf_op jit(solution)/shard_map/concatenate | solution.py:410
  1.8 0.0 copy-start.2
  1.8 0.0 copy-start.3
  1.9 0.5 %collective-permute-start.2 = (f32[16,8,640]{2,1,0:T(8,128)S(1)}, f32[16,8,640]{2,1,0:T(8,128)S(1)}, u32[]{:S(2)}, u32[]{:S(2)}) collective-permute-start(f32[16,8,640]{2,1,0:T(8,128)S(1)} %pad_maximum_fusion.waves), channel_id=1, source_target_pairs={{0,1},{1,0},{2,3},{3,2},{4,5},{5,4},{6,7},{7,6},{8,9},{9,8},{10,11... | collective-permute-start | bytes 983048 | tf_op jit(solution)/shard_map/ppermute | solution.py:421
  2.4 0.1 collective-permute-start
  2.5 4.0 %collective-permute-start.1 = (f32[4,8,640]{2,1,0:T(8,128)S(1)}, f32[4,8,640]{2,1,0:T(8,128)S(1)}, u32[]{:S(2)}, u32[]{:S(2)}) collective-permute-start(f32[4,8,640]{2,1,0:T(8,128)S(1)} %get-tuple-element.45), channel_id=1, source_target_pairs={{0,2},{2,0},{4,6},{6,4},{8,10},{10,8},{12,14},{14,12},{1,3},{3,1},... | collective-permute-start | bytes 245768 | tf_op jit(solution)/shard_map/ppermute | solution.py:420
  6.5 0.0 copy-done.4
  6.5 0.0 copy-done.5
  6.5 0.0 copy-done.6
  6.5 0.0 copy-done.7
  6.5 0.0 copy-done.8
  6.5 0.0 copy-done.2
  6.5 0.0 copy-done.3
  6.6 1.0 %weights.1 = (f32[16,8,640]{2,1,0:T(8,128)S(1)}, f32[16,8,640]{2,1,0:T(8,128)S(1)}, f32[16,8,640]{2,1,0:T(8,128)S(1)}, f32[16,8,640]{2,1,0:T(8,128)S(1)}, f32[16...) custom-call(f32[16,8,640]{2,1,0:T(8,128)S(1)} %pad_maximum_fusion.wa, ...), custom_call_target="tpu_custom_call" | custom-call | flops 4096000 | bytes 1638400 | tf_op jit(solution)/shard_map/weights/pallas_call | solution.py:424
  7.5 0.7 %interior.1 = (f32[16,8,640]{2,1,0:T(8,128)S(1)}, f32[16,8,640]{2,1,0:T(8,128)S(1)}) custom-call(f32[16,8,640]{2,1,0:T(8,128)S(1)} %pad_maximum_fusion.waves, f32[16,8,640]{2,1,0:T(8,128)S(1)} %get-tuple-element.39.axis_x, f32[16,8,640]{2,1,0:T(8,128)S(1)} %get-tuple-element.40.axis_y, bf16[512,256]{1,0:T(8,128)(2,1)S(1)} %get-tuple-element.41.taps_first, ...), custom_call_target="tpu_custom_call" | custom-call | flops 4096000 | bytes 1638400 | tf_op jit(solution)/shard_map/interior/pallas_call | solution.py:428
  8.2 0.0 collective-permute-done
  8.2 1.8 %collective-permute-done.1 = f32[4,8,640]{2,1,0:T(8,128)S(1)} collective-permute-done((f32[4,8,640]{2,1,0:T(8,128)S(1)}, f32[4,8,640]{2,1,0:T(8,128)S(1)}, u32[]{:S(2)}, u32[]{:S(2)}) %collective-permute-start.1) | collective-permute-done | bytes 81952 | tf_op jit(solution)/shard_map/ppermute | solution.py:420
  10.0 0.0 collective-permute-done.2.other
  10.0 0.1 collective-permute-start.3
  10.1 0.0 copy-start
  10.1 0.0 copy-start.1
  10.1 0.0 copy-start.9
  10.1 0.0 copy-start.10
  10.1 1.0 %depth.1 = (f32[16,8,640]{2,1,0:T(8,128)S(1)}, f32[16,8,640]{2,1,0:T(8,128)S(1)}) custom-call(f32[16,8,640]{2,1,0:T(8,128)S(1)} %pad_maximum_fusion.waves, f32[16,8,640]{2,1,0:T(8,128)S(1)} %collective-permute-done.2.other, f32[8,8,640]{2,1,0:T(8,128)S(1)} %pad_maximum_fusion.1.edges, f32[16,8,640]{2,1,0:T(8,128)S(1)} %get-tuple-element.39.axis_x, ...), custom_call_target="tpu_custom_call" | custom-call | flops 4096000 | bytes 1638400 | tf_op jit(solution)/shard_map/depth/pallas_call | solution.py:434
  11.1 0.4 %collective-permute-done.3.edges_other = f32[8,8,640]{2,1,0:T(8,128)S(1)} collective-permute-done((f32[8,8,640]{2,1,0:T(8,128)S(1)}, f32[8,8,640]{2,1,0:T(8,128)S(1)}, u32[]{:S(2)}, u32[]{:S(2)}) %collective-permute-start.3) | collective-permute-done | bytes 163872 | tf_op jit(solution)/shard_map/ppermute | solution.py:433
  11.4 0.0 copy-done
  11.4 0.0 copy-done.1
  11.5 0.0 copy-done.9
  11.5 0.0 copy-done.10
  11.5 0.0 copy-start.12
  11.5 0.9 %step.1 = (f32[16,8,640]{2,1,0:T(8,128)S(1)}, f32[64,640]{1,0:T(8,128)S(1)}, f32[24,640]{1,0:T(8,128)S(1)}, f32[24,640]{1,0:T(8,128)S(1)}, f32[8,640]{1,0:T(8,128)S(1)}, /*index=5*/f32[8,640]{1,0:T(8,128)S(1)}) custom-call(f32[8,8,640]{2,1,0:T(8,128)S(1)} %pad_maximum_fusion.1.edges, f32[8,8,640]{2,1,0:T(8,128)S(1)} %collective-permute-done.3.edges_other, ...), custom_call_target="tpu_custom_call" | custom-call | flops 16384000 | bytes 1638400 | tf_op jit(solution)/shard_map/step/pallas_call | solution.py:454
  12.4 3.6 %collective-permute-start.4 = (f32[24,640]{1,0:T(8,128)S(1)}, f32[24,640]{1,0:T(8,128)S(1)}, u32[]{:S(2)}, u32[]{:S(2)}) collective-permute-start(f32[24,640]{1,0:T(8,128)S(1)} %get-tuple-element.64), channel_id=1, source_target_pairs={{0,14},{2,4},{4,2},{6,8},{8,6},{10,12},{12,10},{14,0},{1,15},{3,5}... | collective-permute-start | bytes 184328 | tf_op jit(solution)/shard_map/ppermute | solution.py:470
  16.0 0.4 %collective-permute-start.5 = (f32[24,640]{1,0:T(8,128)S(1)}, f32[24,640]{1,0:T(8,128)S(1)}, u32[]{:S(2)}, u32[]{:S(2)}) collective-permute-start(f32[24,640]{1,0:T(8,128)S(1)} %get-tuple-element.65), channel_id=1, source_target_pairs={{0,2},{2,0},{4,6},{6,4},{8,10},{10,8},{12,14},{14,12},{1,3},{3,1},... | collective-permute-start | bytes 184328 | tf_op jit(solution)/shard_map/ppermute | solution.py:470
  16.5 1.9 %collective-permute-start.6 = (f32[8,640]{1,0:T(8,128)S(1)}, f32[8,640]{1,0:T(8,128)S(1)}, u32[]{:S(2)}, u32[]{:S(2)}) collective-permute-start(f32[8,640]{1,0:T(8,128)S(1)} %get-tuple-element.66), channel_id=1, source_target_pairs={{0,12},{2,14},{4,8},{6,10},{8,4},{10,6},{12,0},{14,2},{1,13},{3,15... | collective-permute-start | bytes 61448 | tf_op jit(solution)/shard_map/ppermute | solution.py:470
  18.4 1.2 %collective-permute-start.7 = (f32[8,640]{1,0:T(8,128)S(1)}, f32[8,640]{1,0:T(8,128)S(1)}, u32[]{:S(2)}, u32[]{:S(2)}) collective-permute-start(f32[8,640]{1,0:T(8,128)S(1)} %get-tuple-element.67), channel_id=1, source_target_pairs={{0,4},{2,6},{4,0},{6,2},{8,12},{10,14},{12,8},{14,10},{1,5},{3,7},... | collective-permute-start | bytes 61448 | tf_op jit(solution)/shard_map/ppermute | solution.py:470
  19.6 0.0 copy-done.11
  19.6 0.0 copy-done.12
  19.6 0.8 %own.1 = (f32[16,4,640]{2,1,0:T(4,128)}, f32[16,4,640]{2,1,0:T(4,128)}, f32[64,640]{1,0:T(8,128)S(1)}) custom-call(f32[16,8,640]{2,1,0:T(8,128)S(1)} %get-tuple-element.59.pressure, f32[64,640]{1,0:T(8,128)S(1)} %get-tuple-element.60.crossline, bf16[64,64]{1,0:T(8,128)(2,1)S(1)} %copy-done.12, bf16[64,64]{1,0:T(8,128)(2,1)S(1)} %copy-done.11), custom_call_target="tpu_custom_call" | custom-call | flops 4096000 | bytes 1638400 | tf_op jit(solution)/shard_map/own/pallas_call | solution.py:472
  20.5 1.6 %collective-permute-done.6.rest_2_ = f32[8,640]{1,0:T(8,128)S(1)} collective-permute-done((f32[8,640]{1,0:T(8,128)S(1)}, f32[8,640]{1,0:T(8,128)S(1)}, u32[]{:S(2)}, u32[]{:S(2)}) %collective-permute-start.6) | collective-permute-done | bytes 20512 | tf_op jit(solution)/shard_map/ppermute | solution.py:470
  22.1 0.2 collective-permute-done.7.rest_3_
  22.3 0.0 collective-permute-done.4.rest_0_
  22.3 0.0 collective-permute-done.5.rest_1_
  22.3 0.8 %finish.1 = (f32[8,4,640]{2,1,0:T(4,128)}, f32[4,4,640]{2,1,0:T(4,128)}, f32[2,4,640]{2,1,0:T(4,128)}, f32[2,4,640]{2,1,0:T(4,128)}) custom-call(f32[64,640]{1,0:T(8,128)S(1)} %get-tuple-element.63.mine, f32[24,640]{1,0:T(8,128)S(1)} %collective-permute-done.4.rest_0_, f32[24,640]{1,0:T(8,128)S(1)} %collective-permute-done.5.rest_1_, ...), custom_call_target="tpu_custom_call" | custom-call | flops 819200 | bytes 1638400 | tf_op jit(solution)/shard_map/finish/pallas_call | solution.py:475
  (3 shorter events, 0.0 us)
Async XLA Ops:
  0.6 5.9 %copy-start.4 = (bf16[16,4,640]{2,1,0:T(4,128)(2,1)S(1)}, bf16[16,4,640]{2,1,0:T(4,128)(2,1)}, u32[]{:S(2)}) copy-start(bf16[16,4,640]{2,1,0:T(4,128)(2,1)} %courant.1) | copy-start | bytes 245764
  0.7 5.9 %copy-start.5 = (bf16[16,4,640]{2,1,0:T(4,128)(2,1)S(1)}, bf16[16,4,640]{2,1,0:T(4,128)(2,1)}, u32[]{:S(2)}) copy-start(bf16[16,4,640]{2,1,0:T(4,128)(2,1)} %epsilon.1) | copy-start | bytes 245764
  0.7 5.9 %copy-start.6 = (bf16[16,4,640]{2,1,0:T(4,128)(2,1)S(1)}, bf16[16,4,640]{2,1,0:T(4,128)(2,1)}, u32[]{:S(2)}) copy-start(bf16[16,4,640]{2,1,0:T(4,128)(2,1)} %delta.1) | copy-start | bytes 245764
  0.7 5.8 %copy-start.7 = (bf16[16,4,640]{2,1,0:T(4,128)(2,1)S(1)}, bf16[16,4,640]{2,1,0:T(4,128)(2,1)}, u32[]{:S(2)}) copy-start(bf16[16,4,640]{2,1,0:T(4,128)(2,1)} %tilt.1) | copy-start | bytes 245764
  0.7 5.8 %copy-start.8 = (bf16[16,4,640]{2,1,0:T(4,128)(2,1)S(1)}, bf16[16,4,640]{2,1,0:T(4,128)(2,1)}, u32[]{:S(2)}) copy-start(bf16[16,4,640]{2,1,0:T(4,128)(2,1)} %azimuth.1) | copy-start | bytes 245764
  1.8 4.7 %copy-start.2 = (f32[16,4,640]{2,1,0:T(4,128)S(1)}, f32[16,4,640]{2,1,0:T(4,128)}, u32[]{:S(2)}) copy-start(f32[16,4,640]{2,1,0:T(4,128)} %prior_p.1) | copy-start | bytes 491524
  1.8 4.7 %copy-start.3 = (f32[16,4,640]{2,1,0:T(4,128)S(1)}, f32[16,4,640]{2,1,0:T(4,128)}, u32[]{:S(2)}) copy-start(f32[16,4,640]{2,1,0:T(4,128)} %prior_q.1) | copy-start | bytes 491524
  1.9 8.1 %collective-permute-start.2 = (f32[16,8,640]{2,1,0:T(8,128)S(1)}, f32[16,8,640]{2,1,0:T(8,128)S(1)}, u32[]{:S(2)}, u32[]{:S(2)}) collective-permute-start(f32[16,8,640]{2,1,0:T(8,128)S(1)} %pad_maximum_fusion.waves), channel_id=1, source_target_pairs={{0,1},{1,0},{2,3},{3,2},{4,5},{5,4},{6,7},{7,6},{8,9},{9,8},{10,11... | collective-permute-start | bytes 983048 | tf_op jit(solution)/shard_map/ppermute | solution.py:421
  2.4 5.8 %collective-permute-start = (f32[4,8,640]{2,1,0:T(8,128)S(1)}, f32[4,8,640]{2,1,0:T(8,128)S(1)}, u32[]{:S(2)}, u32[]{:S(2)}) collective-permute-start(f32[4,8,640]{2,1,0:T(8,128)S(1)} %get-tuple-element.44), channel_id=1, source_target_pairs={{0,1},{1,0},{2,4},{3,5},{4,2},{5,3},{6,8},{7,9},{8,6},{9,7},{10,12... | collective-permute-start | bytes 245768 | tf_op jit(solution)/shard_map/ppermute | solution.py:419
  2.5 7.5 %collective-permute-start.1 = (f32[4,8,640]{2,1,0:T(8,128)S(1)}, f32[4,8,640]{2,1,0:T(8,128)S(1)}, u32[]{:S(2)}, u32[]{:S(2)}) collective-permute-start(f32[4,8,640]{2,1,0:T(8,128)S(1)} %get-tuple-element.45), channel_id=1, source_target_pairs={{0,2},{2,0},{4,6},{6,4},{8,10},{10,8},{12,14},{14,12},{1,3},{3,1},... | collective-permute-start | bytes 245768 | tf_op jit(solution)/shard_map/ppermute | solution.py:420
  10.0 1.5 %collective-permute-start.3 = (f32[8,8,640]{2,1,0:T(8,128)S(1)}, f32[8,8,640]{2,1,0:T(8,128)S(1)}, u32[]{:S(2)}, u32[]{:S(2)}) collective-permute-start(f32[8,8,640]{2,1,0:T(8,128)S(1)} %pad_maximum_fusion.1.edges), channel_id=1, source_target_pairs={{0,1},{1,0},{2,3},{3,2},{4,5},{5,4},{6,7},{7,6},{8,9},{9,8},{10,11... | collective-permute-start | bytes 491528 | tf_op jit(solution)/shard_map/ppermute | solution.py:433
  10.1 1.4 %copy-start = (bf16[640,640]{1,0:T(8,128)(2,1)S(1)}, bf16[640,640]{1,0:T(8,128)(2,1)}, u32[]{:S(2)}) copy-start(bf16[640,640]{1,0:T(8,128)(2,1)} %constant.37.clone.across_low) | copy-start | bytes 2457604
  10.1 1.4 %copy-start.1 = (bf16[640,640]{1,0:T(8,128)(2,1)S(1)}, bf16[640,640]{1,0:T(8,128)(2,1)}, u32[]{:S(2)}) copy-start(bf16[640,640]{1,0:T(8,128)(2,1)} %constant.36.clone.across_high) | copy-start | bytes 2457604
  10.1 1.4 %copy-start.9 = (bf16[64,64]{1,0:T(8,128)(2,1)S(1)}, bf16[64,64]{1,0:T(8,128)(2,1)}, u32[]{:S(2)}) copy-start(bf16[64,64]{1,0:T(8,128)(2,1)} %constant.33.clone.inline_low) | copy-start | bytes 24580
  10.1 1.4 %copy-start.10 = (bf16[64,64]{1,0:T(8,128)(2,1)S(1)}, bf16[64,64]{1,0:T(8,128)(2,1)}, u32[]{:S(2)}) copy-start(bf16[64,64]{1,0:T(8,128)(2,1)} %constant.32.clone.inline_high) | copy-start | bytes 24580
  11.5 8.2 %copy-start.11 = (bf16[64,64]{1,0:T(8,128)(2,1)S(1)}, bf16[64,64]{1,0:T(8,128)(2,1)}, u32[]{:S(2)}) copy-start(bf16[64,64]{1,0:T(8,128)(2,1)} %constant.35.clone.own_low) | copy-start | bytes 24580
  11.5 8.2 %copy-start.12 = (bf16[64,64]{1,0:T(8,128)(2,1)S(1)}, bf16[64,64]{1,0:T(8,128)(2,1)}, u32[]{:S(2)}) copy-start(bf16[64,64]{1,0:T(8,128)(2,1)} %constant.34.clone.own_high) | copy-start | bytes 24580
  12.4 9.9 %collective-permute-start.4 = (f32[24,640]{1,0:T(8,128)S(1)}, f32[24,640]{1,0:T(8,128)S(1)}, u32[]{:S(2)}, u32[]{:S(2)}) collective-permute-start(f32[24,640]{1,0:T(8,128)S(1)} %get-tuple-element.64), channel_id=1, source_target_pairs={{0,14},{2,4},{4,2},{6,8},{8,6},{10,12},{12,10},{14,0},{1,15},{3,5}... | collective-permute-start | bytes 184328 | tf_op jit(solution)/shard_map/ppermute | solution.py:470
  16.0 6.3 %collective-permute-start.5 = (f32[24,640]{1,0:T(8,128)S(1)}, f32[24,640]{1,0:T(8,128)S(1)}, u32[]{:S(2)}, u32[]{:S(2)}) collective-permute-start(f32[24,640]{1,0:T(8,128)S(1)} %get-tuple-element.65), channel_id=1, source_target_pairs={{0,2},{2,0},{4,6},{6,4},{8,10},{10,8},{12,14},{14,12},{1,3},{3,1},... | collective-permute-start | bytes 184328 | tf_op jit(solution)/shard_map/ppermute | solution.py:470
  16.5 5.6 %collective-permute-start.6 = (f32[8,640]{1,0:T(8,128)S(1)}, f32[8,640]{1,0:T(8,128)S(1)}, u32[]{:S(2)}, u32[]{:S(2)}) collective-permute-start(f32[8,640]{1,0:T(8,128)S(1)} %get-tuple-element.66), channel_id=1, source_target_pairs={{0,12},{2,14},{4,8},{6,10},{8,4},{10,6},{12,0},{14,2},{1,13},{3,15... | collective-permute-start | bytes 61448 | tf_op jit(solution)/shard_map/ppermute | solution.py:470
  18.4 3.9 %collective-permute-start.7 = (f32[8,640]{1,0:T(8,128)S(1)}, f32[8,640]{1,0:T(8,128)S(1)}, u32[]{:S(2)}, u32[]{:S(2)}) collective-permute-start(f32[8,640]{1,0:T(8,128)S(1)} %get-tuple-element.67), channel_id=1, source_target_pairs={{0,4},{2,6},{4,0},{6,2},{8,12},{10,14},{12,8},{14,10},{1,5},{3,7},... | collective-permute-start | bytes 61448 | tf_op jit(solution)/shard_map/ppermute | solution.py:470

commit v11 on v10

--- a/solution.py
+++ b/solution.py
@@ -238,7 +238,8 @@
 def depth_kernel(
     size,
     waves,
-    other,
+    layers_p,
+    layers_q,
     edges,
     axis_x,
     axis_y,
@@ -254,10 +255,12 @@
 ):
     rows, sub, width = waves.shape
     flat = rows * sub
-    lower = lax.axis_index("gz") == 0
+    half = lax.axis_index("gz")
+    lower = half == 0
     for x in range(rows):
         own = waves[x]
-        ahead, behind = depth_neighbours(own, other[x], lower)
+        far = jnp.concatenate([layers_p[1 - half, x], layers_q[1 - half, x]], axis=0)
+        ahead, behind = depth_neighbours(own, far, lower)
         dz[x] = first_of(ahead, behind)
         dzz[x] = second_of(own, ahead, behind)
     slope = jnp.concatenate(halves(dz[...].reshape(flat, width)), axis=0)
@@ -414,11 +417,9 @@
         for i, j in pairs[0]
         for g in range(2)
     ]
-    to_inner, to_outer = jnp.where(even, last, leading), jnp.where(even, leading, last)
-    to_inner, to_outer, fields = lax.optimization_barrier((to_inner, to_outer, waves))
-    outer = lax.ppermute(to_outer, ("xy", "gz"), open_outer)
-    inner = lax.ppermute(to_inner, "xy", pairs[1])
-    other = lax.ppermute(fields, "gz", cores)
+    outer = lax.ppermute(jnp.where(even, leading, last), ("xy", "gz"), open_outer)
+    inner = lax.ppermute(jnp.where(even, last, leading), "xy", pairs[1])
+    layers_p, layers_q = lax.all_gather(wave_p, "gz"), lax.all_gather(wave_q, "gz")
 
     taps = jax.ShapeDtypeStruct((4 * LANES, 2 * LANES), jnp.bfloat16)
     axis_x, axis_y, axis_z, *gains, taps_first, taps_second = kernel(
@@ -428,11 +429,13 @@
     h_part, sum_part = kernel(interior_kernel, [stack] * 2, 100, "interior", [work] * 2)(
         waves, axis_x, axis_y, taps_first, taps_second
     )
-    h_part, outer, inner = lax.optimization_barrier((h_part, outer, inner))
-    edges, other = lax.optimization_barrier((jnp.concatenate([outer, inner], axis=0), other))
+    h_part, layers_p, layers_q, outer, inner = lax.optimization_barrier(
+        (h_part, layers_p, layers_q, outer, inner)
+    )
+    edges = jnp.concatenate([outer, inner], axis=0)
     edges_other = lax.ppermute(edges, "gz", cores)
     h_own, sum_own = kernel(functools.partial(depth_kernel, size), [stack] * 2, 100, "depth", [work] * 3)(
-        waves, other, edges, axis_x, axis_y, axis_z, h_part, sum_part, taps_first
+        waves, layers_p, layers_q, edges, axis_x, axis_y, axis_z, h_part, sum_part, taps_first
     )
 
     own, factors = inline_blocks(rows)

time: 23.3 us -> 24.9 us (1.069)
  blocking collectives: 0 us -> 4.2 us
  starting transfers between devices: 12 us -> 9.81 us
  waiting for transfers between devices: 3.95 us -> 2.91 us
  local copies, waits for them, and re-layouts: 0.08 us -> 0.65 us
    all_gather x0 -> x2, blocking collectives: none -> 4.2 us  [the longest x1 2.17 us: body(): lax.all_gather(wave_p, 'gz')]
    ppermute x3 -> x2, waiting for transfers between devices: 1.76 us -> 0.01 us  [the longest x1 0.01 us: body(): inner = lax.ppermute(jnp.where(even, last, leading), 'xy', pairs[1])]
    ppermute x3 -> x2, starting transfers between devices: 4.63 us -> 3.07 us  [the longest x1 3 us: body(): inner = lax.ppermute(jnp.where(even, last, leading), 'xy', pairs[1])]
    ppermute x4, waiting for transfers between devices: 1.83 us -> 2.87 us  [body(): lax.ppermute(send, 'xy', pair)]
    ppermute x4, starting transfers between devices: 7.25 us -> 6.32 us  [body(): lax.ppermute(send, 'xy', pair)]
    unnamed x26 -> x31, local copies, waits for them, and re-layouts: 0.08 us -> 0.65 us
    ppermute x1, waiting for transfers between devices: 0.36 us -> 0.03 us  [body(): edges_other = lax.ppermute(edges, 'gz', cores)]
    ppermute x1, starting transfers between devices: 0.09 us -> 0.41 us  [body(): edges_other = lax.ppermute(edges, 'gz', cores)]
  transfers between devices with their start and end apart: 8 -> 7, of which waited for: 4 -> 2; matrix products, arithmetic and copies ran while one was open for 0% -> 0% of each run, Pallas kernels for 15% -> 14%
where the time goes in v11:
time: 24.9 us; the launch traced here: 24.7 us
  starting transfers between devices  9.81 us (39%)
  Pallas kernels  5.16 us (21%)
  blocking collectives  4.2 us (17%)
  waiting for transfers between devices  2.91 us (12%)
  other arithmetic  1.12 us (4%)
  between operations  0.81 us (3%)
  local copies, waits for them, and re-layouts  0.65 us (3%)
    ppermute x4, starting transfers between devices, body(): lax.ppermute(send, 'xy', pair)  6.32 us
    ppermute x1, starting transfers between devices, body(): inner = lax.ppermute(jnp.where(even, last, leading), 'xy', pairs[1])  3 us
    ppermute x4, waiting for transfers between devices, body(): lax.ppermute(send, 'xy', pair)  2.87 us
    all_gather x1, blocking collectives, body(): lax.all_gather(wave_p, 'gz')  2.17 us
    all_gather x1, blocking collectives, body(): lax.all_gather(wave_q, 'gz')  2.03 us
    concatenate x1, other arithmetic, body(): waves = lax.optimization_barrier(jnp.concatenate([wave_p, wave_q], axis=1))  1.1 us
    pallas_call x1, Pallas kernels, body(): kernel(functools.partial(depth_kernel, size), [stack] * 2, 100, 'depth',...  1 us
    pallas_call x1, Pallas kernels, body(): kernel(weights_kernel, [stack] * 6 + [taps] * 2, 100, 'weights')  0.95 us
  transfers between devices with their start and end apart: 7, of which 2 were waited for; matrix products, arithmetic and copies ran while one was open for 0% of the time, Pallas kernels for 14%

profile of v11, /device:TPU:0, one launch (start us, length us, event | category | flops | bytes accessed | tf_op | source)
XLA Modules:
  0.0 24.7 jit_solution(9056379473876417814)
XLA Ops:
  0.6 0.0 copy-start.13
  0.7 1.1 %pad_maximum_fusion.waves = f32[16,8,640]{2,1,0:T(8,128)S(1)} fusion(f32[16,4,640]{2,1,0:T(4,128)} %param.16, f32[16,4,640]{2,1,0:T(4,128)} %param.15), kind=kLoop, calls=%fused_computation | loop fusion | flops 81920 | bytes 655360 | tf_op jit(solution)/shard_map/concatenate | solution.py:413
  1.8 0.0 copy-start.6
  1.8 0.0 copy-start.7
  1.8 0.0 copy-start.8
  1.8 3.0 %collective-permute-start.1 = (f32[4,8,640]{2,1,0:T(8,128)S(1)}, f32[4,8,640]{2,1,0:T(8,128)S(1)}, u32[]{:S(2)}, u32[]{:S(2)}) collective-permute-start(f32[4,8,640]{2,1,0:T(8,128)S(1)} %get-tuple-element.66), channel_id=1, source_target_pairs={{0,2},{2,0},{4,6},{6,4},{8,10},{10,8},{12,14},{14,12},{1,3},{3,1},... | collective-permute-start | bytes 245768 | tf_op jit(solution)/shard_map/ppermute | solution.py:421
  4.8 0.0 copy-start.2
  4.8 0.0 copy-start.3
  4.8 0.0 copy-start.4
  4.8 0.0 copy-start.5
  4.8 0.1 collective-permute-start
  4.9 0.0 copy-done.13
  4.9 2.2 %all-gather = f32[32,4,640]{2,1,0:T(4,128)S(1)} all-gather(f32[16,4,640]{2,1,0:T(4,128)S(1)} %copy-done.13), channel_id=2, replica_groups=mesh['shot'=2,'xy'=8,'gz'=2] {'gz'}, dimensions={0}, use_global_device_ids=true | all-gather | bytes 491520 | tf_op jit(solution)/shard_map/all_gather | solution.py:422
  7.1 0.0 copy-done.6
  7.1 0.0 copy-done.7
  7.1 0.0 copy-done.8
  7.1 0.0 copy-done.2
  7.1 0.0 copy-done.3
  7.1 0.0 copy-done.4
  7.1 0.0 copy-done.5
  7.1 1.0 %weights.1 = (f32[16,8,640]{2,1,0:T(8,128)S(1)}, f32[16,8,640]{2,1,0:T(8,128)S(1)}, f32[16,8,640]{2,1,0:T(8,128)S(1)}, f32[16,8,640]{2,1,0:T(8,128)S(1)}, f32[16...) custom-call(f32[16,8,640]{2,1,0:T(8,128)S(1)} %pad_maximum_fusion.wa, ...), custom_call_target="tpu_custom_call" | custom-call | flops 4096000 | bytes 1638400 | tf_op jit(solution)/shard_map/weights/pallas_call | solution.py:425
  8.1 0.0 copy-start.14
  8.1 0.7 %interior.1 = (f32[16,8,640]{2,1,0:T(8,128)S(1)}, f32[16,8,640]{2,1,0:T(8,128)S(1)}) custom-call(f32[16,8,640]{2,1,0:T(8,128)S(1)} %pad_maximum_fusion.waves, f32[16,8,640]{2,1,0:T(8,128)S(1)} %get-tuple-element.36.axis_x, f32[16,8,640]{2,1,0:T(8,128)S(1)} %get-tuple-element.37.axis_y, bf16[512,256]{1,0:T(8,128)(2,1)S(1)} %get-tuple-element.38.taps_first, ...), custom_call_target="tpu_custom_call" | custom-call | flops 4096000 | bytes 1638400 | tf_op jit(solution)/shard_map/interior/pallas_call | solution.py:429
  8.8 0.2 copy-done.14
  9.0 2.0 %all-gather.1 = f32[32,4,640]{2,1,0:T(4,128)S(1)} all-gather(f32[16,4,640]{2,1,0:T(4,128)S(1)} %copy-done.14), channel_id=3, replica_groups=mesh['shot'=2,'xy'=8,'gz'=2] {'gz'}, dimensions={0}, use_global_device_ids=true | all-gather | bytes 491520 | tf_op jit(solution)/shard_map/all_gather | solution.py:422
  11.1 0.0 collective-permute-done.1
  11.1 0.0 collective-permute-done
  11.1 0.4 %collective-permute-start.2 = (f32[8,8,640]{2,1,0:T(8,128)S(1)}, f32[8,8,640]{2,1,0:T(8,128)S(1)}, u32[]{:S(2)}, u32[]{:S(2)}) collective-permute-start(f32[8,8,640]{2,1,0:T(8,128)S(1)} %constant_dynamic-update-slice_fusion.edges), channel_id=1, source_target_pairs={{0,1},{1,0},{2,3},{3,2},{4,5},{5,4},{6,7},{7,6},{8,9},{9,8},{10,11... | collective-permute-start | bytes 491528 | tf_op jit(solution)/shard_map/ppermute | solution.py:436
  11.5 0.0 copy-start
  11.5 1.0 %depth.1 = (f32[16,8,640]{2,1,0:T(8,128)S(1)}, f32[16,8,640]{2,1,0:T(8,128)S(1)}) custom-call(f32[16,8,640]{2,1,0:T(8,128)S(1)} %pad_maximum_fusion.waves, f32[2,16,4,640]{3,2,1,0:T(4,128)S(1)} %bitcast.2, f32[2,16,4,640]{3,2,1,0:T(4,128)S(1)} %bitcast.3, f32[8,8,640]{2,1,0:T(8,128)S(1)} %constant_dynamic-update-slice_fusion.edges, ...), custom_call_target="tpu_custom_call" | custom-call | flops 4096000 | bytes 1638400 | tf_op jit(solution)/shard_map/depth/pallas_call | solution.py:437
  12.5 0.0 collective-permute-done.2.edges_other
  12.5 0.1 copy-done
  12.6 0.2 copy-done.1
  12.9 0.0 copy-done.9
  12.9 0.0 copy-done.10
  12.9 0.9 %step.1 = (f32[16,8,640]{2,1,0:T(8,128)S(1)}, f32[64,640]{1,0:T(8,128)S(1)}, f32[24,640]{1,0:T(8,128)S(1)}, f32[24,640]{1,0:T(8,128)S(1)}, f32[8,640]{1,0:T(8,128)S(1)}, /*index=5*/f32[8,640]{1,0:T(8,128)S(1)}) custom-call(f32[8,8,640]{2,1,0:T(8,128)S(1)} %constant_dynamic-update-slice_fusion.edges, f32[8,8,640]{2,1,0:T(8,128)S(1)} %collective-permute-done.2.edges_other, ...), custom_call_target="tpu_custom_call" | custom-call | flops 16384000 | bytes 1638400 | tf_op jit(solution)/shard_map/step/pallas_call | solution.py:457
  13.8 3.6 %collective-permute-start.3 = (f32[24,640]{1,0:T(8,128)S(1)}, f32[24,640]{1,0:T(8,128)S(1)}, u32[]{:S(2)}, u32[]{:S(2)}) collective-permute-start(f32[24,640]{1,0:T(8,128)S(1)} %get-tuple-element.58), channel_id=1, source_target_pairs={{0,14},{2,4},{4,2},{6,8},{8,6},{10,12},{12,10},{14,0},{1,15},{3,5}... | collective-permute-start | bytes 184328 | tf_op jit(solution)/shard_map/ppermute | solution.py:473
  17.5 0.0 collective-permute-start.4
  17.5 2.6 %collective-permute-start.5 = (f32[8,640]{1,0:T(8,128)S(1)}, f32[8,640]{1,0:T(8,128)S(1)}, u32[]{:S(2)}, u32[]{:S(2)}) collective-permute-start(f32[8,640]{1,0:T(8,128)S(1)} %get-tuple-element.60), channel_id=1, source_target_pairs={{0,12},{2,14},{4,8},{6,10},{8,4},{10,6},{12,0},{14,2},{1,13},{3,15... | collective-permute-start | bytes 61448 | tf_op jit(solution)/shard_map/ppermute | solution.py:473
  20.1 0.1 collective-permute-start.6
  20.2 0.0 copy-done.11
  20.2 0.0 copy-done.12
  20.2 0.8 %own.1 = (f32[16,4,640]{2,1,0:T(4,128)}, f32[16,4,640]{2,1,0:T(4,128)}, f32[64,640]{1,0:T(8,128)S(1)}) custom-call(f32[16,8,640]{2,1,0:T(8,128)S(1)} %get-tuple-element.53.pressure, f32[64,640]{1,0:T(8,128)S(1)} %get-tuple-element.54.crossline, bf16[64,64]{1,0:T(8,128)(2,1)S(1)} %copy-done.12, bf16[64,64]{1,0:T(8,128)(2,1)S(1)} %copy-done.11), custom_call_target="tpu_custom_call" | custom-call | flops 4096000 | bytes 1638400 | tf_op jit(solution)/shard_map/own/pallas_call | solution.py:475
  21.0 2.1 %collective-permute-done.5.rest_2_ = f32[8,640]{1,0:T(8,128)S(1)} collective-permute-done((f32[8,640]{1,0:T(8,128)S(1)}, f32[8,640]{1,0:T(8,128)S(1)}, u32[]{:S(2)}, u32[]{:S(2)}) %collective-permute-start.5) | collective-permute-done | bytes 20512 | tf_op jit(solution)/shard_map/ppermute | solution.py:473
  23.0 0.8 %collective-permute-done.6.rest_3_ = f32[8,640]{1,0:T(8,128)S(1)} collective-permute-done((f32[8,640]{1,0:T(8,128)S(1)}, f32[8,640]{1,0:T(8,128)S(1)}, u32[]{:S(2)}, u32[]{:S(2)}) %collective-permute-start.6) | collective-permute-done | bytes 20512 | tf_op jit(solution)/shard_map/ppermute | solution.py:473
  23.8 0.0 collective-permute-done.3.rest_0_
  23.8 0.0 collective-permute-done.4.rest_1_
  23.9 0.8 %finish.1 = (f32[8,4,640]{2,1,0:T(4,128)}, f32[4,4,640]{2,1,0:T(4,128)}, f32[2,4,640]{2,1,0:T(4,128)}, f32[2,4,640]{2,1,0:T(4,128)}) custom-call(f32[64,640]{1,0:T(8,128)S(1)} %get-tuple-element.57.mine, f32[24,640]{1,0:T(8,128)S(1)} %collective-permute-done.3.rest_0_, f32[24,640]{1,0:T(8,128)S(1)} %collective-permute-done.4.rest_1_, ...), custom_call_target="tpu_custom_call" | custom-call | flops 819200 | bytes 1638400 | tf_op jit(solution)/shard_map/finish/pallas_call | solution.py:478
  (8 shorter events, 0.0 us)
Async XLA Ops:
  0.6 4.3 %copy-start.13 = (f32[16,4,640]{2,1,0:T(4,128)S(1)}, f32[16,4,640]{2,1,0:T(4,128)}, u32[]{:S(2)}) copy-start(f32[16,4,640]{2,1,0:T(4,128)} %param.15) | copy-start | bytes 491524
  1.8 5.3 %copy-start.6 = (bf16[16,4,640]{2,1,0:T(4,128)(2,1)S(1)}, bf16[16,4,640]{2,1,0:T(4,128)(2,1)}, u32[]{:S(2)}) copy-start(bf16[16,4,640]{2,1,0:T(4,128)(2,1)} %delta.1) | copy-start | bytes 245764
  1.8 5.3 %copy-start.7 = (bf16[16,4,640]{2,1,0:T(4,128)(2,1)S(1)}, bf16[16,4,640]{2,1,0:T(4,128)(2,1)}, u32[]{:S(2)}) copy-start(bf16[16,4,640]{2,1,0:T(4,128)(2,1)} %tilt.1) | copy-start | bytes 245764
  1.8 5.3 %copy-start.8 = (bf16[16,4,640]{2,1,0:T(4,128)(2,1)S(1)}, bf16[16,4,640]{2,1,0:T(4,128)(2,1)}, u32[]{:S(2)}) copy-start(bf16[16,4,640]{2,1,0:T(4,128)(2,1)} %azimuth.1) | copy-start | bytes 245764
  1.8 9.2 %collective-permute-start.1 = (f32[4,8,640]{2,1,0:T(8,128)S(1)}, f32[4,8,640]{2,1,0:T(8,128)S(1)}, u32[]{:S(2)}, u32[]{:S(2)}) collective-permute-start(f32[4,8,640]{2,1,0:T(8,128)S(1)} %get-tuple-element.66), channel_id=1, source_target_pairs={{0,2},{2,0},{4,6},{6,4},{8,10},{10,8},{12,14},{14,12},{1,3},{3,1},... | collective-permute-start | bytes 245768 | tf_op jit(solution)/shard_map/ppermute | solution.py:421
  4.8 2.3 %copy-start.2 = (f32[16,4,640]{2,1,0:T(4,128)S(1)}, f32[16,4,640]{2,1,0:T(4,128)}, u32[]{:S(2)}) copy-start(f32[16,4,640]{2,1,0:T(4,128)} %prior_p.1) | copy-start | bytes 491524
  4.8 2.3 %copy-start.3 = (f32[16,4,640]{2,1,0:T(4,128)S(1)}, f32[16,4,640]{2,1,0:T(4,128)}, u32[]{:S(2)}) copy-start(f32[16,4,640]{2,1,0:T(4,128)} %prior_q.1) | copy-start | bytes 491524
  4.8 2.3 %copy-start.4 = (bf16[16,4,640]{2,1,0:T(4,128)(2,1)S(1)}, bf16[16,4,640]{2,1,0:T(4,128)(2,1)}, u32[]{:S(2)}) copy-start(bf16[16,4,640]{2,1,0:T(4,128)(2,1)} %courant.1) | copy-start | bytes 245764
  4.8 2.3 %copy-start.5 = (bf16[16,4,640]{2,1,0:T(4,128)(2,1)S(1)}, bf16[16,4,640]{2,1,0:T(4,128)(2,1)}, u32[]{:S(2)}) copy-start(bf16[16,4,640]{2,1,0:T(4,128)(2,1)} %epsilon.1) | copy-start | bytes 245764
  4.8 6.2 %collective-permute-start = (f32[4,8,640]{2,1,0:T(8,128)S(1)}, f32[4,8,640]{2,1,0:T(8,128)S(1)}, u32[]{:S(2)}, u32[]{:S(2)}) collective-permute-start(f32[4,8,640]{2,1,0:T(8,128)S(1)} %get-tuple-element.67), channel_id=1, source_target_pairs={{0,1},{1,0},{2,4},{3,5},{4,2},{5,3},{6,8},{7,9},{8,6},{9,7},{10,12... | collective-permute-start | bytes 245768 | tf_op jit(solution)/shard_map/ppermute | solution.py:420
  8.1 0.9 %copy-start.14 = (f32[16,4,640]{2,1,0:T(4,128)S(1)}, f32[16,4,640]{2,1,0:T(4,128)}, u32[]{:S(2)}) copy-start(f32[16,4,640]{2,1,0:T(4,128)} %param.16) | copy-start | bytes 491524
  11.1 1.5 %collective-permute-start.2 = (f32[8,8,640]{2,1,0:T(8,128)S(1)}, f32[8,8,640]{2,1,0:T(8,128)S(1)}, u32[]{:S(2)}, u32[]{:S(2)}) collective-permute-start(f32[8,8,640]{2,1,0:T(8,128)S(1)} %constant_dynamic-update-slice_fusion.edges), channel_id=1, source_target_pairs={{0,1},{1,0},{2,3},{3,2},{4,5},{5,4},{6,7},{7,6},{8,9},{9,8},{10,11... | collective-permute-start | bytes 491528 | tf_op jit(solution)/shard_map/ppermute | solution.py:436
  11.5 1.1 %copy-start = (bf16[640,640]{1,0:T(8,128)(2,1)S(1)}, bf16[640,640]{1,0:T(8,128)(2,1)}, u32[]{:S(2)}) copy-start(bf16[640,640]{1,0:T(8,128)(2,1)} %constant.37.clone.across_low) | copy-start | bytes 2457604
  11.5 1.4 %copy-start.1 = (bf16[640,640]{1,0:T(8,128)(2,1)S(1)}, bf16[640,640]{1,0:T(8,128)(2,1)}, u32[]{:S(2)}) copy-start(bf16[640,640]{1,0:T(8,128)(2,1)} %constant.36.clone.across_high) | copy-start | bytes 2457604
  11.5 1.4 %copy-start.9 = (bf16[64,64]{1,0:T(8,128)(2,1)S(1)}, bf16[64,64]{1,0:T(8,128)(2,1)}, u32[]{:S(2)}) copy-start(bf16[64,64]{1,0:T(8,128)(2,1)} %constant.33.clone.inline_low) | copy-start | bytes 24580
  11.5 1.4 %copy-start.10 = (bf16[64,64]{1,0:T(8,128)(2,1)S(1)}, bf16[64,64]{1,0:T(8,128)(2,1)}, u32[]{:S(2)}) copy-start(bf16[64,64]{1,0:T(8,128)(2,1)} %constant.32.clone.inline_high) | copy-start | bytes 24580
  12.9 7.3 %copy-start.11 = (bf16[64,64]{1,0:T(8,128)(2,1)S(1)}, bf16[64,64]{1,0:T(8,128)(2,1)}, u32[]{:S(2)}) copy-start(bf16[64,64]{1,0:T(8,128)(2,1)} %constant.35.clone.own_low) | copy-start | bytes 24580
  12.9 7.3 %copy-start.12 = (bf16[64,64]{1,0:T(8,128)(2,1)S(1)}, bf16[64,64]{1,0:T(8,128)(2,1)}, u32[]{:S(2)}) copy-start(bf16[64,64]{1,0:T(8,128)(2,1)} %constant.34.clone.own_high) | copy-start | bytes 24580
  13.8 10.0 %collective-permute-start.3 = (f32[24,640]{1,0:T(8,128)S(1)}, f32[24,640]{1,0:T(8,128)S(1)}, u32[]{:S(2)}, u32[]{:S(2)}) collective-permute-start(f32[24,640]{1,0:T(8,128)S(1)} %get-tuple-element.58), channel_id=1, source_target_pairs={{0,14},{2,4},{4,2},{6,8},{8,6},{10,12},{12,10},{14,0},{1,15},{3,5}... | collective-permute-start | bytes 184328 | tf_op jit(solution)/shard_map/ppermute | solution.py:473
  17.5 6.4 %collective-permute-start.4 = (f32[24,640]{1,0:T(8,128)S(1)}, f32[24,640]{1,0:T(8,128)S(1)}, u32[]{:S(2)}, u32[]{:S(2)}) collective-permute-start(f32[24,640]{1,0:T(8,128)S(1)} %get-tuple-element.59), channel_id=1, source_target_pairs={{0,2},{2,0},{4,6},{6,4},{8,10},{10,8},{12,14},{14,12},{1,3},{3,1},... | collective-permute-start | bytes 184328 | tf_op jit(solution)/shard_map/ppermute | solution.py:473
  17.5 5.6 %collective-permute-start.5 = (f32[8,640]{1,0:T(8,128)S(1)}, f32[8,640]{1,0:T(8,128)S(1)}, u32[]{:S(2)}, u32[]{:S(2)}) collective-permute-start(f32[8,640]{1,0:T(8,128)S(1)} %get-tuple-element.60), channel_id=1, source_target_pairs={{0,12},{2,14},{4,8},{6,10},{8,4},{10,6},{12,0},{14,2},{1,13},{3,15... | collective-permute-start | bytes 61448 | tf_op jit(solution)/shard_map/ppermute | solution.py:473
  20.1 3.8 %collective-permute-start.6 = (f32[8,640]{1,0:T(8,128)S(1)}, f32[8,640]{1,0:T(8,128)S(1)}, u32[]{:S(2)}, u32[]{:S(2)}) collective-permute-start(f32[8,640]{1,0:T(8,128)S(1)} %get-tuple-element.61), channel_id=1, source_target_pairs={{0,4},{2,6},{4,0},{6,2},{8,12},{10,14},{12,8},{14,10},{1,5},{3,7},... | collective-permute-start | bytes 61448 | tf_op jit(solution)/shard_map/ppermute | solution.py:473

commit v12 on v11

--- a/solution.py
+++ b/solution.py
@@ -238,8 +238,7 @@
 def depth_kernel(
     size,
     waves,
-    layers_p,
-    layers_q,
+    all_layers,
     edges,
     axis_x,
     axis_y,
@@ -259,8 +258,7 @@
     lower = half == 0
     for x in range(rows):
         own = waves[x]
-        far = jnp.concatenate([layers_p[1 - half, x], layers_q[1 - half, x]], axis=0)
-        ahead, behind = depth_neighbours(own, far, lower)
+        ahead, behind = depth_neighbours(own, all_layers[1 - half, x], lower)
         dz[x] = first_of(ahead, behind)
         dzz[x] = second_of(own, ahead, behind)
     slope = jnp.concatenate(halves(dz[...].reshape(flat, width)), axis=0)
@@ -419,7 +417,7 @@
     ]
     outer = lax.ppermute(jnp.where(even, leading, last), ("xy", "gz"), open_outer)
     inner = lax.ppermute(jnp.where(even, last, leading), "xy", pairs[1])
-    layers_p, layers_q = lax.all_gather(wave_p, "gz"), lax.all_gather(wave_q, "gz")
+    all_layers = lax.all_gather(waves, "gz")
 
     taps = jax.ShapeDtypeStruct((4 * LANES, 2 * LANES), jnp.bfloat16)
     axis_x, axis_y, axis_z, *gains, taps_first, taps_second = kernel(
@@ -429,13 +427,11 @@
     h_part, sum_part = kernel(interior_kernel, [stack] * 2, 100, "interior", [work] * 2)(
         waves, axis_x, axis_y, taps_first, taps_second
     )
-    h_part, layers_p, layers_q, outer, inner = lax.optimization_barrier(
-        (h_part, layers_p, layers_q, outer, inner)
-    )
+    h_part, all_layers, outer, inner = lax.optimization_barrier((h_part, all_layers, outer, inner))
     edges = jnp.concatenate([outer, inner], axis=0)
     edges_other = lax.ppermute(edges, "gz", cores)
     h_own, sum_own = kernel(functools.partial(depth_kernel, size), [stack] * 2, 100, "depth", [work] * 3)(
-        waves, layers_p, layers_q, edges, axis_x, axis_y, axis_z, h_part, sum_part, taps_first
+        waves, all_layers, edges, axis_x, axis_y, axis_z, h_part, sum_part, taps_first
     )
 
     own, factors = inline_blocks(rows)

time: 24.9 us -> 22.8 us (0.916)
  blocking collectives: 4.2 us -> 2.41 us
  starting transfers between devices: 9.81 us -> 10.6 us
  waiting for transfers between devices: 2.91 us -> 2.13 us
    all_gather x2 -> x1, blocking collectives: 4.2 us -> 2.41 us  [body(): all_layers = lax.all_gather(waves, 'gz')]
    ppermute x4, starting transfers between devices: 6.32 us -> 7.14 us  [body(): lax.ppermute(send, 'xy', pair)]
    ppermute x4, waiting for transfers between devices: 2.87 us -> 2.06 us  [body(): lax.ppermute(send, 'xy', pair)]
    unnamed x31 -> x27, local copies, waits for them, and re-layouts: 0.65 us -> 0.41 us
  transfers between devices with their start and end apart: 7 -> 7, of which waited for: 2 -> 3; matrix products, arithmetic and copies ran while one was open for 0% -> 0% of each run, Pallas kernels for 14% -> 15%
where the time goes in v12:
time: 22.8 us; the launch traced here: 22.6 us
  starting transfers between devices  10.6 us (46%)
  Pallas kernels  5.11 us (22%)
  blocking collectives  2.41 us (11%)
  waiting for transfers between devices  2.13 us (9%)
  other arithmetic  1.08 us (5%)
  between operations  0.81 us (4%)
  local copies, waits for them, and re-layouts  0.41 us (2%)
    ppermute x4, starting transfers between devices, body(): lax.ppermute(send, 'xy', pair)  7.14 us
    ppermute x1, starting transfers between devices, body(): inner = lax.ppermute(jnp.where(even, last, leading), 'xy', pairs[1])  3 us
    all_gather x1, blocking collectives, body(): all_layers = lax.all_gather(waves, 'gz')  2.41 us
    ppermute x4, waiting for transfers between devices, body(): lax.ppermute(send, 'xy', pair)  2.06 us
    concatenate x1, other arithmetic, body(): waves = lax.optimization_barrier(jnp.concatenate([wave_p, wave_q], axis=1))  1.07 us
    pallas_call x1, Pallas kernels, body(): kernel(functools.partial(depth_kernel, size), [stack] * 2, 100, 'depth',...  0.96 us
    pallas_call x1, Pallas kernels, body(): kernel(weights_kernel, [stack] * 6 + [taps] * 2, 100, 'weights')  0.95 us
    pallas_call x1, Pallas kernels, body(): kernel(functools.partial(step_kernel, size, gives), [stack, flat] + [jax....  0.9 us
  transfers between devices with their start and end apart: 7, of which 3 were waited for; matrix products, arithmetic and copies ran while one was open for 0% of the time, Pallas kernels for 15%

profile of v12, /device:TPU:0, one launch (start us, length us, event | category | flops | bytes accessed | tf_op | source)
XLA Modules:
  0.0 22.6 jit_solution(656416266701763012)
XLA Ops:
  0.6 1.1 %pad_maximum_fusion.waves = f32[16,8,640]{2,1,0:T(8,128)S(1)} fusion(f32[16,4,640]{2,1,0:T(4,128)} %param.16, f32[16,4,640]{2,1,0:T(4,128)} %param.15), kind=kLoop, calls=%fused_computation | loop fusion | flops 81920 | bytes 655360 | tf_op jit(solution)/shard_map/concatenate | solution.py:411
  1.7 3.0 %collective-permute-start.1 = (f32[4,8,640]{2,1,0:T(8,128)S(1)}, f32[4,8,640]{2,1,0:T(8,128)S(1)}, u32[]{:S(2)}, u32[]{:S(2)}) collective-permute-start(f32[4,8,640]{2,1,0:T(8,128)S(1)} %get-tuple-element.64), channel_id=1, source_target_pairs={{0,2},{2,0},{4,6},{6,4},{8,10},{10,8},{12,14},{14,12},{1,3},{3,1},... | collective-permute-start | bytes 245768 | tf_op jit(solution)/shard_map/ppermute | solution.py:419
  4.7 0.0 copy-start.2
  4.7 0.0 copy-start.3
  4.7 0.0 copy-start.4
  4.7 0.0 copy-start.5
  4.8 0.0 copy-start.6
  4.8 0.0 copy-start.7
  4.8 0.0 copy-start.8
  4.8 0.1 collective-permute-start
  4.9 2.4 %all-gather = f32[32,8,640]{2,1,0:T(8,128)S(1)} all-gather(f32[16,8,640]{2,1,0:T(8,128)S(1)} %pad_maximum_fusion.waves), channel_id=2, replica_groups=mesh['shot'=2,'xy'=8,'gz'=2] {'gz'}, dimensions={0}, use_global_device_ids=true | all-gather | bytes 983040 | tf_op jit(solution)/shard_map/all_gather | solution.py:420
  7.3 0.0 copy-done.2
  7.3 0.0 copy-done.3
  7.3 0.0 copy-done.4
  7.3 0.0 copy-done.5
  7.3 0.0 copy-done.6
  7.3 0.0 copy-done.7
  7.3 0.0 copy-done.8
  7.3 1.0 %weights.1 = (f32[16,8,640]{2,1,0:T(8,128)S(1)}, f32[16,8,640]{2,1,0:T(8,128)S(1)}, f32[16,8,640]{2,1,0:T(8,128)S(1)}, f32[16,8,640]{2,1,0:T(8,128)S(1)}, f32[16...) custom-call(f32[16,8,640]{2,1,0:T(8,128)S(1)} %pad_maximum_fusion.wa, ...), custom_call_target="tpu_custom_call" | custom-call | flops 4096000 | bytes 1638400 | tf_op jit(solution)/shard_map/weights/pallas_call | solution.py:423
  8.3 0.7 %interior.1 = (f32[16,8,640]{2,1,0:T(8,128)S(1)}, f32[16,8,640]{2,1,0:T(8,128)S(1)}) custom-call(f32[16,8,640]{2,1,0:T(8,128)S(1)} %pad_maximum_fusion.waves, f32[16,8,640]{2,1,0:T(8,128)S(1)} %get-tuple-element.35.axis_x, f32[16,8,640]{2,1,0:T(8,128)S(1)} %get-tuple-element.36.axis_y, bf16[512,256]{1,0:T(8,128)(2,1)S(1)} %get-tuple-element.37.taps_first, ...), custom_call_target="tpu_custom_call" | custom-call | flops 4096000 | bytes 1638400 | tf_op jit(solution)/shard_map/interior/pallas_call | solution.py:427
  9.0 0.0 collective-permute-done.1
  9.0 0.0 collective-permute-done
  9.0 0.4 %collective-permute-start.2 = (f32[8,8,640]{2,1,0:T(8,128)S(1)}, f32[8,8,640]{2,1,0:T(8,128)S(1)}, u32[]{:S(2)}, u32[]{:S(2)}) collective-permute-start(f32[8,8,640]{2,1,0:T(8,128)S(1)} %constant_dynamic-update-slice_fusion.edges), channel_id=1, source_target_pairs={{0,1},{1,0},{2,3},{3,2},{4,5},{5,4},{6,7},{7,6},{8,9},{9,8},{10,11... | collective-permute-start | bytes 491528 | tf_op jit(solution)/shard_map/ppermute | solution.py:432
  9.4 0.0 copy-start
  9.4 0.0 copy-start.1
  9.4 0.0 copy-start.9
  9.4 0.0 copy-start.10
  9.4 1.0 %depth.1 = (f32[16,8,640]{2,1,0:T(8,128)S(1)}, f32[16,8,640]{2,1,0:T(8,128)S(1)}) custom-call(f32[16,8,640]{2,1,0:T(8,128)S(1)} %pad_maximum_fusion.waves, f32[2,16,8,640]{3,2,1,0:T(8,128)S(1)} %bitcast.1, f32[8,8,640]{2,1,0:T(8,128)S(1)} %constant_dynamic-update-slice_fusion.edges, f32[16,8,640]{2,1,0:T(8,128)S(1)} %get-tuple-element.35.axis_x, ...), custom_call_target="tpu_custom_call" | custom-call | flops 4096000 | bytes 1638400 | tf_op jit(solution)/shard_map/depth/pallas_call | solution.py:433
  10.4 0.1 collective-permute-done.2.edges_other
  10.5 0.1 copy-done
  10.6 0.2 %copy-done.1 = bf16[640,640]{1,0:T(8,128)(2,1)S(1)} copy-done((bf16[640,640]{1,0:T(8,128)(2,1)S(1)}, bf16[640,640]{1,0:T(8,128)(2,1)}, u32[]{:S(2)}) %copy-start.1) | copy-done | bytes 819224
  10.8 0.0 copy-done.9
  10.8 0.0 copy-done.10
  10.8 0.0 copy-start.11
  10.8 0.0 copy-start.12
  10.8 0.9 %step.1 = (f32[16,8,640]{2,1,0:T(8,128)S(1)}, f32[64,640]{1,0:T(8,128)S(1)}, f32[24,640]{1,0:T(8,128)S(1)}, f32[24,640]{1,0:T(8,128)S(1)}, f32[8,640]{1,0:T(8,128)S(1)}, /*index=5*/f32[8,640]{1,0:T(8,128)S(1)}) custom-call(f32[8,8,640]{2,1,0:T(8,128)S(1)} %constant_dynamic-update-slice_fusion.edges, f32[8,8,640]{2,1,0:T(8,128)S(1)} %collective-permute-done.2.edges_other, ...), custom_call_target="tpu_custom_call" | custom-call | flops 16384000 | bytes 1638400 | tf_op jit(solution)/shard_map/step/pallas_call | solution.py:453
  11.7 3.6 %collective-permute-start.3 = (f32[24,640]{1,0:T(8,128)S(1)}, f32[24,640]{1,0:T(8,128)S(1)}, u32[]{:S(2)}, u32[]{:S(2)}) collective-permute-start(f32[24,640]{1,0:T(8,128)S(1)} %get-tuple-element.56), channel_id=1, source_target_pairs={{0,14},{2,4},{4,2},{6,8},{8,6},{10,12},{12,10},{14,0},{1,15},{3,5}... | collective-permute-start | bytes 184328 | tf_op jit(solution)/shard_map/ppermute | solution.py:469
  15.4 0.4 %collective-permute-start.4 = (f32[24,640]{1,0:T(8,128)S(1)}, f32[24,640]{1,0:T(8,128)S(1)}, u32[]{:S(2)}, u32[]{:S(2)}) collective-permute-start(f32[24,640]{1,0:T(8,128)S(1)} %get-tuple-element.57), channel_id=1, source_target_pairs={{0,2},{2,0},{4,6},{6,4},{8,10},{10,8},{12,14},{14,12},{1,3},{3,1},... | collective-permute-start | bytes 184328 | tf_op jit(solution)/shard_map/ppermute | solution.py:469
  15.7 2.2 %collective-permute-start.5 = (f32[8,640]{1,0:T(8,128)S(1)}, f32[8,640]{1,0:T(8,128)S(1)}, u32[]{:S(2)}, u32[]{:S(2)}) collective-permute-start(f32[8,640]{1,0:T(8,128)S(1)} %get-tuple-element.58), channel_id=1, source_target_pairs={{0,12},{2,14},{4,8},{6,10},{8,4},{10,6},{12,0},{14,2},{1,13},{3,15... | collective-permute-start | bytes 61448 | tf_op jit(solution)/shard_map/ppermute | solution.py:469
  18.0 0.9 %collective-permute-start.6 = (f32[8,640]{1,0:T(8,128)S(1)}, f32[8,640]{1,0:T(8,128)S(1)}, u32[]{:S(2)}, u32[]{:S(2)}) collective-permute-start(f32[8,640]{1,0:T(8,128)S(1)} %get-tuple-element.59), channel_id=1, source_target_pairs={{0,4},{2,6},{4,0},{6,2},{8,12},{10,14},{12,8},{14,10},{1,5},{3,7},... | collective-permute-start | bytes 61448 | tf_op jit(solution)/shard_map/ppermute | solution.py:469
  18.9 0.0 copy-done.11
  18.9 0.0 copy-done.12
  18.9 0.8 %own.1 = (f32[16,4,640]{2,1,0:T(4,128)}, f32[16,4,640]{2,1,0:T(4,128)}, f32[64,640]{1,0:T(8,128)S(1)}) custom-call(f32[16,8,640]{2,1,0:T(8,128)S(1)} %get-tuple-element.51.pressure, f32[64,640]{1,0:T(8,128)S(1)} %get-tuple-element.52.crossline, bf16[64,64]{1,0:T(8,128)(2,1)S(1)} %copy-done.12, bf16[64,64]{1,0:T(8,128)(2,1)S(1)} %copy-done.11), custom_call_target="tpu_custom_call" | custom-call | flops 4096000 | bytes 1638400 | tf_op jit(solution)/shard_map/own/pallas_call | solution.py:471
  19.7 1.6 %collective-permute-done.5.rest_2_ = f32[8,640]{1,0:T(8,128)S(1)} collective-permute-done((f32[8,640]{1,0:T(8,128)S(1)}, f32[8,640]{1,0:T(8,128)S(1)}, u32[]{:S(2)}, u32[]{:S(2)}) %collective-permute-start.5) | collective-permute-done | bytes 20512 | tf_op jit(solution)/shard_map/ppermute | solution.py:469
  21.3 0.4 %collective-permute-done.6.rest_3_ = f32[8,640]{1,0:T(8,128)S(1)} collective-permute-done((f32[8,640]{1,0:T(8,128)S(1)}, f32[8,640]{1,0:T(8,128)S(1)}, u32[]{:S(2)}, u32[]{:S(2)}) %collective-permute-start.6) | collective-permute-done | bytes 20512 | tf_op jit(solution)/shard_map/ppermute | solution.py:469
  21.8 0.0 collective-permute-done.3.rest_0_
  21.8 0.0 collective-permute-done.4.rest_1_
  21.8 0.8 %finish.1 = (f32[8,4,640]{2,1,0:T(4,128)}, f32[4,4,640]{2,1,0:T(4,128)}, f32[2,4,640]{2,1,0:T(4,128)}, f32[2,4,640]{2,1,0:T(4,128)}) custom-call(f32[64,640]{1,0:T(8,128)S(1)} %get-tuple-element.55.mine, f32[24,640]{1,0:T(8,128)S(1)} %collective-permute-done.3.rest_0_, f32[24,640]{1,0:T(8,128)S(1)} %collective-permute-done.4.rest_1_, ...), custom_call_target="tpu_custom_call" | custom-call | flops 819200 | bytes 1638400 | tf_op jit(solution)/shard_map/finish/pallas_call | solution.py:474
  (3 shorter events, 0.0 us)
Async XLA Ops:
  1.7 7.2 %collective-permute-start.1 = (f32[4,8,640]{2,1,0:T(8,128)S(1)}, f32[4,8,640]{2,1,0:T(8,128)S(1)}, u32[]{:S(2)}, u32[]{:S(2)}) collective-permute-start(f32[4,8,640]{2,1,0:T(8,128)S(1)} %get-tuple-element.64), channel_id=1, source_target_pairs={{0,2},{2,0},{4,6},{6,4},{8,10},{10,8},{12,14},{14,12},{1,3},{3,1},... | collective-permute-start | bytes 245768 | tf_op jit(solution)/shard_map/ppermute | solution.py:419
  4.7 2.5 %copy-start.2 = (f32[16,4,640]{2,1,0:T(4,128)S(1)}, f32[16,4,640]{2,1,0:T(4,128)}, u32[]{:S(2)}) copy-start(f32[16,4,640]{2,1,0:T(4,128)} %prior_p.1) | copy-start | bytes 491524
  4.7 2.5 %copy-start.3 = (f32[16,4,640]{2,1,0:T(4,128)S(1)}, f32[16,4,640]{2,1,0:T(4,128)}, u32[]{:S(2)}) copy-start(f32[16,4,640]{2,1,0:T(4,128)} %prior_q.1) | copy-start | bytes 491524
  4.7 2.5 %copy-start.4 = (bf16[16,4,640]{2,1,0:T(4,128)(2,1)S(1)}, bf16[16,4,640]{2,1,0:T(4,128)(2,1)}, u32[]{:S(2)}) copy-start(bf16[16,4,640]{2,1,0:T(4,128)(2,1)} %courant.1) | copy-start | bytes 245764
  4.7 2.5 %copy-start.5 = (bf16[16,4,640]{2,1,0:T(4,128)(2,1)S(1)}, bf16[16,4,640]{2,1,0:T(4,128)(2,1)}, u32[]{:S(2)}) copy-start(bf16[16,4,640]{2,1,0:T(4,128)(2,1)} %epsilon.1) | copy-start | bytes 245764
  4.8 2.5 %copy-start.6 = (bf16[16,4,640]{2,1,0:T(4,128)(2,1)S(1)}, bf16[16,4,640]{2,1,0:T(4,128)(2,1)}, u32[]{:S(2)}) copy-start(bf16[16,4,640]{2,1,0:T(4,128)(2,1)} %delta.1) | copy-start | bytes 245764
  4.8 2.5 %copy-start.7 = (bf16[16,4,640]{2,1,0:T(4,128)(2,1)S(1)}, bf16[16,4,640]{2,1,0:T(4,128)(2,1)}, u32[]{:S(2)}) copy-start(bf16[16,4,640]{2,1,0:T(4,128)(2,1)} %tilt.1) | copy-start | bytes 245764
  4.8 2.5 %copy-start.8 = (bf16[16,4,640]{2,1,0:T(4,128)(2,1)S(1)}, bf16[16,4,640]{2,1,0:T(4,128)(2,1)}, u32[]{:S(2)}) copy-start(bf16[16,4,640]{2,1,0:T(4,128)(2,1)} %azimuth.1) | copy-start | bytes 245764
  4.8 4.2 %collective-permute-start = (f32[4,8,640]{2,1,0:T(8,128)S(1)}, f32[4,8,640]{2,1,0:T(8,128)S(1)}, u32[]{:S(2)}, u32[]{:S(2)}) collective-permute-start(f32[4,8,640]{2,1,0:T(8,128)S(1)} %get-tuple-element.65), channel_id=1, source_target_pairs={{0,1},{1,0},{2,4},{3,5},{4,2},{5,3},{6,8},{7,9},{8,6},{9,7},{10,12... | collective-permute-start | bytes 245768 | tf_op jit(solution)/shard_map/ppermute | solution.py:418
  9.0 1.5 %collective-permute-start.2 = (f32[8,8,640]{2,1,0:T(8,128)S(1)}, f32[8,8,640]{2,1,0:T(8,128)S(1)}, u32[]{:S(2)}, u32[]{:S(2)}) collective-permute-start(f32[8,8,640]{2,1,0:T(8,128)S(1)} %constant_dynamic-update-slice_fusion.edges), channel_id=1, source_target_pairs={{0,1},{1,0},{2,3},{3,2},{4,5},{5,4},{6,7},{7,6},{8,9},{9,8},{10,11... | collective-permute-start | bytes 491528 | tf_op jit(solution)/shard_map/ppermute | solution.py:432
  9.4 1.1 %copy-start = (bf16[640,640]{1,0:T(8,128)(2,1)S(1)}, bf16[640,640]{1,0:T(8,128)(2,1)}, u32[]{:S(2)}) copy-start(bf16[640,640]{1,0:T(8,128)(2,1)} %constant.37.clone.across_low) | copy-start | bytes 2457604
  9.4 1.4 %copy-start.1 = (bf16[640,640]{1,0:T(8,128)(2,1)S(1)}, bf16[640,640]{1,0:T(8,128)(2,1)}, u32[]{:S(2)}) copy-start(bf16[640,640]{1,0:T(8,128)(2,1)} %constant.36.clone.across_high) | copy-start | bytes 2457604
  9.4 1.4 %copy-start.9 = (bf16[64,64]{1,0:T(8,128)(2,1)S(1)}, bf16[64,64]{1,0:T(8,128)(2,1)}, u32[]{:S(2)}) copy-start(bf16[64,64]{1,0:T(8,128)(2,1)} %constant.33.clone.inline_low) | copy-start | bytes 24580
  9.4 1.4 %copy-start.10 = (bf16[64,64]{1,0:T(8,128)(2,1)S(1)}, bf16[64,64]{1,0:T(8,128)(2,1)}, u32[]{:S(2)}) copy-start(bf16[64,64]{1,0:T(8,128)(2,1)} %constant.32.clone.inline_high) | copy-start | bytes 24580
  10.8 8.1 %copy-start.11 = (bf16[64,64]{1,0:T(8,128)(2,1)S(1)}, bf16[64,64]{1,0:T(8,128)(2,1)}, u32[]{:S(2)}) copy-start(bf16[64,64]{1,0:T(8,128)(2,1)} %constant.35.clone.own_low) | copy-start | bytes 24580
  10.8 8.1 %copy-start.12 = (bf16[64,64]{1,0:T(8,128)(2,1)S(1)}, bf16[64,64]{1,0:T(8,128)(2,1)}, u32[]{:S(2)}) copy-start(bf16[64,64]{1,0:T(8,128)(2,1)} %constant.34.clone.own_high) | copy-start | bytes 24580
  11.7 10.0 %collective-permute-start.3 = (f32[24,640]{1,0:T(8,128)S(1)}, f32[24,640]{1,0:T(8,128)S(1)}, u32[]{:S(2)}, u32[]{:S(2)}) collective-permute-start(f32[24,640]{1,0:T(8,128)S(1)} %get-tuple-element.56), channel_id=1, source_target_pairs={{0,14},{2,4},{4,2},{6,8},{8,6},{10,12},{12,10},{14,0},{1,15},{3,5}... | collective-permute-start | bytes 184328 | tf_op jit(solution)/shard_map/ppermute | solution.py:469
  15.4 6.4 %collective-permute-start.4 = (f32[24,640]{1,0:T(8,128)S(1)}, f32[24,640]{1,0:T(8,128)S(1)}, u32[]{:S(2)}, u32[]{:S(2)}) collective-permute-start(f32[24,640]{1,0:T(8,128)S(1)} %get-tuple-element.57), channel_id=1, source_target_pairs={{0,2},{2,0},{4,6},{6,4},{8,10},{10,8},{12,14},{14,12},{1,3},{3,1},... | collective-permute-start | bytes 184328 | tf_op jit(solution)/shard_map/ppermute | solution.py:469
  15.7 5.6 %collective-permute-start.5 = (f32[8,640]{1,0:T(8,128)S(1)}, f32[8,640]{1,0:T(8,128)S(1)}, u32[]{:S(2)}, u32[]{:S(2)}) collective-permute-start(f32[8,640]{1,0:T(8,128)S(1)} %get-tuple-element.58), channel_id=1, source_target_pairs={{0,12},{2,14},{4,8},{6,10},{8,4},{10,6},{12,0},{14,2},{1,13},{3,15... | collective-permute-start | bytes 61448 | tf_op jit(solution)/shard_map/ppermute | solution.py:469
  18.0 3.8 %collective-permute-start.6 = (f32[8,640]{1,0:T(8,128)S(1)}, f32[8,640]{1,0:T(8,128)S(1)}, u32[]{:S(2)}, u32[]{:S(2)}) collective-permute-start(f32[8,640]{1,0:T(8,128)S(1)} %get-tuple-element.59), channel_id=1, source_target_pairs={{0,4},{2,6},{4,0},{6,2},{8,12},{10,14},{12,8},{14,10},{1,5},{3,7},... | collective-permute-start | bytes 61448 | tf_op jit(solution)/shard_map/ppermute | solution.py:469

commit v13 on v9

--- a/solution.py
+++ b/solution.py
@@ -290,7 +290,7 @@
     rows, sub, width = h_own.shape
     lower = lax.axis_index("gz") == 0
     place = lax.axis_index("xy")
-    even, early = place % 2 == 0, place % 4 < 2
+    even = place % 2 == 0
     top = lax.broadcasted_iota(jnp.int32, (sub, width), 0) < 4
 
     slopes = [
@@ -322,27 +322,25 @@
     )
     sends[0][...] = jnp.where(even, to_previous, to_next)
     sends[1][...] = jnp.where(even, to_next, to_previous)
-    sends[2][...] = jnp.where(early, to_second_previous, to_second_next)
-    sends[3][...] = jnp.where(early, to_second_next, to_second_previous)
-
-
-def own_kernel(pressure, crossline, own_high, own_low, next_p, next_q, mine):
+    sends[2][...] = jnp.concatenate([to_second_next, to_second_previous], axis=0)
+
+
+def finish_kernel(
+    takes, pressure, crossline, own_high, own_low, outer, inner, second, next_p, next_q, *outs
+):
     for x in range(pressure.shape[0]):
         next_p[x] = pressure[x, :4]
         next_q[x] = pressure[x, 4:]
-    mine[...] = dot3(own_high[...], own_low[...], *halves(crossline[...]))
-
-
-def finish_kernel(takes, mine, *rest):
-    outer, inner, outer_second, inner_second = (ref[...] for ref in rest[:4])
-    outs = rest[4:]
+    mine = dot3(own_high[...], own_low[...], *halves(crossline[...]))
     place = lax.axis_index("xy")
-    even, early = place % 2 == 0, place % 4 < 2
+    even = place % 2 == 0
+    count, rows = second.shape[0], second.shape[1] // 2
+    before, after = (place // 2 + count - 1) % count, (place // 2 + 1) % count
     received = (
-        jnp.where(even, outer, inner),
-        jnp.where(even, inner, outer),
-        jnp.where(early, outer_second, inner_second),
-        jnp.where(early, inner_second, outer_second),
+        jnp.where(even, outer[...], inner[...]),
+        jnp.where(even, inner[...], outer[...]),
+        second[before, :rows],
+        second[after, rows:],
     )
     at = 0
     for out in outs:
@@ -359,12 +357,9 @@
 
 def pair_swaps(size):
     one = [1 if i % 2 == 0 else -1 for i in range(size)]
-    two = [2 if i % 4 < 2 else -2 for i in range(size)]
     return [
         [(i, (i - one[i]) % size) for i in range(size)],
         [(i, i + one[i]) for i in range(size)],
-        [(i, (i - two[i]) % size) for i in range(size)],
-        [(i, i + two[i]) for i in range(size)],
     ]
 
 
@@ -432,9 +427,10 @@
     inline = parts(np.kron(np.concatenate(pieces), np.eye(4)))
     inline_own = parts(np.kron(own, np.eye(4)))
     flat = jax.ShapeDtypeStruct((layers * rows, width), f32)
+    first, second = gives[0][1], gives[2][1]
     pressure, crossline, *sends = kernel(
         functools.partial(step_kernel, size, gives),
-        [stack, flat] + [jax.ShapeDtypeStruct((count, width), f32) for _, count in gives],
+        [stack, flat] + [jax.ShapeDtypeStruct((count, width), f32) for count in (first, first, 2 * second)],
         400,
         "step",
     )(
@@ -451,19 +447,19 @@
         *inline,
     )
     received = [lax.ppermute(send, "xy", pair) for send, pair in zip(sends, pairs)]
+    lines = [list(range(first, size, 2)) for first in range(2)]
+    received.append(lax.all_gather(sends[2], "xy", axis_index_groups=lines))
     grid = jax.ShapeDtypeStruct(wave_p.shape, f32)
-    next_p, next_q, mine = kernel(own_kernel, [grid, grid, flat], 100, "own")(
-        pressure, crossline, *inline_own
-    )
-    outs = kernel(
+    next_p, next_q, *outs = kernel(
         functools.partial(finish_kernel, [factors[offset][0] for offset in offsets]),
-        [
+        [grid, grid]
+        + [
             jax.ShapeDtypeStruct((count, layers, width), f32)
             for count in (rows // 2, rows // 4, rows // 8, rows // 8)
         ],
         20,
         "finish",
-    )(mine, *received)
+    )(pressure, crossline, *inline_own, *received)
     return (next_p, next_q, *outs)
 
 

time: 22.5 us -> 31.3 us (1.39)
  blocking collectives: 0 us -> 14.1 us
  starting transfers between devices: 11 us -> 7.81 us
  waiting for transfers between devices: 4.22 us -> 2.59 us
  Pallas kernels: 5.16 us -> 4.58 us
    all_gather x0 -> x1, blocking collectives: none -> 14.1 us  [body(): received.append(lax.all_gather(sends[2], 'xy', axis_index_groups=lines))]
    ppermute x4 -> x2, starting transfers between devices: 7.59 us -> 4.44 us  [body(): lax.ppermute(send, 'xy', pair)]
    ppermute x4 -> x2, waiting for transfers between devices: 1.63 us -> 0.01 us  [body(): lax.ppermute(send, 'xy', pair)]
    pallas_call x1 -> x0, Pallas kernels: 0.81 us -> none  [body(): kernel(own_kernel, [grid, grid, flat], 100, 'own')]
  transfers between devices with their start and end apart: 8 -> 6, of which waited for: 3 -> 2; matrix products, arithmetic and copies ran while one was open for 0% -> 0% of each run, Pallas kernels for 15% -> 8%
where the time goes in v13:
time: 31.3 us; the launch traced here: 31.1 us
  blocking collectives  14.1 us (45%)
  starting transfers between devices  7.81 us (25%)
  Pallas kernels  4.58 us (15%)
  waiting for transfers between devices  2.59 us (8%)
  other arithmetic  1.15 us (4%)
  between operations  0.82 us (3%)
    all_gather x1, blocking collectives, body(): received.append(lax.all_gather(sends[2], 'xy', axis_index_groups=lines))  14.1 us
    ppermute x2, starting transfers between devices, body(): lax.ppermute(send, 'xy', pair)  4.44 us
    ppermute x1, starting transfers between devices, body(): inner = lax.ppermute(jnp.where(even, last, leading), 'xy', pairs[1])  2.6 us
    ppermute x1, waiting for transfers between devices, body(): inner = lax.ppermute(jnp.where(even, last, leading), 'xy', pairs[1])  1.49 us
    pallas_call x1, Pallas kernels, body(): kernel(interior_kernel, [stack] * 2, 100, 'interior', [work] * 5)  1.4 us
    concatenate x1, other arithmetic, body(): waves = lax.optimization_barrier(jnp.concatenate([wave_p, wave_q], axis=1))  1.13 us
    ppermute x1, waiting for transfers between devices, body(): edges_other = lax.ppermute(edges, 'gz', cores)  1.09 us
    pallas_call x1, Pallas kernels, body(): kernel(functools.partial(finish_kernel, [factors[offset][0] for offset in...  1.07 us
  transfers between devices with their start and end apart: 6, of which 2 were waited for; matrix products, arithmetic and copies ran while one was open for 0% of the time, Pallas kernels for 8%

profile of v13, /device:TPU:0, one launch (start us, length us, event | category | flops | bytes accessed | tf_op | source)
XLA Modules:
  0.0 31.1 jit_solution(5884227466234355089)
XLA Ops:
  0.6 0.0 copy-start.4
  0.6 0.0 copy-start.5
  0.7 0.0 copy-start.6
  0.7 0.0 copy-start.7
  0.7 0.0 copy-start.8
  0.7 1.1 %pad_maximum_fusion.waves = f32[16,8,640]{2,1,0:T(8,128)S(1)} fusion(f32[16,4,640]{2,1,0:T(4,128)} %param.16, f32[16,4,640]{2,1,0:T(4,128)} %param.15), kind=kLoop, calls=%fused_computation | loop fusion | flops 81920 | bytes 655360 | tf_op jit(solution)/shard_map/concatenate | solution.py:387
  1.8 0.5 %collective-permute-start = (f32[16,8,640]{2,1,0:T(8,128)S(1)}, f32[16,8,640]{2,1,0:T(8,128)S(1)}, u32[]{:S(2)}, u32[]{:S(2)}) collective-permute-start(f32[16,8,640]{2,1,0:T(8,128)S(1)} %pad_maximum_fusion.waves), channel_id=1, source_target_pairs={{0,1},{1,0},{2,3},{3,2},{4,5},{5,4},{6,7},{7,6},{8,9},{9,8},{10,11... | collective-permute-start | bytes 983048 | tf_op jit(solution)/shard_map/ppermute | solution.py:394
  2.3 0.0 copy-start.2
  2.3 0.0 copy-start.3
  2.4 2.6 %collective-permute-start.1 = (f32[4,8,640]{2,1,0:T(8,128)S(1)}, f32[4,8,640]{2,1,0:T(8,128)S(1)}, u32[]{:S(2)}, u32[]{:S(2)}) collective-permute-start(f32[4,8,640]{2,1,0:T(8,128)S(1)} %get-tuple-element.49), channel_id=1, source_target_pairs={{0,2},{2,0},{4,6},{6,4},{8,10},{10,8},{12,14},{14,12},{1,3},{3,1},... | collective-permute-start | bytes 245768 | tf_op jit(solution)/shard_map/ppermute | solution.py:395
  5.0 0.2 collective-permute-start.2
  5.1 0.0 copy-done.4
  5.1 0.0 copy-done.5
  5.1 0.0 copy-done.6
  5.2 0.0 copy-done.7
  5.2 0.0 copy-done.8
  5.2 0.0 copy-done.2
  5.2 0.0 copy-done.3
  5.2 1.0 %weights.1 = (f32[16,8,640]{2,1,0:T(8,128)S(1)}, f32[16,8,640]{2,1,0:T(8,128)S(1)}, f32[16,8,640]{2,1,0:T(8,128)S(1)}, f32[16,8,640]{2,1,0:T(8,128)S(1)}, f32[16...) custom-call(f32[16,8,640]{2,1,0:T(8,128)S(1)} %pad_maximum_fusion.wa, ...), custom_call_target="tpu_custom_call" | custom-call | flops 4096000 | bytes 1638400 | tf_op jit(solution)/shard_map/weights/pallas_call | solution.py:399
  6.1 0.0 collective-permute-done.other
  6.2 1.4 %interior.1 = (f32[16,8,640]{2,1,0:T(8,128)S(1)}, f32[16,8,640]{2,1,0:T(8,128)S(1)}) custom-call(f32[16,8,640]{2,1,0:T(8,128)S(1)} %pad_maximum_fusion.waves, f32[16,8,640]{2,1,0:T(8,128)S(1)} %collective-permute-done.other, f32[16,8,640]{2,1,0:T(8,128)S(1)} %get-tuple-element.27.axis_x, f32[16,8,640]{2,1,0:T(8,128)S(1)} %get-tuple-element.28.axis_y, ...), custom_call_target="tpu_custom_call" | custom-call | flops 4096000 | bytes 1638400 | tf_op jit(solution)/shard_map/interior/pallas_call | solution.py:403
  7.6 1.5 %collective-permute-done.1 = f32[4,8,640]{2,1,0:T(8,128)S(1)} collective-permute-done((f32[4,8,640]{2,1,0:T(8,128)S(1)}, f32[4,8,640]{2,1,0:T(8,128)S(1)}, u32[]{:S(2)}, u32[]{:S(2)}) %collective-permute-start.1) | collective-permute-done | bytes 81952 | tf_op jit(solution)/shard_map/ppermute | solution.py:395
  9.0 0.0 collective-permute-done.2
  9.1 0.0 copy-start
  9.1 0.0 copy-start.1
  9.1 0.1 collective-permute-start.3
  9.2 0.0 copy-start.9
  9.2 0.0 copy-start.10
  9.2 0.3 halo.1
  9.5 1.1 %collective-permute-done.3.edges_other = f32[8,8,640]{2,1,0:T(8,128)S(1)} collective-permute-done((f32[8,8,640]{2,1,0:T(8,128)S(1)}, f32[8,8,640]{2,1,0:T(8,128)S(1)}, u32[]{:S(2)}, u32[]{:S(2)}) %collective-permute-start.3) | collective-permute-done | bytes 163872 | tf_op jit(solution)/shard_map/ppermute | solution.py:408
  10.6 0.0 copy-done
  10.6 0.0 copy-done.1
  10.6 0.0 copy-done.9
  10.6 0.0 copy-done.10
  10.6 0.9 %step.1 = (f32[16,8,640]{2,1,0:T(8,128)S(1)}, f32[64,640]{1,0:T(8,128)S(1)}, f32[24,640]{1,0:T(8,128)S(1)}, f32[24,640]{1,0:T(8,128)S(1)}, f32[16,640]{1,0:T(8,128)S(1)}) custom-call(f32[8,8,640]{2,1,0:T(8,128)S(1)} %constant_dynamic-update-slice_fusion.edges, f32[8,8,640]{2,1,0:T(8,128)S(1)} %collective-permute-done.3.edges_other, ...), custom_call_target="tpu_custom_call" | custom-call | flops 16384000 | bytes 1638400 | tf_op jit(solution)/shard_map/step/pallas_call | solution.py:431
  11.5 3.8 %collective-permute-start.4 = (f32[24,640]{1,0:T(8,128)S(1)}, f32[24,640]{1,0:T(8,128)S(1)}, u32[]{:S(2)}, u32[]{:S(2)}) collective-permute-start(f32[24,640]{1,0:T(8,128)S(1)} %get-tuple-element.45), channel_id=1, source_target_pairs={{0,14},{2,4},{4,2},{6,8},{8,6},{10,12},{12,10},{14,0},{1,15},{3,5}... | collective-permute-start | bytes 184328 | tf_op jit(solution)/shard_map/ppermute | solution.py:449
  15.3 0.6 %collective-permute-start.5 = (f32[24,640]{1,0:T(8,128)S(1)}, f32[24,640]{1,0:T(8,128)S(1)}, u32[]{:S(2)}, u32[]{:S(2)}) collective-permute-start(f32[24,640]{1,0:T(8,128)S(1)} %get-tuple-element.46), channel_id=1, source_target_pairs={{0,2},{2,0},{4,6},{6,4},{8,10},{10,8},{12,14},{14,12},{1,3},{3,1},... | collective-permute-start | bytes 184328 | tf_op jit(solution)/shard_map/ppermute | solution.py:449
  15.9 0.0 copy-start.11
  15.9 0.0 copy-start.12
  15.9 14.1 %all-gather = f32[64,640]{1,0:T(8,128)S(1)} all-gather(f32[16,640]{1,0:T(8,128)S(1)} %get-tuple-element.47), channel_id=2, replica_groups={{0,4,8,12},{2,6,10,14},{1,5,9,13},{3,7,11,15},{16,20,24,28},{18,22,26,3..., dimensions={0}, use_global_device_ids=true | all-gather | bytes 204800 | tf_op jit(solution)/shard_map/all_gather | solution.py:451
  30.0 0.0 collective-permute-done.4.outer
  30.0 0.0 collective-permute-done.5.inner
  30.0 0.0 copy-done.11
  30.0 0.0 copy-done.12
  30.0 1.1 %finish.1 = (f32[16,4,640]{2,1,0:T(4,128)}, f32[16,4,640]{2,1,0:T(4,128)}, f32[8,4,640]{2,1,0:T(4,128)}, f32[4,4,640]{2,1,0:T(4,128)}, f32[2,4,640]{2,1,0:T(4,128)}, /*index=5*/f32[2,4,640]{2,1,0:T(4,128)}) custom-call(f32[16,8,640]{2,1,0:T(8,128)S(1)} %get-tuple-element.43.pressure, f32[64,640]{1,0:T(8,128)S(1)} %get-tuple-element.44.crossline, ...), custom_call_target="tpu_custom_call" | custom-call | flops 819200 | bytes 1638400 | tf_op jit(solution)/shard_map/finish/pallas_call | solution.py:453
  (3 shorter events, 0.0 us)
Async XLA Ops:
  0.6 4.5 %copy-start.4 = (bf16[16,4,640]{2,1,0:T(4,128)(2,1)S(1)}, bf16[16,4,640]{2,1,0:T(4,128)(2,1)}, u32[]{:S(2)}) copy-start(bf16[16,4,640]{2,1,0:T(4,128)(2,1)} %courant.1) | copy-start | bytes 245764
  0.6 4.5 %copy-start.5 = (bf16[16,4,640]{2,1,0:T(4,128)(2,1)S(1)}, bf16[16,4,640]{2,1,0:T(4,128)(2,1)}, u32[]{:S(2)}) copy-start(bf16[16,4,640]{2,1,0:T(4,128)(2,1)} %epsilon.1) | copy-start | bytes 245764
  0.7 4.5 %copy-start.6 = (bf16[16,4,640]{2,1,0:T(4,128)(2,1)S(1)}, bf16[16,4,640]{2,1,0:T(4,128)(2,1)}, u32[]{:S(2)}) copy-start(bf16[16,4,640]{2,1,0:T(4,128)(2,1)} %delta.1) | copy-start | bytes 245764
  0.7 4.5 %copy-start.7 = (bf16[16,4,640]{2,1,0:T(4,128)(2,1)S(1)}, bf16[16,4,640]{2,1,0:T(4,128)(2,1)}, u32[]{:S(2)}) copy-start(bf16[16,4,640]{2,1,0:T(4,128)(2,1)} %tilt.1) | copy-start | bytes 245764
  0.7 4.5 %copy-start.8 = (bf16[16,4,640]{2,1,0:T(4,128)(2,1)S(1)}, bf16[16,4,640]{2,1,0:T(4,128)(2,1)}, u32[]{:S(2)}) copy-start(bf16[16,4,640]{2,1,0:T(4,128)(2,1)} %azimuth.1) | copy-start | bytes 245764
  1.8 4.3 %collective-permute-start = (f32[16,8,640]{2,1,0:T(8,128)S(1)}, f32[16,8,640]{2,1,0:T(8,128)S(1)}, u32[]{:S(2)}, u32[]{:S(2)}) collective-permute-start(f32[16,8,640]{2,1,0:T(8,128)S(1)} %pad_maximum_fusion.waves), channel_id=1, source_target_pairs={{0,1},{1,0},{2,3},{3,2},{4,5},{5,4},{6,7},{7,6},{8,9},{9,8},{10,11... | collective-permute-start | bytes 983048 | tf_op jit(solution)/shard_map/ppermute | solution.py:394
  2.3 2.8 %copy-start.2 = (f32[16,4,640]{2,1,0:T(4,128)S(1)}, f32[16,4,640]{2,1,0:T(4,128)}, u32[]{:S(2)}) copy-start(f32[16,4,640]{2,1,0:T(4,128)} %prior_p.1) | copy-start | bytes 491524
  2.3 2.8 %copy-start.3 = (f32[16,4,640]{2,1,0:T(4,128)S(1)}, f32[16,4,640]{2,1,0:T(4,128)}, u32[]{:S(2)}) copy-start(f32[16,4,640]{2,1,0:T(4,128)} %prior_q.1) | copy-start | bytes 491524
  2.4 6.7 %collective-permute-start.1 = (f32[4,8,640]{2,1,0:T(8,128)S(1)}, f32[4,8,640]{2,1,0:T(8,128)S(1)}, u32[]{:S(2)}, u32[]{:S(2)}) collective-permute-start(f32[4,8,640]{2,1,0:T(8,128)S(1)} %get-tuple-element.49), channel_id=1, source_target_pairs={{0,2},{2,0},{4,6},{6,4},{8,10},{10,8},{12,14},{14,12},{1,3},{3,1},... | collective-permute-start | bytes 245768 | tf_op jit(solution)/shard_map/ppermute | solution.py:395
  5.0 4.1 %collective-permute-start.2 = (f32[4,8,640]{2,1,0:T(8,128)S(1)}, f32[4,8,640]{2,1,0:T(8,128)S(1)}, u32[]{:S(2)}, u32[]{:S(2)}) collective-permute-start(f32[4,8,640]{2,1,0:T(8,128)S(1)} %get-tuple-element.48), channel_id=1, source_target_pairs={{0,1},{1,0},{2,4},{3,5},{4,2},{5,3},{6,8},{7,9},{8,6},{9,7},{10,12... | collective-permute-start | bytes 245768 | tf_op jit(solution)/shard_map/ppermute | solution.py:396
  9.1 1.5 %copy-start = (bf16[640,640]{1,0:T(8,128)(2,1)S(1)}, bf16[640,640]{1,0:T(8,128)(2,1)}, u32[]{:S(2)}) copy-start(bf16[640,640]{1,0:T(8,128)(2,1)} %constant.36.clone.across_high) | copy-start | bytes 2457604
  9.1 1.5 %copy-start.1 = (bf16[640,640]{1,0:T(8,128)(2,1)S(1)}, bf16[640,640]{1,0:T(8,128)(2,1)}, u32[]{:S(2)}) copy-start(bf16[640,640]{1,0:T(8,128)(2,1)} %constant.37.clone.across_low) | copy-start | bytes 2457604
  9.1 1.5 %collective-permute-start.3 = (f32[8,8,640]{2,1,0:T(8,128)S(1)}, f32[8,8,640]{2,1,0:T(8,128)S(1)}, u32[]{:S(2)}, u32[]{:S(2)}) collective-permute-start(f32[8,8,640]{2,1,0:T(8,128)S(1)} %constant_dynamic-update-slice_fusion.edges), channel_id=1, source_target_pairs={{0,1},{1,0},{2,3},{3,2},{4,5},{5,4},{6,7},{7,6},{8,9},{9,8},{10,11... | collective-permute-start | bytes 491528 | tf_op jit(solution)/shard_map/ppermute | solution.py:408
  9.2 1.4 %copy-start.9 = (bf16[64,64]{1,0:T(8,128)(2,1)S(1)}, bf16[64,64]{1,0:T(8,128)(2,1)}, u32[]{:S(2)}) copy-start(bf16[64,64]{1,0:T(8,128)(2,1)} %constant.32.clone.inline_high) | copy-start | bytes 24580
  9.2 1.4 %copy-start.10 = (bf16[64,64]{1,0:T(8,128)(2,1)S(1)}, bf16[64,64]{1,0:T(8,128)(2,1)}, u32[]{:S(2)}) copy-start(bf16[64,64]{1,0:T(8,128)(2,1)} %constant.33.clone.inline_low) | copy-start | bytes 24580
  11.5 18.5 %collective-permute-start.4 = (f32[24,640]{1,0:T(8,128)S(1)}, f32[24,640]{1,0:T(8,128)S(1)}, u32[]{:S(2)}, u32[]{:S(2)}) collective-permute-start(f32[24,640]{1,0:T(8,128)S(1)} %get-tuple-element.45), channel_id=1, source_target_pairs={{0,14},{2,4},{4,2},{6,8},{8,6},{10,12},{12,10},{14,0},{1,15},{3,5}... | collective-permute-start | bytes 184328 | tf_op jit(solution)/shard_map/ppermute | solution.py:449
  15.3 14.7 %collective-permute-start.5 = (f32[24,640]{1,0:T(8,128)S(1)}, f32[24,640]{1,0:T(8,128)S(1)}, u32[]{:S(2)}, u32[]{:S(2)}) collective-permute-start(f32[24,640]{1,0:T(8,128)S(1)} %get-tuple-element.46), channel_id=1, source_target_pairs={{0,2},{2,0},{4,6},{6,4},{8,10},{10,8},{12,14},{14,12},{1,3},{3,1},... | collective-permute-start | bytes 184328 | tf_op jit(solution)/shard_map/ppermute | solution.py:449
  15.9 14.1 %copy-start.11 = (bf16[64,64]{1,0:T(8,128)(2,1)S(1)}, bf16[64,64]{1,0:T(8,128)(2,1)}, u32[]{:S(2)}) copy-start(bf16[64,64]{1,0:T(8,128)(2,1)} %constant.34.clone.own_high) | copy-start | bytes 24580
  15.9 14.1 %copy-start.12 = (bf16[64,64]{1,0:T(8,128)(2,1)S(1)}, bf16[64,64]{1,0:T(8,128)(2,1)}, u32[]{:S(2)}) copy-start(bf16[64,64]{1,0:T(8,128)(2,1)} %constant.35.clone.own_low) | copy-start | bytes 24580

commit v14 on v9

--- a/solution.py
+++ b/solution.py
@@ -31,6 +31,16 @@
         coarse, detail = lift_level(coarse)
         members.append(detail)
     return members + [coarse]
+
+
+def crossline_block(width):
+    tiles = width // LANES
+    members = three_levels(width)
+    tile = tiles // 2
+    wanted = np.concatenate(
+        [m[tile * len(m) // tiles : (tile + 1) * len(m) // tiles] for m in members]
+    )
+    return wanted[:, (tile - 1) * LANES : (tile + 2) * LANES].T
 
 
 def split_bf16(matrix):
@@ -167,6 +177,53 @@
     return high, (value - high.astype(jnp.float32)).astype(jnp.bfloat16)
 
 
+def packed_rows(rows):
+    top = lax.broadcasted_iota(jnp.int32, rows[0].shape, 0) < 4
+    return jnp.concatenate(
+        [
+            jnp.where(top, rows[x], pltpu.roll(rows[x + 1], 4, 0))
+            for x in range(0, len(rows), 2)
+        ],
+        axis=0,
+    )
+
+
+def crossline_of(rows, block_high, block_low):
+    count, width = rows.shape
+    tiles = width // LANES
+
+    def windows(values):
+        parts = [values[:, LANES * t : LANES * (t + 1)] for t in range(tiles)]
+        return [
+            jnp.concatenate([parts[t - 1], parts[t], parts[(t + 1) % tiles]], axis=1)
+            for t in range(tiles)
+        ]
+
+    high, low = (jnp.concatenate(windows(part), axis=0) for part in halves(rows))
+    result = dot3(high, low, block_high, block_low)
+    lane = lax.broadcasted_iota(jnp.int32, (count, LANES), 1)
+    ordered = [jnp.zeros((count, LANES), jnp.float32)] * tiles
+    source, target = 0, 0
+    for size in (LANES // 2, LANES // 4, LANES // 8, LANES // 8):
+        for t in range(tiles):
+            tile, offset = divmod(target + size * t, LANES)
+            piece = result[count * t : count * (t + 1)]
+            shift = (offset - source) % LANES
+            if shift:
+                piece = pltpu.roll(piece, shift, 1)
+            inside = (lane >= offset) & (lane < offset + size)
+            ordered[tile] = jnp.where(inside, piece, ordered[tile])
+        source += size
+        target += size * tiles
+    return jnp.concatenate(ordered, axis=1)
+
+
+def pressure_of(h_one, total, gain_a, gain_b, base):
+    top = lax.broadcasted_iota(jnp.int32, h_one.shape, 0) < 4
+    mixed = jnp.where(top, total - h_one, h_one)
+    return base + gain_a * mixed + gain_b * pltpu.roll(mixed, 4, 0)
+
+
 def depth_neighbours(own, far, lower):
     layer = lax.broadcasted_iota(jnp.int32, own.shape, 0) & 3
     up = far * jnp.where(lower, 1.0, 0.0)
@@ -195,7 +252,27 @@
 
 
 def interior_kernel(
-    waves, other, axis_x, axis_y, axis_z, taps_first, taps_second, h_own, sum_own, dz, dzz, dy, dyy, dzy
+    waves,
+    other,
+    axis_x,
+    axis_y,
+    axis_z,
+    gain_a,
+    gain_b,
+    base,
+    taps_first,
+    taps_second,
+    block_high,
+    block_low,
+    h_own,
+    sum_own,
+    inside,
+    crossline,
+    dz,
+    dzz,
+    dy,
+    dyy,
+    dzy,
 ):
     rows, sub, width = waves.shape
     flat = rows * sub
@@ -226,8 +303,15 @@
         n_x, n_y, n_z = axis_x[x], axis_y[x], axis_z[x]
         h_one = n_x * (n_x * dxx + 2.0 * (n_y * dxy + n_z * dxz))
         h_one = h_one + n_y * (n_y * cross + (2.0 / SCALE_FIRST) * (n_z * dzy[x]))
-        h_own[x] = h_one + n_z * (n_z * dzz[x])
-        sum_own[x] = dxx + cross + dzz[x]
+        h_one = h_one + n_z * (n_z * dzz[x])
+        total = dxx + cross + dzz[x]
+        if 4 <= x < rows - 4:
+            inside[x - 4] = pressure_of(h_one, total, gain_a[x], gain_b[x], base[x])
+        else:
+            row = x if x < 4 else x - rows + 8
+            h_own[row], sum_own[row] = h_one, total
+    ready = packed_rows([inside[x] for x in range(rows - 8)])
+    crossline[...] = crossline_of(ready, block_high[...], block_low[...])
 
 
 def halo_rows(size, edges):
@@ -251,7 +335,7 @@
 
 
 def halo_kernel(size, edges, axis_x, axis_y, h_own, sum_own, taps_first, h_edge, sum_edge):
-    rows, sub, width = h_own.shape
+    rows, sub, _ = axis_x.shape
     values = halo_rows(size, edges)
     parts = jnp.concatenate(halves(jnp.concatenate(values, axis=0)), axis=0)
     slopes = joined(across(parts, taps_first), 8 * sub)
@@ -261,8 +345,8 @@
         dxx = reach(values, row, SECOND[1:], 1.0)
         dxy = reach(slopes, row, [c / SCALE_FIRST for c in FIRST], -1.0)
         n_x = axis_x[x]
-        h_edge[row] = h_own[x] + n_x * (n_x * dxx + 2.0 * (axis_y[x] * dxy))
-        sum_edge[row] = sum_own[x] + dxx
+        h_edge[row] = h_own[row] + n_x * (n_x * dxx + 2.0 * (axis_y[x] * dxy))
+        sum_edge[row] = sum_own[row] + dxx
 
 
 def step_kernel(
@@ -270,8 +354,6 @@
     gives,
     edges,
     edges_other,
-    h_own,
-    sum_own,
     h_edge,
     sum_edge,
     axis_x,
@@ -279,42 +361,32 @@
     gain_a,
     gain_b,
     base,
-    across_high,
-    across_low,
+    block_high,
+    block_low,
+    crossline_inside,
     inline_high,
     inline_low,
-    pressure,
+    outside,
     crossline,
     *sends,
 ):
-    rows, sub, width = h_own.shape
+    rows = axis_x.shape[0]
     lower = lax.axis_index("gz") == 0
     place = lax.axis_index("xy")
     even, early = place % 2 == 0, place % 4 < 2
-    top = lax.broadcasted_iota(jnp.int32, (sub, width), 0) < 4
 
     slopes = [
         first_of(*depth_neighbours(own, far, lower))
         for own, far in zip(halo_rows(size, edges), halo_rows(size, edges_other))
     ]
-    for x in range(rows):
-        row = x if x < 4 else x - rows + 8
-        if 4 <= x < rows - 4:
-            h_one, total = h_own[x], sum_own[x]
-        else:
-            dxz = reach(slopes, row, FIRST, -1.0)
-            h_one, total = h_edge[row] + 2.0 * (axis_x[x] * axis_z[x] * dxz), sum_edge[row]
-        mixed = jnp.where(top, total - h_one, h_one)
-        pressure[x] = base[x] + gain_a[x] * mixed + gain_b[x] * pltpu.roll(mixed, 4, 0)
-
-    packed = jnp.concatenate(
-        [
-            jnp.where(top, pressure[x], pltpu.roll(pressure[x + 1], 4, 0))
-            for x in range(0, rows, 2)
-        ],
-        axis=0,
-    )
-    transformed = dot3(*halves(packed), across_high[...], across_low[...])
+    for row in range(8):
+        x = row if row < 4 else rows - 8 + row
+        dxz = reach(slopes, row, FIRST, -1.0)
+        h_one = h_edge[row] + 2.0 * (axis_x[x] * axis_z[x] * dxz)
+        outside[row] = pressure_of(h_one, sum_edge[row], gain_a[x], gain_b[x], base[x])
+    ready = packed_rows([outside[row] for row in range(8)])
+    edge = crossline_of(ready, block_high[...], block_low[...])
+    transformed = jnp.concatenate([edge[:16], crossline_inside[...], edge[16:]], axis=0)
     crossline[...] = transformed
     parts = dot3(inline_high[...], inline_low[...], *halves(transformed))
     to_next, to_previous, to_second_next, to_second_previous = (
@@ -326,25 +398,24 @@
     sends[3][...] = jnp.where(early, to_second_next, to_second_previous)
 
 
-def own_kernel(pressure, crossline, own_high, own_low, next_p, next_q, mine):
-    for x in range(pressure.shape[0]):
-        next_p[x] = pressure[x, :4]
-        next_q[x] = pressure[x, 4:]
+def own_kernel(inside, outside, crossline, own_high, own_low, next_p, next_q, mine):
+    rows = next_p.shape[0]
+    for x in range(rows):
+        if 4 <= x < rows - 4:
+            value = inside[x - 4]
+        else:
+            value = outside[x if x < 4 else x - rows + 8]
+        next_p[x] = value[:4]
+        next_q[x] = value[4:]
     mine[...] = dot3(own_high[...], own_low[...], *halves(crossline[...]))
 
 
-def finish_kernel(takes, mine, *rest):
-    outer, inner, outer_second, inner_second = (ref[...] for ref in rest[:4])
-    outs = rest[4:]
+def finish_kernel(at, takes, mine, *rest):
+    received, outs = [ref[...] for ref in rest[: len(takes)]], rest[len(takes) :]
     place = lax.axis_index("xy")
-    even, early = place % 2 == 0, place % 4 < 2
-    received = (
-        jnp.where(even, outer, inner),
-        jnp.where(even, inner, outer),
-        jnp.where(early, outer_second, inner_second),
-        jnp.where(early, inner_second, outer_second),
-    )
-    at = 0
+    for first, near in zip(range(0, len(takes), 2), (place % 2 == 0, place % 4 < 2)):
+        outer, inner = received[first : first + 2]
+        received[first : first + 2] = jnp.where(near, outer, inner), jnp.where(near, inner, outer)
     for out in outs:
         for row in range(out.shape[0]):
             total = mine[4 * at : 4 * at + 4]
@@ -375,6 +446,10 @@
     pairs = pair_swaps(size)
     cores = [(0, 1), (1, 0)]
     stack = jax.ShapeDtypeStruct((rows, 8, width), f32)
+
+    def parts(matrix):
+        return [jnp.asarray(part) for part in split_bf16(matrix)]
+
     cells = rows * layers * width
     params = pltpu.CompilerParams(vmem_limit_bytes=16 * 1024 * 1024)
 
@@ -404,14 +479,17 @@
     axis_x, axis_y, axis_z, *gains, taps_first, taps_second = kernel(
         weights_kernel, [stack] * 6 + [taps] * 2, 100, "weights"
     )(waves, prior_p, prior_q, courant, epsilon, thomsen_delta, tilt_angle, azimuth)
+    block = parts(crossline_block(width))
     work = pltpu.VMEM((rows, 8, width), f32)
-    h_own, sum_own = kernel(interior_kernel, [stack] * 2, 100, "interior", [work] * 5)(
-        waves, other, axis_x, axis_y, axis_z, taps_first, taps_second
-    )
+    edge = jax.ShapeDtypeStruct((8, 8, width), f32)
+    inside = jax.ShapeDtypeStruct((rows - 8, 8, width), f32)
+    ready = jax.ShapeDtypeStruct((layers * (rows - 8), width), f32)
+    h_own, sum_own, inside, crossline = kernel(
+        interior_kernel, [edge, edge, inside, ready], 100, "interior", [work] * 5
+    )(waves, other, axis_x, axis_y, axis_z, *gains, taps_first, taps_second, *block)
     h_own, sum_own, inner, outer = lax.optimization_barrier((h_own, sum_own, inner, outer))
     edges = jnp.concatenate([outer, inner], axis=0)
     edges_other = lax.ppermute(edges, "gz", cores)
-    edge = jax.ShapeDtypeStruct((8, 8, width), f32)
     h_edge, sum_edge = kernel(functools.partial(halo_kernel, size), [edge] * 2, 100, "halo")(
         edges, axis_x, axis_y, h_own, sum_own, taps_first
     )
@@ -426,45 +504,31 @@
         gives.append((start, 4 * (give.shape[0] + pad)))
         start += gives[-1][1]
 
-    def parts(matrix):
-        return [jnp.asarray(part) for part in split_bf16(matrix)]
-
     inline = parts(np.kron(np.concatenate(pieces), np.eye(4)))
     inline_own = parts(np.kron(own, np.eye(4)))
     flat = jax.ShapeDtypeStruct((layers * rows, width), f32)
-    pressure, crossline, *sends = kernel(
+    outside, crossline, *sends = kernel(
         functools.partial(step_kernel, size, gives),
-        [stack, flat] + [jax.ShapeDtypeStruct((count, width), f32) for _, count in gives],
+        [edge, flat] + [jax.ShapeDtypeStruct((count, width), f32) for _, count in gives],
         400,
         "step",
-    )(
-        edges,
-        edges_other,
-        h_own,
-        sum_own,
-        h_edge,
-        sum_edge,
-        axis_x,
-        axis_z,
-        *gains,
-        *parts(np.concatenate(three_levels(width)).T),
-        *inline,
-    )
+    )(edges, edges_other, h_edge, sum_edge, axis_x, axis_z, *gains, *block, crossline, *inline)
     received = [lax.ppermute(send, "xy", pair) for send, pair in zip(sends, pairs)]
     grid = jax.ShapeDtypeStruct(wave_p.shape, f32)
     next_p, next_q, mine = kernel(own_kernel, [grid, grid, flat], 100, "own")(
-        pressure, crossline, *inline_own
-    )
-    outs = kernel(
-        functools.partial(finish_kernel, [factors[offset][0] for offset in offsets]),
-        [
-            jax.ShapeDtypeStruct((count, layers, width), f32)
-            for count in (rows // 2, rows // 4, rows // 8, rows // 8)
-        ],
-        20,
-        "finish",
+        inside, outside, crossline, *inline_own
+    )
+    takes = [factors[offset][0] for offset in offsets]
+    counts = (rows // 2, rows // 4, rows // 8, rows // 8)
+    outs = [jax.ShapeDtypeStruct((count, layers, width), f32) for count in counts]
+    first, second = kernel(functools.partial(finish_kernel, 0, takes[:2]), outs[:2], 20, "fine")(
+        mine, *received[:2]
+    )
+    first, *received[2:] = lax.optimization_barrier((first, *received[2:]))
+    third, coarse = kernel(
+        functools.partial(finish_kernel, counts[0] + counts[1], takes), outs[2:], 20, "coarse"
     )(mine, *received)
-    return (next_p, next_q, *outs)
+    return (next_p, next_q, first, second, third, coarse)
 
 
 def solution(mesh):

time: 22.5 us -> 22.3 us (level)
  waiting for transfers between devices: 4.22 us -> 3.02 us
  Pallas kernels: 5.16 us -> 6.11 us
    pallas_call x3 -> x4, Pallas kernels: 3.14 us -> 4.08 us  [the longest x1 1.83 us: body(): kernel(interior_kernel, [edge, edge, inside, ready], 100, 'interior', [wo...]
    ppermute x4, waiting for transfers between devices: 1.63 us -> 0.89 us  [body(): lax.ppermute(send, 'xy', pair)]
    ppermute x1, waiting for transfers between devices: 1.49 us -> 1.02 us  [body(): inner = lax.ppermute(jnp.where(even, last, leading), 'xy', pairs[1])]
  transfers between devices with their start and end apart: 8 -> 8, of which waited for: 3 -> 3; matrix products, arithmetic and copies ran while one was open for 0% -> 0% of each run, Pallas kernels for 15% -> 21%
where the time goes in v14:
time: 22.3 us; the launch traced here: 22.1 us
  starting transfers between devices  11 us (49%)
  Pallas kernels  6.11 us (27%)
  waiting for transfers between devices  3.02 us (14%)
  other arithmetic  1.15 us (5%)
  between operations  0.82 us (4%)
    ppermute x4, starting transfers between devices, body(): lax.ppermute(send, 'xy', pair)  7.6 us
    ppermute x1, starting transfers between devices, body(): inner = lax.ppermute(jnp.where(even, last, leading), 'xy', pairs[1])  2.6 us
    pallas_call x1, Pallas kernels, body(): kernel(interior_kernel, [edge, edge, inside, ready], 100, 'interior', [wo...  1.83 us
    concatenate x1, other arithmetic, body(): waves = lax.optimization_barrier(jnp.concatenate([wave_p, wave_q], axis=1))  1.13 us
    ppermute x1, waiting for transfers between devices, body(): edges_other = lax.ppermute(edges, 'gz', cores)  1.09 us
    ppermute x1, waiting for transfers between devices, body(): inner = lax.ppermute(jnp.where(even, last, leading), 'xy', pairs[1])  1.02 us
    pallas_call x1, Pallas kernels, body(): kernel(weights_kernel, [stack] * 6 + [taps] * 2, 100, 'weights')  0.95 us
    ppermute x4, waiting for transfers between devices, body(): lax.ppermute(send, 'xy', pair)  0.89 us
  transfers between devices with their start and end apart: 8, of which 3 were waited for; matrix products, arithmetic and copies ran while one was open for 0% of the time, Pallas kernels for 21%

profile of v14, /device:TPU:0, one launch (start us, length us, event | category | flops | bytes accessed | tf_op | source)
XLA Modules:
  0.0 22.1 jit_solution(4775134205294001100)
XLA Ops:
  0.6 0.0 copy-start.4
  0.6 0.0 copy-start.5
  0.7 0.0 copy-start.6
  0.7 0.0 copy-start.7
  0.7 0.0 copy-start.8
  0.7 1.1 %pad_maximum_fusion.waves = f32[16,8,640]{2,1,0:T(8,128)S(1)} fusion(f32[16,4,640]{2,1,0:T(4,128)} %param.16, f32[16,4,640]{2,1,0:T(4,128)} %param.15), kind=kLoop, calls=%fused_computation | loop fusion | flops 81920 | bytes 655360 | tf_op jit(solution)/shard_map/concatenate | solution.py:467
  1.8 0.5 %collective-permute-start = (f32[16,8,640]{2,1,0:T(8,128)S(1)}, f32[16,8,640]{2,1,0:T(8,128)S(1)}, u32[]{:S(2)}, u32[]{:S(2)}) collective-permute-start(f32[16,8,640]{2,1,0:T(8,128)S(1)} %pad_maximum_fusion.waves), channel_id=1, source_target_pairs={{0,1},{1,0},{2,3},{3,2},{4,5},{5,4},{6,7},{7,6},{8,9},{9,8},{10,11... | collective-permute-start | bytes 983048 | tf_op jit(solution)/shard_map/ppermute | solution.py:474
  2.3 0.0 copy-start.3
  2.4 2.6 %collective-permute-start.1 = (f32[4,8,640]{2,1,0:T(8,128)S(1)}, f32[4,8,640]{2,1,0:T(8,128)S(1)}, u32[]{:S(2)}, u32[]{:S(2)}) collective-permute-start(f32[4,8,640]{2,1,0:T(8,128)S(1)} %get-tuple-element.75), channel_id=1, source_target_pairs={{0,2},{2,0},{4,6},{6,4},{8,10},{10,8},{12,14},{14,12},{1,3},{3,1},... | collective-permute-start | bytes 245768 | tf_op jit(solution)/shard_map/ppermute | solution.py:475
  5.0 0.0 copy-start
  5.0 0.0 copy-start.1
  5.0 0.2 collective-permute-start.2
  5.1 0.0 copy-done.4
  5.1 0.0 copy-done.5
  5.2 0.0 copy-done.6
  5.2 0.0 copy-done.7
  5.2 0.0 copy-done.8
  5.2 0.0 copy-done.2
  5.2 0.0 copy-done.3
  5.2 1.0 %weights.1 = (f32[16,8,640]{2,1,0:T(8,128)S(1)}, f32[16,8,640]{2,1,0:T(8,128)S(1)}, f32[16,8,640]{2,1,0:T(8,128)S(1)}, f32[16,8,640]{2,1,0:T(8,128)S(1)}, f32[16...) custom-call(f32[16,8,640]{2,1,0:T(8,128)S(1)} %pad_maximum_fusion.wa, ...), custom_call_target="tpu_custom_call" | custom-call | flops 4096000 | bytes 1638400 | tf_op jit(solution)/shard_map/weights/pallas_call | solution.py:479
  6.1 0.0 collective-permute-done.other
  6.2 0.0 copy-done
  6.2 0.0 copy-done.1
  6.2 1.8 %interior.1 = (f32[8,8,640]{2,1,0:T(8,128)S(1)}, f32[8,8,640]{2,1,0:T(8,128)S(1)}, f32[8,8,640]{2,1,0:T(8,128)S(1)}, f32[32,640]{1,0:T(8,128)S(1)}) custom-call(f32[16,8,640]{2,1,0:T(8,128)S(1)} %pad_maximum_fusion.waves, f32[16,8,640]{2,1,0:T(8,128)S(1)} %collective-permute-done.other, f32[16,8,640]{2,1,0:T(8,128)S(1)} %get-tuple-element.40.axis_x, ...), custom_call_target="tpu_custom_call" | custom-call | flops 4096000 | bytes 1638400 | tf_op jit(solution)/shard_map/interior/pallas_call | solution.py:487
  8.0 1.0 %collective-permute-done.1 = f32[4,8,640]{2,1,0:T(8,128)S(1)} collective-permute-done((f32[4,8,640]{2,1,0:T(8,128)S(1)}, f32[4,8,640]{2,1,0:T(8,128)S(1)}, u32[]{:S(2)}, u32[]{:S(2)}) %collective-permute-start.1) | collective-permute-done | bytes 81952 | tf_op jit(solution)/shard_map/ppermute | solution.py:475
  9.0 0.0 collective-permute-done.2
  9.1 0.1 collective-permute-start.3
  9.2 0.0 copy-start.9
  9.2 0.0 copy-start.10
  9.2 0.3 %halo.1 = (f32[8,8,640]{2,1,0:T(8,128)S(1)}, f32[8,8,640]{2,1,0:T(8,128)S(1)}) custom-call(f32[8,8,640]{2,1,0:T(8,128)S(1)} %constant_dynamic-update-slice_fusion.edges, f32[16,8,640]{2,1,0:T(8,128)S(1)} %get-tuple-element.40.axis_x, f32[16,8,640]{2,1,0:T(8,128)S(1)} %get-tuple-element.41.axis_y, f32[8,8,640]{2,1,0:T(8,128)S(1)} %get-tuple-element.53.h_own, ...), custom_call_target="tpu_custom_call" | custom-call | flops 4096000 | bytes 1638400 | tf_op jit(solution)/shard_map/halo/pallas_call | solution.py:493
  9.4 1.1 %collective-permute-done.3.edges_other = f32[8,8,640]{2,1,0:T(8,128)S(1)} collective-permute-done((f32[8,8,640]{2,1,0:T(8,128)S(1)}, f32[8,8,640]{2,1,0:T(8,128)S(1)}, u32[]{:S(2)}, u32[]{:S(2)}) %collective-permute-start.3) | collective-permute-done | bytes 163872 | tf_op jit(solution)/shard_map/ppermute | solution.py:492
  10.5 0.0 copy-done.9
  10.5 0.0 copy-done.10
  10.5 0.0 copy-start.11
  10.6 0.8 %step.1 = (f32[8,8,640]{2,1,0:T(8,128)S(1)}, f32[64,640]{1,0:T(8,128)S(1)}, f32[24,640]{1,0:T(8,128)S(1)}, f32[24,640]{1,0:T(8,128)S(1)}, f32[8,640]{1,0:T(8,128)S(1)}, /*index=5*/f32[8,640]{1,0:T(8,128)S(1)}) custom-call(f32[8,8,640]{2,1,0:T(8,128)S(1)} %constant_dynamic-update-slice_fusion.edges, f32[8,8,640]{2,1,0:T(8,128)S(1)} %collective-permute-done.3.edges_other, ...), custom_call_target="tpu_custom_call" | custom-call | flops 16384000 | bytes 1638400 | tf_op jit(solution)/shard_map/step/pallas_call | solution.py:510
  11.4 3.8 %collective-permute-start.4 = (f32[24,640]{1,0:T(8,128)S(1)}, f32[24,640]{1,0:T(8,128)S(1)}, u32[]{:S(2)}, u32[]{:S(2)}) collective-permute-start(f32[24,640]{1,0:T(8,128)S(1)} %get-tuple-element.63), channel_id=1, source_target_pairs={{0,14},{2,4},{4,2},{6,8},{8,6},{10,12},{12,10},{14,0},{1,15},{3,5}... | collective-permute-start | bytes 184328 | tf_op jit(solution)/shard_map/ppermute | solution.py:516
  15.2 0.6 %collective-permute-start.5 = (f32[24,640]{1,0:T(8,128)S(1)}, f32[24,640]{1,0:T(8,128)S(1)}, u32[]{:S(2)}, u32[]{:S(2)}) collective-permute-start(f32[24,640]{1,0:T(8,128)S(1)} %get-tuple-element.64), channel_id=1, source_target_pairs={{0,2},{2,0},{4,6},{6,4},{8,10},{10,8},{12,14},{14,12},{1,3},{3,1},... | collective-permute-start | bytes 184328 | tf_op jit(solution)/shard_map/ppermute | solution.py:516
  15.8 1.6 %collective-permute-start.6 = (f32[8,640]{1,0:T(8,128)S(1)}, f32[8,640]{1,0:T(8,128)S(1)}, u32[]{:S(2)}, u32[]{:S(2)}) collective-permute-start(f32[8,640]{1,0:T(8,128)S(1)} %get-tuple-element.66), channel_id=1, source_target_pairs={{0,12},{2,14},{4,8},{6,10},{8,4},{10,6},{12,0},{14,2},{1,13},{3,15... | collective-permute-start | bytes 61448 | tf_op jit(solution)/shard_map/ppermute | solution.py:516
  17.4 1.6 %collective-permute-start.7 = (f32[8,640]{1,0:T(8,128)S(1)}, f32[8,640]{1,0:T(8,128)S(1)}, u32[]{:S(2)}, u32[]{:S(2)}) collective-permute-start(f32[8,640]{1,0:T(8,128)S(1)} %get-tuple-element.67), channel_id=1, source_target_pairs={{0,4},{2,6},{4,0},{6,2},{8,12},{10,14},{12,8},{14,10},{1,5},{3,7},... | collective-permute-start | bytes 61448 | tf_op jit(solution)/shard_map/ppermute | solution.py:516
  19.0 0.0 copy-done.11
  19.0 0.0 copy-done.12
  19.0 0.8 %own.1 = (f32[16,4,640]{2,1,0:T(4,128)}, f32[16,4,640]{2,1,0:T(4,128)}, f32[64,640]{1,0:T(8,128)S(1)}) custom-call(f32[8,8,640]{2,1,0:T(8,128)S(1)} %get-tuple-element.48.inside, f32[8,8,640]{2,1,0:T(8,128)S(1)} %get-tuple-element.58.outside, f32[64,640]{1,0:T(8,128)S(1)} %get-tuple-element.59.crossline, bf16[64,64]{1,0:T(8,128)(2,1)S(1)} %copy-done.11, ...), custom_call_target="tpu_custom_call" | custom-call | flops 4096000 | bytes 1638400 | tf_op jit(solution)/shard_map/own/pallas_call | solution.py:518
  19.8 0.0 collective-permute-done.4.rest_0_
  19.8 0.0 collective-permute-done.5.rest_1_
  19.8 0.7 %fine.1 = (f32[8,4,640]{2,1,0:T(4,128)}, f32[4,4,640]{2,1,0:T(4,128)}) custom-call(f32[64,640]{1,0:T(8,128)S(1)} %get-tuple-element.62.mine, f32[24,640]{1,0:T(8,128)S(1)} %collective-permute-done.4.rest_0_, f32[24,640]{1,0:T(8,128)S(1)} %collective-permute-done.5.rest_1_), custom_call_target="tpu_custom_call" | custom-call | flops 819200 | bytes 1638400 | tf_op jit(solution)/shard_map/fine/pallas_call | solution.py:524
  20.5 0.9 %collective-permute-done.6.rest_2_ = f32[8,640]{1,0:T(8,128)S(1)} collective-permute-done((f32[8,640]{1,0:T(8,128)S(1)}, f32[8,640]{1,0:T(8,128)S(1)}, u32[]{:S(2)}, u32[]{:S(2)}) %collective-permute-start.6) | collective-permute-done | bytes 20512 | tf_op jit(solution)/shard_map/ppermute | solution.py:516
  21.4 0.0 collective-permute-done.7.rest_3_
  21.4 0.7 %coarse.1 = (f32[2,4,640]{2,1,0:T(4,128)}, f32[2,4,640]{2,1,0:T(4,128)}) custom-call(f32[64,640]{1,0:T(8,128)S(1)} %get-tuple-element.62.mine, f32[24,640]{1,0:T(8,128)S(1)} %collective-permute-done.4.rest_0_, f32[24,640]{1,0:T(8,128)S(1)} %collective-permute-done.5.rest_1_, f32[8,640]{1,0:T(8,128)S(1)} %collective-permute-done.6.rest_2_, ...), custom_call_target="tpu_custom_call" | custom-call | flops 819200 | bytes 1638400 | tf_op jit(solution)/shard_map/coarse/pallas_call | solution.py:528
  (5 shorter events, 0.0 us)
Async XLA Ops:
  0.6 4.5 %copy-start.4 = (bf16[16,4,640]{2,1,0:T(4,128)(2,1)S(1)}, bf16[16,4,640]{2,1,0:T(4,128)(2,1)}, u32[]{:S(2)}) copy-start(bf16[16,4,640]{2,1,0:T(4,128)(2,1)} %courant.1) | copy-start | bytes 245764
  0.6 4.5 %copy-start.5 = (bf16[16,4,640]{2,1,0:T(4,128)(2,1)S(1)}, bf16[16,4,640]{2,1,0:T(4,128)(2,1)}, u32[]{:S(2)}) copy-start(bf16[16,4,640]{2,1,0:T(4,128)(2,1)} %epsilon.1) | copy-start | bytes 245764
  0.7 4.5 %copy-start.6 = (bf16[16,4,640]{2,1,0:T(4,128)(2,1)S(1)}, bf16[16,4,640]{2,1,0:T(4,128)(2,1)}, u32[]{:S(2)}) copy-start(bf16[16,4,640]{2,1,0:T(4,128)(2,1)} %delta.1) | copy-start | bytes 245764
  0.7 4.5 %copy-start.7 = (bf16[16,4,640]{2,1,0:T(4,128)(2,1)S(1)}, bf16[16,4,640]{2,1,0:T(4,128)(2,1)}, u32[]{:S(2)}) copy-start(bf16[16,4,640]{2,1,0:T(4,128)(2,1)} %tilt.1) | copy-start | bytes 245764
  0.7 4.5 %copy-start.8 = (bf16[16,4,640]{2,1,0:T(4,128)(2,1)S(1)}, bf16[16,4,640]{2,1,0:T(4,128)(2,1)}, u32[]{:S(2)}) copy-start(bf16[16,4,640]{2,1,0:T(4,128)(2,1)} %azimuth.1) | copy-start | bytes 245764
  1.8 4.3 %collective-permute-start = (f32[16,8,640]{2,1,0:T(8,128)S(1)}, f32[16,8,640]{2,1,0:T(8,128)S(1)}, u32[]{:S(2)}, u32[]{:S(2)}) collective-permute-start(f32[16,8,640]{2,1,0:T(8,128)S(1)} %pad_maximum_fusion.waves), channel_id=1, source_target_pairs={{0,1},{1,0},{2,3},{3,2},{4,5},{5,4},{6,7},{7,6},{8,9},{9,8},{10,11... | collective-permute-start | bytes 983048 | tf_op jit(solution)/shard_map/ppermute | solution.py:474
  2.3 2.8 %copy-start.2 = (f32[16,4,640]{2,1,0:T(4,128)S(1)}, f32[16,4,640]{2,1,0:T(4,128)}, u32[]{:S(2)}) copy-start(f32[16,4,640]{2,1,0:T(4,128)} %prior_p.1) | copy-start | bytes 491524
  2.3 2.8 %copy-start.3 = (f32[16,4,640]{2,1,0:T(4,128)S(1)}, f32[16,4,640]{2,1,0:T(4,128)}, u32[]{:S(2)}) copy-start(f32[16,4,640]{2,1,0:T(4,128)} %prior_q.1) | copy-start | bytes 491524
  2.4 6.7 %collective-permute-start.1 = (f32[4,8,640]{2,1,0:T(8,128)S(1)}, f32[4,8,640]{2,1,0:T(8,128)S(1)}, u32[]{:S(2)}, u32[]{:S(2)}) collective-permute-start(f32[4,8,640]{2,1,0:T(8,128)S(1)} %get-tuple-element.75), channel_id=1, source_target_pairs={{0,2},{2,0},{4,6},{6,4},{8,10},{10,8},{12,14},{14,12},{1,3},{3,1},... | collective-permute-start | bytes 245768 | tf_op jit(solution)/shard_map/ppermute | solution.py:475
  5.0 1.2 %copy-start = (bf16[384,128]{1,0:T(8,128)(2,1)S(1)}, bf16[384,128]{1,0:T(8,128)(2,1)}, u32[]{:S(2)}) copy-start(bf16[384,128]{1,0:T(8,128)(2,1)} %constant.32.clone.block_high) | copy-start | bytes 294916
  5.0 1.2 %copy-start.1 = (bf16[384,128]{1,0:T(8,128)(2,1)S(1)}, bf16[384,128]{1,0:T(8,128)(2,1)}, u32[]{:S(2)}) copy-start(bf16[384,128]{1,0:T(8,128)(2,1)} %constant.33.clone.block_low) | copy-start | bytes 294916
  5.0 4.1 %collective-permute-start.2 = (f32[4,8,640]{2,1,0:T(8,128)S(1)}, f32[4,8,640]{2,1,0:T(8,128)S(1)}, u32[]{:S(2)}, u32[]{:S(2)}) collective-permute-start(f32[4,8,640]{2,1,0:T(8,128)S(1)} %get-tuple-element.74), channel_id=1, source_target_pairs={{0,1},{1,0},{2,4},{3,5},{4,2},{5,3},{6,8},{7,9},{8,6},{9,7},{10,12... | collective-permute-start | bytes 245768 | tf_op jit(solution)/shard_map/ppermute | solution.py:476
  9.1 1.5 %collective-permute-start.3 = (f32[8,8,640]{2,1,0:T(8,128)S(1)}, f32[8,8,640]{2,1,0:T(8,128)S(1)}, u32[]{:S(2)}, u32[]{:S(2)}) collective-permute-start(f32[8,8,640]{2,1,0:T(8,128)S(1)} %constant_dynamic-update-slice_fusion.edges), channel_id=1, source_target_pairs={{0,1},{1,0},{2,3},{3,2},{4,5},{5,4},{6,7},{7,6},{8,9},{9,8},{10,11... | collective-permute-start | bytes 491528 | tf_op jit(solution)/shard_map/ppermute | solution.py:492
  9.2 1.4 %copy-start.9 = (bf16[64,64]{1,0:T(8,128)(2,1)S(1)}, bf16[64,64]{1,0:T(8,128)(2,1)}, u32[]{:S(2)}) copy-start(bf16[64,64]{1,0:T(8,128)(2,1)} %constant.34.clone.inline_high) | copy-start | bytes 24580
  9.2 1.4 %copy-start.10 = (bf16[64,64]{1,0:T(8,128)(2,1)S(1)}, bf16[64,64]{1,0:T(8,128)(2,1)}, u32[]{:S(2)}) copy-start(bf16[64,64]{1,0:T(8,128)(2,1)} %constant.35.clone.inline_low) | copy-start | bytes 24580
  10.5 8.4 %copy-start.11 = (bf16[64,64]{1,0:T(8,128)(2,1)S(1)}, bf16[64,64]{1,0:T(8,128)(2,1)}, u32[]{:S(2)}) copy-start(bf16[64,64]{1,0:T(8,128)(2,1)} %constant.36.clone.own_high) | copy-start | bytes 24580
  10.5 8.4 %copy-start.12 = (bf16[64,64]{1,0:T(8,128)(2,1)S(1)}, bf16[64,64]{1,0:T(8,128)(2,1)}, u32[]{:S(2)}) copy-start(bf16[64,64]{1,0:T(8,128)(2,1)} %constant.37.clone.own_low) | copy-start | bytes 24580
  11.4 8.4 %collective-permute-start.4 = (f32[24,640]{1,0:T(8,128)S(1)}, f32[24,640]{1,0:T(8,128)S(1)}, u32[]{:S(2)}, u32[]{:S(2)}) collective-permute-start(f32[24,640]{1,0:T(8,128)S(1)} %get-tuple-element.63), channel_id=1, source_target_pairs={{0,14},{2,4},{4,2},{6,8},{8,6},{10,12},{12,10},{14,0},{1,15},{3,5}... | collective-permute-start | bytes 184328 | tf_op jit(solution)/shard_map/ppermute | solution.py:516
  15.2 4.6 %collective-permute-start.5 = (f32[24,640]{1,0:T(8,128)S(1)}, f32[24,640]{1,0:T(8,128)S(1)}, u32[]{:S(2)}, u32[]{:S(2)}) collective-permute-start(f32[24,640]{1,0:T(8,128)S(1)} %get-tuple-element.64), channel_id=1, source_target_pairs={{0,2},{2,0},{4,6},{6,4},{8,10},{10,8},{12,14},{14,12},{1,3},{3,1},... | collective-permute-start | bytes 184328 | tf_op jit(solution)/shard_map/ppermute | solution.py:516
  15.8 5.6 %collective-permute-start.6 = (f32[8,640]{1,0:T(8,128)S(1)}, f32[8,640]{1,0:T(8,128)S(1)}, u32[]{:S(2)}, u32[]{:S(2)}) collective-permute-start(f32[8,640]{1,0:T(8,128)S(1)} %get-tuple-element.66), channel_id=1, source_target_pairs={{0,12},{2,14},{4,8},{6,10},{8,4},{10,6},{12,0},{14,2},{1,13},{3,15... | collective-permute-start | bytes 61448 | tf_op jit(solution)/shard_map/ppermute | solution.py:516
  17.4 4.0 %collective-permute-start.7 = (f32[8,640]{1,0:T(8,128)S(1)}, f32[8,640]{1,0:T(8,128)S(1)}, u32[]{:S(2)}, u32[]{:S(2)}) collective-permute-start(f32[8,640]{1,0:T(8,128)S(1)} %get-tuple-element.67), channel_id=1, source_target_pairs={{0,4},{2,6},{4,0},{6,2},{8,12},{10,14},{12,8},{14,10},{1,5},{3,7},... | collective-permute-start | bytes 61448 | tf_op jit(solution)/shard_map/ppermute | solution.py:516

commit v15 on v14

--- a/solution.py
+++ b/solution.py
@@ -13,6 +13,7 @@
 LIFT = (-1.586134342, -0.05298011854, 0.8829110762, 0.4435068522)
 ZETA = 1.149604398
 LANES = 128
+LONG = 25_000_000
 SCALE_FIRST, SCALE_SECOND = 840.0, 5040.0
 
 
@@ -393,8 +394,8 @@
         parts[start : start + count] for start, count in gives
     )
     sends[0][...] = jnp.where(even, to_previous, to_next)
-    sends[1][...] = jnp.where(even, to_next, to_previous)
-    sends[2][...] = jnp.where(early, to_second_previous, to_second_next)
+    sends[1][...] = jnp.where(early, to_second_previous, to_second_next)
+    sends[2][...] = jnp.where(even, to_next, to_previous)
     sends[3][...] = jnp.where(early, to_second_next, to_second_previous)
 
 
@@ -410,12 +411,18 @@
     mine[...] = dot3(own_high[...], own_low[...], *halves(crossline[...]))
 
 
-def finish_kernel(at, takes, mine, *rest):
-    received, outs = [ref[...] for ref in rest[: len(takes)]], rest[len(takes) :]
+def finish_kernel(takes, mine, *rest):
+    outer, outer_second, inner, inner_second = (ref[...] for ref in rest[:4])
+    outs = rest[4:]
     place = lax.axis_index("xy")
-    for first, near in zip(range(0, len(takes), 2), (place % 2 == 0, place % 4 < 2)):
-        outer, inner = received[first : first + 2]
-        received[first : first + 2] = jnp.where(near, outer, inner), jnp.where(near, inner, outer)
+    even, early = place % 2 == 0, place % 4 < 2
+    received = (
+        jnp.where(even, outer, inner),
+        jnp.where(even, inner, outer),
+        jnp.where(early, outer_second, inner_second),
+        jnp.where(early, inner_second, outer_second),
+    )
+    at = 0
     for out in outs:
         for row in range(out.shape[0]):
             total = mine[4 * at : 4 * at + 4]
@@ -433,8 +440,8 @@
     two = [2 if i % 4 < 2 else -2 for i in range(size)]
     return [
         [(i, (i - one[i]) % size) for i in range(size)],
+        [(i, (i - two[i]) % size) for i in range(size)],
         [(i, i + one[i]) for i in range(size)],
-        [(i, (i - two[i]) % size) for i in range(size)],
         [(i, i + two[i]) for i in range(size)],
     ]
 
@@ -471,13 +478,15 @@
         for i, j in pairs[0]
         for g in range(2)
     ]
-    other = lax.ppermute(waves, "gz", cores)
-    inner = lax.ppermute(jnp.where(even, last, leading), "xy", pairs[1])
-    outer = lax.ppermute(jnp.where(even, leading, last), ("xy", "gz"), open_outer)
+    to_outer, to_inner = jnp.where(even, leading, last), jnp.where(even, last, leading)
+    to_outer, to_inner, fields = lax.optimization_barrier((to_outer, to_inner, waves))
+    outer = lax.ppermute(to_outer, ("xy", "gz"), open_outer)
+    inner = lax.ppermute(to_inner, "xy", pairs[2])
+    other = lax.ppermute(fields, "gz", cores)
 
     taps = jax.ShapeDtypeStruct((4 * LANES, 2 * LANES), jnp.bfloat16)
     axis_x, axis_y, axis_z, *gains, taps_first, taps_second = kernel(
-        weights_kernel, [stack] * 6 + [taps] * 2, 100, "weights"
+        weights_kernel, [stack] * 6 + [taps] * 2, LONG, "weights"
     )(waves, prior_p, prior_q, courant, epsilon, thomsen_delta, tilt_angle, azimuth)
     block = parts(crossline_block(width))
     work = pltpu.VMEM((rows, 8, width), f32)
@@ -507,28 +516,28 @@
     inline = parts(np.kron(np.concatenate(pieces), np.eye(4)))
     inline_own = parts(np.kron(own, np.eye(4)))
     flat = jax.ShapeDtypeStruct((layers * rows, width), f32)
+    sizes = [gives[k][1] for k in (0, 2, 1, 3)]
     outside, crossline, *sends = kernel(
         functools.partial(step_kernel, size, gives),
-        [edge, flat] + [jax.ShapeDtypeStruct((count, width), f32) for _, count in gives],
+        [edge, flat] + [jax.ShapeDtypeStruct((count, width), f32) for count in sizes],
         400,
         "step",
     )(edges, edges_other, h_edge, sum_edge, axis_x, axis_z, *gains, *block, crossline, *inline)
     received = [lax.ppermute(send, "xy", pair) for send, pair in zip(sends, pairs)]
     grid = jax.ShapeDtypeStruct(wave_p.shape, f32)
-    next_p, next_q, mine = kernel(own_kernel, [grid, grid, flat], 100, "own")(
+    next_p, next_q, mine = kernel(own_kernel, [grid, grid, flat], LONG, "own")(
         inside, outside, crossline, *inline_own
     )
-    takes = [factors[offset][0] for offset in offsets]
-    counts = (rows // 2, rows // 4, rows // 8, rows // 8)
-    outs = [jax.ShapeDtypeStruct((count, layers, width), f32) for count in counts]
-    first, second = kernel(functools.partial(finish_kernel, 0, takes[:2]), outs[:2], 20, "fine")(
-        mine, *received[:2]
-    )
-    first, *received[2:] = lax.optimization_barrier((first, *received[2:]))
-    third, coarse = kernel(
-        functools.partial(finish_kernel, counts[0] + counts[1], takes), outs[2:], 20, "coarse"
+    outs = kernel(
+        functools.partial(finish_kernel, [factors[offset][0] for offset in offsets]),
+        [
+            jax.ShapeDtypeStruct((count, layers, width), f32)
+            for count in (rows // 2, rows // 4, rows // 8, rows // 8)
+        ],
+        20,
+        "finish",
     )(mine, *received)
-    return (next_p, next_q, first, second, third, coarse)
+    return (next_p, next_q, *outs)
 
 
 def solution(mesh):

time: 22.3 us -> 31 us (1.39)
  Pallas kernels: 6.11 us -> 9.09 us
  other arithmetic: 1.15 us -> 3.51 us
  local copies, waits for them, and re-layouts: 0.07 us -> 1.84 us
  waiting for transfers between devices: 3.02 us -> 4.72 us
    ppermute x4, waiting for transfers between devices: 0.89 us -> 3.61 us  [body(): lax.ppermute(send, 'xy', pair)]
    select_n x1, other arithmetic: 0.01 us -> 1.65 us  [body(): jnp.where(even, last, leading)]
    pallas_call x4 -> x3, Pallas kernels: 3.22 us -> 4.47 us  [the longest x1 1.96 us: body(): kernel(weights_kernel, [stack] * 6 + [taps] * 2, LONG, 'weights')]
    pallas_call x1, Pallas kernels: 1.83 us -> 2.9 us  [body(): kernel(interior_kernel, [edge, edge, inside, ready], 100, 'interior', [wo...]
    ppermute x3, waiting for transfers between devices: 1.03 us -> 0.01 us  [the longest x1 0.01 us: body(): other = lax.ppermute(fields, 'gz', cores)]
    unnamed x27, local copies, waits for them, and re-layouts: 0.06 us -> 0.95 us
    concatenate x1, local copies, waits for them, and re-layouts: 0.01 us -> 0.89 us  [body(): edges = jnp.concatenate([outer, inner], axis=0)]
    concatenate x1, other arithmetic: 1.13 us -> 1.86 us  [body(): waves = lax.optimization_barrier(jnp.concatenate([wave_p, wave_q], axis=1))]
  transfers between devices with their start and end apart: 8 -> 8, of which waited for: 3 -> 3; matrix products, arithmetic and copies ran while one was open for 0% -> 0% of each run, Pallas kernels for 21% -> 19%
where the time goes in v15:
time: 31 us; the launch traced here: 30.7 us
  starting transfers between devices  10.7 us (35%)
  Pallas kernels  9.09 us (29%)
  waiting for transfers between devices  4.72 us (15%)
  other arithmetic  3.51 us (11%)
  local copies, waits for them, and re-layouts  1.84 us (6%)
  between operations  0.81 us (3%)
    ppermute x4, starting transfers between devices, body(): lax.ppermute(send, 'xy', pair)  7.24 us
    ppermute x4, waiting for transfers between devices, body(): lax.ppermute(send, 'xy', pair)  3.61 us
    ppermute x1, starting transfers between devices, body(): inner = lax.ppermute(to_inner, 'xy', pairs[2])  2.94 us
    pallas_call x1, Pallas kernels, body(): kernel(interior_kernel, [edge, edge, inside, ready], 100, 'interior', [wo...  2.9 us
    pallas_call x1, Pallas kernels, body(): kernel(weights_kernel, [stack] * 6 + [taps] * 2, LONG, 'weights')  1.96 us
    concatenate x1, other arithmetic, body(): waves = lax.optimization_barrier(jnp.concatenate([wave_p, wave_q], axis=1))  1.86 us
    pallas_call x1, Pallas kernels, body(): kernel(functools.partial(finish_kernel, [factors[offset][0] for offset in...  1.69 us
    select_n x1, other arithmetic, body(): jnp.where(even, last, leading)  1.65 us
  transfers between devices with their start and end apart: 8, of which 3 were waited for; matrix products, arithmetic and copies ran while one was open for 0% of the time, Pallas kernels for 19%

profile of v15, /device:TPU:0, one launch (start us, length us, event | category | flops | bytes accessed | tf_op | source)
XLA Modules:
  0.0 30.7 jit_solution(17035801323446148043)
XLA Ops:
  0.6 0.0 copy-start.6
  0.7 0.0 copy-start.7
  0.7 0.0 copy-start.8
  0.7 0.0 copy-start.9
  0.7 0.0 copy-start.10
  0.7 1.9 %pad_maximum_fusion.waves = f32[16,8,640]{2,1,0:T(8,128)} fusion(f32[16,4,640]{2,1,0:T(4,128)} %param.16, f32[16,4,640]{2,1,0:T(4,128)} %param.15), kind=kLoop, calls=%fused_computation | loop fusion | flops 81920 | bytes 655360 | tf_op jit(solution)/shard_map/concatenate | solution.py:474
  2.6 0.0 copy-start.4
  2.6 0.0 copy-start.5
  2.6 1.6 %slice_select_fusion = (f32[4,8,640]{2,1,0:T(8,128)}, f32[4,8,640]{2,1,0:T(8,128)}) fusion(f32[16,8,640]{2,1,0:T(8,128)} %pad_maximum_fusion.waves, pred[]{:T(512)S(6)} %eq.5), kind=kLoop, calls=%fused_computation.1 | loop fusion | flops 40960 | bytes 327681 | tf_op jit(solution)/shard_map/jit(_where)/select_n | solution.py:481
  4.2 2.9 %collective-permute-start.1 = (f32[4,8,640]{2,1,0:T(8,128)}, f32[4,8,640]{2,1,0:T(8,128)}, u32[]{:S(2)}, u32[]{:S(2)}) collective-permute-start(f32[4,8,640]{2,1,0:T(8,128)} %get-tuple-element.52), channel_id=1, source_target_pairs={{0,2},{2,0},{4,6},{6,4},{8,10},{10,8},{12,14},{14,12},{1,3},{3,1},... | collective-permute-start | bytes 245768 | tf_op jit(solution)/shard_map/ppermute | solution.py:484
  7.1 0.0 collective-permute-start.2
  7.2 0.5 %collective-permute-start = (f32[16,8,640]{2,1,0:T(8,128)}, f32[16,8,640]{2,1,0:T(8,128)}, u32[]{:S(2)}, u32[]{:S(2)}) collective-permute-start(f32[16,8,640]{2,1,0:T(8,128)} %pad_maximum_fusion.waves), channel_id=1, source_target_pairs={{0,1},{1,0},{2,3},{3,2},{4,5},{5,4},{6,7},{7,6},{8,9},{9,8},{10,11... | collective-permute-start | bytes 983048 | tf_op jit(solution)/shard_map/ppermute | solution.py:485
  7.7 0.0 copy-done.6
  7.7 0.0 copy-done.7
  7.7 0.0 copy-done.8
  7.7 0.0 copy-done.9
  7.7 0.0 copy-done.10
  7.7 0.0 copy-done.4
  7.7 0.0 copy-done.5
  7.7 0.0 copy-start
  7.7 0.0 copy-start.1
  7.7 2.0 %weights.1 = (f32[16,8,640]{2,1,0:T(8,128)S(1)}, f32[16,8,640]{2,1,0:T(8,128)S(1)}, f32[16,8,640]{2,1,0:T(8,128)S(1)}, f32[16,8,640]{2,1,0:T(8,128)S(1)}, f32[16...) custom-call(f32[16,8,640]{2,1,0:T(8,128)} %pad_maximum_fusion.waves,, ...), custom_call_target="tpu_custom_call" | custom-call | flops 1024000000000 | bytes 1638400 | tf_op jit(solution)/shard_map/weights/pallas_call | solution.py:488
  9.7 0.0 collective-permute-done.other
  9.7 0.0 copy-done
  9.7 0.0 copy-done.1
  9.7 2.9 %interior.1 = (f32[8,8,640]{2,1,0:T(8,128)S(1)}, f32[8,8,640]{2,1,0:T(8,128)S(1)}, f32[8,8,640]{2,1,0:T(8,128)S(1)}, f32[32,640]{1,0:T(8,128)S(1)}) custom-call(f32[16,8,640]{2,1,0:T(8,128)} %pad_maximum_fusion.waves, f32[16,8,640]{2,1,0:T(8,128)} %collective-permute-done.other, f32[16,8,640]{2,1,0:T(8,128)S(1)} %get-tuple-element.41.axis_x, ...), custom_call_target="tpu_custom_call" | custom-call | flops 4096000 | bytes 1638400 | tf_op jit(solution)/shard_map/interior/pallas_call | solution.py:496
  12.6 0.0 collective-permute-done.1
  12.6 0.0 collective-permute-done.2
  12.7 0.9 %constant_dynamic-update-slice_fusion.1 = f32[8,8,640]{2,1,0:T(8,128)S(1)} fusion(f32[4,8,640]{2,1,0:T(8,128)} %collective-permute-done.2), kind=kLoop, calls=%fused_computation.4 | loop fusion | bytes 163840
  13.5 0.9 %constant_dynamic-update-slice_fusion.edges = f32[8,8,640]{2,1,0:T(8,128)S(1)} fusion(f32[8,8,640]{2,1,0:T(8,128)S(1)} %constant_dynamic-update-slice_fusion.1, f32[4,8,640]{2,1,0:T(8,128)} %collective-permute-done.1), kind=kLoop, calls=%fused_computation.3 | loop fusion | bytes 163840 | tf_op jit(solution)/shard_map/concatenate | solution.py:500
  14.4 0.0 collective-permute-start.3
  14.5 0.3 halo.1
  14.7 1.1 %collective-permute-done.3.edges_other = f32[8,8,640]{2,1,0:T(8,128)S(1)} collective-permute-done((f32[8,8,640]{2,1,0:T(8,128)S(1)}, f32[8,8,640]{2,1,0:T(8,128)S(1)}, u32[]{:S(2)}, u32[]{:S(2)}) %collective-permute-start.3) | collective-permute-done | bytes 163872 | tf_op jit(solution)/shard_map/ppermute | solution.py:501
  15.8 0.0 copy-done.2
  15.8 0.0 copy-done.3
  15.9 1.5 %step.1 = (f32[8,8,640]{2,1,0:T(8,128)S(1)}, f32[64,640]{1,0:T(8,128)S(1)}, f32[24,640]{1,0:T(8,128)}, f32[8,640]{1,0:T(8,128)}, f32[24,640]{1,0:T(8,128)}, /*index=5*/f32[8,640]{1,0:T(8,128)}) custom-call(f32[8,8,640]{2,1,0:T(8,128)S(1)} %constant_dynamic-update-slice_fusion.edges, f32[8,8,640]{2,1,0:T(8,128)S(1)} %collective-permute-done.3.edges_other, ...), custom_call_target="tpu_custom_call" | custom-call | flops 16384000 | bytes 1638400 | tf_op jit(solution)/shard_map/step/pallas_call | solution.py:520
  17.3 3.7 %collective-permute-start.5 = (f32[8,640]{1,0:T(8,128)}, f32[8,640]{1,0:T(8,128)}, u32[]{:S(2)}, u32[]{:S(2)}) collective-permute-start(f32[8,640]{1,0:T(8,128)} %get-tuple-element.67), channel_id=1, source_target_pairs={{0,12},{2,14},{4,8},{6,10},{8,4},{10,6},{12,0},{14,2},{1,13},{3,15... | collective-permute-start | bytes 61448 | tf_op jit(solution)/shard_map/ppermute | solution.py:526
  21.1 0.0 collective-permute-start.7
  21.1 2.9 %collective-permute-start.4 = (f32[24,640]{1,0:T(8,128)}, f32[24,640]{1,0:T(8,128)}, u32[]{:S(2)}, u32[]{:S(2)}) collective-permute-start(f32[24,640]{1,0:T(8,128)} %get-tuple-element.66), channel_id=1, source_target_pairs={{0,14},{2,4},{4,2},{6,8},{8,6},{10,12},{12,10},{14,0},{1,15},{3,5}... | collective-permute-start | bytes 184328 | tf_op jit(solution)/shard_map/ppermute | solution.py:526
  23.9 0.6 %collective-permute-start.6 = (f32[24,640]{1,0:T(8,128)}, f32[24,640]{1,0:T(8,128)}, u32[]{:S(2)}, u32[]{:S(2)}) collective-permute-start(f32[24,640]{1,0:T(8,128)} %get-tuple-element.68), channel_id=1, source_target_pairs={{0,2},{2,0},{4,6},{6,4},{8,10},{10,8},{12,14},{14,12},{1,3},{3,1},... | collective-permute-start | bytes 184328 | tf_op jit(solution)/shard_map/ppermute | solution.py:526
  24.6 0.0 copy-done.11
  24.6 0.0 copy-done.12
  24.6 0.8 %own.1 = (f32[16,4,640]{2,1,0:T(4,128)}, f32[16,4,640]{2,1,0:T(4,128)}, f32[64,640]{1,0:T(8,128)S(1)}) custom-call(f32[8,8,640]{2,1,0:T(8,128)S(1)} %get-tuple-element.49.inside, f32[8,8,640]{2,1,0:T(8,128)S(1)} %get-tuple-element.61.outside, f32[64,640]{1,0:T(8,128)S(1)} %get-tuple-element.62.crossline, bf16[64,64]{1,0:T(8,128)(2,1)S(1)} %copy-done.12, ...), custom_call_target="tpu_custom_call" | custom-call | flops 1024000000000 | bytes 1638400 | tf_op jit(solution)/shard_map/own/pallas_call | solution.py:528
  25.4 0.0 collective-permute-done.5.rest_1_
  25.4 0.0 collective-permute-done.7.rest_3_
  25.4 3.0 %collective-permute-done.4.rest_0_ = f32[24,640]{1,0:T(8,128)} collective-permute-done((f32[24,640]{1,0:T(8,128)}, f32[24,640]{1,0:T(8,128)}, u32[]{:S(2)}, u32[]{:S(2)}) %collective-permute-start.4) | collective-permute-done | bytes 61472 | tf_op jit(solution)/shard_map/ppermute | solution.py:526
  28.4 0.6 %collective-permute-done.6.rest_2_ = f32[24,640]{1,0:T(8,128)} collective-permute-done((f32[24,640]{1,0:T(8,128)}, f32[24,640]{1,0:T(8,128)}, u32[]{:S(2)}, u32[]{:S(2)}) %collective-permute-start.6) | collective-permute-done | bytes 61472 | tf_op jit(solution)/shard_map/ppermute | solution.py:526
  29.0 1.7 %finish.1 = (f32[8,4,640]{2,1,0:T(4,128)}, f32[4,4,640]{2,1,0:T(4,128)}, f32[2,4,640]{2,1,0:T(4,128)}, f32[2,4,640]{2,1,0:T(4,128)}) custom-call(f32[64,640]{1,0:T(8,128)S(1)} %get-tuple-element.65.mine, f32[24,640]{1,0:T(8,128)} %collective-permute-done.4.rest_0_, f32[8,640]{1,0:T(8,128)} %collective-permute-done.5.rest_1_, ...), custom_call_target="tpu_custom_call" | custom-call | flops 819200 | bytes 1638400 | tf_op jit(solution)/shard_map/finish/pallas_call | solution.py:531
  (4 shorter events, 0.0 us)
Async XLA Ops:
  0.6 7.0 %copy-start.6 = (bf16[16,4,640]{2,1,0:T(4,128)(2,1)S(1)}, bf16[16,4,640]{2,1,0:T(4,128)(2,1)}, u32[]{:S(2)}) copy-start(bf16[16,4,640]{2,1,0:T(4,128)(2,1)} %courant.1) | copy-start | bytes 245764
  0.7 7.0 %copy-start.7 = (bf16[16,4,640]{2,1,0:T(4,128)(2,1)S(1)}, bf16[16,4,640]{2,1,0:T(4,128)(2,1)}, u32[]{:S(2)}) copy-start(bf16[16,4,640]{2,1,0:T(4,128)(2,1)} %epsilon.1) | copy-start | bytes 245764
  0.7 7.0 %copy-start.8 = (bf16[16,4,640]{2,1,0:T(4,128)(2,1)S(1)}, bf16[16,4,640]{2,1,0:T(4,128)(2,1)}, u32[]{:S(2)}) copy-start(bf16[16,4,640]{2,1,0:T(4,128)(2,1)} %delta.1) | copy-start | bytes 245764
  0.7 7.0 %copy-start.9 = (bf16[16,4,640]{2,1,0:T(4,128)(2,1)S(1)}, bf16[16,4,640]{2,1,0:T(4,128)(2,1)}, u32[]{:S(2)}) copy-start(bf16[16,4,640]{2,1,0:T(4,128)(2,1)} %tilt.1) | copy-start | bytes 245764
  0.7 7.0 %copy-start.10 = (bf16[16,4,640]{2,1,0:T(4,128)(2,1)S(1)}, bf16[16,4,640]{2,1,0:T(4,128)(2,1)}, u32[]{:S(2)}) copy-start(bf16[16,4,640]{2,1,0:T(4,128)(2,1)} %azimuth.1) | copy-start | bytes 245764
  2.6 5.1 %copy-start.4 = (f32[16,4,640]{2,1,0:T(4,128)S(1)}, f32[16,4,640]{2,1,0:T(4,128)}, u32[]{:S(2)}) copy-start(f32[16,4,640]{2,1,0:T(4,128)} %prior_p.1) | copy-start | bytes 491524
  2.6 5.1 %copy-start.5 = (f32[16,4,640]{2,1,0:T(4,128)S(1)}, f32[16,4,640]{2,1,0:T(4,128)}, u32[]{:S(2)}) copy-start(f32[16,4,640]{2,1,0:T(4,128)} %prior_q.1) | copy-start | bytes 491524
  4.2 8.4 %collective-permute-start.1 = (f32[4,8,640]{2,1,0:T(8,128)}, f32[4,8,640]{2,1,0:T(8,128)}, u32[]{:S(2)}, u32[]{:S(2)}) collective-permute-start(f32[4,8,640]{2,1,0:T(8,128)} %get-tuple-element.52), channel_id=1, source_target_pairs={{0,2},{2,0},{4,6},{6,4},{8,10},{10,8},{12,14},{14,12},{1,3},{3,1},... | collective-permute-start | bytes 245768 | tf_op jit(solution)/shard_map/ppermute | solution.py:484
  7.1 5.5 %collective-permute-start.2 = (f32[4,8,640]{2,1,0:T(8,128)}, f32[4,8,640]{2,1,0:T(8,128)}, u32[]{:S(2)}, u32[]{:S(2)}) collective-permute-start(f32[4,8,640]{2,1,0:T(8,128)} %get-tuple-element.53), channel_id=1, source_target_pairs={{0,1},{1,0},{2,4},{3,5},{4,2},{5,3},{6,8},{7,9},{8,6},{9,7},{10,12... | collective-permute-start | bytes 245768 | tf_op jit(solution)/shard_map/ppermute | solution.py:483
  7.2 2.5 %collective-permute-start = (f32[16,8,640]{2,1,0:T(8,128)}, f32[16,8,640]{2,1,0:T(8,128)}, u32[]{:S(2)}, u32[]{:S(2)}) collective-permute-start(f32[16,8,640]{2,1,0:T(8,128)} %pad_maximum_fusion.waves), channel_id=1, source_target_pairs={{0,1},{1,0},{2,3},{3,2},{4,5},{5,4},{6,7},{7,6},{8,9},{9,8},{10,11... | collective-permute-start | bytes 983048 | tf_op jit(solution)/shard_map/ppermute | solution.py:485
  7.7 2.0 %copy-start = (bf16[384,128]{1,0:T(8,128)(2,1)S(1)}, bf16[384,128]{1,0:T(8,128)(2,1)}, u32[]{:S(2)}) copy-start(bf16[384,128]{1,0:T(8,128)(2,1)} %constant.33.clone.block_low) | copy-start | bytes 294916
  7.7 2.0 %copy-start.1 = (bf16[384,128]{1,0:T(8,128)(2,1)S(1)}, bf16[384,128]{1,0:T(8,128)(2,1)}, u32[]{:S(2)}) copy-start(bf16[384,128]{1,0:T(8,128)(2,1)} %constant.32.clone.block_high) | copy-start | bytes 294916
  14.4 1.4 %collective-permute-start.3 = (f32[8,8,640]{2,1,0:T(8,128)S(1)}, f32[8,8,640]{2,1,0:T(8,128)S(1)}, u32[]{:S(2)}, u32[]{:S(2)}) collective-permute-start(f32[8,8,640]{2,1,0:T(8,128)S(1)} %constant_dynamic-update-slice_fusion.edges), channel_id=1, source_target_pairs={{0,1},{1,0},{2,3},{3,2},{4,5},{5,4},{6,7},{7,6},{8,9},{9,8},{10,11... | collective-permute-start | bytes 491528 | tf_op jit(solution)/shard_map/ppermute | solution.py:501
  14.5 1.4 %copy-start.2 = (bf16[64,64]{1,0:T(8,128)(2,1)S(1)}, bf16[64,64]{1,0:T(8,128)(2,1)}, u32[]{:S(2)}) copy-start(bf16[64,64]{1,0:T(8,128)(2,1)} %constant.35.clone.inline_low) | copy-start | bytes 24580
  14.5 1.4 %copy-start.3 = (bf16[64,64]{1,0:T(8,128)(2,1)S(1)}, bf16[64,64]{1,0:T(8,128)(2,1)}, u32[]{:S(2)}) copy-start(bf16[64,64]{1,0:T(8,128)(2,1)} %constant.34.clone.inline_high) | copy-start | bytes 24580
  15.8 8.7 %copy-start.11 = (bf16[64,64]{1,0:T(8,128)(2,1)S(1)}, bf16[64,64]{1,0:T(8,128)(2,1)}, u32[]{:S(2)}) copy-start(bf16[64,64]{1,0:T(8,128)(2,1)} %constant.37.clone.own_low) | copy-start | bytes 24580
  15.8 8.7 %copy-start.12 = (bf16[64,64]{1,0:T(8,128)(2,1)S(1)}, bf16[64,64]{1,0:T(8,128)(2,1)}, u32[]{:S(2)}) copy-start(bf16[64,64]{1,0:T(8,128)(2,1)} %constant.36.clone.own_high) | copy-start | bytes 24580
  17.3 8.1 %collective-permute-start.5 = (f32[8,640]{1,0:T(8,128)}, f32[8,640]{1,0:T(8,128)}, u32[]{:S(2)}, u32[]{:S(2)}) collective-permute-start(f32[8,640]{1,0:T(8,128)} %get-tuple-element.67), channel_id=1, source_target_pairs={{0,12},{2,14},{4,8},{6,10},{8,4},{10,6},{12,0},{14,2},{1,13},{3,15... | collective-permute-start | bytes 61448 | tf_op jit(solution)/shard_map/ppermute | solution.py:526
  21.1 4.3 %collective-permute-start.7 = (f32[8,640]{1,0:T(8,128)}, f32[8,640]{1,0:T(8,128)}, u32[]{:S(2)}, u32[]{:S(2)}) collective-permute-start(f32[8,640]{1,0:T(8,128)} %get-tuple-element.69), channel_id=1, source_target_pairs={{0,4},{2,6},{4,0},{6,2},{8,12},{10,14},{12,8},{14,10},{1,5},{3,7},... | collective-permute-start | bytes 61448 | tf_op jit(solution)/shard_map/ppermute | solution.py:526
  21.1 7.3 %collective-permute-start.4 = (f32[24,640]{1,0:T(8,128)}, f32[24,640]{1,0:T(8,128)}, u32[]{:S(2)}, u32[]{:S(2)}) collective-permute-start(f32[24,640]{1,0:T(8,128)} %get-tuple-element.66), channel_id=1, source_target_pairs={{0,14},{2,4},{4,2},{6,8},{8,6},{10,12},{12,10},{14,0},{1,15},{3,5}... | collective-permute-start | bytes 184328 | tf_op jit(solution)/shard_map/ppermute | solution.py:526
  23.9 5.1 %collective-permute-start.6 = (f32[24,640]{1,0:T(8,128)}, f32[24,640]{1,0:T(8,128)}, u32[]{:S(2)}, u32[]{:S(2)}) collective-permute-start(f32[24,640]{1,0:T(8,128)} %get-tuple-element.68), channel_id=1, source_target_pairs={{0,2},{2,0},{4,6},{6,4},{8,10},{10,8},{12,14},{14,12},{1,3},{3,1},... | collective-permute-start | bytes 184328 | tf_op jit(solution)/shard_map/ppermute | solution.py:526

commit v16 on v15

--- a/solution.py
+++ b/solution.py
@@ -13,7 +13,7 @@
 LIFT = (-1.586134342, -0.05298011854, 0.8829110762, 0.4435068522)
 ZETA = 1.149604398
 LANES = 128
-LONG = 25_000_000
+LONG = 250_000
 SCALE_FIRST, SCALE_SECOND = 840.0, 5040.0
 
 
@@ -103,6 +103,11 @@
     if sign < 0:
         values = jnp.where(offset < 0, -values, values)
     return values.astype(jnp.bfloat16)
+
+
+def taps_kernel(taps_first, taps_second):
+    taps_first[...] = band(taps_first.shape, FIRST, -1.0, SCALE_FIRST)
+    taps_second[...] = band(taps_second.shape, SECOND[1:], 1.0, SCALE_SECOND)
 
 
 def weights_kernel(
@@ -120,12 +125,8 @@
     gain_a,
     gain_b,
     base,
-    taps_first,
-    taps_second,
 ):
     rows = waves.shape[0]
-    taps_first[...] = band(taps_first.shape, FIRST, -1.0, SCALE_FIRST)
-    taps_second[...] = band(taps_second.shape, SECOND[1:], 1.0, SCALE_SECOND)
     top = lax.broadcasted_iota(jnp.int32, waves.shape[1:], 0) < 4
 
     def swap(value):
@@ -485,9 +486,10 @@
     other = lax.ppermute(fields, "gz", cores)
 
     taps = jax.ShapeDtypeStruct((4 * LANES, 2 * LANES), jnp.bfloat16)
-    axis_x, axis_y, axis_z, *gains, taps_first, taps_second = kernel(
-        weights_kernel, [stack] * 6 + [taps] * 2, LONG, "weights"
-    )(waves, prior_p, prior_q, courant, epsilon, thomsen_delta, tilt_angle, azimuth)
+    taps_first, taps_second = kernel(taps_kernel, [taps] * 2, LONG, "taps")()
+    axis_x, axis_y, axis_z, *gains = kernel(weights_kernel, [stack] * 6, 100, "weights")(
+        waves, prior_p, prior_q, courant, epsilon, thomsen_delta, tilt_angle, azimuth
+    )
     block = parts(crossline_block(width))
     work = pltpu.VMEM((rows, 8, width), f32)
     edge = jax.ShapeDtypeStruct((8, 8, width), f32)
@@ -525,7 +527,7 @@
     )(edges, edges_other, h_edge, sum_edge, axis_x, axis_z, *gains, *block, crossline, *inline)
     received = [lax.ppermute(send, "xy", pair) for send, pair in zip(sends, pairs)]
     grid = jax.ShapeDtypeStruct(wave_p.shape, f32)
-    next_p, next_q, mine = kernel(own_kernel, [grid, grid, flat], LONG, "own")(
+    next_p, next_q, mine = kernel(own_kernel, [grid, grid, flat], 100, "own")(
         inside, outside, crossline, *inline_own
     )
     outs = kernel(

time: 31 us -> 22.2 us (0.72)
  Pallas kernels: 9.09 us -> 5.48 us
  other arithmetic: 3.51 us -> 1.08 us
  waiting for transfers between devices: 4.72 us -> 2.66 us
  local copies, waits for them, and re-layouts: 1.84 us -> 0.09 us
  starting transfers between devices: 10.7 us -> 11.9 us
    ppermute x4, waiting for transfers between devices: 3.61 us -> 1.69 us  [body(): lax.ppermute(send, 'xy', pair)]
    select_n x1, other arithmetic: 1.65 us -> 0.02 us  [body(): jnp.where(even, last, leading)]
    pallas_call x1, Pallas kernels: 2.9 us -> 1.83 us  [body(): kernel(interior_kernel, [edge, edge, inside, ready], 100, 'interior', [wo...]
    pallas_call x2 -> x3, Pallas kernels: 2.78 us -> 1.77 us  [the longest x1 0.82 us: body(): kernel(own_kernel, [grid, grid, flat], 100, 'own')]
    concatenate x1, local copies, waits for them, and re-layouts: 0.89 us -> 0.01 us  [body(): edges = jnp.concatenate([outer, inner], axis=0)]
    unnamed x27, local copies, waits for them, and re-layouts: 0.95 us -> 0.08 us
    pallas_call x1, Pallas kernels: 1.69 us -> 0.82 us  [body(): kernel(functools.partial(finish_kernel, [factors[offset][0] for offset in...]
    concatenate x1, other arithmetic: 1.86 us -> 1.07 us  [body(): waves = lax.optimization_barrier(jnp.concatenate([wave_p, wave_q], axis=1))]
  transfers between devices with their start and end apart: 8 -> 8, of which waited for: 3 -> 3; matrix products, arithmetic and copies ran while one was open for 0% -> 0% of each run, Pallas kernels for 19% -> 17%
where the time goes in v16:
time: 22.2 us; the launch traced here: 22.1 us
  starting transfers between devices  11.9 us (54%)
  Pallas kernels  5.48 us (25%)
  waiting for transfers between devices  2.66 us (12%)
  other arithmetic  1.08 us (5%)
  between operations  0.86 us (4%)
    ppermute x4, starting transfers between devices, body(): lax.ppermute(send, 'xy', pair)  7.95 us
    ppermute x1, starting transfers between devices, body(): inner = lax.ppermute(to_inner, 'xy', pairs[2])  3 us
    pallas_call x1, Pallas kernels, body(): kernel(interior_kernel, [edge, edge, inside, ready], 100, 'interior', [wo...  1.83 us
    ppermute x4, waiting for transfers between devices, body(): lax.ppermute(send, 'xy', pair)  1.69 us
    concatenate x1, other arithmetic, body(): waves = lax.optimization_barrier(jnp.concatenate([wave_p, wave_q], axis=1))  1.07 us
    pallas_call x1, Pallas kernels, body(): kernel(functools.partial(finish_kernel, [factors[offset][0] for offset in...  0.82 us
    pallas_call x1, Pallas kernels, body(): kernel(own_kernel, [grid, grid, flat], 100, 'own')  0.82 us
    pallas_call x1, Pallas kernels, body(): kernel(functools.partial(step_kernel, size, gives), [edge, flat] + [jax.S...  0.8 us
  transfers between devices with their start and end apart: 8, of which 3 were waited for; matrix products, arithmetic and copies ran while one was open for 0% of the time, Pallas kernels for 17%

profile of v16, /device:TPU:0, one launch (start us, length us, event | category | flops | bytes accessed | tf_op | source)
XLA Modules:
  0.0 22.1 jit_solution(7062738755579095351)
XLA Ops:
  0.6 1.1 %pad_maximum_fusion.waves = f32[16,8,640]{2,1,0:T(8,128)S(1)} fusion(f32[16,4,640]{2,1,0:T(4,128)} %param.16, f32[16,4,640]{2,1,0:T(4,128)} %param.15), kind=kLoop, calls=%fused_computation | loop fusion | flops 81920 | bytes 655360 | tf_op jit(solution)/shard_map/concatenate | solution.py:475
  1.7 0.0 copy-start.2
  1.7 0.0 copy-start.3
  1.8 0.0 copy-start.4
  1.8 0.0 copy-start.5
  1.8 0.0 copy-start.6
  1.8 0.0 copy-start.7
  1.8 0.0 copy-start.8
  1.8 3.0 %collective-permute-start.1 = (f32[4,8,640]{2,1,0:T(8,128)S(1)}, f32[4,8,640]{2,1,0:T(8,128)S(1)}, u32[]{:S(2)}, u32[]{:S(2)}) collective-permute-start(f32[4,8,640]{2,1,0:T(8,128)S(1)} %get-tuple-element.52), channel_id=1, source_target_pairs={{0,2},{2,0},{4,6},{6,4},{8,10},{10,8},{12,14},{14,12},{1,3},{3,1},... | collective-permute-start | bytes 245768 | tf_op jit(solution)/shard_map/ppermute | solution.py:485
  4.8 0.0 collective-permute-start.2
  4.8 0.5 %collective-permute-start = (f32[16,8,640]{2,1,0:T(8,128)S(1)}, f32[16,8,640]{2,1,0:T(8,128)S(1)}, u32[]{:S(2)}, u32[]{:S(2)}) collective-permute-start(f32[16,8,640]{2,1,0:T(8,128)S(1)} %pad_maximum_fusion.waves), channel_id=1, source_target_pairs={{0,1},{1,0},{2,3},{3,2},{4,5},{5,4},{6,7},{7,6},{8,9},{9,8},{10,11... | collective-permute-start | bytes 983048 | tf_op jit(solution)/shard_map/ppermute | solution.py:486
  5.3 0.2 %taps.1 = (bf16[512,256]{1,0:T(8,128)(2,1)S(1)}, bf16[512,256]{1,0:T(8,128)(2,1)S(1)}) custom-call(), custom_call_target="tpu_custom_call" | custom-call | flops 10240000000 | bytes 1638400 | tf_op jit(solution)/shard_map/taps/pallas_call | solution.py:489
  5.6 0.0 copy-done.2
  5.6 0.0 copy-done.3
  5.6 0.0 copy-done.4
  5.6 0.0 copy-done.5
  5.6 0.0 copy-done.6
  5.6 0.0 copy-done.7
  5.6 0.0 copy-done.8
  5.7 0.0 copy-start
  5.7 0.0 copy-start.1
  5.7 0.7 %weights.1 = (f32[16,8,640]{2,1,0:T(8,128)S(1)}, f32[16,8,640]{2,1,0:T(8,128)S(1)}, f32[16,8,640]{2,1,0:T(8,128)S(1)}, f32[16,8,640]{2,1,0:T(8,128)S(1)}, f32[16...) custom-call(f32[16,8,640]{2,1,0:T(8,128)S(1)} %pad_maximum_fusion.waves, f32[16,4,640]{2,1,0:T(4,128)S(1)} %copy-done.2, ...), custom_call_target="tpu_custom_call" | custom-call | flops 4096000 | bytes 1638400 | tf_op jit(solution)/shard_map/weights/pallas_call | solution.py:490
  6.4 0.2 collective-permute-done.other
  6.6 0.0 copy-done
  6.6 0.0 copy-done.1
  6.6 1.8 %interior.1 = (f32[8,8,640]{2,1,0:T(8,128)S(1)}, f32[8,8,640]{2,1,0:T(8,128)S(1)}, f32[8,8,640]{2,1,0:T(8,128)S(1)}, f32[32,640]{1,0:T(8,128)S(1)}) custom-call(f32[16,8,640]{2,1,0:T(8,128)S(1)} %pad_maximum_fusion.waves, f32[16,8,640]{2,1,0:T(8,128)S(1)} %collective-permute-done.other, f32[16,8,640]{2,1,0:T(8,128)S(1)} %get-tuple-element.41.axis_x, ...), custom_call_target="tpu_custom_call" | custom-call | flops 4096000 | bytes 1638400 | tf_op jit(solution)/shard_map/interior/pallas_call | solution.py:498
  8.4 0.0 collective-permute-done.1
  8.5 0.0 collective-permute-done.2
  8.5 0.4 %collective-permute-start.3 = (f32[8,8,640]{2,1,0:T(8,128)S(1)}, f32[8,8,640]{2,1,0:T(8,128)S(1)}, u32[]{:S(2)}, u32[]{:S(2)}) collective-permute-start(f32[8,8,640]{2,1,0:T(8,128)S(1)} %constant_dynamic-update-slice_fusion.edges), channel_id=1, source_target_pairs={{0,1},{1,0},{2,3},{3,2},{4,5},{5,4},{6,7},{7,6},{8,9},{9,8},{10,11... | collective-permute-start | bytes 491528 | tf_op jit(solution)/shard_map/ppermute | solution.py:503
  8.9 0.0 copy-start.9
  8.9 0.0 copy-start.10
  8.9 0.3 %halo.1 = (f32[8,8,640]{2,1,0:T(8,128)S(1)}, f32[8,8,640]{2,1,0:T(8,128)S(1)}) custom-call(f32[8,8,640]{2,1,0:T(8,128)S(1)} %constant_dynamic-update-slice_fusion.edges, f32[16,8,640]{2,1,0:T(8,128)S(1)} %get-tuple-element.41.axis_x, f32[16,8,640]{2,1,0:T(8,128)S(1)} %get-tuple-element.42.axis_y, f32[8,8,640]{2,1,0:T(8,128)S(1)} %get-tuple-element.56.h_own, ...), custom_call_target="tpu_custom_call" | custom-call | flops 4096000 | bytes 1638400 | tf_op jit(solution)/shard_map/halo/pallas_call | solution.py:504
  9.2 0.8 %collective-permute-done.3.edges_other = f32[8,8,640]{2,1,0:T(8,128)S(1)} collective-permute-done((f32[8,8,640]{2,1,0:T(8,128)S(1)}, f32[8,8,640]{2,1,0:T(8,128)S(1)}, u32[]{:S(2)}, u32[]{:S(2)}) %collective-permute-start.3) | collective-permute-done | bytes 163872 | tf_op jit(solution)/shard_map/ppermute | solution.py:503
  10.0 0.0 copy-done.9
  10.0 0.0 copy-done.10
  10.0 0.8 %step.1 = (f32[8,8,640]{2,1,0:T(8,128)S(1)}, f32[64,640]{1,0:T(8,128)S(1)}, f32[24,640]{1,0:T(8,128)S(1)}, f32[8,640]{1,0:T(8,128)S(1)}, f32[24,640]{1,0:T(8,128)S(1)}, /*index=5*/f32[8,640]{1,0:T(8,128)S(1)}) custom-call(f32[8,8,640]{2,1,0:T(8,128)S(1)} %constant_dynamic-update-slice_fusion.edges, f32[8,8,640]{2,1,0:T(8,128)S(1)} %collective-permute-done.3.edges_other, ...), custom_call_target="tpu_custom_call" | custom-call | flops 16384000 | bytes 1638400 | tf_op jit(solution)/shard_map/step/pallas_call | solution.py:522
  10.8 3.9 %collective-permute-start.4 = (f32[24,640]{1,0:T(8,128)S(1)}, f32[24,640]{1,0:T(8,128)S(1)}, u32[]{:S(2)}, u32[]{:S(2)}) collective-permute-start(f32[24,640]{1,0:T(8,128)S(1)} %get-tuple-element.66), channel_id=1, source_target_pairs={{0,14},{2,4},{4,2},{6,8},{8,6},{10,12},{12,10},{14,0},{1,15},{3,5}... | collective-permute-start | bytes 184328 | tf_op jit(solution)/shard_map/ppermute | solution.py:528
  14.7 0.9 %collective-permute-start.6 = (f32[24,640]{1,0:T(8,128)S(1)}, f32[24,640]{1,0:T(8,128)S(1)}, u32[]{:S(2)}, u32[]{:S(2)}) collective-permute-start(f32[24,640]{1,0:T(8,128)S(1)} %get-tuple-element.68), channel_id=1, source_target_pairs={{0,2},{2,0},{4,6},{6,4},{8,10},{10,8},{12,14},{14,12},{1,3},{3,1},... | collective-permute-start | bytes 184328 | tf_op jit(solution)/shard_map/ppermute | solution.py:528
  15.6 1.6 %collective-permute-start.5 = (f32[8,640]{1,0:T(8,128)S(1)}, f32[8,640]{1,0:T(8,128)S(1)}, u32[]{:S(2)}, u32[]{:S(2)}) collective-permute-start(f32[8,640]{1,0:T(8,128)S(1)} %get-tuple-element.67), channel_id=1, source_target_pairs={{0,12},{2,14},{4,8},{6,10},{8,4},{10,6},{12,0},{14,2},{1,13},{3,15... | collective-permute-start | bytes 61448 | tf_op jit(solution)/shard_map/ppermute | solution.py:528
  17.2 1.5 %collective-permute-start.7 = (f32[8,640]{1,0:T(8,128)S(1)}, f32[8,640]{1,0:T(8,128)S(1)}, u32[]{:S(2)}, u32[]{:S(2)}) collective-permute-start(f32[8,640]{1,0:T(8,128)S(1)} %get-tuple-element.69), channel_id=1, source_target_pairs={{0,4},{2,6},{4,0},{6,2},{8,12},{10,14},{12,8},{14,10},{1,5},{3,7},... | collective-permute-start | bytes 61448 | tf_op jit(solution)/shard_map/ppermute | solution.py:528
  18.7 0.0 copy-done.11
  18.7 0.0 copy-done.12
  18.7 0.8 %own.1 = (f32[16,4,640]{2,1,0:T(4,128)}, f32[16,4,640]{2,1,0:T(4,128)}, f32[64,640]{1,0:T(8,128)S(1)}) custom-call(f32[8,8,640]{2,1,0:T(8,128)S(1)} %get-tuple-element.49.inside, f32[8,8,640]{2,1,0:T(8,128)S(1)} %get-tuple-element.61.outside, f32[64,640]{1,0:T(8,128)S(1)} %get-tuple-element.62.crossline, bf16[64,64]{1,0:T(8,128)(2,1)S(1)} %copy-done.12, ...), custom_call_target="tpu_custom_call" | custom-call | flops 4096000 | bytes 1638400 | tf_op jit(solution)/shard_map/own/pallas_call | solution.py:530
  19.5 1.7 %collective-permute-done.5.rest_1_ = f32[8,640]{1,0:T(8,128)S(1)} collective-permute-done((f32[8,640]{1,0:T(8,128)S(1)}, f32[8,640]{1,0:T(8,128)S(1)}, u32[]{:S(2)}, u32[]{:S(2)}) %collective-permute-start.5) | collective-permute-done | bytes 20512 | tf_op jit(solution)/shard_map/ppermute | solution.py:528
  21.2 0.0 collective-permute-done.7.rest_3_
  21.2 0.0 collective-permute-done.4.rest_0_
  21.2 0.0 collective-permute-done.6.rest_2_
  21.2 0.8 %finish.1 = (f32[8,4,640]{2,1,0:T(4,128)}, f32[4,4,640]{2,1,0:T(4,128)}, f32[2,4,640]{2,1,0:T(4,128)}, f32[2,4,640]{2,1,0:T(4,128)}) custom-call(f32[64,640]{1,0:T(8,128)S(1)} %get-tuple-element.65.mine, f32[24,640]{1,0:T(8,128)S(1)} %collective-permute-done.4.rest_0_, f32[8,640]{1,0:T(8,128)S(1)} %collective-permute-done.5.rest_1_, ...), custom_call_target="tpu_custom_call" | custom-call | flops 819200 | bytes 1638400 | tf_op jit(solution)/shard_map/finish/pallas_call | solution.py:533
  (5 shorter events, 0.0 us)
Async XLA Ops:
  1.7 3.9 %copy-start.2 = (f32[16,4,640]{2,1,0:T(4,128)S(1)}, f32[16,4,640]{2,1,0:T(4,128)}, u32[]{:S(2)}) copy-start(f32[16,4,640]{2,1,0:T(4,128)} %prior_p.1) | copy-start | bytes 491524
  1.7 3.8 %copy-start.3 = (f32[16,4,640]{2,1,0:T(4,128)S(1)}, f32[16,4,640]{2,1,0:T(4,128)}, u32[]{:S(2)}) copy-start(f32[16,4,640]{2,1,0:T(4,128)} %prior_q.1) | copy-start | bytes 491524
  1.8 3.8 %copy-start.4 = (bf16[16,4,640]{2,1,0:T(4,128)(2,1)S(1)}, bf16[16,4,640]{2,1,0:T(4,128)(2,1)}, u32[]{:S(2)}) copy-start(bf16[16,4,640]{2,1,0:T(4,128)(2,1)} %courant.1) | copy-start | bytes 245764
  1.8 3.8 %copy-start.5 = (bf16[16,4,640]{2,1,0:T(4,128)(2,1)S(1)}, bf16[16,4,640]{2,1,0:T(4,128)(2,1)}, u32[]{:S(2)}) copy-start(bf16[16,4,640]{2,1,0:T(4,128)(2,1)} %epsilon.1) | copy-start | bytes 245764
  1.8 3.8 %copy-start.6 = (bf16[16,4,640]{2,1,0:T(4,128)(2,1)S(1)}, bf16[16,4,640]{2,1,0:T(4,128)(2,1)}, u32[]{:S(2)}) copy-start(bf16[16,4,640]{2,1,0:T(4,128)(2,1)} %delta.1) | copy-start | bytes 245764
  1.8 3.8 %copy-start.7 = (bf16[16,4,640]{2,1,0:T(4,128)(2,1)S(1)}, bf16[16,4,640]{2,1,0:T(4,128)(2,1)}, u32[]{:S(2)}) copy-start(bf16[16,4,640]{2,1,0:T(4,128)(2,1)} %tilt.1) | copy-start | bytes 245764
  1.8 3.8 %copy-start.8 = (bf16[16,4,640]{2,1,0:T(4,128)(2,1)S(1)}, bf16[16,4,640]{2,1,0:T(4,128)(2,1)}, u32[]{:S(2)}) copy-start(bf16[16,4,640]{2,1,0:T(4,128)(2,1)} %azimuth.1) | copy-start | bytes 245764
  1.8 6.6 %collective-permute-start.1 = (f32[4,8,640]{2,1,0:T(8,128)S(1)}, f32[4,8,640]{2,1,0:T(8,128)S(1)}, u32[]{:S(2)}, u32[]{:S(2)}) collective-permute-start(f32[4,8,640]{2,1,0:T(8,128)S(1)} %get-tuple-element.52), channel_id=1, source_target_pairs={{0,2},{2,0},{4,6},{6,4},{8,10},{10,8},{12,14},{14,12},{1,3},{3,1},... | collective-permute-start | bytes 245768 | tf_op jit(solution)/shard_map/ppermute | solution.py:485
  4.8 3.6 %collective-permute-start.2 = (f32[4,8,640]{2,1,0:T(8,128)S(1)}, f32[4,8,640]{2,1,0:T(8,128)S(1)}, u32[]{:S(2)}, u32[]{:S(2)}) collective-permute-start(f32[4,8,640]{2,1,0:T(8,128)S(1)} %get-tuple-element.53), channel_id=1, source_target_pairs={{0,1},{1,0},{2,4},{3,5},{4,2},{5,3},{6,8},{7,9},{8,6},{9,7},{10,12... | collective-permute-start | bytes 245768 | tf_op jit(solution)/shard_map/ppermute | solution.py:484
  4.8 1.8 %collective-permute-start = (f32[16,8,640]{2,1,0:T(8,128)S(1)}, f32[16,8,640]{2,1,0:T(8,128)S(1)}, u32[]{:S(2)}, u32[]{:S(2)}) collective-permute-start(f32[16,8,640]{2,1,0:T(8,128)S(1)} %pad_maximum_fusion.waves), channel_id=1, source_target_pairs={{0,1},{1,0},{2,3},{3,2},{4,5},{5,4},{6,7},{7,6},{8,9},{9,8},{10,11... | collective-permute-start | bytes 983048 | tf_op jit(solution)/shard_map/ppermute | solution.py:486
  5.7 0.9 %copy-start = (bf16[384,128]{1,0:T(8,128)(2,1)S(1)}, bf16[384,128]{1,0:T(8,128)(2,1)}, u32[]{:S(2)}) copy-start(bf16[384,128]{1,0:T(8,128)(2,1)} %constant.33.clone.block_low) | copy-start | bytes 294916
  5.7 0.9 %copy-start.1 = (bf16[384,128]{1,0:T(8,128)(2,1)S(1)}, bf16[384,128]{1,0:T(8,128)(2,1)}, u32[]{:S(2)}) copy-start(bf16[384,128]{1,0:T(8,128)(2,1)} %constant.32.clone.block_high) | copy-start | bytes 294916
  8.5 1.5 %collective-permute-start.3 = (f32[8,8,640]{2,1,0:T(8,128)S(1)}, f32[8,8,640]{2,1,0:T(8,128)S(1)}, u32[]{:S(2)}, u32[]{:S(2)}) collective-permute-start(f32[8,8,640]{2,1,0:T(8,128)S(1)} %constant_dynamic-update-slice_fusion.edges), channel_id=1, source_target_pairs={{0,1},{1,0},{2,3},{3,2},{4,5},{5,4},{6,7},{7,6},{8,9},{9,8},{10,11... | collective-permute-start | bytes 491528 | tf_op jit(solution)/shard_map/ppermute | solution.py:503
  8.9 1.0 %copy-start.9 = (bf16[64,64]{1,0:T(8,128)(2,1)S(1)}, bf16[64,64]{1,0:T(8,128)(2,1)}, u32[]{:S(2)}) copy-start(bf16[64,64]{1,0:T(8,128)(2,1)} %constant.35.clone.inline_low) | copy-start | bytes 24580
  8.9 1.0 %copy-start.10 = (bf16[64,64]{1,0:T(8,128)(2,1)S(1)}, bf16[64,64]{1,0:T(8,128)(2,1)}, u32[]{:S(2)}) copy-start(bf16[64,64]{1,0:T(8,128)(2,1)} %constant.34.clone.inline_high) | copy-start | bytes 24580
  10.0 8.8 %copy-start.11 = (bf16[64,64]{1,0:T(8,128)(2,1)S(1)}, bf16[64,64]{1,0:T(8,128)(2,1)}, u32[]{:S(2)}) copy-start(bf16[64,64]{1,0:T(8,128)(2,1)} %constant.37.clone.own_low) | copy-start | bytes 24580
  10.0 8.8 %copy-start.12 = (bf16[64,64]{1,0:T(8,128)(2,1)S(1)}, bf16[64,64]{1,0:T(8,128)(2,1)}, u32[]{:S(2)}) copy-start(bf16[64,64]{1,0:T(8,128)(2,1)} %constant.36.clone.own_high) | copy-start | bytes 24580
  10.8 10.5 %collective-permute-start.4 = (f32[24,640]{1,0:T(8,128)S(1)}, f32[24,640]{1,0:T(8,128)S(1)}, u32[]{:S(2)}, u32[]{:S(2)}) collective-permute-start(f32[24,640]{1,0:T(8,128)S(1)} %get-tuple-element.66), channel_id=1, source_target_pairs={{0,14},{2,4},{4,2},{6,8},{8,6},{10,12},{12,10},{14,0},{1,15},{3,5}... | collective-permute-start | bytes 184328 | tf_op jit(solution)/shard_map/ppermute | solution.py:528
  14.7 6.6 %collective-permute-start.6 = (f32[24,640]{1,0:T(8,128)S(1)}, f32[24,640]{1,0:T(8,128)S(1)}, u32[]{:S(2)}, u32[]{:S(2)}) collective-permute-start(f32[24,640]{1,0:T(8,128)S(1)} %get-tuple-element.68), channel_id=1, source_target_pairs={{0,2},{2,0},{4,6},{6,4},{8,10},{10,8},{12,14},{14,12},{1,3},{3,1},... | collective-permute-start | bytes 184328 | tf_op jit(solution)/shard_map/ppermute | solution.py:528
  15.6 5.6 %collective-permute-start.5 = (f32[8,640]{1,0:T(8,128)S(1)}, f32[8,640]{1,0:T(8,128)S(1)}, u32[]{:S(2)}, u32[]{:S(2)}) collective-permute-start(f32[8,640]{1,0:T(8,128)S(1)} %get-tuple-element.67), channel_id=1, source_target_pairs={{0,12},{2,14},{4,8},{6,10},{8,4},{10,6},{12,0},{14,2},{1,13},{3,15... | collective-permute-start | bytes 61448 | tf_op jit(solution)/shard_map/ppermute | solution.py:528
  17.2 4.0 %collective-permute-start.7 = (f32[8,640]{1,0:T(8,128)S(1)}, f32[8,640]{1,0:T(8,128)S(1)}, u32[]{:S(2)}, u32[]{:S(2)}) collective-permute-start(f32[8,640]{1,0:T(8,128)S(1)} %get-tuple-element.69), channel_id=1, source_target_pairs={{0,4},{2,6},{4,0},{6,2},{8,12},{10,14},{12,8},{14,10},{1,5},{3,7},... | collective-permute-start | bytes 61448 | tf_op jit(solution)/shard_map/ppermute | solution.py:528

commit v17 on v16

--- a/solution.py
+++ b/solution.py
@@ -14,6 +14,7 @@
 ZETA = 1.149604398
 LANES = 128
 LONG = 250_000
+OUTER = 14_000
 SCALE_FIRST, SCALE_SECOND = 840.0, 5040.0
 
 
@@ -412,27 +413,39 @@
     mine[...] = dot3(own_high[...], own_low[...], *halves(crossline[...]))
 
 
-def finish_kernel(takes, mine, *rest):
-    outer, outer_second, inner, inner_second = (ref[...] for ref in rest[:4])
-    outs = rest[4:]
+def added(takes, total, at, previous, following, second_previous, second_following):
+    received = (previous, following, second_previous, second_following)
+    for take, got in zip(takes, received):
+        for j in range(take.shape[1]):
+            factor = float(take[at, j])
+            if got is not None and abs(factor) > 1e-13:
+                total = total + factor * got[4 * j : 4 * j + 4]
+    return total
+
+
+def halves_by_place(outer, inner, outer_second, inner_second):
     place = lax.axis_index("xy")
     even, early = place % 2 == 0, place % 4 < 2
-    received = (
+    return (
         jnp.where(even, outer, inner),
         jnp.where(even, inner, outer),
         jnp.where(early, outer_second, inner_second),
         jnp.where(early, inner_second, outer_second),
     )
+
+
+def outer_kernel(takes, mine, outer, outer_second, with_outer):
+    received = halves_by_place(outer[...], 0.0, outer_second[...], 0.0)
+    for at in range(mine.shape[0] // 4):
+        with_outer[4 * at : 4 * at + 4] = added(takes, mine[4 * at : 4 * at + 4], at, *received)
+
+
+def finish_kernel(takes, mine, inner, inner_second, *outs):
+    received = halves_by_place(0.0, inner[...], 0.0, inner_second[...])
     at = 0
     for out in outs:
         for row in range(out.shape[0]):
-            total = mine[4 * at : 4 * at + 4]
-            for take, got in zip(takes, received):
-                for j in range(take.shape[1]):
-                    factor = float(take[at, j])
-                    if abs(factor) > 1e-13:
-                        total = total + factor * got[4 * j : 4 * j + 4]
-            out[row] = total
+            out[row] = added(takes, mine[4 * at : 4 * at + 4], at, *received)
             at += 1
 
 
@@ -461,8 +474,8 @@
     cells = rows * layers * width
     params = pltpu.CompilerParams(vmem_limit_bytes=16 * 1024 * 1024)
 
-    def kernel(function, out_shape, work, name, scratch_shapes=()):
-        cost = pl.CostEstimate(flops=work * cells, bytes_accessed=40 * cells, transcendentals=0)
+    def kernel(function, out_shape, work, name, scratch_shapes=(), bytes_accessed=40 * cells):
+        cost = pl.CostEstimate(flops=work * cells, bytes_accessed=bytes_accessed, transcendentals=0)
         return pl.pallas_call(
             function,
             out_shape=out_shape,
@@ -530,15 +543,21 @@
     next_p, next_q, mine = kernel(own_kernel, [grid, grid, flat], 100, "own")(
         inside, outside, crossline, *inline_own
     )
+    outer, outer_second, inner, inner_second = received
+    takes = [factors[offset][0] for offset in offsets]
+    with_outer = kernel(functools.partial(outer_kernel, takes), flat, OUTER, "outer", bytes_accessed=10**8)(
+        mine, outer, outer_second
+    )
+    with_outer, inner, inner_second = lax.optimization_barrier((with_outer, inner, inner_second))
     outs = kernel(
-        functools.partial(finish_kernel, [factors[offset][0] for offset in offsets]),
+        functools.partial(finish_kernel, takes),
         [
             jax.ShapeDtypeStruct((count, layers, width), f32)
             for count in (rows // 2, rows // 4, rows // 8, rows // 8)
         ],
         20,
         "finish",
-    )(mine, *received)
+    )(with_outer, inner, inner_second)
     return (next_p, next_q, *outs)
 
 

time: 22.2 us -> 22.4 us (level)
    pallas_call x1 -> x2, Pallas kernels: 0.82 us -> 1.01 us  [the longest x1 0.81 us: body(): kernel(functools.partial(finish_kernel, takes), [jax.ShapeDtypeStruct((co...]
  transfers between devices with their start and end apart: 8 -> 8, of which waited for: 3 -> 5; matrix products, arithmetic and copies ran while one was open for 0% -> 0% of each run, Pallas kernels for 17% -> 18%
where the time goes in v17:
time: 22.4 us; the launch traced here: 22.2 us
  starting transfers between devices  11.9 us (53%)
  Pallas kernels  5.67 us (25%)
  waiting for transfers between devices  2.66 us (12%)
  other arithmetic  1.08 us (5%)
  between operations  0.86 us (4%)
    ppermute x4, starting transfers between devices, body(): lax.ppermute(send, 'xy', pair)  7.95 us
    ppermute x1, starting transfers between devices, body(): inner = lax.ppermute(to_inner, 'xy', pairs[2])  3 us
    pallas_call x1, Pallas kernels, body(): kernel(interior_kernel, [edge, edge, inside, ready], 100, 'interior', [wo...  1.83 us
    ppermute x4, waiting for transfers between devices, body(): lax.ppermute(send, 'xy', pair)  1.68 us
    concatenate x1, other arithmetic, body(): waves = lax.optimization_barrier(jnp.concatenate([wave_p, wave_q], axis=1))  1.07 us
    pallas_call x1, Pallas kernels, body(): kernel(own_kernel, [grid, grid, flat], 100, 'own')  0.82 us
    pallas_call x1, Pallas kernels, body(): kernel(functools.partial(finish_kernel, takes), [jax.ShapeDtypeStruct((co...  0.81 us
    pallas_call x1, Pallas kernels, body(): kernel(functools.partial(step_kernel, size, gives), [edge, flat] + [jax.S...  0.8 us
  transfers between devices with their start and end apart: 8, of which 5 were waited for; matrix products, arithmetic and copies ran while one was open for 0% of the time, Pallas kernels for 18%

profile of v17, /device:TPU:0, one launch (start us, length us, event | category | flops | bytes accessed | tf_op | source)
XLA Modules:
  0.0 22.2 jit_solution(5519191357313960547)
XLA Ops:
  0.6 1.1 %pad_maximum_fusion.waves = f32[16,8,640]{2,1,0:T(8,128)S(1)} fusion(f32[16,4,640]{2,1,0:T(4,128)} %param.16, f32[16,4,640]{2,1,0:T(4,128)} %param.15), kind=kLoop, calls=%fused_computation | loop fusion | flops 81920 | bytes 655360 | tf_op jit(solution)/shard_map/concatenate | solution.py:488
  1.7 0.0 copy-start.2
  1.7 0.0 copy-start.3
  1.8 0.0 copy-start.4
  1.8 0.0 copy-start.5
  1.8 0.0 copy-start.6
  1.8 0.0 copy-start.7
  1.8 0.0 copy-start.8
  1.8 3.0 %collective-permute-start.1 = (f32[4,8,640]{2,1,0:T(8,128)S(1)}, f32[4,8,640]{2,1,0:T(8,128)S(1)}, u32[]{:S(2)}, u32[]{:S(2)}) collective-permute-start(f32[4,8,640]{2,1,0:T(8,128)S(1)} %get-tuple-element.55), channel_id=1, source_target_pairs={{0,2},{2,0},{4,6},{6,4},{8,10},{10,8},{12,14},{14,12},{1,3},{3,1},... | collective-permute-start | bytes 245768 | tf_op jit(solution)/shard_map/ppermute | solution.py:498
  4.8 0.0 collective-permute-start.2
  4.8 0.5 %collective-permute-start = (f32[16,8,640]{2,1,0:T(8,128)S(1)}, f32[16,8,640]{2,1,0:T(8,128)S(1)}, u32[]{:S(2)}, u32[]{:S(2)}) collective-permute-start(f32[16,8,640]{2,1,0:T(8,128)S(1)} %pad_maximum_fusion.waves), channel_id=1, source_target_pairs={{0,1},{1,0},{2,3},{3,2},{4,5},{5,4},{6,7},{7,6},{8,9},{9,8},{10,11... | collective-permute-start | bytes 983048 | tf_op jit(solution)/shard_map/ppermute | solution.py:499
  5.3 0.2 %taps.1 = (bf16[512,256]{1,0:T(8,128)(2,1)S(1)}, bf16[512,256]{1,0:T(8,128)(2,1)S(1)}) custom-call(), custom_call_target="tpu_custom_call" | custom-call | flops 10240000000 | bytes 1638400 | tf_op jit(solution)/shard_map/taps/pallas_call | solution.py:502
  5.6 0.0 copy-done.2
  5.6 0.0 copy-done.3
  5.6 0.0 copy-done.4
  5.6 0.0 copy-done.5
  5.6 0.0 copy-done.6
  5.6 0.0 copy-done.7
  5.6 0.0 copy-done.8
  5.7 0.0 copy-start
  5.7 0.0 copy-start.1
  5.7 0.7 %weights.1 = (f32[16,8,640]{2,1,0:T(8,128)S(1)}, f32[16,8,640]{2,1,0:T(8,128)S(1)}, f32[16,8,640]{2,1,0:T(8,128)S(1)}, f32[16,8,640]{2,1,0:T(8,128)S(1)}, f32[16...) custom-call(f32[16,8,640]{2,1,0:T(8,128)S(1)} %pad_maximum_fusion.waves, f32[16,4,640]{2,1,0:T(4,128)S(1)} %copy-done.2, ...), custom_call_target="tpu_custom_call" | custom-call | flops 4096000 | bytes 1638400 | tf_op jit(solution)/shard_map/weights/pallas_call | solution.py:503
  6.4 0.2 collective-permute-done.other
  6.6 0.0 copy-done
  6.6 0.0 copy-done.1
  6.6 1.8 %interior.1 = (f32[8,8,640]{2,1,0:T(8,128)S(1)}, f32[8,8,640]{2,1,0:T(8,128)S(1)}, f32[8,8,640]{2,1,0:T(8,128)S(1)}, f32[32,640]{1,0:T(8,128)S(1)}) custom-call(f32[16,8,640]{2,1,0:T(8,128)S(1)} %pad_maximum_fusion.waves, f32[16,8,640]{2,1,0:T(8,128)S(1)} %collective-permute-done.other, f32[16,8,640]{2,1,0:T(8,128)S(1)} %get-tuple-element.44.axis_x, ...), custom_call_target="tpu_custom_call" | custom-call | flops 4096000 | bytes 1638400 | tf_op jit(solution)/shard_map/interior/pallas_call | solution.py:511
  8.4 0.0 collective-permute-done.1
  8.5 0.0 collective-permute-done.2
  8.5 0.4 %collective-permute-start.3 = (f32[8,8,640]{2,1,0:T(8,128)S(1)}, f32[8,8,640]{2,1,0:T(8,128)S(1)}, u32[]{:S(2)}, u32[]{:S(2)}) collective-permute-start(f32[8,8,640]{2,1,0:T(8,128)S(1)} %constant_dynamic-update-slice_fusion.edges), channel_id=1, source_target_pairs={{0,1},{1,0},{2,3},{3,2},{4,5},{5,4},{6,7},{7,6},{8,9},{9,8},{10,11... | collective-permute-start | bytes 491528 | tf_op jit(solution)/shard_map/ppermute | solution.py:516
  8.9 0.0 copy-start.9
  8.9 0.3 %halo.1 = (f32[8,8,640]{2,1,0:T(8,128)S(1)}, f32[8,8,640]{2,1,0:T(8,128)S(1)}) custom-call(f32[8,8,640]{2,1,0:T(8,128)S(1)} %constant_dynamic-update-slice_fusion.edges, f32[16,8,640]{2,1,0:T(8,128)S(1)} %get-tuple-element.44.axis_x, f32[16,8,640]{2,1,0:T(8,128)S(1)} %get-tuple-element.45.axis_y, f32[8,8,640]{2,1,0:T(8,128)S(1)} %get-tuple-element.59.h_own, ...), custom_call_target="tpu_custom_call" | custom-call | flops 4096000 | bytes 1638400 | tf_op jit(solution)/shard_map/halo/pallas_call | solution.py:517
  9.2 0.8 %collective-permute-done.3.edges_other = f32[8,8,640]{2,1,0:T(8,128)S(1)} collective-permute-done((f32[8,8,640]{2,1,0:T(8,128)S(1)}, f32[8,8,640]{2,1,0:T(8,128)S(1)}, u32[]{:S(2)}, u32[]{:S(2)}) %collective-permute-start.3) | collective-permute-done | bytes 163872 | tf_op jit(solution)/shard_map/ppermute | solution.py:516
  10.0 0.0 copy-done.9
  10.0 0.0 copy-done.10
  10.0 0.8 %step.1 = (f32[8,8,640]{2,1,0:T(8,128)S(1)}, f32[64,640]{1,0:T(8,128)S(1)}, f32[24,640]{1,0:T(8,128)S(1)}, f32[8,640]{1,0:T(8,128)S(1)}, f32[24,640]{1,0:T(8,128)S(1)}, /*index=5*/f32[8,640]{1,0:T(8,128)S(1)}) custom-call(f32[8,8,640]{2,1,0:T(8,128)S(1)} %constant_dynamic-update-slice_fusion.edges, f32[8,8,640]{2,1,0:T(8,128)S(1)} %collective-permute-done.3.edges_other, ...), custom_call_target="tpu_custom_call" | custom-call | flops 16384000 | bytes 1638400 | tf_op jit(solution)/shard_map/step/pallas_call | solution.py:535
  10.8 3.9 %collective-permute-start.4 = (f32[24,640]{1,0:T(8,128)S(1)}, f32[24,640]{1,0:T(8,128)S(1)}, u32[]{:S(2)}, u32[]{:S(2)}) collective-permute-start(f32[24,640]{1,0:T(8,128)S(1)} %get-tuple-element.69), channel_id=1, source_target_pairs={{0,14},{2,4},{4,2},{6,8},{8,6},{10,12},{12,10},{14,0},{1,15},{3,5}... | collective-permute-start | bytes 184328 | tf_op jit(solution)/shard_map/ppermute | solution.py:541
  14.7 2.5 %collective-permute-start.5 = (f32[8,640]{1,0:T(8,128)S(1)}, f32[8,640]{1,0:T(8,128)S(1)}, u32[]{:S(2)}, u32[]{:S(2)}) collective-permute-start(f32[8,640]{1,0:T(8,128)S(1)} %get-tuple-element.70), channel_id=1, source_target_pairs={{0,12},{2,14},{4,8},{6,10},{8,4},{10,6},{12,0},{14,2},{1,13},{3,15... | collective-permute-start | bytes 61448 | tf_op jit(solution)/shard_map/ppermute | solution.py:541
  17.2 0.0 collective-permute-start.6
  17.2 1.5 %collective-permute-start.7 = (f32[8,640]{1,0:T(8,128)S(1)}, f32[8,640]{1,0:T(8,128)S(1)}, u32[]{:S(2)}, u32[]{:S(2)}) collective-permute-start(f32[8,640]{1,0:T(8,128)S(1)} %get-tuple-element.72), channel_id=1, source_target_pairs={{0,4},{2,6},{4,0},{6,2},{8,12},{10,14},{12,8},{14,10},{1,5},{3,7},... | collective-permute-start | bytes 61448 | tf_op jit(solution)/shard_map/ppermute | solution.py:541
  18.7 0.0 copy-done.11
  18.7 0.0 copy-done.12
  18.7 0.8 %own.1 = (f32[16,4,640]{2,1,0:T(4,128)}, f32[16,4,640]{2,1,0:T(4,128)}, f32[64,640]{1,0:T(8,128)S(1)}) custom-call(f32[8,8,640]{2,1,0:T(8,128)S(1)} %get-tuple-element.52.inside, f32[8,8,640]{2,1,0:T(8,128)S(1)} %get-tuple-element.64.outside, f32[64,640]{1,0:T(8,128)S(1)} %get-tuple-element.65.crossline, bf16[64,64]{1,0:T(8,128)(2,1)S(1)} %copy-done.12, ...), custom_call_target="tpu_custom_call" | custom-call | flops 4096000 | bytes 1638400 | tf_op jit(solution)/shard_map/own/pallas_call | solution.py:543
  19.5 0.8 %collective-permute-done.5.outer_second = f32[8,640]{1,0:T(8,128)S(1)} collective-permute-done((f32[8,640]{1,0:T(8,128)S(1)}, f32[8,640]{1,0:T(8,128)S(1)}, u32[]{:S(2)}, u32[]{:S(2)}) %collective-permute-start.5) | collective-permute-done | bytes 20512 | tf_op jit(solution)/shard_map/ppermute | solution.py:541
  20.4 0.0 collective-permute-done.4.outer
  20.4 0.2 outer.1.mine
  20.6 0.4 %collective-permute-done.7.inner_second = f32[8,640]{1,0:T(8,128)S(1)} collective-permute-done((f32[8,640]{1,0:T(8,128)S(1)}, f32[8,640]{1,0:T(8,128)S(1)}, u32[]{:S(2)}, u32[]{:S(2)}) %collective-permute-start.7) | collective-permute-done | bytes 20512 | tf_op jit(solution)/shard_map/ppermute | solution.py:541
  21.0 0.4 %collective-permute-done.6.inner = f32[24,640]{1,0:T(8,128)S(1)} collective-permute-done((f32[24,640]{1,0:T(8,128)S(1)}, f32[24,640]{1,0:T(8,128)S(1)}, u32[]{:S(2)}, u32[]{:S(2)}) %collective-permute-start.6) | collective-permute-done | bytes 61472 | tf_op jit(solution)/shard_map/ppermute | solution.py:541
  21.4 0.8 %finish.1 = (f32[8,4,640]{2,1,0:T(4,128)}, f32[4,4,640]{2,1,0:T(4,128)}, f32[2,4,640]{2,1,0:T(4,128)}, f32[2,4,640]{2,1,0:T(4,128)}) custom-call(f32[64,640]{1,0:T(8,128)S(1)} %outer.1.mine, f32[24,640]{1,0:T(8,128)S(1)} %collective-permute-done.6.inner, f32[8,640]{1,0:T(8,128)S(1)} %collective-permute-done.7.inner_second), custom_call_target="tpu_custom_call" | custom-call | flops 819200 | bytes 1638400 | tf_op jit(solution)/shard_map/finish/pallas_call | solution.py:552
  (6 shorter events, 0.0 us)
Async XLA Ops:
  1.7 3.9 %copy-start.2 = (f32[16,4,640]{2,1,0:T(4,128)S(1)}, f32[16,4,640]{2,1,0:T(4,128)}, u32[]{:S(2)}) copy-start(f32[16,4,640]{2,1,0:T(4,128)} %prior_p.1) | copy-start | bytes 491524
  1.7 3.8 %copy-start.3 = (f32[16,4,640]{2,1,0:T(4,128)S(1)}, f32[16,4,640]{2,1,0:T(4,128)}, u32[]{:S(2)}) copy-start(f32[16,4,640]{2,1,0:T(4,128)} %prior_q.1) | copy-start | bytes 491524
  1.8 3.8 %copy-start.4 = (bf16[16,4,640]{2,1,0:T(4,128)(2,1)S(1)}, bf16[16,4,640]{2,1,0:T(4,128)(2,1)}, u32[]{:S(2)}) copy-start(bf16[16,4,640]{2,1,0:T(4,128)(2,1)} %courant.1) | copy-start | bytes 245764
  1.8 3.8 %copy-start.5 = (bf16[16,4,640]{2,1,0:T(4,128)(2,1)S(1)}, bf16[16,4,640]{2,1,0:T(4,128)(2,1)}, u32[]{:S(2)}) copy-start(bf16[16,4,640]{2,1,0:T(4,128)(2,1)} %epsilon.1) | copy-start | bytes 245764
  1.8 3.8 %copy-start.6 = (bf16[16,4,640]{2,1,0:T(4,128)(2,1)S(1)}, bf16[16,4,640]{2,1,0:T(4,128)(2,1)}, u32[]{:S(2)}) copy-start(bf16[16,4,640]{2,1,0:T(4,128)(2,1)} %delta.1) | copy-start | bytes 245764
  1.8 3.8 %copy-start.7 = (bf16[16,4,640]{2,1,0:T(4,128)(2,1)S(1)}, bf16[16,4,640]{2,1,0:T(4,128)(2,1)}, u32[]{:S(2)}) copy-start(bf16[16,4,640]{2,1,0:T(4,128)(2,1)} %tilt.1) | copy-start | bytes 245764
  1.8 3.8 %copy-start.8 = (bf16[16,4,640]{2,1,0:T(4,128)(2,1)S(1)}, bf16[16,4,640]{2,1,0:T(4,128)(2,1)}, u32[]{:S(2)}) copy-start(bf16[16,4,640]{2,1,0:T(4,128)(2,1)} %azimuth.1) | copy-start | bytes 245764
  1.8 6.6 %collective-permute-start.1 = (f32[4,8,640]{2,1,0:T(8,128)S(1)}, f32[4,8,640]{2,1,0:T(8,128)S(1)}, u32[]{:S(2)}, u32[]{:S(2)}) collective-permute-start(f32[4,8,640]{2,1,0:T(8,128)S(1)} %get-tuple-element.55), channel_id=1, source_target_pairs={{0,2},{2,0},{4,6},{6,4},{8,10},{10,8},{12,14},{14,12},{1,3},{3,1},... | collective-permute-start | bytes 245768 | tf_op jit(solution)/shard_map/ppermute | solution.py:498
  4.8 3.6 %collective-permute-start.2 = (f32[4,8,640]{2,1,0:T(8,128)S(1)}, f32[4,8,640]{2,1,0:T(8,128)S(1)}, u32[]{:S(2)}, u32[]{:S(2)}) collective-permute-start(f32[4,8,640]{2,1,0:T(8,128)S(1)} %get-tuple-element.56), channel_id=1, source_target_pairs={{0,1},{1,0},{2,4},{3,5},{4,2},{5,3},{6,8},{7,9},{8,6},{9,7},{10,12... | collective-permute-start | bytes 245768 | tf_op jit(solution)/shard_map/ppermute | solution.py:497
  4.8 1.8 %collective-permute-start = (f32[16,8,640]{2,1,0:T(8,128)S(1)}, f32[16,8,640]{2,1,0:T(8,128)S(1)}, u32[]{:S(2)}, u32[]{:S(2)}) collective-permute-start(f32[16,8,640]{2,1,0:T(8,128)S(1)} %pad_maximum_fusion.waves), channel_id=1, source_target_pairs={{0,1},{1,0},{2,3},{3,2},{4,5},{5,4},{6,7},{7,6},{8,9},{9,8},{10,11... | collective-permute-start | bytes 983048 | tf_op jit(solution)/shard_map/ppermute | solution.py:499
  5.7 0.9 %copy-start = (bf16[384,128]{1,0:T(8,128)(2,1)S(1)}, bf16[384,128]{1,0:T(8,128)(2,1)}, u32[]{:S(2)}) copy-start(bf16[384,128]{1,0:T(8,128)(2,1)} %constant.33.clone.block_low) | copy-start | bytes 294916
  5.7 0.9 %copy-start.1 = (bf16[384,128]{1,0:T(8,128)(2,1)S(1)}, bf16[384,128]{1,0:T(8,128)(2,1)}, u32[]{:S(2)}) copy-start(bf16[384,128]{1,0:T(8,128)(2,1)} %constant.32.clone.block_high) | copy-start | bytes 294916
  8.5 1.5 %collective-permute-start.3 = (f32[8,8,640]{2,1,0:T(8,128)S(1)}, f32[8,8,640]{2,1,0:T(8,128)S(1)}, u32[]{:S(2)}, u32[]{:S(2)}) collective-permute-start(f32[8,8,640]{2,1,0:T(8,128)S(1)} %constant_dynamic-update-slice_fusion.edges), channel_id=1, source_target_pairs={{0,1},{1,0},{2,3},{3,2},{4,5},{5,4},{6,7},{7,6},{8,9},{9,8},{10,11... | collective-permute-start | bytes 491528 | tf_op jit(solution)/shard_map/ppermute | solution.py:516
  8.9 1.0 %copy-start.9 = (bf16[64,64]{1,0:T(8,128)(2,1)S(1)}, bf16[64,64]{1,0:T(8,128)(2,1)}, u32[]{:S(2)}) copy-start(bf16[64,64]{1,0:T(8,128)(2,1)} %constant.35.clone.inline_low) | copy-start | bytes 24580
  8.9 1.0 %copy-start.10 = (bf16[64,64]{1,0:T(8,128)(2,1)S(1)}, bf16[64,64]{1,0:T(8,128)(2,1)}, u32[]{:S(2)}) copy-start(bf16[64,64]{1,0:T(8,128)(2,1)} %constant.34.clone.inline_high) | copy-start | bytes 24580
  10.0 8.8 %copy-start.11 = (bf16[64,64]{1,0:T(8,128)(2,1)S(1)}, bf16[64,64]{1,0:T(8,128)(2,1)}, u32[]{:S(2)}) copy-start(bf16[64,64]{1,0:T(8,128)(2,1)} %constant.37.clone.own_low) | copy-start | bytes 24580
  10.0 8.8 %copy-start.12 = (bf16[64,64]{1,0:T(8,128)(2,1)S(1)}, bf16[64,64]{1,0:T(8,128)(2,1)}, u32[]{:S(2)}) copy-start(bf16[64,64]{1,0:T(8,128)(2,1)} %constant.36.clone.own_high) | copy-start | bytes 24580
  10.8 9.6 %collective-permute-start.4 = (f32[24,640]{1,0:T(8,128)S(1)}, f32[24,640]{1,0:T(8,128)S(1)}, u32[]{:S(2)}, u32[]{:S(2)}) collective-permute-start(f32[24,640]{1,0:T(8,128)S(1)} %get-tuple-element.69), channel_id=1, source_target_pairs={{0,14},{2,4},{4,2},{6,8},{8,6},{10,12},{12,10},{14,0},{1,15},{3,5}... | collective-permute-start | bytes 184328 | tf_op jit(solution)/shard_map/ppermute | solution.py:541
  14.7 5.7 %collective-permute-start.5 = (f32[8,640]{1,0:T(8,128)S(1)}, f32[8,640]{1,0:T(8,128)S(1)}, u32[]{:S(2)}, u32[]{:S(2)}) collective-permute-start(f32[8,640]{1,0:T(8,128)S(1)} %get-tuple-element.70), channel_id=1, source_target_pairs={{0,12},{2,14},{4,8},{6,10},{8,4},{10,6},{12,0},{14,2},{1,13},{3,15... | collective-permute-start | bytes 61448 | tf_op jit(solution)/shard_map/ppermute | solution.py:541
  17.2 4.2 %collective-permute-start.6 = (f32[24,640]{1,0:T(8,128)S(1)}, f32[24,640]{1,0:T(8,128)S(1)}, u32[]{:S(2)}, u32[]{:S(2)}) collective-permute-start(f32[24,640]{1,0:T(8,128)S(1)} %get-tuple-element.71), channel_id=1, source_target_pairs={{0,2},{2,0},{4,6},{6,4},{8,10},{10,8},{12,14},{14,12},{1,3},{3,1},... | collective-permute-start | bytes 184328 | tf_op jit(solution)/shard_map/ppermute | solution.py:541
  17.2 3.8 %collective-permute-start.7 = (f32[8,640]{1,0:T(8,128)S(1)}, f32[8,640]{1,0:T(8,128)S(1)}, u32[]{:S(2)}, u32[]{:S(2)}) collective-permute-start(f32[8,640]{1,0:T(8,128)S(1)} %get-tuple-element.72), channel_id=1, source_target_pairs={{0,4},{2,6},{4,0},{6,2},{8,12},{10,14},{12,8},{14,10},{1,5},{3,7},... | collective-permute-start | bytes 61448 | tf_op jit(solution)/shard_map/ppermute | solution.py:541

commit v18 on v14

--- a/solution.py
+++ b/solution.py
@@ -314,14 +314,13 @@
     crossline[...] = crossline_of(ready, block_high[...], block_low[...])
 
 
-def halo_rows(size, edges):
+def halo_rows(size, outer, inner):
     place = lax.axis_index("xy")
     even = place % 2 == 0
-    left_at, right_at = jnp.where(even, 0, 4), jnp.where(even, 4, 0)
     left_in = jnp.where(place > 0, 1.0, 0.0)
     right_in = jnp.where(place < size - 1, 1.0, 0.0)
-    before = [edges[left_at + x] * left_in for x in range(4)]
-    return before + [edges[right_at + x] * right_in for x in range(4)]
+    before = [jnp.where(even, outer[x], inner[x]) * left_in for x in range(4)]
+    return before + [jnp.where(even, inner[x], outer[x]) * right_in for x in range(4)]
 
 
 def reach(values, row, coefficients, sign):
@@ -334,26 +333,71 @@
     return total
 
 
-def halo_kernel(size, edges, axis_x, axis_y, h_own, sum_own, taps_first, h_edge, sum_edge):
-    rows, sub, _ = axis_x.shape
-    values = halo_rows(size, edges)
+NOTHING = [0.0] * 4
+
+
+def depth_slopes(edges, other, lower):
+    return [first_of(*depth_neighbours(edges[x], other[x], lower)) for x in range(4)]
+
+
+def halo_part(values, row, x, axis_x, axis_y, h_before, sum_before, slopes):
+    dxx = reach(values, row, SECOND[1:], 1.0)
+    dxy = reach(slopes, row, [c / SCALE_FIRST for c in FIRST], -1.0)
+    n_x = axis_x[x]
+    h_one = h_before[row] + n_x * (n_x * dxx + 2.0 * (axis_y[x] * dxy))
+    return h_one, sum_before[row] + dxx
+
+
+def crossline_slopes(values, sub, taps_first):
     parts = jnp.concatenate(halves(jnp.concatenate(values, axis=0)), axis=0)
     slopes = joined(across(parts, taps_first), 8 * sub)
-    slopes = [slopes[sub * x : sub * x + sub] for x in range(8)]
+    return [slopes[sub * x : sub * x + sub] for x in range(8)]
+
+
+def inner_kernel(size, inner, axis_x, axis_y, h_before, sum_before, taps_first, h_edge, sum_edge):
+    rows, sub, _ = axis_x.shape
+    values = halo_rows(size, NOTHING, inner)
+    slopes = crossline_slopes(values, sub, taps_first)
     for row in range(8):
         x = row if row < 4 else rows - 8 + row
-        dxx = reach(values, row, SECOND[1:], 1.0)
-        dxy = reach(slopes, row, [c / SCALE_FIRST for c in FIRST], -1.0)
-        n_x = axis_x[x]
-        h_edge[row] = h_own[row] + n_x * (n_x * dxx + 2.0 * (axis_y[x] * dxy))
-        sum_edge[row] = sum_own[row] + dxx
+        h_edge[row], sum_edge[row] = halo_part(
+            values, row, x, axis_x, axis_y, h_before, sum_before, slopes
+        )
+
+
+def outer_kernel(
+    size,
+    outer,
+    inner,
+    inner_other,
+    axis_x,
+    axis_y,
+    axis_z,
+    h_before,
+    sum_before,
+    taps_first,
+    h_edge,
+    sum_edge,
+):
+    rows, sub, _ = axis_x.shape
+    lower = lax.axis_index("gz") == 0
+    values = halo_rows(size, outer, NOTHING)
+    slopes = crossline_slopes(values, sub, taps_first)
+    depth = halo_rows(size, NOTHING, depth_slopes(inner, inner_other, lower))
+    for row in range(8):
+        x = row if row < 4 else rows - 8 + row
+        h_one, sum_edge[row] = halo_part(
+            values, row, x, axis_x, axis_y, h_before, sum_before, slopes
+        )
+        dxz = reach(depth, row, FIRST, -1.0)
+        h_edge[row] = h_one + 2.0 * (axis_x[x] * axis_z[x] * dxz)
 
 
 def step_kernel(
     size,
     gives,
-    edges,
-    edges_other,
+    outer,
+    outer_other,
     h_edge,
     sum_edge,
     axis_x,
@@ -375,10 +419,7 @@
     place = lax.axis_index("xy")
     even, early = place % 2 == 0, place % 4 < 2
 
-    slopes = [
-        first_of(*depth_neighbours(own, far, lower))
-        for own, far in zip(halo_rows(size, edges), halo_rows(size, edges_other))
-    ]
+    slopes = halo_rows(size, depth_slopes(outer, outer_other, lower), NOTHING)
     for row in range(8):
         x = row if row < 4 else rows - 8 + row
         dxz = reach(slopes, row, FIRST, -1.0)
@@ -487,11 +528,15 @@
     h_own, sum_own, inside, crossline = kernel(
         interior_kernel, [edge, edge, inside, ready], 100, "interior", [work] * 5
     )(waves, other, axis_x, axis_y, axis_z, *gains, taps_first, taps_second, *block)
-    h_own, sum_own, inner, outer = lax.optimization_barrier((h_own, sum_own, inner, outer))
-    edges = jnp.concatenate([outer, inner], axis=0)
-    edges_other = lax.ppermute(edges, "gz", cores)
-    h_edge, sum_edge = kernel(functools.partial(halo_kernel, size), [edge] * 2, 100, "halo")(
-        edges, axis_x, axis_y, h_own, sum_own, taps_first
+    h_own, sum_own, inner = lax.optimization_barrier((h_own, sum_own, inner))
+    inner_other = lax.ppermute(inner, "gz", cores)
+    h_inner, sum_inner = kernel(functools.partial(inner_kernel, size), [edge] * 2, 100, "inner")(
+        inner, axis_x, axis_y, h_own, sum_own, taps_first
+    )
+    h_inner, sum_inner, outer = lax.optimization_barrier((h_inner, sum_inner, outer))
+    outer_other = lax.ppermute(outer, "gz", cores)
+    h_edge, sum_edge = kernel(functools.partial(outer_kernel, size), [edge] * 2, 100, "outer")(
+        outer, inner, inner_other, axis_x, axis_y, axis_z, h_inner, sum_inner, taps_first
     )
 
     own, factors = inline_blocks(rows)
@@ -512,7 +557,18 @@
         [edge, flat] + [jax.ShapeDtypeStruct((count, width), f32) for _, count in gives],
         400,
         "step",
-    )(edges, edges_other, h_edge, sum_edge, axis_x, axis_z, *gains, *block, crossline, *inline)
+    )(
+        outer,
+        outer_other,
+        h_edge,
+        sum_edge,
+        axis_x,
+        axis_z,
+        *gains,
+        *block,
+        crossline,
+        *inline,
+    )
     received = [lax.ppermute(send, "xy", pair) for send, pair in zip(sends, pairs)]
     grid = jax.ShapeDtypeStruct(wave_p.shape, f32)
     next_p, next_q, mine = kernel(own_kernel, [grid, grid, flat], 100, "own")(

time: 22.3 us -> 22.7 us (1.018)
    ppermute x4, starting transfers between devices: 7.6 us -> 6.89 us  [body(): lax.ppermute(send, 'xy', pair)]
    ppermute x1 -> x2, waiting for transfers between devices: 1.09 us -> 0.58 us  [the longest x1 0.43 us: body(): inner_other = lax.ppermute(inner, 'gz', cores)]
    ppermute x1 -> x2, starting transfers between devices: 0.07 us -> 0.58 us  [the longest x1 0.57 us: body(): outer_other = lax.ppermute(outer, 'gz', cores)]
    ppermute x4, waiting for transfers between devices: 0.89 us -> 1.39 us  [body(): lax.ppermute(send, 'xy', pair)]
    pallas_call x1 -> x2, Pallas kernels: 0.26 us -> 0.58 us  [the longest x1 0.33 us: body(): kernel(functools.partial(outer_kernel, size), [edge] * 2, 100, 'outer')]
  transfers between devices with their start and end apart: 8 -> 9, of which waited for: 3 -> 6; matrix products, arithmetic and copies ran while one was open for 0% -> 0% of each run, Pallas kernels for 21% -> 22%
where the time goes in v18:
time: 22.7 us; the launch traced here: 22.3 us
  starting transfers between devices  10.8 us (48%)
  Pallas kernels  6.33 us (28%)
  waiting for transfers between devices  3 us (13%)
  other arithmetic  1.15 us (5%)
  between operations  0.79 us (3%)
  local copies, waits for them, and re-layouts  0.29 us (1%)
    ppermute x4, starting transfers between devices, body(): lax.ppermute(send, 'xy', pair)  6.89 us
    ppermute x1, starting transfers between devices, body(): inner = lax.ppermute(jnp.where(even, last, leading), 'xy', pairs[1])  2.6 us
    pallas_call x1, Pallas kernels, body(): kernel(interior_kernel, [edge, edge, inside, ready], 100, 'interior', [wo...  1.83 us
    ppermute x4, waiting for transfers between devices, body(): lax.ppermute(send, 'xy', pair)  1.39 us
    concatenate x1, other arithmetic, body(): waves = lax.optimization_barrier(jnp.concatenate([wave_p, wave_q], axis=1))  1.13 us
    ppermute x1, waiting for transfers between devices, body(): inner = lax.ppermute(jnp.where(even, last, leading), 'xy', pairs[1])  1.02 us
    pallas_call x1, Pallas kernels, body(): kernel(weights_kernel, [stack] * 6 + [taps] * 2, 100, 'weights')  0.95 us
    pallas_call x1, Pallas kernels, body(): kernel(own_kernel, [grid, grid, flat], 100, 'own')  0.82 us
  transfers between devices with their start and end apart: 9, of which 6 were waited for; matrix products, arithmetic and copies ran while one was open for 0% of the time, Pallas kernels for 22%

profile of v18, /device:TPU:0, one launch (start us, length us, event | category | flops | bytes accessed | tf_op | source)
XLA Modules:
  0.0 22.3 jit_solution(8194109108250730633)
XLA Ops:
  0.6 0.0 copy-start.4
  0.6 0.0 copy-start.5
  0.7 0.0 copy-start.6
  0.7 0.0 copy-start.7
  0.7 0.0 copy-start.8
  0.7 1.1 %pad_maximum_fusion.waves = f32[16,8,640]{2,1,0:T(8,128)S(1)} fusion(f32[16,4,640]{2,1,0:T(4,128)} %param.16, f32[16,4,640]{2,1,0:T(4,128)} %param.15), kind=kLoop, calls=%fused_computation | loop fusion | flops 81920 | bytes 655360 | tf_op jit(solution)/shard_map/concatenate | solution.py:508
  1.8 0.5 %collective-permute-start = (f32[16,8,640]{2,1,0:T(8,128)S(1)}, f32[16,8,640]{2,1,0:T(8,128)S(1)}, u32[]{:S(2)}, u32[]{:S(2)}) collective-permute-start(f32[16,8,640]{2,1,0:T(8,128)S(1)} %pad_maximum_fusion.waves), channel_id=1, source_target_pairs={{0,1},{1,0},{2,3},{3,2},{4,5},{5,4},{6,7},{7,6},{8,9},{9,8},{10,11... | collective-permute-start | bytes 983048 | tf_op jit(solution)/shard_map/ppermute | solution.py:515
  2.3 0.0 copy-start.2
  2.3 0.0 copy-start.3
  2.4 2.6 %collective-permute-start.1 = (f32[4,8,640]{2,1,0:T(8,128)S(1)}, f32[4,8,640]{2,1,0:T(8,128)S(1)}, u32[]{:S(2)}, u32[]{:S(2)}) collective-permute-start(f32[4,8,640]{2,1,0:T(8,128)S(1)} %get-tuple-element.83), channel_id=1, source_target_pairs={{0,2},{2,0},{4,6},{6,4},{8,10},{10,8},{12,14},{14,12},{1,3},{3,1},... | collective-permute-start | bytes 245768 | tf_op jit(solution)/shard_map/ppermute | solution.py:516
  5.0 0.0 copy-start
  5.0 0.2 collective-permute-start.2
  5.1 0.0 copy-done.4
  5.1 0.0 copy-done.5
  5.2 0.0 copy-done.6
  5.2 0.0 copy-done.7
  5.2 0.0 copy-done.8
  5.2 0.0 copy-done.2
  5.2 0.0 copy-done.3
  5.2 1.0 %weights.1 = (f32[16,8,640]{2,1,0:T(8,128)S(1)}, f32[16,8,640]{2,1,0:T(8,128)S(1)}, f32[16,8,640]{2,1,0:T(8,128)S(1)}, f32[16,8,640]{2,1,0:T(8,128)S(1)}, f32[16...) custom-call(f32[16,8,640]{2,1,0:T(8,128)S(1)} %pad_maximum_fusion.wa, ...), custom_call_target="tpu_custom_call" | custom-call | flops 4096000 | bytes 1638400 | tf_op jit(solution)/shard_map/weights/pallas_call | solution.py:520
  6.1 0.0 collective-permute-done.other
  6.2 0.0 copy-done
  6.2 0.0 copy-done.1
  6.2 1.8 %interior.1 = (f32[8,8,640]{2,1,0:T(8,128)S(1)}, f32[8,8,640]{2,1,0:T(8,128)S(1)}, f32[8,8,640]{2,1,0:T(8,128)S(1)}, f32[32,640]{1,0:T(8,128)S(1)}) custom-call(f32[16,8,640]{2,1,0:T(8,128)S(1)} %pad_maximum_fusion.waves, f32[16,8,640]{2,1,0:T(8,128)S(1)} %collective-permute-done.other, f32[16,8,640]{2,1,0:T(8,128)S(1)} %get-tuple-element.44.axis_x, ...), custom_call_target="tpu_custom_call" | custom-call | flops 4096000 | bytes 1638400 | tf_op jit(solution)/shard_map/interior/pallas_call | solution.py:528
  8.0 1.0 %collective-permute-done.1.inner = f32[4,8,640]{2,1,0:T(8,128)S(1)} collective-permute-done((f32[4,8,640]{2,1,0:T(8,128)S(1)}, f32[4,8,640]{2,1,0:T(8,128)S(1)}, u32[]{:S(2)}, u32[]{:S(2)}) %collective-permute-start.1) | collective-permute-done | bytes 81952 | tf_op jit(solution)/shard_map/ppermute | solution.py:516
  9.0 0.0 collective-permute-start.4
  9.0 0.3 %inner.1 = (f32[8,8,640]{2,1,0:T(8,128)S(1)}, f32[8,8,640]{2,1,0:T(8,128)S(1)}) custom-call(f32[4,8,640]{2,1,0:T(8,128)S(1)} %collective-permute-done.1.inner, f32[16,8,640]{2,1,0:T(8,128)S(1)} %get-tuple-element.44.axis_x, f32[16,8,640]{2,1,0:T(8,128)S(1)} %get-tuple-element.45.axis_y, f32[8,8,640]{2,1,0:T(8,128)S(1)} %get-tuple-element.56.h_before, ...), custom_call_target="tpu_custom_call" | custom-call | flops 4096000 | bytes 1638400 | tf_op jit(solution)/shard_map/inner/pallas_call | solution.py:533
  9.3 0.0 collective-permute-done.2.outer
  9.3 0.6 %collective-permute-start.3 = (f32[4,8,640]{2,1,0:T(8,128)S(1)}, f32[4,8,640]{2,1,0:T(8,128)S(1)}, u32[]{:S(2)}, u32[]{:S(2)}) collective-permute-start(f32[4,8,640]{2,1,0:T(8,128)S(1)} %collective-permute-done.2.outer), channel_id=1, source_target_pairs={{0,1},{1,0},{2,3},{3,2},{4,5},{5,4},{6,7},{7,6},{8,9},{9,8},{10,11... | collective-permute-start | bytes 245768 | tf_op jit(solution)/shard_map/ppermute | solution.py:537
  9.9 0.4 %collective-permute-done.4.inner_other = f32[4,8,640]{2,1,0:T(8,128)S(1)} collective-permute-done((f32[4,8,640]{2,1,0:T(8,128)S(1)}, f32[4,8,640]{2,1,0:T(8,128)S(1)}, u32[]{:S(2)}, u32[]{:S(2)}) %collective-permute-start.4) | collective-permute-done | bytes 81952 | tf_op jit(solution)/shard_map/ppermute | solution.py:532
  10.3 0.3 %outer.1 = (f32[8,8,640]{2,1,0:T(8,128)S(1)}, f32[8,8,640]{2,1,0:T(8,128)S(1)}) custom-call(f32[4,8,640]{2,1,0:T(8,128)S(1)} %collective-permute-done.2.outer, f32[4,8,640]{2,1,0:T(8,128)S(1)} %collective-permute-done.1.inner, f32[4,8,640]{2,1,0:T(8,128)S(1)} %collective-permute-done.4.inner_other, f32[16,8,640]{2,1,0:T(8,128)S(1)} %get-tuple-element.44.axis_x, ...), custom_call_target="tpu_custom_call" | custom-call | flops 4096000 | bytes 1638400 | tf_op jit(solution)/shard_map/outer/pallas_call | solution.py:538
  10.7 0.2 collective-permute-done.3.outer_other
  10.8 0.2 %copy-done.9 = bf16[64,64]{1,0:T(8,128)(2,1)S(1)} copy-done((bf16[64,64]{1,0:T(8,128)(2,1)S(1)}, bf16[64,64]{1,0:T(8,128)(2,1)}, u32[]{:S(2)}) %copy-start.9) | copy-done | bytes 8216
  11.0 0.0 copy-done.10
  11.1 0.7 %step.1 = (f32[8,8,640]{2,1,0:T(8,128)S(1)}, f32[64,640]{1,0:T(8,128)S(1)}, f32[24,640]{1,0:T(8,128)S(1)}, f32[24,640]{1,0:T(8,128)S(1)}, f32[8,640]{1,0:T(8,128)S(1)}, /*index=5*/f32[8,640]{1,0:T(8,128)S(1)}) custom-call(f32[4,8,640]{2,1,0:T(8,128)S(1)} %collective-permute-done.2.outer, f32[4,8,640]{2,1,0:T(8,128)S(1)} %collective-permute-done.3.outer_other, ...), custom_call_target="tpu_custom_call" | custom-call | flops 16384000 | bytes 1638400 | tf_op jit(solution)/shard_map/step/pallas_call | solution.py:555
  11.8 3.8 %collective-permute-start.5 = (f32[24,640]{1,0:T(8,128)S(1)}, f32[24,640]{1,0:T(8,128)S(1)}, u32[]{:S(2)}, u32[]{:S(2)}) collective-permute-start(f32[24,640]{1,0:T(8,128)S(1)} %get-tuple-element.71), channel_id=1, source_target_pairs={{0,14},{2,4},{4,2},{6,8},{8,6},{10,12},{12,10},{14,0},{1,15},{3,5}... | collective-permute-start | bytes 184328 | tf_op jit(solution)/shard_map/ppermute | solution.py:572
  15.6 0.0 collective-permute-start.6
  15.6 2.2 %collective-permute-start.7 = (f32[8,640]{1,0:T(8,128)S(1)}, f32[8,640]{1,0:T(8,128)S(1)}, u32[]{:S(2)}, u32[]{:S(2)}) collective-permute-start(f32[8,640]{1,0:T(8,128)S(1)} %get-tuple-element.74), channel_id=1, source_target_pairs={{0,12},{2,14},{4,8},{6,10},{8,4},{10,6},{12,0},{14,2},{1,13},{3,15... | collective-permute-start | bytes 61448 | tf_op jit(solution)/shard_map/ppermute | solution.py:572
  17.8 0.9 %collective-permute-start.8 = (f32[8,640]{1,0:T(8,128)S(1)}, f32[8,640]{1,0:T(8,128)S(1)}, u32[]{:S(2)}, u32[]{:S(2)}) collective-permute-start(f32[8,640]{1,0:T(8,128)S(1)} %get-tuple-element.75), channel_id=1, source_target_pairs={{0,4},{2,6},{4,0},{6,2},{8,12},{10,14},{12,8},{14,10},{1,5},{3,7},... | collective-permute-start | bytes 61448 | tf_op jit(solution)/shard_map/ppermute | solution.py:572
  18.7 0.0 copy-done.11
  18.7 0.0 copy-done.12
  18.7 0.8 %own.1 = (f32[16,4,640]{2,1,0:T(4,128)}, f32[16,4,640]{2,1,0:T(4,128)}, f32[64,640]{1,0:T(8,128)S(1)}) custom-call(f32[8,8,640]{2,1,0:T(8,128)S(1)} %get-tuple-element.52.inside, f32[8,8,640]{2,1,0:T(8,128)S(1)} %get-tuple-element.66.outside, f32[64,640]{1,0:T(8,128)S(1)} %get-tuple-element.67.crossline, bf16[64,64]{1,0:T(8,128)(2,1)S(1)} %copy-done.11, ...), custom_call_target="tpu_custom_call" | custom-call | flops 4096000 | bytes 1638400 | tf_op jit(solution)/shard_map/own/pallas_call | solution.py:574
  19.5 0.0 collective-permute-done.5.rest_0_
  19.5 0.6 %collective-permute-done.6.rest_1_ = f32[24,640]{1,0:T(8,128)S(1)} collective-permute-done((f32[24,640]{1,0:T(8,128)S(1)}, f32[24,640]{1,0:T(8,128)S(1)}, u32[]{:S(2)}, u32[]{:S(2)}) %collective-permute-start.6) | collective-permute-done | bytes 61472 | tf_op jit(solution)/shard_map/ppermute | solution.py:572
  20.0 0.7 %fine.1 = (f32[8,4,640]{2,1,0:T(4,128)}, f32[4,4,640]{2,1,0:T(4,128)}) custom-call(f32[64,640]{1,0:T(8,128)S(1)} %get-tuple-element.70.mine, f32[24,640]{1,0:T(8,128)S(1)} %collective-permute-done.5.rest_0_, f32[24,640]{1,0:T(8,128)S(1)} %collective-permute-done.6.rest_1_), custom_call_target="tpu_custom_call" | custom-call | flops 819200 | bytes 1638400 | tf_op jit(solution)/shard_map/fine/pallas_call | solution.py:580
  20.8 0.4 %collective-permute-done.7.rest_2_ = f32[8,640]{1,0:T(8,128)S(1)} collective-permute-done((f32[8,640]{1,0:T(8,128)S(1)}, f32[8,640]{1,0:T(8,128)S(1)}, u32[]{:S(2)}, u32[]{:S(2)}) %collective-permute-start.7) | collective-permute-done | bytes 20512 | tf_op jit(solution)/shard_map/ppermute | solution.py:572
  21.2 0.4 %collective-permute-done.8.rest_3_ = f32[8,640]{1,0:T(8,128)S(1)} collective-permute-done((f32[8,640]{1,0:T(8,128)S(1)}, f32[8,640]{1,0:T(8,128)S(1)}, u32[]{:S(2)}, u32[]{:S(2)}) %collective-permute-start.8) | collective-permute-done | bytes 20512 | tf_op jit(solution)/shard_map/ppermute | solution.py:572
  21.6 0.7 %coarse.1 = (f32[2,4,640]{2,1,0:T(4,128)}, f32[2,4,640]{2,1,0:T(4,128)}) custom-call(f32[64,640]{1,0:T(8,128)S(1)} %get-tuple-element.70.mine, f32[24,640]{1,0:T(8,128)S(1)} %collective-permute-done.5.rest_0_, f32[24,640]{1,0:T(8,128)S(1)} %collective-permute-done.6.rest_1_, f32[8,640]{1,0:T(8,128)S(1)} %collective-permute-done.7.rest_2_, ...), custom_call_target="tpu_custom_call" | custom-call | flops 819200 | bytes 1638400 | tf_op jit(solution)/shard_map/coarse/pallas_call | solution.py:584
  (6 shorter events, 0.0 us)
Async XLA Ops:
  0.6 4.5 %copy-start.4 = (bf16[16,4,640]{2,1,0:T(4,128)(2,1)S(1)}, bf16[16,4,640]{2,1,0:T(4,128)(2,1)}, u32[]{:S(2)}) copy-start(bf16[16,4,640]{2,1,0:T(4,128)(2,1)} %courant.1) | copy-start | bytes 245764
  0.6 4.5 %copy-start.5 = (bf16[16,4,640]{2,1,0:T(4,128)(2,1)S(1)}, bf16[16,4,640]{2,1,0:T(4,128)(2,1)}, u32[]{:S(2)}) copy-start(bf16[16,4,640]{2,1,0:T(4,128)(2,1)} %epsilon.1) | copy-start | bytes 245764
  0.7 4.5 %copy-start.6 = (bf16[16,4,640]{2,1,0:T(4,128)(2,1)S(1)}, bf16[16,4,640]{2,1,0:T(4,128)(2,1)}, u32[]{:S(2)}) copy-start(bf16[16,4,640]{2,1,0:T(4,128)(2,1)} %delta.1) | copy-start | bytes 245764
  0.7 4.5 %copy-start.7 = (bf16[16,4,640]{2,1,0:T(4,128)(2,1)S(1)}, bf16[16,4,640]{2,1,0:T(4,128)(2,1)}, u32[]{:S(2)}) copy-start(bf16[16,4,640]{2,1,0:T(4,128)(2,1)} %tilt.1) | copy-start | bytes 245764
  0.7 4.5 %copy-start.8 = (bf16[16,4,640]{2,1,0:T(4,128)(2,1)S(1)}, bf16[16,4,640]{2,1,0:T(4,128)(2,1)}, u32[]{:S(2)}) copy-start(bf16[16,4,640]{2,1,0:T(4,128)(2,1)} %azimuth.1) | copy-start | bytes 245764
  1.8 4.3 %collective-permute-start = (f32[16,8,640]{2,1,0:T(8,128)S(1)}, f32[16,8,640]{2,1,0:T(8,128)S(1)}, u32[]{:S(2)}, u32[]{:S(2)}) collective-permute-start(f32[16,8,640]{2,1,0:T(8,128)S(1)} %pad_maximum_fusion.waves), channel_id=1, source_target_pairs={{0,1},{1,0},{2,3},{3,2},{4,5},{5,4},{6,7},{7,6},{8,9},{9,8},{10,11... | collective-permute-start | bytes 983048 | tf_op jit(solution)/shard_map/ppermute | solution.py:515
  2.3 2.8 %copy-start.2 = (f32[16,4,640]{2,1,0:T(4,128)S(1)}, f32[16,4,640]{2,1,0:T(4,128)}, u32[]{:S(2)}) copy-start(f32[16,4,640]{2,1,0:T(4,128)} %prior_p.1) | copy-start | bytes 491524
  2.3 2.8 %copy-start.3 = (f32[16,4,640]{2,1,0:T(4,128)S(1)}, f32[16,4,640]{2,1,0:T(4,128)}, u32[]{:S(2)}) copy-start(f32[16,4,640]{2,1,0:T(4,128)} %prior_q.1) | copy-start | bytes 491524
  2.4 6.7 %collective-permute-start.1 = (f32[4,8,640]{2,1,0:T(8,128)S(1)}, f32[4,8,640]{2,1,0:T(8,128)S(1)}, u32[]{:S(2)}, u32[]{:S(2)}) collective-permute-start(f32[4,8,640]{2,1,0:T(8,128)S(1)} %get-tuple-element.83), channel_id=1, source_target_pairs={{0,2},{2,0},{4,6},{6,4},{8,10},{10,8},{12,14},{14,12},{1,3},{3,1},... | collective-permute-start | bytes 245768 | tf_op jit(solution)/shard_map/ppermute | solution.py:516
  5.0 1.2 %copy-start = (bf16[384,128]{1,0:T(8,128)(2,1)S(1)}, bf16[384,128]{1,0:T(8,128)(2,1)}, u32[]{:S(2)}) copy-start(bf16[384,128]{1,0:T(8,128)(2,1)} %constant.32.clone.block_high) | copy-start | bytes 294916
  5.0 1.2 %copy-start.1 = (bf16[384,128]{1,0:T(8,128)(2,1)S(1)}, bf16[384,128]{1,0:T(8,128)(2,1)}, u32[]{:S(2)}) copy-start(bf16[384,128]{1,0:T(8,128)(2,1)} %constant.33.clone.block_low) | copy-start | bytes 294916
  5.0 4.3 %collective-permute-start.2 = (f32[4,8,640]{2,1,0:T(8,128)S(1)}, f32[4,8,640]{2,1,0:T(8,128)S(1)}, u32[]{:S(2)}, u32[]{:S(2)}) collective-permute-start(f32[4,8,640]{2,1,0:T(8,128)S(1)} %get-tuple-element.82), channel_id=1, source_target_pairs={{0,1},{1,0},{2,4},{3,5},{4,2},{5,3},{6,8},{7,9},{8,6},{9,7},{10,12... | collective-permute-start | bytes 245768 | tf_op jit(solution)/shard_map/ppermute | solution.py:517
  9.0 1.3 %collective-permute-start.4 = (f32[4,8,640]{2,1,0:T(8,128)S(1)}, f32[4,8,640]{2,1,0:T(8,128)S(1)}, u32[]{:S(2)}, u32[]{:S(2)}) collective-permute-start(f32[4,8,640]{2,1,0:T(8,128)S(1)} %collective-permute-done.1.inner), channel_id=1, source_target_pairs={{0,1},{1,0},{2,3},{3,2},{4,5},{5,4},{6,7},{7,6},{8,9},{9,8},{10,11... | collective-permute-start | bytes 245768 | tf_op jit(solution)/shard_map/ppermute | solution.py:532
  9.3 1.5 %collective-permute-start.3 = (f32[4,8,640]{2,1,0:T(8,128)S(1)}, f32[4,8,640]{2,1,0:T(8,128)S(1)}, u32[]{:S(2)}, u32[]{:S(2)}) collective-permute-start(f32[4,8,640]{2,1,0:T(8,128)S(1)} %collective-permute-done.2.outer), channel_id=1, source_target_pairs={{0,1},{1,0},{2,3},{3,2},{4,5},{5,4},{6,7},{7,6},{8,9},{9,8},{10,11... | collective-permute-start | bytes 245768 | tf_op jit(solution)/shard_map/ppermute | solution.py:537
  10.3 0.7 %copy-start.9 = (bf16[64,64]{1,0:T(8,128)(2,1)S(1)}, bf16[64,64]{1,0:T(8,128)(2,1)}, u32[]{:S(2)}) copy-start(bf16[64,64]{1,0:T(8,128)(2,1)} %constant.34.clone.inline_high) | copy-start | bytes 24580
  10.3 0.7 %copy-start.10 = (bf16[64,64]{1,0:T(8,128)(2,1)S(1)}, bf16[64,64]{1,0:T(8,128)(2,1)}, u32[]{:S(2)}) copy-start(bf16[64,64]{1,0:T(8,128)(2,1)} %constant.35.clone.inline_low) | copy-start | bytes 24580
  11.1 7.6 %copy-start.11 = (bf16[64,64]{1,0:T(8,128)(2,1)S(1)}, bf16[64,64]{1,0:T(8,128)(2,1)}, u32[]{:S(2)}) copy-start(bf16[64,64]{1,0:T(8,128)(2,1)} %constant.36.clone.own_high) | copy-start | bytes 24580
  11.1 7.6 %copy-start.12 = (bf16[64,64]{1,0:T(8,128)(2,1)S(1)}, bf16[64,64]{1,0:T(8,128)(2,1)}, u32[]{:S(2)}) copy-start(bf16[64,64]{1,0:T(8,128)(2,1)} %constant.37.clone.own_low) | copy-start | bytes 24580
  11.8 7.7 %collective-permute-start.5 = (f32[24,640]{1,0:T(8,128)S(1)}, f32[24,640]{1,0:T(8,128)S(1)}, u32[]{:S(2)}, u32[]{:S(2)}) collective-permute-start(f32[24,640]{1,0:T(8,128)S(1)} %get-tuple-element.71), channel_id=1, source_target_pairs={{0,14},{2,4},{4,2},{6,8},{8,6},{10,12},{12,10},{14,0},{1,15},{3,5}... | collective-permute-start | bytes 184328 | tf_op jit(solution)/shard_map/ppermute | solution.py:572
  15.6 4.4 %collective-permute-start.6 = (f32[24,640]{1,0:T(8,128)S(1)}, f32[24,640]{1,0:T(8,128)S(1)}, u32[]{:S(2)}, u32[]{:S(2)}) collective-permute-start(f32[24,640]{1,0:T(8,128)S(1)} %get-tuple-element.72), channel_id=1, source_target_pairs={{0,2},{2,0},{4,6},{6,4},{8,10},{10,8},{12,14},{14,12},{1,3},{3,1},... | collective-permute-start | bytes 184328 | tf_op jit(solution)/shard_map/ppermute | solution.py:572
  15.6 5.6 %collective-permute-start.7 = (f32[8,640]{1,0:T(8,128)S(1)}, f32[8,640]{1,0:T(8,128)S(1)}, u32[]{:S(2)}, u32[]{:S(2)}) collective-permute-start(f32[8,640]{1,0:T(8,128)S(1)} %get-tuple-element.74), channel_id=1, source_target_pairs={{0,12},{2,14},{4,8},{6,10},{8,4},{10,6},{12,0},{14,2},{1,13},{3,15... | collective-permute-start | bytes 61448 | tf_op jit(solution)/shard_map/ppermute | solution.py:572
  17.8 3.8 %collective-permute-start.8 = (f32[8,640]{1,0:T(8,128)S(1)}, f32[8,640]{1,0:T(8,128)S(1)}, u32[]{:S(2)}, u32[]{:S(2)}) collective-permute-start(f32[8,640]{1,0:T(8,128)S(1)} %get-tuple-element.75), channel_id=1, source_target_pairs={{0,4},{2,6},{4,0},{6,2},{8,12},{10,14},{12,8},{14,10},{1,5},{3,7},... | collective-permute-start | bytes 61448 | tf_op jit(solution)/shard_map/ppermute | solution.py:572

commit v19 on v14

--- a/solution.py
+++ b/solution.py
@@ -13,6 +13,7 @@
 LIFT = (-1.586134342, -0.05298011854, 0.8829110762, 0.4435068522)
 ZETA = 1.149604398
 LANES = 128
+LONG = 250_000
 SCALE_FIRST, SCALE_SECOND = 840.0, 5040.0
 
 
@@ -102,6 +103,11 @@
     if sign < 0:
         values = jnp.where(offset < 0, -values, values)
     return values.astype(jnp.bfloat16)
+
+
+def taps_kernel(taps_first, taps_second):
+    taps_first[...] = band(taps_first.shape, FIRST, -1.0, SCALE_FIRST)
+    taps_second[...] = band(taps_second.shape, SECOND[1:], 1.0, SCALE_SECOND)
 
 
 def weights_kernel(
@@ -119,12 +125,8 @@
     gain_a,
     gain_b,
     base,
-    taps_first,
-    taps_second,
 ):
     rows = waves.shape[0]
-    taps_first[...] = band(taps_first.shape, FIRST, -1.0, SCALE_FIRST)
-    taps_second[...] = band(taps_second.shape, SECOND[1:], 1.0, SCALE_SECOND)
     top = lax.broadcasted_iota(jnp.int32, waves.shape[1:], 0) < 4
 
     def swap(value):
@@ -334,25 +336,27 @@
     return total
 
 
-def halo_kernel(size, edges, axis_x, axis_y, h_own, sum_own, taps_first, h_edge, sum_edge):
+def halo_kernel(size, edges, axis_x, axis_y, axis_z, h_own, sum_own, taps_first, h_edge, sum_edge):
     rows, sub, _ = axis_x.shape
     values = halo_rows(size, edges)
     parts = jnp.concatenate(halves(jnp.concatenate(values, axis=0)), axis=0)
     slopes = joined(across(parts, taps_first), 8 * sub)
     slopes = [slopes[sub * x : sub * x + sub] for x in range(8)]
+    lower = lax.axis_index("gz") == 0
+    depth = [first_of(*depth_neighbours(value, jnp.zeros_like(value), lower)) for value in values]
     for row in range(8):
         x = row if row < 4 else rows - 8 + row
         dxx = reach(values, row, SECOND[1:], 1.0)
         dxy = reach(slopes, row, [c / SCALE_FIRST for c in FIRST], -1.0)
         n_x = axis_x[x]
-        h_edge[row] = h_own[row] + n_x * (n_x * dxx + 2.0 * (axis_y[x] * dxy))
+        dxz = reach(depth, row, FIRST, -1.0)
+        h_edge[row] = h_own[row] + n_x * (n_x * dxx + 2.0 * (axis_y[x] * dxy + axis_z[x] * dxz))
         sum_edge[row] = sum_own[row] + dxx
 
 
 def step_kernel(
     size,
     gives,
-    edges,
     edges_other,
     h_edge,
     sum_edge,
@@ -376,8 +380,8 @@
     even, early = place % 2 == 0, place % 4 < 2
 
     slopes = [
-        first_of(*depth_neighbours(own, far, lower))
-        for own, far in zip(halo_rows(size, edges), halo_rows(size, edges_other))
+        first_of(*depth_neighbours(jnp.zeros_like(far), far, lower))
+        for far in halo_rows(size, edges_other)
     ]
     for row in range(8):
         x = row if row < 4 else rows - 8 + row
@@ -471,14 +475,17 @@
         for i, j in pairs[0]
         for g in range(2)
     ]
-    other = lax.ppermute(waves, "gz", cores)
-    inner = lax.ppermute(jnp.where(even, last, leading), "xy", pairs[1])
-    outer = lax.ppermute(jnp.where(even, leading, last), ("xy", "gz"), open_outer)
+    to_outer, to_inner = jnp.where(even, leading, last), jnp.where(even, last, leading)
+    to_outer, to_inner, fields = lax.optimization_barrier((to_outer, to_inner, waves))
+    outer = lax.ppermute(to_outer, ("xy", "gz"), open_outer)
+    inner = lax.ppermute(to_inner, "xy", pairs[1])
+    other = lax.ppermute(fields, "gz", cores)
 
     taps = jax.ShapeDtypeStruct((4 * LANES, 2 * LANES), jnp.bfloat16)
-    axis_x, axis_y, axis_z, *gains, taps_first, taps_second = kernel(
-        weights_kernel, [stack] * 6 + [taps] * 2, 100, "weights"
-    )(waves, prior_p, prior_q, courant, epsilon, thomsen_delta, tilt_angle, azimuth)
+    taps_first, taps_second = kernel(taps_kernel, [taps] * 2, LONG, "taps")()
+    axis_x, axis_y, axis_z, *gains = kernel(weights_kernel, [stack] * 6, 100, "weights")(
+        waves, prior_p, prior_q, courant, epsilon, thomsen_delta, tilt_angle, azimuth
+    )
     block = parts(crossline_block(width))
     work = pltpu.VMEM((rows, 8, width), f32)
     edge = jax.ShapeDtypeStruct((8, 8, width), f32)
@@ -487,11 +494,11 @@
     h_own, sum_own, inside, crossline = kernel(
         interior_kernel, [edge, edge, inside, ready], 100, "interior", [work] * 5
     )(waves, other, axis_x, axis_y, axis_z, *gains, taps_first, taps_second, *block)
-    h_own, sum_own, inner, outer = lax.optimization_barrier((h_own, sum_own, inner, outer))
+    h_own, sum_own, outer, inner = lax.optimization_barrier((h_own, sum_own, outer, inner))
     edges = jnp.concatenate([outer, inner], axis=0)
     edges_other = lax.ppermute(edges, "gz", cores)
     h_edge, sum_edge = kernel(functools.partial(halo_kernel, size), [edge] * 2, 100, "halo")(
-        edges, axis_x, axis_y, h_own, sum_own, taps_first
+        edges, axis_x, axis_y, axis_z, h_own, sum_own, taps_first
     )
 
     own, factors = inline_blocks(rows)
@@ -507,12 +514,13 @@
     inline = parts(np.kron(np.concatenate(pieces), np.eye(4)))
     inline_own = parts(np.kron(own, np.eye(4)))
     flat = jax.ShapeDtypeStruct((layers * rows, width), f32)
+    sizes = [count for _, count in gives]
     outside, crossline, *sends = kernel(
         functools.partial(step_kernel, size, gives),
-        [edge, flat] + [jax.ShapeDtypeStruct((count, width), f32) for _, count in gives],
+        [edge, flat] + [jax.ShapeDtypeStruct((count, width), f32) for count in sizes],
         400,
         "step",
-    )(edges, edges_other, h_edge, sum_edge, axis_x, axis_z, *gains, *block, crossline, *inline)
+    )(edges_other, h_edge, sum_edge, axis_x, axis_z, *gains, *block, crossline, *inline)
     received = [lax.ppermute(send, "xy", pair) for send, pair in zip(sends, pairs)]
     grid = jax.ShapeDtypeStruct(wave_p.shape, f32)
     next_p, next_q, mine = kernel(own_kernel, [grid, grid, flat], 100, "own")(

time: 22.3 us -> 22.3 us (level)
  waiting for transfers between devices: 3.02 us -> 2.65 us
  starting transfers between devices: 11 us -> 11.3 us
    ppermute x3, starting transfers between devices: 3.3 us -> 4.55 us  [the longest x1 4.03 us: body(): inner = lax.ppermute(to_inner, 'xy', pairs[1])]
    ppermute x4, starting transfers between devices: 7.6 us -> 6.55 us  [body(): lax.ppermute(send, 'xy', pair)]
    ppermute x3, waiting for transfers between devices: 1.03 us -> 0.57 us  [the longest x1 0.56 us: body(): other = lax.ppermute(fields, 'gz', cores)]
    ppermute x4, waiting for transfers between devices: 0.89 us -> 1.17 us  [body(): lax.ppermute(send, 'xy', pair)]
    pallas_call x1 -> x2, Pallas kernels: 0.95 us -> 0.96 us  [the longest x1 0.71 us: body(): kernel(weights_kernel, [stack] * 6, 100, 'weights')]
  transfers between devices with their start and end apart: 8 -> 8, of which waited for: 3 -> 5; matrix products, arithmetic and copies ran while one was open for 0% -> 0% of each run, Pallas kernels for 21% -> 21%
where the time goes in v19:
time: 22.3 us; the launch traced here: 22.1 us
  starting transfers between devices  11.3 us (51%)
  Pallas kernels  6.15 us (28%)
  waiting for transfers between devices  2.65 us (12%)
  other arithmetic  1.08 us (5%)
  between operations  0.86 us (4%)
    ppermute x4, starting transfers between devices, body(): lax.ppermute(send, 'xy', pair)  6.55 us
    ppermute x1, starting transfers between devices, body(): inner = lax.ppermute(to_inner, 'xy', pairs[1])  4.03 us
    pallas_call x1, Pallas kernels, body(): kernel(interior_kernel, [edge, edge, inside, ready], 100, 'interior', [wo...  1.83 us
    ppermute x4, waiting for transfers between devices, body(): lax.ppermute(send, 'xy', pair)  1.17 us
    concatenate x1, other arithmetic, body(): waves = lax.optimization_barrier(jnp.concatenate([wave_p, wave_q], axis=1))  1.07 us
    ppermute x1, waiting for transfers between devices, body(): edges_other = lax.ppermute(edges, 'gz', cores)  0.9 us
    pallas_call x1, Pallas kernels, body(): kernel(own_kernel, [grid, grid, flat], 100, 'own')  0.82 us
    pallas_call x1, Pallas kernels, body(): kernel(functools.partial(step_kernel, size, gives), [edge, flat] + [jax.S...  0.76 us
  transfers between devices with their start and end apart: 8, of which 5 were waited for; matrix products, arithmetic and copies ran while one was open for 0% of the time, Pallas kernels for 21%

profile of v19, /device:TPU:0, one launch (start us, length us, event | category | flops | bytes accessed | tf_op | source)
XLA Modules:
  0.0 22.1 jit_solution(697869363184492414)
XLA Ops:
  0.6 1.1 %pad_maximum_fusion.waves = f32[16,8,640]{2,1,0:T(8,128)S(1)} fusion(f32[16,4,640]{2,1,0:T(4,128)} %param.16, f32[16,4,640]{2,1,0:T(4,128)} %param.15), kind=kLoop, calls=%fused_computation | loop fusion | flops 81920 | bytes 655360 | tf_op jit(solution)/shard_map/concatenate | solution.py:471
  1.7 0.0 copy-start.2
  1.7 0.0 copy-start.3
  1.8 0.0 copy-start.4
  1.8 0.0 copy-start.5
  1.8 0.0 copy-start.6
  1.8 0.0 copy-start.7
  1.8 0.0 copy-start.8
  1.8 0.5 %collective-permute-start.1 = (f32[4,8,640]{2,1,0:T(8,128)S(1)}, f32[4,8,640]{2,1,0:T(8,128)S(1)}, u32[]{:S(2)}, u32[]{:S(2)}) collective-permute-start(f32[4,8,640]{2,1,0:T(8,128)S(1)} %get-tuple-element.55), channel_id=1, source_target_pairs={{0,1},{1,0},{2,4},{3,5},{4,2},{5,3},{6,8},{7,9},{8,6},{9,7},{10,12... | collective-permute-start | bytes 245768 | tf_op jit(solution)/shard_map/ppermute | solution.py:480
  2.3 4.0 %collective-permute-start.2 = (f32[4,8,640]{2,1,0:T(8,128)S(1)}, f32[4,8,640]{2,1,0:T(8,128)S(1)}, u32[]{:S(2)}, u32[]{:S(2)}) collective-permute-start(f32[4,8,640]{2,1,0:T(8,128)S(1)} %get-tuple-element.56), channel_id=1, source_target_pairs={{0,2},{2,0},{4,6},{6,4},{8,10},{10,8},{12,14},{14,12},{1,3},{3,1},... | collective-permute-start | bytes 245768 | tf_op jit(solution)/shard_map/ppermute | solution.py:481
  6.4 0.0 collective-permute-start
  6.4 0.2 %taps.1 = (bf16[512,256]{1,0:T(8,128)(2,1)S(1)}, bf16[512,256]{1,0:T(8,128)(2,1)S(1)}) custom-call(), custom_call_target="tpu_custom_call" | custom-call | flops 10240000000 | bytes 1638400 | tf_op jit(solution)/shard_map/taps/pallas_call | solution.py:485
  6.6 0.0 copy-done.2
  6.6 0.0 copy-done.3
  6.6 0.0 copy-done.4
  6.7 0.0 copy-done.5
  6.7 0.0 copy-done.6
  6.7 0.0 copy-done.7
  6.7 0.0 copy-done.8
  6.7 0.0 copy-start
  6.7 0.0 copy-start.1
  6.7 0.7 %weights.1 = (f32[16,8,640]{2,1,0:T(8,128)S(1)}, f32[16,8,640]{2,1,0:T(8,128)S(1)}, f32[16,8,640]{2,1,0:T(8,128)S(1)}, f32[16,8,640]{2,1,0:T(8,128)S(1)}, f32[16...) custom-call(f32[16,8,640]{2,1,0:T(8,128)S(1)} %pad_maximum_fusion.waves, f32[16,4,640]{2,1,0:T(4,128)S(1)} %copy-done.2, ...), custom_call_target="tpu_custom_call" | custom-call | flops 4096000 | bytes 1638400 | tf_op jit(solution)/shard_map/weights/pallas_call | solution.py:486
  7.4 0.6 %collective-permute-done.other = f32[16,8,640]{2,1,0:T(8,128)S(1)} collective-permute-done((f32[16,8,640]{2,1,0:T(8,128)S(1)}, f32[16,8,640]{2,1,0:T(8,128)S(1)}, u32[]{:S(2)}, u32[]{:S(2)}) %collective-permute-start) | collective-permute-done | bytes 327712 | tf_op jit(solution)/shard_map/ppermute | solution.py:482
  8.0 0.0 copy-done
  8.0 0.0 copy-done.1
  8.0 1.8 %interior.1 = (f32[8,8,640]{2,1,0:T(8,128)S(1)}, f32[8,8,640]{2,1,0:T(8,128)S(1)}, f32[8,8,640]{2,1,0:T(8,128)S(1)}, f32[32,640]{1,0:T(8,128)S(1)}) custom-call(f32[16,8,640]{2,1,0:T(8,128)S(1)} %pad_maximum_fusion.waves, f32[16,8,640]{2,1,0:T(8,128)S(1)} %collective-permute-done.other, f32[16,8,640]{2,1,0:T(8,128)S(1)} %get-tuple-element.44.axis_x, ...), custom_call_target="tpu_custom_call" | custom-call | flops 4096000 | bytes 1638400 | tf_op jit(solution)/shard_map/interior/pallas_call | solution.py:494
  9.8 0.0 collective-permute-done.1
  9.9 0.0 collective-permute-done.2
  9.9 0.2 collective-permute-start.3
  10.1 0.0 copy-start.9
  10.1 0.3 %halo.1 = (f32[8,8,640]{2,1,0:T(8,128)S(1)}, f32[8,8,640]{2,1,0:T(8,128)S(1)}) custom-call(f32[8,8,640]{2,1,0:T(8,128)S(1)} %constant_dynamic-update-slice_fusion.edges, f32[16,8,640]{2,1,0:T(8,128)S(1)} %get-tuple-element.44.axis_x, f32[16,8,640]{2,1,0:T(8,128)S(1)} %get-tuple-element.45.axis_y, f32[16,8,640]{2,1,0:T(8,128)S(1)} %get-tuple-element.46.axis_z, ...), custom_call_target="tpu_custom_call" | custom-call | flops 4096000 | bytes 1638400 | tf_op jit(solution)/shard_map/halo/pallas_call | solution.py:500
  10.4 0.9 %collective-permute-done.3.edges_other = f32[8,8,640]{2,1,0:T(8,128)S(1)} collective-permute-done((f32[8,8,640]{2,1,0:T(8,128)S(1)}, f32[8,8,640]{2,1,0:T(8,128)S(1)}, u32[]{:S(2)}, u32[]{:S(2)}) %collective-permute-start.3) | collective-permute-done | bytes 163872 | tf_op jit(solution)/shard_map/ppermute | solution.py:499
  11.4 0.0 copy-done.9
  11.4 0.0 copy-done.10
  11.4 0.8 %step.1 = (f32[8,8,640]{2,1,0:T(8,128)S(1)}, f32[64,640]{1,0:T(8,128)S(1)}, f32[24,640]{1,0:T(8,128)S(1)}, f32[24,640]{1,0:T(8,128)S(1)}, f32[8,640]{1,0:T(8,128)S(1)}, /*index=5*/f32[8,640]{1,0:T(8,128)S(1)}) custom-call(f32[8,8,640]{2,1,0:T(8,128)S(1)} %collective-permute-done.3.edges_other, f32[8,8,640]{2,1,0:T(8,128)S(1)} %get-tuple-element.61.h_edge, ...), custom_call_target="tpu_custom_call" | custom-call | flops 16384000 | bytes 1638400 | tf_op jit(solution)/shard_map/step/pallas_call | solution.py:518
  12.1 3.5 %collective-permute-start.4 = (f32[24,640]{1,0:T(8,128)S(1)}, f32[24,640]{1,0:T(8,128)S(1)}, u32[]{:S(2)}, u32[]{:S(2)}) collective-permute-start(f32[24,640]{1,0:T(8,128)S(1)} %get-tuple-element.69), channel_id=1, source_target_pairs={{0,14},{2,4},{4,2},{6,8},{8,6},{10,12},{12,10},{14,0},{1,15},{3,5}... | collective-permute-start | bytes 184328 | tf_op jit(solution)/shard_map/ppermute | solution.py:524
  15.6 0.0 collective-permute-start.5
  15.6 1.9 %collective-permute-start.6 = (f32[8,640]{1,0:T(8,128)S(1)}, f32[8,640]{1,0:T(8,128)S(1)}, u32[]{:S(2)}, u32[]{:S(2)}) collective-permute-start(f32[8,640]{1,0:T(8,128)S(1)} %get-tuple-element.72), channel_id=1, source_target_pairs={{0,12},{2,14},{4,8},{6,10},{8,4},{10,6},{12,0},{14,2},{1,13},{3,15... | collective-permute-start | bytes 61448 | tf_op jit(solution)/shard_map/ppermute | solution.py:524
  17.5 1.2 %collective-permute-start.7 = (f32[8,640]{1,0:T(8,128)S(1)}, f32[8,640]{1,0:T(8,128)S(1)}, u32[]{:S(2)}, u32[]{:S(2)}) collective-permute-start(f32[8,640]{1,0:T(8,128)S(1)} %get-tuple-element.73), channel_id=1, source_target_pairs={{0,4},{2,6},{4,0},{6,2},{8,12},{10,14},{12,8},{14,10},{1,5},{3,7},... | collective-permute-start | bytes 61448 | tf_op jit(solution)/shard_map/ppermute | solution.py:524
  18.7 0.0 copy-done.11
  18.7 0.0 copy-done.12
  18.7 0.8 %own.1 = (f32[16,4,640]{2,1,0:T(4,128)}, f32[16,4,640]{2,1,0:T(4,128)}, f32[64,640]{1,0:T(8,128)S(1)}) custom-call(f32[8,8,640]{2,1,0:T(8,128)S(1)} %get-tuple-element.52.inside, f32[8,8,640]{2,1,0:T(8,128)S(1)} %get-tuple-element.64.outside, f32[64,640]{1,0:T(8,128)S(1)} %get-tuple-element.65.crossline, bf16[64,64]{1,0:T(8,128)(2,1)S(1)} %copy-done.12, ...), custom_call_target="tpu_custom_call" | custom-call | flops 4096000 | bytes 1638400 | tf_op jit(solution)/shard_map/own/pallas_call | solution.py:526
  19.5 0.0 collective-permute-done.4.rest_0_
  19.5 0.7 %collective-permute-done.5.rest_1_ = f32[24,640]{1,0:T(8,128)S(1)} collective-permute-done((f32[24,640]{1,0:T(8,128)S(1)}, f32[24,640]{1,0:T(8,128)S(1)}, u32[]{:S(2)}, u32[]{:S(2)}) %collective-permute-start.5) | collective-permute-done | bytes 61472 | tf_op jit(solution)/shard_map/ppermute | solution.py:524
  20.3 0.7 %fine.1 = (f32[8,4,640]{2,1,0:T(4,128)}, f32[4,4,640]{2,1,0:T(4,128)}) custom-call(f32[64,640]{1,0:T(8,128)S(1)} %get-tuple-element.68.mine, f32[24,640]{1,0:T(8,128)S(1)} %collective-permute-done.4.rest_0_, f32[24,640]{1,0:T(8,128)S(1)} %collective-permute-done.5.rest_1_), custom_call_target="tpu_custom_call" | custom-call | flops 819200 | bytes 1638400 | tf_op jit(solution)/shard_map/fine/pallas_call | solution.py:532
  21.0 0.2 collective-permute-done.6.rest_2_
  21.2 0.2 collective-permute-done.7.rest_3_
  21.4 0.7 %coarse.1 = (f32[2,4,640]{2,1,0:T(4,128)}, f32[2,4,640]{2,1,0:T(4,128)}) custom-call(f32[64,640]{1,0:T(8,128)S(1)} %get-tuple-element.68.mine, f32[24,640]{1,0:T(8,128)S(1)} %collective-permute-done.4.rest_0_, f32[24,640]{1,0:T(8,128)S(1)} %collective-permute-done.5.rest_1_, f32[8,640]{1,0:T(8,128)S(1)} %collective-permute-done.6.rest_2_, ...), custom_call_target="tpu_custom_call" | custom-call | flops 819200 | bytes 1638400 | tf_op jit(solution)/shard_map/coarse/pallas_call | solution.py:536
  (6 shorter events, 0.0 us)
Async XLA Ops:
  1.7 4.9 %copy-start.2 = (f32[16,4,640]{2,1,0:T(4,128)S(1)}, f32[16,4,640]{2,1,0:T(4,128)}, u32[]{:S(2)}) copy-start(f32[16,4,640]{2,1,0:T(4,128)} %prior_p.1) | copy-start | bytes 491524
  1.7 4.9 %copy-start.3 = (f32[16,4,640]{2,1,0:T(4,128)S(1)}, f32[16,4,640]{2,1,0:T(4,128)}, u32[]{:S(2)}) copy-start(f32[16,4,640]{2,1,0:T(4,128)} %prior_q.1) | copy-start | bytes 491524
  1.8 4.9 %copy-start.4 = (bf16[16,4,640]{2,1,0:T(4,128)(2,1)S(1)}, bf16[16,4,640]{2,1,0:T(4,128)(2,1)}, u32[]{:S(2)}) copy-start(bf16[16,4,640]{2,1,0:T(4,128)(2,1)} %courant.1) | copy-start | bytes 245764
  1.8 4.9 %copy-start.5 = (bf16[16,4,640]{2,1,0:T(4,128)(2,1)S(1)}, bf16[16,4,640]{2,1,0:T(4,128)(2,1)}, u32[]{:S(2)}) copy-start(bf16[16,4,640]{2,1,0:T(4,128)(2,1)} %epsilon.1) | copy-start | bytes 245764
  1.8 4.9 %copy-start.6 = (bf16[16,4,640]{2,1,0:T(4,128)(2,1)S(1)}, bf16[16,4,640]{2,1,0:T(4,128)(2,1)}, u32[]{:S(2)}) copy-start(bf16[16,4,640]{2,1,0:T(4,128)(2,1)} %delta.1) | copy-start | bytes 245764
  1.8 4.9 %copy-start.7 = (bf16[16,4,640]{2,1,0:T(4,128)(2,1)S(1)}, bf16[16,4,640]{2,1,0:T(4,128)(2,1)}, u32[]{:S(2)}) copy-start(bf16[16,4,640]{2,1,0:T(4,128)(2,1)} %tilt.1) | copy-start | bytes 245764
  1.8 4.9 %copy-start.8 = (bf16[16,4,640]{2,1,0:T(4,128)(2,1)S(1)}, bf16[16,4,640]{2,1,0:T(4,128)(2,1)}, u32[]{:S(2)}) copy-start(bf16[16,4,640]{2,1,0:T(4,128)(2,1)} %azimuth.1) | copy-start | bytes 245764
  1.8 8.0 %collective-permute-start.1 = (f32[4,8,640]{2,1,0:T(8,128)S(1)}, f32[4,8,640]{2,1,0:T(8,128)S(1)}, u32[]{:S(2)}, u32[]{:S(2)}) collective-permute-start(f32[4,8,640]{2,1,0:T(8,128)S(1)} %get-tuple-element.55), channel_id=1, source_target_pairs={{0,1},{1,0},{2,4},{3,5},{4,2},{5,3},{6,8},{7,9},{8,6},{9,7},{10,12... | collective-permute-start | bytes 245768 | tf_op jit(solution)/shard_map/ppermute | solution.py:480
  2.3 7.5 %collective-permute-start.2 = (f32[4,8,640]{2,1,0:T(8,128)S(1)}, f32[4,8,640]{2,1,0:T(8,128)S(1)}, u32[]{:S(2)}, u32[]{:S(2)}) collective-permute-start(f32[4,8,640]{2,1,0:T(8,128)S(1)} %get-tuple-element.56), channel_id=1, source_target_pairs={{0,2},{2,0},{4,6},{6,4},{8,10},{10,8},{12,14},{14,12},{1,3},{3,1},... | collective-permute-start | bytes 245768 | tf_op jit(solution)/shard_map/ppermute | solution.py:481
  6.4 1.6 %collective-permute-start = (f32[16,8,640]{2,1,0:T(8,128)S(1)}, f32[16,8,640]{2,1,0:T(8,128)S(1)}, u32[]{:S(2)}, u32[]{:S(2)}) collective-permute-start(f32[16,8,640]{2,1,0:T(8,128)S(1)} %pad_maximum_fusion.waves), channel_id=1, source_target_pairs={{0,1},{1,0},{2,3},{3,2},{4,5},{5,4},{6,7},{7,6},{8,9},{9,8},{10,11... | collective-permute-start | bytes 983048 | tf_op jit(solution)/shard_map/ppermute | solution.py:482
  6.7 1.3 %copy-start = (bf16[384,128]{1,0:T(8,128)(2,1)S(1)}, bf16[384,128]{1,0:T(8,128)(2,1)}, u32[]{:S(2)}) copy-start(bf16[384,128]{1,0:T(8,128)(2,1)} %constant.33.clone.block_low) | copy-start | bytes 294916
  6.7 1.3 %copy-start.1 = (bf16[384,128]{1,0:T(8,128)(2,1)S(1)}, bf16[384,128]{1,0:T(8,128)(2,1)}, u32[]{:S(2)}) copy-start(bf16[384,128]{1,0:T(8,128)(2,1)} %constant.32.clone.block_high) | copy-start | bytes 294916
  9.9 1.5 %collective-permute-start.3 = (f32[8,8,640]{2,1,0:T(8,128)S(1)}, f32[8,8,640]{2,1,0:T(8,128)S(1)}, u32[]{:S(2)}, u32[]{:S(2)}) collective-permute-start(f32[8,8,640]{2,1,0:T(8,128)S(1)} %constant_dynamic-update-slice_fusion.edges), channel_id=1, source_target_pairs={{0,1},{1,0},{2,3},{3,2},{4,5},{5,4},{6,7},{7,6},{8,9},{9,8},{10,11... | collective-permute-start | bytes 491528 | tf_op jit(solution)/shard_map/ppermute | solution.py:499
  10.1 1.3 %copy-start.9 = (bf16[64,64]{1,0:T(8,128)(2,1)S(1)}, bf16[64,64]{1,0:T(8,128)(2,1)}, u32[]{:S(2)}) copy-start(bf16[64,64]{1,0:T(8,128)(2,1)} %constant.35.clone.inline_low) | copy-start | bytes 24580
  10.1 1.3 %copy-start.10 = (bf16[64,64]{1,0:T(8,128)(2,1)S(1)}, bf16[64,64]{1,0:T(8,128)(2,1)}, u32[]{:S(2)}) copy-start(bf16[64,64]{1,0:T(8,128)(2,1)} %constant.34.clone.inline_high) | copy-start | bytes 24580
  11.4 7.3 %copy-start.11 = (bf16[64,64]{1,0:T(8,128)(2,1)S(1)}, bf16[64,64]{1,0:T(8,128)(2,1)}, u32[]{:S(2)}) copy-start(bf16[64,64]{1,0:T(8,128)(2,1)} %constant.37.clone.own_low) | copy-start | bytes 24580
  11.4 7.3 %copy-start.12 = (bf16[64,64]{1,0:T(8,128)(2,1)S(1)}, bf16[64,64]{1,0:T(8,128)(2,1)}, u32[]{:S(2)}) copy-start(bf16[64,64]{1,0:T(8,128)(2,1)} %constant.36.clone.own_high) | copy-start | bytes 24580
  12.1 7.4 %collective-permute-start.4 = (f32[24,640]{1,0:T(8,128)S(1)}, f32[24,640]{1,0:T(8,128)S(1)}, u32[]{:S(2)}, u32[]{:S(2)}) collective-permute-start(f32[24,640]{1,0:T(8,128)S(1)} %get-tuple-element.69), channel_id=1, source_target_pairs={{0,14},{2,4},{4,2},{6,8},{8,6},{10,12},{12,10},{14,0},{1,15},{3,5}... | collective-permute-start | bytes 184328 | tf_op jit(solution)/shard_map/ppermute | solution.py:524
  15.6 4.7 %collective-permute-start.5 = (f32[24,640]{1,0:T(8,128)S(1)}, f32[24,640]{1,0:T(8,128)S(1)}, u32[]{:S(2)}, u32[]{:S(2)}) collective-permute-start(f32[24,640]{1,0:T(8,128)S(1)} %get-tuple-element.70), channel_id=1, source_target_pairs={{0,2},{2,0},{4,6},{6,4},{8,10},{10,8},{12,14},{14,12},{1,3},{3,1},... | collective-permute-start | bytes 184328 | tf_op jit(solution)/shard_map/ppermute | solution.py:524
  15.6 5.6 %collective-permute-start.6 = (f32[8,640]{1,0:T(8,128)S(1)}, f32[8,640]{1,0:T(8,128)S(1)}, u32[]{:S(2)}, u32[]{:S(2)}) collective-permute-start(f32[8,640]{1,0:T(8,128)S(1)} %get-tuple-element.72), channel_id=1, source_target_pairs={{0,12},{2,14},{4,8},{6,10},{8,4},{10,6},{12,0},{14,2},{1,13},{3,15... | collective-permute-start | bytes 61448 | tf_op jit(solution)/shard_map/ppermute | solution.py:524
  17.5 3.9 %collective-permute-start.7 = (f32[8,640]{1,0:T(8,128)S(1)}, f32[8,640]{1,0:T(8,128)S(1)}, u32[]{:S(2)}, u32[]{:S(2)}) collective-permute-start(f32[8,640]{1,0:T(8,128)S(1)} %get-tuple-element.73), channel_id=1, source_target_pairs={{0,4},{2,6},{4,0},{6,2},{8,12},{10,14},{12,8},{14,10},{1,5},{3,7},... | collective-permute-start | bytes 61448 | tf_op jit(solution)/shard_map/ppermute | solution.py:524

commit v20 on v14

--- a/solution.py
+++ b/solution.py
@@ -314,10 +314,10 @@
     crossline[...] = crossline_of(ready, block_high[...], block_low[...])
 
 
-def halo_rows(size, edges):
+def halo_rows(size, edges, other_core=False):
     place = lax.axis_index("xy")
-    even = place % 2 == 0
-    left_at, right_at = jnp.where(even, 0, 4), jnp.where(even, 4, 0)
+    first = (place % 2 == 0) == (lax.axis_index("gz") == (1 if other_core else 0))
+    left_at, right_at = jnp.where(first, 0, 4), jnp.where(first, 4, 0)
     left_in = jnp.where(place > 0, 1.0, 0.0)
     right_in = jnp.where(place < size - 1, 1.0, 0.0)
     before = [edges[left_at + x] * left_in for x in range(4)]
@@ -377,7 +377,7 @@
 
     slopes = [
         first_of(*depth_neighbours(own, far, lower))
-        for own, far in zip(halo_rows(size, edges), halo_rows(size, edges_other))
+        for own, far in zip(halo_rows(size, edges), halo_rows(size, edges_other, True))
     ]
     for row in range(8):
         x = row if row < 4 else rows - 8 + row
@@ -466,14 +466,23 @@
 
     waves = lax.optimization_barrier(jnp.concatenate([wave_p, wave_q], axis=1))
     leading, last = waves[:4], waves[rows - 4 :]
-    open_outer = [
-        (2 * i + g, 2 * i + 1 - g) if abs(i - j) > 1 else (2 * i + g, 2 * j + g)
-        for i, j in pairs[0]
-        for g in range(2)
-    ]
+    shots = lax.axis_size("shot")
+
+    def mixed(outer_core):
+        swaps = []
+        for shot in range(shots):
+            for i in range(size):
+                for core in range(2):
+                    j = pairs[0 if core == outer_core else 1][i][1]
+                    to = (shot, j) if abs(i - j) == 1 else ((shot + 1) % shots, i)
+                    swaps.append(((shot * size + i) * 2 + core, (to[0] * size + to[1]) * 2 + core))
+        return swaps
+
+    first = even == (lax.axis_index("gz") == 0)
+    everywhere = ("shot", "xy", "gz")
     other = lax.ppermute(waves, "gz", cores)
-    inner = lax.ppermute(jnp.where(even, last, leading), "xy", pairs[1])
-    outer = lax.ppermute(jnp.where(even, leading, last), ("xy", "gz"), open_outer)
+    edges_first = lax.ppermute(jnp.where(first, leading, last), everywhere, mixed(0))
+    edges_second = lax.ppermute(jnp.where(first, last, leading), everywhere, mixed(1))
 
     taps = jax.ShapeDtypeStruct((4 * LANES, 2 * LANES), jnp.bfloat16)
     axis_x, axis_y, axis_z, *gains, taps_first, taps_second = kernel(
@@ -487,8 +496,10 @@
     h_own, sum_own, inside, crossline = kernel(
         interior_kernel, [edge, edge, inside, ready], 100, "interior", [work] * 5
     )(waves, other, axis_x, axis_y, axis_z, *gains, taps_first, taps_second, *block)
-    h_own, sum_own, inner, outer = lax.optimization_barrier((h_own, sum_own, inner, outer))
-    edges = jnp.concatenate([outer, inner], axis=0)
+    h_own, sum_own, edges_first, edges_second = lax.optimization_barrier(
+        (h_own, sum_own, edges_first, edges_second)
+    )
+    edges = jnp.concatenate([edges_first, edges_second], axis=0)
     edges_other = lax.ppermute(edges, "gz", cores)
     h_edge, sum_edge = kernel(functools.partial(halo_kernel, size), [edge] * 2, 100, "halo")(
         edges, axis_x, axis_y, h_own, sum_own, taps_first

time: 22.3 us -> 22.8 us (1.022)
  starting transfers between devices: 11 us -> 12.1 us
  waiting for transfers between devices: 3.02 us -> 2.38 us
    ppermute x2, starting transfers between devices: 2.78 us -> 4.16 us  [the longest x1 2.64 us: body(): lax.ppermute(jnp.where(first, leading, last), everywhere, mixed(0))]
    ppermute x2, waiting for transfers between devices: 1.03 us -> 0.04 us  [the longest x1 0.04 us: body(): lax.ppermute(jnp.where(first, last, leading), everywhere, mixed(1))]
    ppermute x4, waiting for transfers between devices: 0.89 us -> 1.25 us  [body(): lax.ppermute(send, 'xy', pair)]
  transfers between devices with their start and end apart: 8 -> 8, of which waited for: 3 -> 3; matrix products, arithmetic and copies ran while one was open for 0% -> 0% of each run, Pallas kernels for 21% -> 20%
where the time goes in v20:
time: 22.8 us; the launch traced here: 22.7 us
  starting transfers between devices  12.1 us (53%)
  Pallas kernels  6.11 us (27%)
  waiting for transfers between devices  2.38 us (10%)
  other arithmetic  1.15 us (5%)
  between operations  0.82 us (4%)
    ppermute x4, starting transfers between devices, body(): lax.ppermute(send, 'xy', pair)  7.39 us
    ppermute x1, starting transfers between devices, body(): lax.ppermute(jnp.where(first, leading, last), everywhere, mixed(0))  2.64 us
    pallas_call x1, Pallas kernels, body(): kernel(interior_kernel, [edge, edge, inside, ready], 100, 'interior', [wo...  1.83 us
    ppermute x1, starting transfers between devices, body(): lax.ppermute(jnp.where(first, last, leading), everywhere, mixed(1))  1.52 us
    ppermute x4, waiting for transfers between devices, body(): lax.ppermute(send, 'xy', pair)  1.25 us
    concatenate x1, other arithmetic, body(): waves = lax.optimization_barrier(jnp.concatenate([wave_p, wave_q], axis=1))  1.13 us
    ppermute x1, waiting for transfers between devices, body(): edges_other = lax.ppermute(edges, 'gz', cores)  1.08 us
    pallas_call x1, Pallas kernels, body(): kernel(weights_kernel, [stack] * 6 + [taps] * 2, 100, 'weights')  0.95 us
  transfers between devices with their start and end apart: 8, of which 3 were waited for; matrix products, arithmetic and copies ran while one was open for 0% of the time, Pallas kernels for 20%

profile of v20, /device:TPU:0, one launch (start us, length us, event | category | flops | bytes accessed | tf_op | source)
XLA Modules:
  0.0 22.7 jit_solution(8410541380570019577)
XLA Ops:
  0.6 0.0 copy-start.4
  0.6 0.0 copy-start.5
  0.7 0.0 copy-start.6
  0.7 0.0 copy-start.7
  0.7 0.0 copy-start.8
  0.7 1.1 %pad_maximum_fusion.waves = f32[16,8,640]{2,1,0:T(8,128)S(1)} fusion(f32[16,4,640]{2,1,0:T(4,128)} %param.16, f32[16,4,640]{2,1,0:T(4,128)} %param.15), kind=kLoop, calls=%fused_computation | loop fusion | flops 81920 | bytes 655360 | tf_op jit(solution)/shard_map/concatenate | solution.py:467
  1.8 0.5 %collective-permute-start = (f32[16,8,640]{2,1,0:T(8,128)S(1)}, f32[16,8,640]{2,1,0:T(8,128)S(1)}, u32[]{:S(2)}, u32[]{:S(2)}) collective-permute-start(f32[16,8,640]{2,1,0:T(8,128)S(1)} %pad_maximum_fusion.waves), channel_id=1, source_target_pairs={{0,1},{1,0},{2,3},{3,2},{4,5},{5,4},{6,7},{7,6},{8,9},{9,8},{10,11... | collective-permute-start | bytes 983048 | tf_op jit(solution)/shard_map/ppermute | solution.py:483
  2.3 0.0 copy-start.2
  2.3 0.0 copy-start.3
  2.4 2.6 %collective-permute-start.1 = (f32[4,8,640]{2,1,0:T(8,128)S(1)}, f32[4,8,640]{2,1,0:T(8,128)S(1)}, u32[]{:S(2)}, u32[]{:S(2)}) collective-permute-start(f32[4,8,640]{2,1,0:T(8,128)S(1)} %get-tuple-element.75), channel_id=1, source_target_pairs={{0,16},{1,3},{2,4},{3,1},{4,2},{5,7},{6,8},{7,5},{8,6},{9,11},{10,... | collective-permute-start | bytes 245768 | tf_op jit(solution)/shard_map/ppermute | solution.py:484
  5.0 0.0 copy-start
  5.0 0.0 copy-start.1
  5.0 1.5 %collective-permute-start.2 = (f32[4,8,640]{2,1,0:T(8,128)S(1)}, f32[4,8,640]{2,1,0:T(8,128)S(1)}, u32[]{:S(2)}, u32[]{:S(2)}) collective-permute-start(f32[4,8,640]{2,1,0:T(8,128)S(1)} %get-tuple-element.74), channel_id=1, source_target_pairs={{0,2},{1,17},{2,0},{3,5},{4,6},{5,3},{6,4},{7,9},{8,10},{9,7},{10,... | collective-permute-start | bytes 245768 | tf_op jit(solution)/shard_map/ppermute | solution.py:485
  6.5 0.0 copy-done.4
  6.5 0.0 copy-done.5
  6.5 0.0 copy-done.6
  6.5 0.0 copy-done.7
  6.5 0.0 copy-done.8
  6.5 0.0 copy-done.2
  6.6 0.0 copy-done.3
  6.6 1.0 %weights.1 = (f32[16,8,640]{2,1,0:T(8,128)S(1)}, f32[16,8,640]{2,1,0:T(8,128)S(1)}, f32[16,8,640]{2,1,0:T(8,128)S(1)}, f32[16,8,640]{2,1,0:T(8,128)S(1)}, f32[16...) custom-call(f32[16,8,640]{2,1,0:T(8,128)S(1)} %pad_maximum_fusion.wa, ...), custom_call_target="tpu_custom_call" | custom-call | flops 4096000 | bytes 1638400 | tf_op jit(solution)/shard_map/weights/pallas_call | solution.py:488
  7.5 0.0 collective-permute-done.other
  7.5 0.0 copy-done
  7.5 0.0 copy-done.1
  7.6 1.8 %interior.1 = (f32[8,8,640]{2,1,0:T(8,128)S(1)}, f32[8,8,640]{2,1,0:T(8,128)S(1)}, f32[8,8,640]{2,1,0:T(8,128)S(1)}, f32[32,640]{1,0:T(8,128)S(1)}) custom-call(f32[16,8,640]{2,1,0:T(8,128)S(1)} %pad_maximum_fusion.waves, f32[16,8,640]{2,1,0:T(8,128)S(1)} %collective-permute-done.other, f32[16,8,640]{2,1,0:T(8,128)S(1)} %get-tuple-element.40.axis_x, ...), custom_call_target="tpu_custom_call" | custom-call | flops 4096000 | bytes 1638400 | tf_op jit(solution)/shard_map/interior/pallas_call | solution.py:496
  9.4 0.0 collective-permute-done.1
  9.4 0.0 collective-permute-done.2
  9.5 0.1 collective-permute-start.3
  9.5 0.0 copy-start.9
  9.6 0.0 copy-start.10
  9.6 0.3 %halo.1 = (f32[8,8,640]{2,1,0:T(8,128)S(1)}, f32[8,8,640]{2,1,0:T(8,128)S(1)}) custom-call(f32[8,8,640]{2,1,0:T(8,128)S(1)} %constant_dynamic-update-slice_fusion.edges, f32[16,8,640]{2,1,0:T(8,128)S(1)} %get-tuple-element.40.axis_x, f32[16,8,640]{2,1,0:T(8,128)S(1)} %get-tuple-element.41.axis_y, f32[8,8,640]{2,1,0:T(8,128)S(1)} %get-tuple-element.53.h_own, ...), custom_call_target="tpu_custom_call" | custom-call | flops 4096000 | bytes 1638400 | tf_op jit(solution)/shard_map/halo/pallas_call | solution.py:504
  9.8 1.1 %collective-permute-done.3.edges_other = f32[8,8,640]{2,1,0:T(8,128)S(1)} collective-permute-done((f32[8,8,640]{2,1,0:T(8,128)S(1)}, f32[8,8,640]{2,1,0:T(8,128)S(1)}, u32[]{:S(2)}, u32[]{:S(2)}) %collective-permute-start.3) | collective-permute-done | bytes 163872 | tf_op jit(solution)/shard_map/ppermute | solution.py:503
  10.9 0.0 copy-done.9
  10.9 0.0 copy-done.10
  10.9 0.8 %step.1 = (f32[8,8,640]{2,1,0:T(8,128)S(1)}, f32[64,640]{1,0:T(8,128)S(1)}, f32[24,640]{1,0:T(8,128)S(1)}, f32[24,640]{1,0:T(8,128)S(1)}, f32[8,640]{1,0:T(8,128)S(1)}, /*index=5*/f32[8,640]{1,0:T(8,128)S(1)}) custom-call(f32[8,8,640]{2,1,0:T(8,128)S(1)} %constant_dynamic-update-slice_fusion.edges, f32[8,8,640]{2,1,0:T(8,128)S(1)} %collective-permute-done.3.edges_other, ...), custom_call_target="tpu_custom_call" | custom-call | flops 16384000 | bytes 1638400 | tf_op jit(solution)/shard_map/step/pallas_call | solution.py:521
  11.7 4.6 %collective-permute-start.4 = (f32[24,640]{1,0:T(8,128)S(1)}, f32[24,640]{1,0:T(8,128)S(1)}, u32[]{:S(2)}, u32[]{:S(2)}) collective-permute-start(f32[24,640]{1,0:T(8,128)S(1)} %get-tuple-element.63), channel_id=1, source_target_pairs={{0,14},{2,4},{4,2},{6,8},{8,6},{10,12},{12,10},{14,0},{1,15},{3,5}... | collective-permute-start | bytes 184328 | tf_op jit(solution)/shard_map/ppermute | solution.py:527
  16.3 0.0 collective-permute-start.5
  16.3 1.3 %collective-permute-start.6 = (f32[8,640]{1,0:T(8,128)S(1)}, f32[8,640]{1,0:T(8,128)S(1)}, u32[]{:S(2)}, u32[]{:S(2)}) collective-permute-start(f32[8,640]{1,0:T(8,128)S(1)} %get-tuple-element.66), channel_id=1, source_target_pairs={{0,12},{2,14},{4,8},{6,10},{8,4},{10,6},{12,0},{14,2},{1,13},{3,15... | collective-permute-start | bytes 61448 | tf_op jit(solution)/shard_map/ppermute | solution.py:527
  17.7 1.5 %collective-permute-start.7 = (f32[8,640]{1,0:T(8,128)S(1)}, f32[8,640]{1,0:T(8,128)S(1)}, u32[]{:S(2)}, u32[]{:S(2)}) collective-permute-start(f32[8,640]{1,0:T(8,128)S(1)} %get-tuple-element.67), channel_id=1, source_target_pairs={{0,4},{2,6},{4,0},{6,2},{8,12},{10,14},{12,8},{14,10},{1,5},{3,7},... | collective-permute-start | bytes 61448 | tf_op jit(solution)/shard_map/ppermute | solution.py:527
  19.1 0.0 copy-done.11
  19.1 0.0 copy-done.12
  19.1 0.8 %own.1 = (f32[16,4,640]{2,1,0:T(4,128)}, f32[16,4,640]{2,1,0:T(4,128)}, f32[64,640]{1,0:T(8,128)S(1)}) custom-call(f32[8,8,640]{2,1,0:T(8,128)S(1)} %get-tuple-element.48.inside, f32[8,8,640]{2,1,0:T(8,128)S(1)} %get-tuple-element.58.outside, f32[64,640]{1,0:T(8,128)S(1)} %get-tuple-element.59.crossline, bf16[64,64]{1,0:T(8,128)(2,1)S(1)} %copy-done.11, ...), custom_call_target="tpu_custom_call" | custom-call | flops 4096000 | bytes 1638400 | tf_op jit(solution)/shard_map/own/pallas_call | solution.py:529
  20.0 0.0 collective-permute-done.4.rest_0_
  20.0 0.6 %collective-permute-done.5.rest_1_ = f32[24,640]{1,0:T(8,128)S(1)} collective-permute-done((f32[24,640]{1,0:T(8,128)S(1)}, f32[24,640]{1,0:T(8,128)S(1)}, u32[]{:S(2)}, u32[]{:S(2)}) %collective-permute-start.5) | collective-permute-done | bytes 61472 | tf_op jit(solution)/shard_map/ppermute | solution.py:527
  20.6 0.7 %fine.1 = (f32[8,4,640]{2,1,0:T(4,128)}, f32[4,4,640]{2,1,0:T(4,128)}) custom-call(f32[64,640]{1,0:T(8,128)S(1)} %get-tuple-element.62.mine, f32[24,640]{1,0:T(8,128)S(1)} %collective-permute-done.4.rest_0_, f32[24,640]{1,0:T(8,128)S(1)} %collective-permute-done.5.rest_1_), custom_call_target="tpu_custom_call" | custom-call | flops 819200 | bytes 1638400 | tf_op jit(solution)/shard_map/fine/pallas_call | solution.py:535
  21.3 0.6 %collective-permute-done.6.rest_2_ = f32[8,640]{1,0:T(8,128)S(1)} collective-permute-done((f32[8,640]{1,0:T(8,128)S(1)}, f32[8,640]{1,0:T(8,128)S(1)}, u32[]{:S(2)}, u32[]{:S(2)}) %collective-permute-start.6) | collective-permute-done | bytes 20512 | tf_op jit(solution)/shard_map/ppermute | solution.py:527
  21.9 0.0 collective-permute-done.7.rest_3_
  21.9 0.7 %coarse.1 = (f32[2,4,640]{2,1,0:T(4,128)}, f32[2,4,640]{2,1,0:T(4,128)}) custom-call(f32[64,640]{1,0:T(8,128)S(1)} %get-tuple-element.62.mine, f32[24,640]{1,0:T(8,128)S(1)} %collective-permute-done.4.rest_0_, f32[24,640]{1,0:T(8,128)S(1)} %collective-permute-done.5.rest_1_, f32[8,640]{1,0:T(8,128)S(1)} %collective-permute-done.6.rest_2_, ...), custom_call_target="tpu_custom_call" | custom-call | flops 819200 | bytes 1638400 | tf_op jit(solution)/shard_map/coarse/pallas_call | solution.py:539
  (5 shorter events, 0.0 us)
Async XLA Ops:
  0.6 5.9 %copy-start.4 = (bf16[16,4,640]{2,1,0:T(4,128)(2,1)S(1)}, bf16[16,4,640]{2,1,0:T(4,128)(2,1)}, u32[]{:S(2)}) copy-start(bf16[16,4,640]{2,1,0:T(4,128)(2,1)} %courant.1) | copy-start | bytes 245764
  0.6 5.9 %copy-start.5 = (bf16[16,4,640]{2,1,0:T(4,128)(2,1)S(1)}, bf16[16,4,640]{2,1,0:T(4,128)(2,1)}, u32[]{:S(2)}) copy-start(bf16[16,4,640]{2,1,0:T(4,128)(2,1)} %epsilon.1) | copy-start | bytes 245764
  0.7 5.9 %copy-start.6 = (bf16[16,4,640]{2,1,0:T(4,128)(2,1)S(1)}, bf16[16,4,640]{2,1,0:T(4,128)(2,1)}, u32[]{:S(2)}) copy-start(bf16[16,4,640]{2,1,0:T(4,128)(2,1)} %delta.1) | copy-start | bytes 245764
  0.7 5.9 %copy-start.7 = (bf16[16,4,640]{2,1,0:T(4,128)(2,1)S(1)}, bf16[16,4,640]{2,1,0:T(4,128)(2,1)}, u32[]{:S(2)}) copy-start(bf16[16,4,640]{2,1,0:T(4,128)(2,1)} %tilt.1) | copy-start | bytes 245764
  0.7 5.9 %copy-start.8 = (bf16[16,4,640]{2,1,0:T(4,128)(2,1)S(1)}, bf16[16,4,640]{2,1,0:T(4,128)(2,1)}, u32[]{:S(2)}) copy-start(bf16[16,4,640]{2,1,0:T(4,128)(2,1)} %azimuth.1) | copy-start | bytes 245764
  1.8 5.7 %collective-permute-start = (f32[16,8,640]{2,1,0:T(8,128)S(1)}, f32[16,8,640]{2,1,0:T(8,128)S(1)}, u32[]{:S(2)}, u32[]{:S(2)}) collective-permute-start(f32[16,8,640]{2,1,0:T(8,128)S(1)} %pad_maximum_fusion.waves), channel_id=1, source_target_pairs={{0,1},{1,0},{2,3},{3,2},{4,5},{5,4},{6,7},{7,6},{8,9},{9,8},{10,11... | collective-permute-start | bytes 983048 | tf_op jit(solution)/shard_map/ppermute | solution.py:483
  2.3 4.2 %copy-start.2 = (f32[16,4,640]{2,1,0:T(4,128)S(1)}, f32[16,4,640]{2,1,0:T(4,128)}, u32[]{:S(2)}) copy-start(f32[16,4,640]{2,1,0:T(4,128)} %prior_p.1) | copy-start | bytes 491524
  2.3 4.2 %copy-start.3 = (f32[16,4,640]{2,1,0:T(4,128)S(1)}, f32[16,4,640]{2,1,0:T(4,128)}, u32[]{:S(2)}) copy-start(f32[16,4,640]{2,1,0:T(4,128)} %prior_q.1) | copy-start | bytes 491524
  2.4 7.0 %collective-permute-start.1 = (f32[4,8,640]{2,1,0:T(8,128)S(1)}, f32[4,8,640]{2,1,0:T(8,128)S(1)}, u32[]{:S(2)}, u32[]{:S(2)}) collective-permute-start(f32[4,8,640]{2,1,0:T(8,128)S(1)} %get-tuple-element.75), channel_id=1, source_target_pairs={{0,16},{1,3},{2,4},{3,1},{4,2},{5,7},{6,8},{7,5},{8,6},{9,11},{10,... | collective-permute-start | bytes 245768 | tf_op jit(solution)/shard_map/ppermute | solution.py:484
  5.0 2.5 %copy-start = (bf16[384,128]{1,0:T(8,128)(2,1)S(1)}, bf16[384,128]{1,0:T(8,128)(2,1)}, u32[]{:S(2)}) copy-start(bf16[384,128]{1,0:T(8,128)(2,1)} %constant.34.clone.block_high) | copy-start | bytes 294916
  5.0 2.5 %copy-start.1 = (bf16[384,128]{1,0:T(8,128)(2,1)S(1)}, bf16[384,128]{1,0:T(8,128)(2,1)}, u32[]{:S(2)}) copy-start(bf16[384,128]{1,0:T(8,128)(2,1)} %constant.35.clone.block_low) | copy-start | bytes 294916
  5.0 4.4 %collective-permute-start.2 = (f32[4,8,640]{2,1,0:T(8,128)S(1)}, f32[4,8,640]{2,1,0:T(8,128)S(1)}, u32[]{:S(2)}, u32[]{:S(2)}) collective-permute-start(f32[4,8,640]{2,1,0:T(8,128)S(1)} %get-tuple-element.74), channel_id=1, source_target_pairs={{0,2},{1,17},{2,0},{3,5},{4,6},{5,3},{6,4},{7,9},{8,10},{9,7},{10,... | collective-permute-start | bytes 245768 | tf_op jit(solution)/shard_map/ppermute | solution.py:485
  9.5 1.5 %collective-permute-start.3 = (f32[8,8,640]{2,1,0:T(8,128)S(1)}, f32[8,8,640]{2,1,0:T(8,128)S(1)}, u32[]{:S(2)}, u32[]{:S(2)}) collective-permute-start(f32[8,8,640]{2,1,0:T(8,128)S(1)} %constant_dynamic-update-slice_fusion.edges), channel_id=1, source_target_pairs={{0,1},{1,0},{2,3},{3,2},{4,5},{5,4},{6,7},{7,6},{8,9},{9,8},{10,11... | collective-permute-start | bytes 491528 | tf_op jit(solution)/shard_map/ppermute | solution.py:503
  9.5 1.4 %copy-start.9 = (bf16[64,64]{1,0:T(8,128)(2,1)S(1)}, bf16[64,64]{1,0:T(8,128)(2,1)}, u32[]{:S(2)}) copy-start(bf16[64,64]{1,0:T(8,128)(2,1)} %constant.36.clone.inline_high) | copy-start | bytes 24580
  9.6 1.4 %copy-start.10 = (bf16[64,64]{1,0:T(8,128)(2,1)S(1)}, bf16[64,64]{1,0:T(8,128)(2,1)}, u32[]{:S(2)}) copy-start(bf16[64,64]{1,0:T(8,128)(2,1)} %constant.37.clone.inline_low) | copy-start | bytes 24580
  10.9 8.2 %copy-start.11 = (bf16[64,64]{1,0:T(8,128)(2,1)S(1)}, bf16[64,64]{1,0:T(8,128)(2,1)}, u32[]{:S(2)}) copy-start(bf16[64,64]{1,0:T(8,128)(2,1)} %constant.38.clone.own_high) | copy-start | bytes 24580
  10.9 8.2 %copy-start.12 = (bf16[64,64]{1,0:T(8,128)(2,1)S(1)}, bf16[64,64]{1,0:T(8,128)(2,1)}, u32[]{:S(2)}) copy-start(bf16[64,64]{1,0:T(8,128)(2,1)} %constant.39.clone.own_low) | copy-start | bytes 24580
  11.7 8.2 %collective-permute-start.4 = (f32[24,640]{1,0:T(8,128)S(1)}, f32[24,640]{1,0:T(8,128)S(1)}, u32[]{:S(2)}, u32[]{:S(2)}) collective-permute-start(f32[24,640]{1,0:T(8,128)S(1)} %get-tuple-element.63), channel_id=1, source_target_pairs={{0,14},{2,4},{4,2},{6,8},{8,6},{10,12},{12,10},{14,0},{1,15},{3,5}... | collective-permute-start | bytes 184328 | tf_op jit(solution)/shard_map/ppermute | solution.py:527
  16.3 4.2 %collective-permute-start.5 = (f32[24,640]{1,0:T(8,128)S(1)}, f32[24,640]{1,0:T(8,128)S(1)}, u32[]{:S(2)}, u32[]{:S(2)}) collective-permute-start(f32[24,640]{1,0:T(8,128)S(1)} %get-tuple-element.64), channel_id=1, source_target_pairs={{0,2},{2,0},{4,6},{6,4},{8,10},{10,8},{12,14},{14,12},{1,3},{3,1},... | collective-permute-start | bytes 184328 | tf_op jit(solution)/shard_map/ppermute | solution.py:527
  16.3 5.6 %collective-permute-start.6 = (f32[8,640]{1,0:T(8,128)S(1)}, f32[8,640]{1,0:T(8,128)S(1)}, u32[]{:S(2)}, u32[]{:S(2)}) collective-permute-start(f32[8,640]{1,0:T(8,128)S(1)} %get-tuple-element.66), channel_id=1, source_target_pairs={{0,12},{2,14},{4,8},{6,10},{8,4},{10,6},{12,0},{14,2},{1,13},{3,15... | collective-permute-start | bytes 61448 | tf_op jit(solution)/shard_map/ppermute | solution.py:527
  17.7 4.3 %collective-permute-start.7 = (f32[8,640]{1,0:T(8,128)S(1)}, f32[8,640]{1,0:T(8,128)S(1)}, u32[]{:S(2)}, u32[]{:S(2)}) collective-permute-start(f32[8,640]{1,0:T(8,128)S(1)} %get-tuple-element.67), channel_id=1, source_target_pairs={{0,4},{2,6},{4,0},{6,2},{8,12},{10,14},{12,8},{14,10},{1,5},{3,7},... | collective-permute-start | bytes 61448 | tf_op jit(solution)/shard_map/ppermute | solution.py:527

commit v21 on v19

--- a/solution.py
+++ b/solution.py
@@ -494,7 +494,7 @@
     h_own, sum_own, inside, crossline = kernel(
         interior_kernel, [edge, edge, inside, ready], 100, "interior", [work] * 5
     )(waves, other, axis_x, axis_y, axis_z, *gains, taps_first, taps_second, *block)
-    h_own, sum_own, outer, inner = lax.optimization_barrier((h_own, sum_own, outer, inner))
+    h_own, sum_own, inner, outer = lax.optimization_barrier((h_own, sum_own, inner, outer))
     edges = jnp.concatenate([outer, inner], axis=0)
     edges_other = lax.ppermute(edges, "gz", cores)
     h_edge, sum_edge = kernel(functools.partial(halo_kernel, size), [edge] * 2, 100, "halo")(

time: 22.3 us -> 22.1 us (level)
  waiting for transfers between devices: 2.65 us -> 1.85 us
  starting transfers between devices: 11.3 us -> 11.9 us
    ppermute x4, starting transfers between devices: 6.55 us -> 7.95 us  [body(): lax.ppermute(send, 'xy', pair)]
    ppermute x1, starting transfers between devices: 4.03 us -> 3 us  [body(): inner = lax.ppermute(to_inner, 'xy', pairs[1])]
    ppermute x1, starting transfers between devices: 0.52 us -> 0.01 us  [body(): outer = lax.ppermute(to_outer, ('xy', 'gz'), open_outer)]
    ppermute x1, starting transfers between devices: 0.01 us -> 0.51 us  [body(): other = lax.ppermute(fields, 'gz', cores)]
    ppermute x1, waiting for transfers between devices: 0.56 us -> 0.19 us  [body(): other = lax.ppermute(fields, 'gz', cores)]
    ppermute x1, waiting for transfers between devices: 0.9 us -> 0.68 us  [body(): edges_other = lax.ppermute(edges, 'gz', cores)]
    ppermute x1, starting transfers between devices: 0.2 us -> 0.43 us  [body(): edges_other = lax.ppermute(edges, 'gz', cores)]
  transfers between devices with their start and end apart: 8 -> 8, of which waited for: 5 -> 3; matrix products, arithmetic and copies ran while one was open for 0% -> 0% of each run, Pallas kernels for 21% -> 21%
where the time goes in v21:
time: 22.1 us; the launch traced here: 21.9 us
  starting transfers between devices  11.9 us (54%)
  Pallas kernels  6.16 us (28%)
  waiting for transfers between devices  1.85 us (8%)
  other arithmetic  1.08 us (5%)
  between operations  0.85 us (4%)
    ppermute x4, starting transfers between devices, body(): lax.ppermute(send, 'xy', pair)  7.95 us
    ppermute x1, starting transfers between devices, body(): inner = lax.ppermute(to_inner, 'xy', pairs[1])  3 us
    pallas_call x1, Pallas kernels, body(): kernel(interior_kernel, [edge, edge, inside, ready], 100, 'interior', [wo...  1.83 us
    concatenate x1, other arithmetic, body(): waves = lax.optimization_barrier(jnp.concatenate([wave_p, wave_q], axis=1))  1.07 us
    ppermute x4, waiting for transfers between devices, body(): lax.ppermute(send, 'xy', pair)  0.96 us
    pallas_call x1, Pallas kernels, body(): kernel(own_kernel, [grid, grid, flat], 100, 'own')  0.82 us
    pallas_call x1, Pallas kernels, body(): kernel(functools.partial(step_kernel, size, gives), [edge, flat] + [jax.S...  0.76 us
    pallas_call x1, Pallas kernels, body(): kernel(functools.partial(finish_kernel, counts[0] + counts[1], takes), ou...  0.73 us
  transfers between devices with their start and end apart: 8, of which 3 were waited for; matrix products, arithmetic and copies ran while one was open for 0% of the time, Pallas kernels for 21%

profile of v21, /device:TPU:0, one launch (start us, length us, event | category | flops | bytes accessed | tf_op | source)
XLA Modules:
  0.0 21.9 jit_solution(13517875135760534259)
XLA Ops:
  0.6 1.1 %pad_maximum_fusion.waves = f32[16,8,640]{2,1,0:T(8,128)S(1)} fusion(f32[16,4,640]{2,1,0:T(4,128)} %param.16, f32[16,4,640]{2,1,0:T(4,128)} %param.15), kind=kLoop, calls=%fused_computation | loop fusion | flops 81920 | bytes 655360 | tf_op jit(solution)/shard_map/concatenate | solution.py:471
  1.7 0.0 copy-start.2
  1.7 0.0 copy-start.3
  1.8 0.0 copy-start.4
  1.8 0.0 copy-start.5
  1.8 0.0 copy-start.6
  1.8 0.0 copy-start.7
  1.8 0.0 copy-start.8
  1.8 3.0 %collective-permute-start.1 = (f32[4,8,640]{2,1,0:T(8,128)S(1)}, f32[4,8,640]{2,1,0:T(8,128)S(1)}, u32[]{:S(2)}, u32[]{:S(2)}) collective-permute-start(f32[4,8,640]{2,1,0:T(8,128)S(1)} %get-tuple-element.55), channel_id=1, source_target_pairs={{0,2},{2,0},{4,6},{6,4},{8,10},{10,8},{12,14},{14,12},{1,3},{3,1},... | collective-permute-start | bytes 245768 | tf_op jit(solution)/shard_map/ppermute | solution.py:481
  4.8 0.0 collective-permute-start.2
  4.8 0.5 %collective-permute-start = (f32[16,8,640]{2,1,0:T(8,128)S(1)}, f32[16,8,640]{2,1,0:T(8,128)S(1)}, u32[]{:S(2)}, u32[]{:S(2)}) collective-permute-start(f32[16,8,640]{2,1,0:T(8,128)S(1)} %pad_maximum_fusion.waves), channel_id=1, source_target_pairs={{0,1},{1,0},{2,3},{3,2},{4,5},{5,4},{6,7},{7,6},{8,9},{9,8},{10,11... | collective-permute-start | bytes 983048 | tf_op jit(solution)/shard_map/ppermute | solution.py:482
  5.3 0.2 %taps.1 = (bf16[512,256]{1,0:T(8,128)(2,1)S(1)}, bf16[512,256]{1,0:T(8,128)(2,1)S(1)}) custom-call(), custom_call_target="tpu_custom_call" | custom-call | flops 10240000000 | bytes 1638400 | tf_op jit(solution)/shard_map/taps/pallas_call | solution.py:485
  5.6 0.0 copy-done.2
  5.6 0.0 copy-done.3
  5.6 0.0 copy-done.4
  5.6 0.0 copy-done.5
  5.6 0.0 copy-done.6
  5.6 0.0 copy-done.7
  5.6 0.0 copy-done.8
  5.7 0.0 copy-start
  5.7 0.0 copy-start.1
  5.7 0.7 %weights.1 = (f32[16,8,640]{2,1,0:T(8,128)S(1)}, f32[16,8,640]{2,1,0:T(8,128)S(1)}, f32[16,8,640]{2,1,0:T(8,128)S(1)}, f32[16,8,640]{2,1,0:T(8,128)S(1)}, f32[16...) custom-call(f32[16,8,640]{2,1,0:T(8,128)S(1)} %pad_maximum_fusion.waves, f32[16,4,640]{2,1,0:T(4,128)S(1)} %copy-done.2, ...), custom_call_target="tpu_custom_call" | custom-call | flops 4096000 | bytes 1638400 | tf_op jit(solution)/shard_map/weights/pallas_call | solution.py:486
  6.4 0.2 collective-permute-done.other
  6.6 0.0 copy-done
  6.6 0.0 copy-done.1
  6.6 1.8 %interior.1 = (f32[8,8,640]{2,1,0:T(8,128)S(1)}, f32[8,8,640]{2,1,0:T(8,128)S(1)}, f32[8,8,640]{2,1,0:T(8,128)S(1)}, f32[32,640]{1,0:T(8,128)S(1)}) custom-call(f32[16,8,640]{2,1,0:T(8,128)S(1)} %pad_maximum_fusion.waves, f32[16,8,640]{2,1,0:T(8,128)S(1)} %collective-permute-done.other, f32[16,8,640]{2,1,0:T(8,128)S(1)} %get-tuple-element.44.axis_x, ...), custom_call_target="tpu_custom_call" | custom-call | flops 4096000 | bytes 1638400 | tf_op jit(solution)/shard_map/interior/pallas_call | solution.py:494
  8.4 0.0 collective-permute-done.1
  8.5 0.0 collective-permute-done.2
  8.5 0.4 %collective-permute-start.3 = (f32[8,8,640]{2,1,0:T(8,128)S(1)}, f32[8,8,640]{2,1,0:T(8,128)S(1)}, u32[]{:S(2)}, u32[]{:S(2)}) collective-permute-start(f32[8,8,640]{2,1,0:T(8,128)S(1)} %constant_dynamic-update-slice_fusion.edges), channel_id=1, source_target_pairs={{0,1},{1,0},{2,3},{3,2},{4,5},{5,4},{6,7},{7,6},{8,9},{9,8},{10,11... | collective-permute-start | bytes 491528 | tf_op jit(solution)/shard_map/ppermute | solution.py:499
  8.9 0.0 copy-start.9
  8.9 0.3 %halo.1 = (f32[8,8,640]{2,1,0:T(8,128)S(1)}, f32[8,8,640]{2,1,0:T(8,128)S(1)}) custom-call(f32[8,8,640]{2,1,0:T(8,128)S(1)} %constant_dynamic-update-slice_fusion.edges, f32[16,8,640]{2,1,0:T(8,128)S(1)} %get-tuple-element.44.axis_x, f32[16,8,640]{2,1,0:T(8,128)S(1)} %get-tuple-element.45.axis_y, f32[16,8,640]{2,1,0:T(8,128)S(1)} %get-tuple-element.46.axis_z, ...), custom_call_target="tpu_custom_call" | custom-call | flops 4096000 | bytes 1638400 | tf_op jit(solution)/shard_map/halo/pallas_call | solution.py:500
  9.3 0.7 %collective-permute-done.3.edges_other = f32[8,8,640]{2,1,0:T(8,128)S(1)} collective-permute-done((f32[8,8,640]{2,1,0:T(8,128)S(1)}, f32[8,8,640]{2,1,0:T(8,128)S(1)}, u32[]{:S(2)}, u32[]{:S(2)}) %collective-permute-start.3) | collective-permute-done | bytes 163872 | tf_op jit(solution)/shard_map/ppermute | solution.py:499
  10.0 0.0 copy-done.9
  10.0 0.0 copy-done.10
  10.0 0.8 %step.1 = (f32[8,8,640]{2,1,0:T(8,128)S(1)}, f32[64,640]{1,0:T(8,128)S(1)}, f32[24,640]{1,0:T(8,128)S(1)}, f32[24,640]{1,0:T(8,128)S(1)}, f32[8,640]{1,0:T(8,128)S(1)}, /*index=5*/f32[8,640]{1,0:T(8,128)S(1)}) custom-call(f32[8,8,640]{2,1,0:T(8,128)S(1)} %collective-permute-done.3.edges_other, f32[8,8,640]{2,1,0:T(8,128)S(1)} %get-tuple-element.61.h_edge, ...), custom_call_target="tpu_custom_call" | custom-call | flops 16384000 | bytes 1638400 | tf_op jit(solution)/shard_map/step/pallas_call | solution.py:518
  10.7 3.9 %collective-permute-start.4 = (f32[24,640]{1,0:T(8,128)S(1)}, f32[24,640]{1,0:T(8,128)S(1)}, u32[]{:S(2)}, u32[]{:S(2)}) collective-permute-start(f32[24,640]{1,0:T(8,128)S(1)} %get-tuple-element.69), channel_id=1, source_target_pairs={{0,14},{2,4},{4,2},{6,8},{8,6},{10,12},{12,10},{14,0},{1,15},{3,5}... | collective-permute-start | bytes 184328 | tf_op jit(solution)/shard_map/ppermute | solution.py:524
  14.6 0.9 %collective-permute-start.5 = (f32[24,640]{1,0:T(8,128)S(1)}, f32[24,640]{1,0:T(8,128)S(1)}, u32[]{:S(2)}, u32[]{:S(2)}) collective-permute-start(f32[24,640]{1,0:T(8,128)S(1)} %get-tuple-element.70), channel_id=1, source_target_pairs={{0,2},{2,0},{4,6},{6,4},{8,10},{10,8},{12,14},{14,12},{1,3},{3,1},... | collective-permute-start | bytes 184328 | tf_op jit(solution)/shard_map/ppermute | solution.py:524
  15.5 1.7 %collective-permute-start.6 = (f32[8,640]{1,0:T(8,128)S(1)}, f32[8,640]{1,0:T(8,128)S(1)}, u32[]{:S(2)}, u32[]{:S(2)}) collective-permute-start(f32[8,640]{1,0:T(8,128)S(1)} %get-tuple-element.72), channel_id=1, source_target_pairs={{0,12},{2,14},{4,8},{6,10},{8,4},{10,6},{12,0},{14,2},{1,13},{3,15... | collective-permute-start | bytes 61448 | tf_op jit(solution)/shard_map/ppermute | solution.py:524
  17.2 1.5 %collective-permute-start.7 = (f32[8,640]{1,0:T(8,128)S(1)}, f32[8,640]{1,0:T(8,128)S(1)}, u32[]{:S(2)}, u32[]{:S(2)}) collective-permute-start(f32[8,640]{1,0:T(8,128)S(1)} %get-tuple-element.73), channel_id=1, source_target_pairs={{0,4},{2,6},{4,0},{6,2},{8,12},{10,14},{12,8},{14,10},{1,5},{3,7},... | collective-permute-start | bytes 61448 | tf_op jit(solution)/shard_map/ppermute | solution.py:524
  18.7 0.0 copy-done.11
  18.7 0.0 copy-done.12
  18.7 0.8 %own.1 = (f32[16,4,640]{2,1,0:T(4,128)}, f32[16,4,640]{2,1,0:T(4,128)}, f32[64,640]{1,0:T(8,128)S(1)}) custom-call(f32[8,8,640]{2,1,0:T(8,128)S(1)} %get-tuple-element.52.inside, f32[8,8,640]{2,1,0:T(8,128)S(1)} %get-tuple-element.64.outside, f32[64,640]{1,0:T(8,128)S(1)} %get-tuple-element.65.crossline, bf16[64,64]{1,0:T(8,128)(2,1)S(1)} %copy-done.12, ...), custom_call_target="tpu_custom_call" | custom-call | flops 4096000 | bytes 1638400 | tf_op jit(solution)/shard_map/own/pallas_call | solution.py:526
  19.5 0.0 collective-permute-done.4.rest_0_
  19.5 0.0 collective-permute-done.5.rest_1_
  19.5 0.7 %fine.1 = (f32[8,4,640]{2,1,0:T(4,128)}, f32[4,4,640]{2,1,0:T(4,128)}) custom-call(f32[64,640]{1,0:T(8,128)S(1)} %get-tuple-element.68.mine, f32[24,640]{1,0:T(8,128)S(1)} %collective-permute-done.4.rest_0_, f32[24,640]{1,0:T(8,128)S(1)} %collective-permute-done.5.rest_1_), custom_call_target="tpu_custom_call" | custom-call | flops 819200 | bytes 1638400 | tf_op jit(solution)/shard_map/fine/pallas_call | solution.py:532
  20.2 0.9 %collective-permute-done.6.rest_2_ = f32[8,640]{1,0:T(8,128)S(1)} collective-permute-done((f32[8,640]{1,0:T(8,128)S(1)}, f32[8,640]{1,0:T(8,128)S(1)}, u32[]{:S(2)}, u32[]{:S(2)}) %collective-permute-start.6) | collective-permute-done | bytes 20512 | tf_op jit(solution)/shard_map/ppermute | solution.py:524
  21.2 0.0 collective-permute-done.7.rest_3_
  21.2 0.7 %coarse.1 = (f32[2,4,640]{2,1,0:T(4,128)}, f32[2,4,640]{2,1,0:T(4,128)}) custom-call(f32[64,640]{1,0:T(8,128)S(1)} %get-tuple-element.68.mine, f32[24,640]{1,0:T(8,128)S(1)} %collective-permute-done.4.rest_0_, f32[24,640]{1,0:T(8,128)S(1)} %collective-permute-done.5.rest_1_, f32[8,640]{1,0:T(8,128)S(1)} %collective-permute-done.6.rest_2_, ...), custom_call_target="tpu_custom_call" | custom-call | flops 819200 | bytes 1638400 | tf_op jit(solution)/shard_map/coarse/pallas_call | solution.py:536
  (6 shorter events, 0.0 us)
Async XLA Ops:
  1.7 3.9 %copy-start.2 = (f32[16,4,640]{2,1,0:T(4,128)S(1)}, f32[16,4,640]{2,1,0:T(4,128)}, u32[]{:S(2)}) copy-start(f32[16,4,640]{2,1,0:T(4,128)} %prior_p.1) | copy-start | bytes 491524
  1.7 3.8 %copy-start.3 = (f32[16,4,640]{2,1,0:T(4,128)S(1)}, f32[16,4,640]{2,1,0:T(4,128)}, u32[]{:S(2)}) copy-start(f32[16,4,640]{2,1,0:T(4,128)} %prior_q.1) | copy-start | bytes 491524
  1.8 3.8 %copy-start.4 = (bf16[16,4,640]{2,1,0:T(4,128)(2,1)S(1)}, bf16[16,4,640]{2,1,0:T(4,128)(2,1)}, u32[]{:S(2)}) copy-start(bf16[16,4,640]{2,1,0:T(4,128)(2,1)} %courant.1) | copy-start | bytes 245764
  1.8 3.8 %copy-start.5 = (bf16[16,4,640]{2,1,0:T(4,128)(2,1)S(1)}, bf16[16,4,640]{2,1,0:T(4,128)(2,1)}, u32[]{:S(2)}) copy-start(bf16[16,4,640]{2,1,0:T(4,128)(2,1)} %epsilon.1) | copy-start | bytes 245764
  1.8 3.8 %copy-start.6 = (bf16[16,4,640]{2,1,0:T(4,128)(2,1)S(1)}, bf16[16,4,640]{2,1,0:T(4,128)(2,1)}, u32[]{:S(2)}) copy-start(bf16[16,4,640]{2,1,0:T(4,128)(2,1)} %delta.1) | copy-start | bytes 245764
  1.8 3.8 %copy-start.7 = (bf16[16,4,640]{2,1,0:T(4,128)(2,1)S(1)}, bf16[16,4,640]{2,1,0:T(4,128)(2,1)}, u32[]{:S(2)}) copy-start(bf16[16,4,640]{2,1,0:T(4,128)(2,1)} %tilt.1) | copy-start | bytes 245764
  1.8 3.8 %copy-start.8 = (bf16[16,4,640]{2,1,0:T(4,128)(2,1)S(1)}, bf16[16,4,640]{2,1,0:T(4,128)(2,1)}, u32[]{:S(2)}) copy-start(bf16[16,4,640]{2,1,0:T(4,128)(2,1)} %azimuth.1) | copy-start | bytes 245764
  1.8 6.6 %collective-permute-start.1 = (f32[4,8,640]{2,1,0:T(8,128)S(1)}, f32[4,8,640]{2,1,0:T(8,128)S(1)}, u32[]{:S(2)}, u32[]{:S(2)}) collective-permute-start(f32[4,8,640]{2,1,0:T(8,128)S(1)} %get-tuple-element.55), channel_id=1, source_target_pairs={{0,2},{2,0},{4,6},{6,4},{8,10},{10,8},{12,14},{14,12},{1,3},{3,1},... | collective-permute-start | bytes 245768 | tf_op jit(solution)/shard_map/ppermute | solution.py:481
  4.8 3.6 %collective-permute-start.2 = (f32[4,8,640]{2,1,0:T(8,128)S(1)}, f32[4,8,640]{2,1,0:T(8,128)S(1)}, u32[]{:S(2)}, u32[]{:S(2)}) collective-permute-start(f32[4,8,640]{2,1,0:T(8,128)S(1)} %get-tuple-element.56), channel_id=1, source_target_pairs={{0,1},{1,0},{2,4},{3,5},{4,2},{5,3},{6,8},{7,9},{8,6},{9,7},{10,12... | collective-permute-start | bytes 245768 | tf_op jit(solution)/shard_map/ppermute | solution.py:480
  4.8 1.8 %collective-permute-start = (f32[16,8,640]{2,1,0:T(8,128)S(1)}, f32[16,8,640]{2,1,0:T(8,128)S(1)}, u32[]{:S(2)}, u32[]{:S(2)}) collective-permute-start(f32[16,8,640]{2,1,0:T(8,128)S(1)} %pad_maximum_fusion.waves), channel_id=1, source_target_pairs={{0,1},{1,0},{2,3},{3,2},{4,5},{5,4},{6,7},{7,6},{8,9},{9,8},{10,11... | collective-permute-start | bytes 983048 | tf_op jit(solution)/shard_map/ppermute | solution.py:482
  5.7 0.9 %copy-start = (bf16[384,128]{1,0:T(8,128)(2,1)S(1)}, bf16[384,128]{1,0:T(8,128)(2,1)}, u32[]{:S(2)}) copy-start(bf16[384,128]{1,0:T(8,128)(2,1)} %constant.33.clone.block_low) | copy-start | bytes 294916
  5.7 0.9 %copy-start.1 = (bf16[384,128]{1,0:T(8,128)(2,1)S(1)}, bf16[384,128]{1,0:T(8,128)(2,1)}, u32[]{:S(2)}) copy-start(bf16[384,128]{1,0:T(8,128)(2,1)} %constant.32.clone.block_high) | copy-start | bytes 294916
  8.5 1.5 %collective-permute-start.3 = (f32[8,8,640]{2,1,0:T(8,128)S(1)}, f32[8,8,640]{2,1,0:T(8,128)S(1)}, u32[]{:S(2)}, u32[]{:S(2)}) collective-permute-start(f32[8,8,640]{2,1,0:T(8,128)S(1)} %constant_dynamic-update-slice_fusion.edges), channel_id=1, source_target_pairs={{0,1},{1,0},{2,3},{3,2},{4,5},{5,4},{6,7},{7,6},{8,9},{9,8},{10,11... | collective-permute-start | bytes 491528 | tf_op jit(solution)/shard_map/ppermute | solution.py:499
  8.9 1.0 %copy-start.9 = (bf16[64,64]{1,0:T(8,128)(2,1)S(1)}, bf16[64,64]{1,0:T(8,128)(2,1)}, u32[]{:S(2)}) copy-start(bf16[64,64]{1,0:T(8,128)(2,1)} %constant.35.clone.inline_low) | copy-start | bytes 24580
  8.9 1.0 %copy-start.10 = (bf16[64,64]{1,0:T(8,128)(2,1)S(1)}, bf16[64,64]{1,0:T(8,128)(2,1)}, u32[]{:S(2)}) copy-start(bf16[64,64]{1,0:T(8,128)(2,1)} %constant.34.clone.inline_high) | copy-start | bytes 24580
  10.0 8.7 %copy-start.11 = (bf16[64,64]{1,0:T(8,128)(2,1)S(1)}, bf16[64,64]{1,0:T(8,128)(2,1)}, u32[]{:S(2)}) copy-start(bf16[64,64]{1,0:T(8,128)(2,1)} %constant.37.clone.own_low) | copy-start | bytes 24580
  10.0 8.7 %copy-start.12 = (bf16[64,64]{1,0:T(8,128)(2,1)S(1)}, bf16[64,64]{1,0:T(8,128)(2,1)}, u32[]{:S(2)}) copy-start(bf16[64,64]{1,0:T(8,128)(2,1)} %constant.36.clone.own_high) | copy-start | bytes 24580
  10.7 8.8 %collective-permute-start.4 = (f32[24,640]{1,0:T(8,128)S(1)}, f32[24,640]{1,0:T(8,128)S(1)}, u32[]{:S(2)}, u32[]{:S(2)}) collective-permute-start(f32[24,640]{1,0:T(8,128)S(1)} %get-tuple-element.69), channel_id=1, source_target_pairs={{0,14},{2,4},{4,2},{6,8},{8,6},{10,12},{12,10},{14,0},{1,15},{3,5}... | collective-permute-start | bytes 184328 | tf_op jit(solution)/shard_map/ppermute | solution.py:524
  14.6 4.9 %collective-permute-start.5 = (f32[24,640]{1,0:T(8,128)S(1)}, f32[24,640]{1,0:T(8,128)S(1)}, u32[]{:S(2)}, u32[]{:S(2)}) collective-permute-start(f32[24,640]{1,0:T(8,128)S(1)} %get-tuple-element.70), channel_id=1, source_target_pairs={{0,2},{2,0},{4,6},{6,4},{8,10},{10,8},{12,14},{14,12},{1,3},{3,1},... | collective-permute-start | bytes 184328 | tf_op jit(solution)/shard_map/ppermute | solution.py:524
  15.5 5.7 %collective-permute-start.6 = (f32[8,640]{1,0:T(8,128)S(1)}, f32[8,640]{1,0:T(8,128)S(1)}, u32[]{:S(2)}, u32[]{:S(2)}) collective-permute-start(f32[8,640]{1,0:T(8,128)S(1)} %get-tuple-element.72), channel_id=1, source_target_pairs={{0,12},{2,14},{4,8},{6,10},{8,4},{10,6},{12,0},{14,2},{1,13},{3,15... | collective-permute-start | bytes 61448 | tf_op jit(solution)/shard_map/ppermute | solution.py:524
  17.2 4.0 %collective-permute-start.7 = (f32[8,640]{1,0:T(8,128)S(1)}, f32[8,640]{1,0:T(8,128)S(1)}, u32[]{:S(2)}, u32[]{:S(2)}) collective-permute-start(f32[8,640]{1,0:T(8,128)S(1)} %get-tuple-element.73), channel_id=1, source_target_pairs={{0,4},{2,6},{4,0},{6,2},{8,12},{10,14},{12,8},{14,10},{1,5},{3,7},... | collective-permute-start | bytes 61448 | tf_op jit(solution)/shard_map/ppermute | solution.py:524

commit v22 on v21

--- a/solution.py
+++ b/solution.py
@@ -269,6 +269,7 @@
     h_own,
     sum_own,
     inside,
+    packed,
     crossline,
     dz,
     dzz,
@@ -313,6 +314,7 @@
             row = x if x < 4 else x - rows + 8
             h_own[row], sum_own[row] = h_one, total
     ready = packed_rows([inside[x] for x in range(rows - 8)])
+    packed[...] = ready
     crossline[...] = crossline_of(ready, block_high[...], block_low[...])
 
 
@@ -365,13 +367,11 @@
     gain_a,
     gain_b,
     base,
-    block_high,
-    block_low,
-    crossline_inside,
+    packed_inside,
     inline_high,
     inline_low,
     outside,
-    crossline,
+    packed,
     *sends,
 ):
     rows = axis_x.shape[0]
@@ -389,10 +389,9 @@
         h_one = h_edge[row] + 2.0 * (axis_x[x] * axis_z[x] * dxz)
         outside[row] = pressure_of(h_one, sum_edge[row], gain_a[x], gain_b[x], base[x])
     ready = packed_rows([outside[row] for row in range(8)])
-    edge = crossline_of(ready, block_high[...], block_low[...])
-    transformed = jnp.concatenate([edge[:16], crossline_inside[...], edge[16:]], axis=0)
-    crossline[...] = transformed
-    parts = dot3(inline_high[...], inline_low[...], *halves(transformed))
+    packed[...] = ready
+    ordered = jnp.concatenate([ready[:16], packed_inside[...], ready[16:]], axis=0)
+    parts = dot3(inline_high[...], inline_low[...], *halves(ordered))
     to_next, to_previous, to_second_next, to_second_previous = (
         parts[start : start + count] for start, count in gives
     )
@@ -402,7 +401,9 @@
     sends[3][...] = jnp.where(early, to_second_next, to_second_previous)
 
 
-def own_kernel(inside, outside, crossline, own_high, own_low, next_p, next_q, mine):
+def own_kernel(
+    inside, outside, packed, crossline, block_high, block_low, own_high, own_low, next_p, next_q, mine
+):
     rows = next_p.shape[0]
     for x in range(rows):
         if 4 <= x < rows - 4:
@@ -411,23 +412,36 @@
             value = outside[x if x < 4 else x - rows + 8]
         next_p[x] = value[:4]
         next_q[x] = value[4:]
-    mine[...] = dot3(own_high[...], own_low[...], *halves(crossline[...]))
-
-
-def finish_kernel(at, takes, mine, *rest):
+    edge = crossline_of(packed[...], block_high[...], block_low[...])
+    ordered = jnp.concatenate([edge[:16], crossline[...], edge[16:]], axis=0)
+    mine[...] = dot3(own_high[...], own_low[...], *halves(ordered))
+
+
+def finish_kernel(at, takes, mine, block_high, block_low, *rest):
     received, outs = [ref[...] for ref in rest[: len(takes)]], rest[len(takes) :]
     place = lax.axis_index("xy")
     for first, near in zip(range(0, len(takes), 2), (place % 2 == 0, place % 4 < 2)):
         outer, inner = received[first : first + 2]
         received[first : first + 2] = jnp.where(near, outer, inner), jnp.where(near, inner, outer)
+    wanted = range(at, at + sum(out.shape[0] for out in outs))
+    given = {}
+    for row in wanted:
+        for take, got in zip(takes, received):
+            for j in range(take.shape[1]):
+                factor = float(take[row, j])
+                if abs(factor) > 1e-13:
+                    term = factor * got[4 * j : 4 * j + 4]
+                    given[row] = given[row] + term if row in given else term
+    places = {row: 4 * k for k, row in enumerate(given)}
+    pieces = list(given.values())
+    pieces += [jnp.zeros_like(pieces[0])] * (-len(pieces) % 4)
+    pairs = [jnp.concatenate(pieces[k : k + 2], axis=0) for k in range(0, len(pieces), 2)]
+    across_rows = crossline_of(jnp.concatenate(pairs, axis=0), block_high[...], block_low[...])
     for out in outs:
         for row in range(out.shape[0]):
             total = mine[4 * at : 4 * at + 4]
-            for take, got in zip(takes, received):
-                for j in range(take.shape[1]):
-                    factor = float(take[at, j])
-                    if abs(factor) > 1e-13:
-                        total = total + factor * got[4 * j : 4 * j + 4]
+            if at in places:
+                total = total + across_rows[places[at] : places[at] + 4]
             out[row] = total
             at += 1
 
@@ -491,8 +505,8 @@
     edge = jax.ShapeDtypeStruct((8, 8, width), f32)
     inside = jax.ShapeDtypeStruct((rows - 8, 8, width), f32)
     ready = jax.ShapeDtypeStruct((layers * (rows - 8), width), f32)
-    h_own, sum_own, inside, crossline = kernel(
-        interior_kernel, [edge, edge, inside, ready], 100, "interior", [work] * 5
+    h_own, sum_own, inside, packed_inside, crossline = kernel(
+        interior_kernel, [edge, edge, inside, ready, ready], 100, "interior", [work] * 5
     )(waves, other, axis_x, axis_y, axis_z, *gains, taps_first, taps_second, *block)
     h_own, sum_own, inner, outer = lax.optimization_barrier((h_own, sum_own, inner, outer))
     edges = jnp.concatenate([outer, inner], axis=0)
@@ -515,27 +529,28 @@
     inline_own = parts(np.kron(own, np.eye(4)))
     flat = jax.ShapeDtypeStruct((layers * rows, width), f32)
     sizes = [count for _, count in gives]
-    outside, crossline, *sends = kernel(
+    packed_edge = jax.ShapeDtypeStruct((layers * 8, width), f32)
+    outside, packed, *sends = kernel(
         functools.partial(step_kernel, size, gives),
-        [edge, flat] + [jax.ShapeDtypeStruct((count, width), f32) for count in sizes],
+        [edge, packed_edge] + [jax.ShapeDtypeStruct((count, width), f32) for count in sizes],
         400,
         "step",
-    )(edges_other, h_edge, sum_edge, axis_x, axis_z, *gains, *block, crossline, *inline)
+    )(edges_other, h_edge, sum_edge, axis_x, axis_z, *gains, packed_inside, *inline)
     received = [lax.ppermute(send, "xy", pair) for send, pair in zip(sends, pairs)]
     grid = jax.ShapeDtypeStruct(wave_p.shape, f32)
     next_p, next_q, mine = kernel(own_kernel, [grid, grid, flat], 100, "own")(
-        inside, outside, crossline, *inline_own
+        inside, outside, packed, crossline, *block, *inline_own
     )
     takes = [factors[offset][0] for offset in offsets]
     counts = (rows // 2, rows // 4, rows // 8, rows // 8)
     outs = [jax.ShapeDtypeStruct((count, layers, width), f32) for count in counts]
     first, second = kernel(functools.partial(finish_kernel, 0, takes[:2]), outs[:2], 20, "fine")(
-        mine, *received[:2]
+        mine, *block, *received[:2]
     )
     first, *received[2:] = lax.optimization_barrier((first, *received[2:]))
     third, coarse = kernel(
         functools.partial(finish_kernel, counts[0] + counts[1], takes), outs[2:], 20, "coarse"
-    )(mine, *received)
+    )(mine, *block, *received)
     return (next_p, next_q, first, second, third, coarse)
 
 

time: 22.1 us -> 22 us (level)
  waiting for transfers between devices: 1.85 us -> 1.12 us
  Pallas kernels: 6.16 us -> 6.83 us
    ppermute x4, waiting for transfers between devices: 0.96 us -> 0.23 us  [body(): lax.ppermute(send, 'xy', pair)]
    pallas_call x1, Pallas kernels: 0.72 us -> 1.09 us  [body(): kernel(functools.partial(finish_kernel, 0, takes[:2]), outs[:2], 20, 'fine')]
    pallas_call x1, Pallas kernels: 0.82 us -> 1.18 us  [body(): kernel(own_kernel, [grid, grid, flat], 100, 'own')]
    pallas_call x2, Pallas kernels: 2.59 us -> 2.26 us  [the longest x1 1.83 us: body(): kernel(interior_kernel, [edge, edge, inside, ready, ready], 100, 'interio...]
    pallas_call x1, Pallas kernels: 0.73 us -> 1 us  [body(): kernel(functools.partial(finish_kernel, counts[0] + counts[1], takes), ou...]
  transfers between devices with their start and end apart: 8 -> 8, of which waited for: 3 -> 3; matrix products, arithmetic and copies ran while one was open for 0% -> 0% of each run, Pallas kernels for 21% -> 25%
where the time goes in v22:
time: 22 us; the launch traced here: 21.9 us
  starting transfers between devices  11.9 us (54%)
  Pallas kernels  6.83 us (31%)
  waiting for transfers between devices  1.12 us (5%)
  other arithmetic  1.08 us (5%)
  between operations  0.84 us (4%)
    ppermute x4, starting transfers between devices, body(): lax.ppermute(send, 'xy', pair)  7.95 us
    ppermute x1, starting transfers between devices, body(): inner = lax.ppermute(to_inner, 'xy', pairs[1])  3 us
    pallas_call x1, Pallas kernels, body(): kernel(interior_kernel, [edge, edge, inside, ready, ready], 100, 'interio...  1.83 us
    pallas_call x1, Pallas kernels, body(): kernel(own_kernel, [grid, grid, flat], 100, 'own')  1.18 us
    pallas_call x1, Pallas kernels, body(): kernel(functools.partial(finish_kernel, 0, takes[:2]), outs[:2], 20, 'fine')  1.09 us
    concatenate x1, other arithmetic, body(): waves = lax.optimization_barrier(jnp.concatenate([wave_p, wave_q], axis=1))  1.07 us
    pallas_call x1, Pallas kernels, body(): kernel(functools.partial(finish_kernel, counts[0] + counts[1], takes), ou...  1 us
    pallas_call x1, Pallas kernels, body(): kernel(weights_kernel, [stack] * 6, 100, 'weights')  0.71 us
  transfers between devices with their start and end apart: 8, of which 3 were waited for; matrix products, arithmetic and copies ran while one was open for 0% of the time, Pallas kernels for 25%

profile of v22, /device:TPU:0, one launch (start us, length us, event | category | flops | bytes accessed | tf_op | source)
XLA Modules:
  0.0 21.9 jit_solution(4698441235983569128)
XLA Ops:
  0.6 1.1 %pad_maximum_fusion.waves = f32[16,8,640]{2,1,0:T(8,128)S(1)} fusion(f32[16,4,640]{2,1,0:T(4,128)} %param.16, f32[16,4,640]{2,1,0:T(4,128)} %param.15), kind=kLoop, calls=%fused_computation | loop fusion | flops 81920 | bytes 655360 | tf_op jit(solution)/shard_map/concatenate | solution.py:485
  1.7 0.0 copy-start.2
  1.7 0.0 copy-start.3
  1.8 0.0 copy-start.4
  1.8 0.0 copy-start.5
  1.8 0.0 copy-start.6
  1.8 0.0 copy-start.7
  1.8 0.0 copy-start.8
  1.8 3.0 %collective-permute-start.1 = (f32[4,8,640]{2,1,0:T(8,128)S(1)}, f32[4,8,640]{2,1,0:T(8,128)S(1)}, u32[]{:S(2)}, u32[]{:S(2)}) collective-permute-start(f32[4,8,640]{2,1,0:T(8,128)S(1)} %get-tuple-element.56), channel_id=1, source_target_pairs={{0,2},{2,0},{4,6},{6,4},{8,10},{10,8},{12,14},{14,12},{1,3},{3,1},... | collective-permute-start | bytes 245768 | tf_op jit(solution)/shard_map/ppermute | solution.py:495
  4.8 0.0 collective-permute-start.2
  4.8 0.5 %collective-permute-start = (f32[16,8,640]{2,1,0:T(8,128)S(1)}, f32[16,8,640]{2,1,0:T(8,128)S(1)}, u32[]{:S(2)}, u32[]{:S(2)}) collective-permute-start(f32[16,8,640]{2,1,0:T(8,128)S(1)} %pad_maximum_fusion.waves), channel_id=1, source_target_pairs={{0,1},{1,0},{2,3},{3,2},{4,5},{5,4},{6,7},{7,6},{8,9},{9,8},{10,11... | collective-permute-start | bytes 983048 | tf_op jit(solution)/shard_map/ppermute | solution.py:496
  5.3 0.2 %taps.1 = (bf16[512,256]{1,0:T(8,128)(2,1)S(1)}, bf16[512,256]{1,0:T(8,128)(2,1)S(1)}) custom-call(), custom_call_target="tpu_custom_call" | custom-call | flops 10240000000 | bytes 1638400 | tf_op jit(solution)/shard_map/taps/pallas_call | solution.py:499
  5.6 0.0 copy-done.2
  5.6 0.0 copy-done.3
  5.6 0.0 copy-done.4
  5.6 0.0 copy-done.5
  5.6 0.0 copy-done.6
  5.6 0.0 copy-done.7
  5.6 0.0 copy-done.8
  5.7 0.0 copy-start
  5.7 0.0 copy-start.1
  5.7 0.7 %weights.1 = (f32[16,8,640]{2,1,0:T(8,128)S(1)}, f32[16,8,640]{2,1,0:T(8,128)S(1)}, f32[16,8,640]{2,1,0:T(8,128)S(1)}, f32[16,8,640]{2,1,0:T(8,128)S(1)}, f32[16...) custom-call(f32[16,8,640]{2,1,0:T(8,128)S(1)} %pad_maximum_fusion.waves, f32[16,4,640]{2,1,0:T(4,128)S(1)} %copy-done.2, ...), custom_call_target="tpu_custom_call" | custom-call | flops 4096000 | bytes 1638400 | tf_op jit(solution)/shard_map/weights/pallas_call | solution.py:500
  6.4 0.2 collective-permute-done.other
  6.6 0.0 copy-done
  6.6 0.0 copy-done.1
  6.6 1.8 %interior.1 = (f32[8,8,640]{2,1,0:T(8,128)S(1)}, f32[8,8,640]{2,1,0:T(8,128)S(1)}, f32[8,8,640]{2,1,0:T(8,128)S(1)}, f32[32,640]{1,0:T(8,128)S(1)}, f32[32,640]{1,0:T(8,128)S(1)}) custom-call(f32[16,8,640]{2,1,0:T(8,128)S(1)} %pad_maximum_fusion.waves, f32[16,8,640]{2,1,0:T(8,128)S(1)} %collective-permute-done.other, ...), custom_call_target="tpu_custom_call" | custom-call | flops 4096000 | bytes 1638400 | tf_op jit(solution)/shard_map/interior/pallas_call | solution.py:508
  8.4 0.0 collective-permute-done.1
  8.5 0.0 collective-permute-done.2
  8.5 0.4 %collective-permute-start.3 = (f32[8,8,640]{2,1,0:T(8,128)S(1)}, f32[8,8,640]{2,1,0:T(8,128)S(1)}, u32[]{:S(2)}, u32[]{:S(2)}) collective-permute-start(f32[8,8,640]{2,1,0:T(8,128)S(1)} %constant_dynamic-update-slice_fusion.edges), channel_id=1, source_target_pairs={{0,1},{1,0},{2,3},{3,2},{4,5},{5,4},{6,7},{7,6},{8,9},{9,8},{10,11... | collective-permute-start | bytes 491528 | tf_op jit(solution)/shard_map/ppermute | solution.py:513
  8.9 0.0 copy-start.9
  8.9 0.3 %halo.1 = (f32[8,8,640]{2,1,0:T(8,128)S(1)}, f32[8,8,640]{2,1,0:T(8,128)S(1)}) custom-call(f32[8,8,640]{2,1,0:T(8,128)S(1)} %constant_dynamic-update-slice_fusion.edges, f32[16,8,640]{2,1,0:T(8,128)S(1)} %get-tuple-element.45.axis_x, f32[16,8,640]{2,1,0:T(8,128)S(1)} %get-tuple-element.46.axis_y, f32[16,8,640]{2,1,0:T(8,128)S(1)} %get-tuple-element.47.axis_z, ...), custom_call_target="tpu_custom_call" | custom-call | flops 4096000 | bytes 1638400 | tf_op jit(solution)/shard_map/halo/pallas_call | solution.py:514
  9.3 0.7 %collective-permute-done.3.edges_other = f32[8,8,640]{2,1,0:T(8,128)S(1)} collective-permute-done((f32[8,8,640]{2,1,0:T(8,128)S(1)}, f32[8,8,640]{2,1,0:T(8,128)S(1)}, u32[]{:S(2)}, u32[]{:S(2)}) %collective-permute-start.3) | collective-permute-done | bytes 163872 | tf_op jit(solution)/shard_map/ppermute | solution.py:513
  10.0 0.0 copy-done.9
  10.0 0.0 copy-done.10
  10.0 0.4 %step.1 = (f32[8,8,640]{2,1,0:T(8,128)S(1)}, f32[32,640]{1,0:T(8,128)S(1)}, f32[24,640]{1,0:T(8,128)S(1)}, f32[24,640]{1,0:T(8,128)S(1)}, f32[8,640]{1,0:T(8,128)S(1)}, /*index=5*/f32[8,640]{1,0:T(8,128)S(1)}) custom-call(f32[8,8,640]{2,1,0:T(8,128)S(1)} %collective-permute-done.3.edges_other, f32[8,8,640]{2,1,0:T(8,128)S(1)} %get-tuple-element.62.h_edge, ...), custom_call_target="tpu_custom_call" | custom-call | flops 16384000 | bytes 1638400 | tf_op jit(solution)/shard_map/step/pallas_call | solution.py:533
  10.4 3.9 %collective-permute-start.4 = (f32[24,640]{1,0:T(8,128)S(1)}, f32[24,640]{1,0:T(8,128)S(1)}, u32[]{:S(2)}, u32[]{:S(2)}) collective-permute-start(f32[24,640]{1,0:T(8,128)S(1)} %get-tuple-element.71), channel_id=1, source_target_pairs={{0,14},{2,4},{4,2},{6,8},{8,6},{10,12},{12,10},{14,0},{1,15},{3,5}... | collective-permute-start | bytes 184328 | tf_op jit(solution)/shard_map/ppermute | solution.py:539
  14.3 0.9 %collective-permute-start.5 = (f32[24,640]{1,0:T(8,128)S(1)}, f32[24,640]{1,0:T(8,128)S(1)}, u32[]{:S(2)}, u32[]{:S(2)}) collective-permute-start(f32[24,640]{1,0:T(8,128)S(1)} %get-tuple-element.72), channel_id=1, source_target_pairs={{0,2},{2,0},{4,6},{6,4},{8,10},{10,8},{12,14},{14,12},{1,3},{3,1},... | collective-permute-start | bytes 184328 | tf_op jit(solution)/shard_map/ppermute | solution.py:539
  15.2 1.7 %collective-permute-start.6 = (f32[8,640]{1,0:T(8,128)S(1)}, f32[8,640]{1,0:T(8,128)S(1)}, u32[]{:S(2)}, u32[]{:S(2)}) collective-permute-start(f32[8,640]{1,0:T(8,128)S(1)} %get-tuple-element.74), channel_id=1, source_target_pairs={{0,12},{2,14},{4,8},{6,10},{8,4},{10,6},{12,0},{14,2},{1,13},{3,15... | collective-permute-start | bytes 61448 | tf_op jit(solution)/shard_map/ppermute | solution.py:539
  16.9 1.5 %collective-permute-start.7 = (f32[8,640]{1,0:T(8,128)S(1)}, f32[8,640]{1,0:T(8,128)S(1)}, u32[]{:S(2)}, u32[]{:S(2)}) collective-permute-start(f32[8,640]{1,0:T(8,128)S(1)} %get-tuple-element.75), channel_id=1, source_target_pairs={{0,4},{2,6},{4,0},{6,2},{8,12},{10,14},{12,8},{14,10},{1,5},{3,7},... | collective-permute-start | bytes 61448 | tf_op jit(solution)/shard_map/ppermute | solution.py:539
  18.4 0.0 copy-done.11
  18.4 0.0 copy-done.12
  18.4 1.2 %own.1 = (f32[16,4,640]{2,1,0:T(4,128)}, f32[16,4,640]{2,1,0:T(4,128)}, f32[64,640]{1,0:T(8,128)S(1)}) custom-call(f32[8,8,640]{2,1,0:T(8,128)S(1)} %get-tuple-element.53.inside, f32[8,8,640]{2,1,0:T(8,128)S(1)} %get-tuple-element.65.outside, f32[32,640]{1,0:T(8,128)S(1)} %get-tuple-element.66.packed, f32[32,640]{1,0:T(8,128)S(1)} %get-tuple-element.67.crossline, ...), custom_call_target="tpu_custom_call" | custom-call | flops 4096000 | bytes 1638400 | tf_op jit(solution)/shard_map/own/pallas_call | solution.py:541
  19.5 0.0 collective-permute-done.4.rest_0_
  19.5 0.0 collective-permute-done.5.rest_1_
  19.5 1.1 %fine.1 = (f32[8,4,640]{2,1,0:T(4,128)}, f32[4,4,640]{2,1,0:T(4,128)}) custom-call(f32[64,640]{1,0:T(8,128)S(1)} %get-tuple-element.70.mine, bf16[384,128]{1,0:T(8,128)(2,1)S(1)} %copy-done.1, bf16[384,128]{1,0:T(8,128)(2,1)S(1)} %copy-done, f32[24,640]{1,0:T(8,128)S(1)} %collective-permute-done.4.rest_0_, f32[24,640]{1,0:T(8,128)S(1)} %collective-permute-done.5.rest_1_), custom_call_target="tpu_custom_call" | custom-call | flops 819200 | bytes 1638400 | tf_op jit(solution)/shard_map/fine/pallas_call | solution.py:547
  20.6 0.2 %collective-permute-done.6.rest_2_ = f32[8,640]{1,0:T(8,128)S(1)} collective-permute-done((f32[8,640]{1,0:T(8,128)S(1)}, f32[8,640]{1,0:T(8,128)S(1)}, u32[]{:S(2)}, u32[]{:S(2)}) %collective-permute-start.6) | collective-permute-done | bytes 20512 | tf_op jit(solution)/shard_map/ppermute | solution.py:539
  20.9 0.0 collective-permute-done.7.rest_3_
  20.9 1.0 %coarse.1 = (f32[2,4,640]{2,1,0:T(4,128)}, f32[2,4,640]{2,1,0:T(4,128)}) custom-call(f32[64,640]{1,0:T(8,128)S(1)} %get-tuple-element.70.mine, bf16[384,128]{1,0:T(8,128)(2,1)S(1)} %copy-done.1, bf16[384,128]{1,0:T(8,128)(2,1)S(1)} %copy-done, f32[24,640]{1,0:T(8,128)S(1)} %collective-permute-done.4.rest_0_, f32[24,640]{1,0:T(8,128)S(1)} %collective-permute-done.5.rest_1_, ...), custom_call_target="tpu_custom_call" | custom-call | flops 819200 | bytes 1638400 | tf_op jit(solution)/shard_map/coarse/pallas_call | solution.py:551
  (6 shorter events, 0.0 us)
Async XLA Ops:
  1.7 3.9 %copy-start.2 = (f32[16,4,640]{2,1,0:T(4,128)S(1)}, f32[16,4,640]{2,1,0:T(4,128)}, u32[]{:S(2)}) copy-start(f32[16,4,640]{2,1,0:T(4,128)} %prior_p.1) | copy-start | bytes 491524
  1.7 3.8 %copy-start.3 = (f32[16,4,640]{2,1,0:T(4,128)S(1)}, f32[16,4,640]{2,1,0:T(4,128)}, u32[]{:S(2)}) copy-start(f32[16,4,640]{2,1,0:T(4,128)} %prior_q.1) | copy-start | bytes 491524
  1.8 3.8 %copy-start.4 = (bf16[16,4,640]{2,1,0:T(4,128)(2,1)S(1)}, bf16[16,4,640]{2,1,0:T(4,128)(2,1)}, u32[]{:S(2)}) copy-start(bf16[16,4,640]{2,1,0:T(4,128)(2,1)} %courant.1) | copy-start | bytes 245764
  1.8 3.8 %copy-start.5 = (bf16[16,4,640]{2,1,0:T(4,128)(2,1)S(1)}, bf16[16,4,640]{2,1,0:T(4,128)(2,1)}, u32[]{:S(2)}) copy-start(bf16[16,4,640]{2,1,0:T(4,128)(2,1)} %epsilon.1) | copy-start | bytes 245764
  1.8 3.8 %copy-start.6 = (bf16[16,4,640]{2,1,0:T(4,128)(2,1)S(1)}, bf16[16,4,640]{2,1,0:T(4,128)(2,1)}, u32[]{:S(2)}) copy-start(bf16[16,4,640]{2,1,0:T(4,128)(2,1)} %delta.1) | copy-start | bytes 245764
  1.8 3.8 %copy-start.7 = (bf16[16,4,640]{2,1,0:T(4,128)(2,1)S(1)}, bf16[16,4,640]{2,1,0:T(4,128)(2,1)}, u32[]{:S(2)}) copy-start(bf16[16,4,640]{2,1,0:T(4,128)(2,1)} %tilt.1) | copy-start | bytes 245764
  1.8 3.8 %copy-start.8 = (bf16[16,4,640]{2,1,0:T(4,128)(2,1)S(1)}, bf16[16,4,640]{2,1,0:T(4,128)(2,1)}, u32[]{:S(2)}) copy-start(bf16[16,4,640]{2,1,0:T(4,128)(2,1)} %azimuth.1) | copy-start | bytes 245764
  1.8 6.6 %collective-permute-start.1 = (f32[4,8,640]{2,1,0:T(8,128)S(1)}, f32[4,8,640]{2,1,0:T(8,128)S(1)}, u32[]{:S(2)}, u32[]{:S(2)}) collective-permute-start(f32[4,8,640]{2,1,0:T(8,128)S(1)} %get-tuple-element.56), channel_id=1, source_target_pairs={{0,2},{2,0},{4,6},{6,4},{8,10},{10,8},{12,14},{14,12},{1,3},{3,1},... | collective-permute-start | bytes 245768 | tf_op jit(solution)/shard_map/ppermute | solution.py:495
  4.8 3.6 %collective-permute-start.2 = (f32[4,8,640]{2,1,0:T(8,128)S(1)}, f32[4,8,640]{2,1,0:T(8,128)S(1)}, u32[]{:S(2)}, u32[]{:S(2)}) collective-permute-start(f32[4,8,640]{2,1,0:T(8,128)S(1)} %get-tuple-element.57), channel_id=1, source_target_pairs={{0,1},{1,0},{2,4},{3,5},{4,2},{5,3},{6,8},{7,9},{8,6},{9,7},{10,12... | collective-permute-start | bytes 245768 | tf_op jit(solution)/shard_map/ppermute | solution.py:494
  4.8 1.8 %collective-permute-start = (f32[16,8,640]{2,1,0:T(8,128)S(1)}, f32[16,8,640]{2,1,0:T(8,128)S(1)}, u32[]{:S(2)}, u32[]{:S(2)}) collective-permute-start(f32[16,8,640]{2,1,0:T(8,128)S(1)} %pad_maximum_fusion.waves), channel_id=1, source_target_pairs={{0,1},{1,0},{2,3},{3,2},{4,5},{5,4},{6,7},{7,6},{8,9},{9,8},{10,11... | collective-permute-start | bytes 983048 | tf_op jit(solution)/shard_map/ppermute | solution.py:496
  5.7 0.9 %copy-start = (bf16[384,128]{1,0:T(8,128)(2,1)S(1)}, bf16[384,128]{1,0:T(8,128)(2,1)}, u32[]{:S(2)}) copy-start(bf16[384,128]{1,0:T(8,128)(2,1)} %constant.33.clone.block_low) | copy-start | bytes 294916
  5.7 0.9 %copy-start.1 = (bf16[384,128]{1,0:T(8,128)(2,1)S(1)}, bf16[384,128]{1,0:T(8,128)(2,1)}, u32[]{:S(2)}) copy-start(bf16[384,128]{1,0:T(8,128)(2,1)} %constant.32.clone.block_high) | copy-start | bytes 294916
  8.5 1.5 %collective-permute-start.3 = (f32[8,8,640]{2,1,0:T(8,128)S(1)}, f32[8,8,640]{2,1,0:T(8,128)S(1)}, u32[]{:S(2)}, u32[]{:S(2)}) collective-permute-start(f32[8,8,640]{2,1,0:T(8,128)S(1)} %constant_dynamic-update-slice_fusion.edges), channel_id=1, source_target_pairs={{0,1},{1,0},{2,3},{3,2},{4,5},{5,4},{6,7},{7,6},{8,9},{9,8},{10,11... | collective-permute-start | bytes 491528 | tf_op jit(solution)/shard_map/ppermute | solution.py:513
  8.9 1.0 %copy-start.9 = (bf16[64,64]{1,0:T(8,128)(2,1)S(1)}, bf16[64,64]{1,0:T(8,128)(2,1)}, u32[]{:S(2)}) copy-start(bf16[64,64]{1,0:T(8,128)(2,1)} %constant.35.clone.inline_low) | copy-start | bytes 24580
  8.9 1.0 %copy-start.10 = (bf16[64,64]{1,0:T(8,128)(2,1)S(1)}, bf16[64,64]{1,0:T(8,128)(2,1)}, u32[]{:S(2)}) copy-start(bf16[64,64]{1,0:T(8,128)(2,1)} %constant.34.clone.inline_high) | copy-start | bytes 24580
  10.0 8.4 %copy-start.11 = (bf16[64,64]{1,0:T(8,128)(2,1)S(1)}, bf16[64,64]{1,0:T(8,128)(2,1)}, u32[]{:S(2)}) copy-start(bf16[64,64]{1,0:T(8,128)(2,1)} %constant.37.clone.own_low) | copy-start | bytes 24580
  10.0 8.4 %copy-start.12 = (bf16[64,64]{1,0:T(8,128)(2,1)S(1)}, bf16[64,64]{1,0:T(8,128)(2,1)}, u32[]{:S(2)}) copy-start(bf16[64,64]{1,0:T(8,128)(2,1)} %constant.36.clone.own_high) | copy-start | bytes 24580
  10.4 9.1 %collective-permute-start.4 = (f32[24,640]{1,0:T(8,128)S(1)}, f32[24,640]{1,0:T(8,128)S(1)}, u32[]{:S(2)}, u32[]{:S(2)}) collective-permute-start(f32[24,640]{1,0:T(8,128)S(1)} %get-tuple-element.71), channel_id=1, source_target_pairs={{0,14},{2,4},{4,2},{6,8},{8,6},{10,12},{12,10},{14,0},{1,15},{3,5}... | collective-permute-start | bytes 184328 | tf_op jit(solution)/shard_map/ppermute | solution.py:539
  14.3 5.2 %collective-permute-start.5 = (f32[24,640]{1,0:T(8,128)S(1)}, f32[24,640]{1,0:T(8,128)S(1)}, u32[]{:S(2)}, u32[]{:S(2)}) collective-permute-start(f32[24,640]{1,0:T(8,128)S(1)} %get-tuple-element.72), channel_id=1, source_target_pairs={{0,2},{2,0},{4,6},{6,4},{8,10},{10,8},{12,14},{14,12},{1,3},{3,1},... | collective-permute-start | bytes 184328 | tf_op jit(solution)/shard_map/ppermute | solution.py:539
  15.2 5.7 %collective-permute-start.6 = (f32[8,640]{1,0:T(8,128)S(1)}, f32[8,640]{1,0:T(8,128)S(1)}, u32[]{:S(2)}, u32[]{:S(2)}) collective-permute-start(f32[8,640]{1,0:T(8,128)S(1)} %get-tuple-element.74), channel_id=1, source_target_pairs={{0,12},{2,14},{4,8},{6,10},{8,4},{10,6},{12,0},{14,2},{1,13},{3,15... | collective-permute-start | bytes 61448 | tf_op jit(solution)/shard_map/ppermute | solution.py:539
  16.9 4.0 %collective-permute-start.7 = (f32[8,640]{1,0:T(8,128)S(1)}, f32[8,640]{1,0:T(8,128)S(1)}, u32[]{:S(2)}, u32[]{:S(2)}) collective-permute-start(f32[8,640]{1,0:T(8,128)S(1)} %get-tuple-element.75), channel_id=1, source_target_pairs={{0,4},{2,6},{4,0},{6,2},{8,12},{10,14},{12,8},{14,10},{1,5},{3,7},... | collective-permute-start | bytes 61448 | tf_op jit(solution)/shard_map/ppermute | solution.py:539

commit v23 on v22

--- a/solution.py
+++ b/solution.py
@@ -368,6 +368,8 @@
     gain_b,
     base,
     packed_inside,
+    block_high,
+    block_low,
     inline_high,
     inline_low,
     outside,
@@ -392,9 +394,9 @@
     packed[...] = ready
     ordered = jnp.concatenate([ready[:16], packed_inside[...], ready[16:]], axis=0)
     parts = dot3(inline_high[...], inline_low[...], *halves(ordered))
-    to_next, to_previous, to_second_next, to_second_previous = (
-        parts[start : start + count] for start, count in gives
-    )
+    to_next, to_previous = (parts[start : start + count] for start, count in gives[:2])
+    seconds = crossline_of(parts[gives[2][0] :], block_high[...], block_low[...])
+    to_second_next, to_second_previous = seconds[: gives[2][1]], seconds[gives[2][1] :]
     sends[0][...] = jnp.where(even, to_previous, to_next)
     sends[1][...] = jnp.where(even, to_next, to_previous)
     sends[2][...] = jnp.where(early, to_second_previous, to_second_next)
@@ -417,13 +419,11 @@
     mine[...] = dot3(own_high[...], own_low[...], *halves(ordered))
 
 
-def finish_kernel(at, takes, mine, block_high, block_low, *rest):
-    received, outs = [ref[...] for ref in rest[: len(takes)]], rest[len(takes) :]
-    place = lax.axis_index("xy")
-    for first, near in zip(range(0, len(takes), 2), (place % 2 == 0, place % 4 < 2)):
-        outer, inner = received[first : first + 2]
-        received[first : first + 2] = jnp.where(near, outer, inner), jnp.where(near, inner, outer)
-    wanted = range(at, at + sum(out.shape[0] for out in outs))
+def fine_kernel(takes, mine, block_high, block_low, outer, inner, first, second, rest):
+    even = lax.axis_index("xy") % 2 == 0
+    outer, inner = outer[...], inner[...]
+    received = jnp.where(even, outer, inner), jnp.where(even, inner, outer)
+    wanted = range(mine.shape[0] // 4)
     given = {}
     for row in wanted:
         for take, got in zip(takes, received):
@@ -437,13 +437,36 @@
     pieces += [jnp.zeros_like(pieces[0])] * (-len(pieces) % 4)
     pairs = [jnp.concatenate(pieces[k : k + 2], axis=0) for k in range(0, len(pieces), 2)]
     across_rows = crossline_of(jnp.concatenate(pairs, axis=0), block_high[...], block_low[...])
-    for out in outs:
-        for row in range(out.shape[0]):
-            total = mine[4 * at : 4 * at + 4]
-            if at in places:
-                total = total + across_rows[places[at] : places[at] + 4]
-            out[row] = total
-            at += 1
+    for row in wanted:
+        total = mine[4 * row : 4 * row + 4]
+        if row in places:
+            total = total + across_rows[places[row] : places[row] + 4]
+        at = row - first.shape[0]
+        if at < 0:
+            first[row] = total
+        elif at < second.shape[0]:
+            second[at] = total
+        else:
+            at = 4 * (at - second.shape[0])
+            rest[at : at + 4] = total
+
+
+def coarse_kernel(takes, begun, outer, inner, third, coarse):
+    early = lax.axis_index("xy") % 4 < 2
+    outer, inner = outer[...], inner[...]
+    received = jnp.where(early, outer, inner), jnp.where(early, inner, outer)
+    last = begun.shape[0] // 4
+    for row in range(last):
+        total = begun[4 * row : 4 * row + 4]
+        for take, got in zip(takes, received):
+            for j in range(take.shape[1]):
+                factor = float(take[row - last, j])
+                if abs(factor) > 1e-13:
+                    total = total + factor * got[4 * j : 4 * j + 4]
+        if row < third.shape[0]:
+            third[row] = total
+        else:
+            coarse[row - third.shape[0]] = total
 
 
 def pair_swaps(size):
@@ -535,7 +558,7 @@
         [edge, packed_edge] + [jax.ShapeDtypeStruct((count, width), f32) for count in sizes],
         400,
         "step",
-    )(edges_other, h_edge, sum_edge, axis_x, axis_z, *gains, packed_inside, *inline)
+    )(edges_other, h_edge, sum_edge, axis_x, axis_z, *gains, packed_inside, *block, *inline)
     received = [lax.ppermute(send, "xy", pair) for send, pair in zip(sends, pairs)]
     grid = jax.ShapeDtypeStruct(wave_p.shape, f32)
     next_p, next_q, mine = kernel(own_kernel, [grid, grid, flat], 100, "own")(
@@ -544,13 +567,14 @@
     takes = [factors[offset][0] for offset in offsets]
     counts = (rows // 2, rows // 4, rows // 8, rows // 8)
     outs = [jax.ShapeDtypeStruct((count, layers, width), f32) for count in counts]
-    first, second = kernel(functools.partial(finish_kernel, 0, takes[:2]), outs[:2], 20, "fine")(
-        mine, *block, *received[:2]
-    )
-    first, *received[2:] = lax.optimization_barrier((first, *received[2:]))
-    third, coarse = kernel(
-        functools.partial(finish_kernel, counts[0] + counts[1], takes), outs[2:], 20, "coarse"
-    )(mine, *block, *received)
+    begun = jax.ShapeDtypeStruct((layers * (counts[2] + counts[3]), width), f32)
+    first, second, begun = kernel(
+        functools.partial(fine_kernel, takes[:2]), [*outs[:2], begun], 20, "fine"
+    )(mine, *block, *received[:2])
+    begun, *received[2:] = lax.optimization_barrier((begun, *received[2:]))
+    third, coarse = kernel(functools.partial(coarse_kernel, takes[2:]), outs[2:], 20, "coarse")(
+        begun, *received[2:]
+    )
     return (next_p, next_q, first, second, third, coarse)
 
 

time: 22 us -> 21.9 us (level)
    pallas_call x1, Pallas kernels: 0.43 us -> 0.7 us  [body(): kernel(functools.partial(step_kernel, size, gives), [edge, packed_edge] +...]
    pallas_call x2, Pallas kernels: 2.09 us -> 1.86 us  [the longest x1 1.23 us: body(): kernel(functools.partial(fine_kernel, takes[:2]), [*outs[:2], begun], 20,...]
where the time goes in v23:
time: 21.9 us; the launch traced here: 21.8 us
  starting transfers between devices  11.9 us (54%)
  Pallas kernels  6.86 us (31%)
  other arithmetic  1.08 us (5%)
  waiting for transfers between devices  0.99 us (5%)
  between operations  0.85 us (4%)
    ppermute x4, starting transfers between devices, body(): lax.ppermute(send, 'xy', pair)  7.95 us
    ppermute x1, starting transfers between devices, body(): inner = lax.ppermute(to_inner, 'xy', pairs[1])  3 us
    pallas_call x1, Pallas kernels, body(): kernel(interior_kernel, [edge, edge, inside, ready, ready], 100, 'interio...  1.83 us
    pallas_call x1, Pallas kernels, body(): kernel(functools.partial(fine_kernel, takes[:2]), [*outs[:2], begun], 20,...  1.23 us
    pallas_call x1, Pallas kernels, body(): kernel(own_kernel, [grid, grid, flat], 100, 'own')  1.18 us
    concatenate x1, other arithmetic, body(): waves = lax.optimization_barrier(jnp.concatenate([wave_p, wave_q], axis=1))  1.07 us
    pallas_call x1, Pallas kernels, body(): kernel(weights_kernel, [stack] * 6, 100, 'weights')  0.71 us
    pallas_call x1, Pallas kernels, body(): kernel(functools.partial(step_kernel, size, gives), [edge, packed_edge] +...  0.7 us
  transfers between devices with their start and end apart: 8, of which 3 were waited for; matrix products, arithmetic and copies ran while one was open for 0% of the time, Pallas kernels for 25%

profile of v23, /device:TPU:0, one launch (start us, length us, event | category | flops | bytes accessed | tf_op | source)
XLA Modules:
  0.0 21.8 jit_solution(3150082441329087922)
XLA Ops:
  0.6 1.1 %pad_maximum_fusion.waves = f32[16,8,640]{2,1,0:T(8,128)S(1)} fusion(f32[16,4,640]{2,1,0:T(4,128)} %param.16, f32[16,4,640]{2,1,0:T(4,128)} %param.15), kind=kLoop, calls=%fused_computation | loop fusion | flops 81920 | bytes 655360 | tf_op jit(solution)/shard_map/concatenate | solution.py:508
  1.7 0.0 copy-start.2
  1.7 0.0 copy-start.3
  1.8 0.0 copy-start.4
  1.8 0.0 copy-start.5
  1.8 0.0 copy-start.6
  1.8 0.0 copy-start.7
  1.8 0.0 copy-start.8
  1.8 3.0 %collective-permute-start.1 = (f32[4,8,640]{2,1,0:T(8,128)S(1)}, f32[4,8,640]{2,1,0:T(8,128)S(1)}, u32[]{:S(2)}, u32[]{:S(2)}) collective-permute-start(f32[4,8,640]{2,1,0:T(8,128)S(1)} %get-tuple-element.57), channel_id=1, source_target_pairs={{0,2},{2,0},{4,6},{6,4},{8,10},{10,8},{12,14},{14,12},{1,3},{3,1},... | collective-permute-start | bytes 245768 | tf_op jit(solution)/shard_map/ppermute | solution.py:518
  4.8 0.0 collective-permute-start.2
  4.8 0.5 %collective-permute-start = (f32[16,8,640]{2,1,0:T(8,128)S(1)}, f32[16,8,640]{2,1,0:T(8,128)S(1)}, u32[]{:S(2)}, u32[]{:S(2)}) collective-permute-start(f32[16,8,640]{2,1,0:T(8,128)S(1)} %pad_maximum_fusion.waves), channel_id=1, source_target_pairs={{0,1},{1,0},{2,3},{3,2},{4,5},{5,4},{6,7},{7,6},{8,9},{9,8},{10,11... | collective-permute-start | bytes 983048 | tf_op jit(solution)/shard_map/ppermute | solution.py:519
  5.3 0.2 %taps.1 = (bf16[512,256]{1,0:T(8,128)(2,1)S(1)}, bf16[512,256]{1,0:T(8,128)(2,1)S(1)}) custom-call(), custom_call_target="tpu_custom_call" | custom-call | flops 10240000000 | bytes 1638400 | tf_op jit(solution)/shard_map/taps/pallas_call | solution.py:522
  5.6 0.0 copy-done.2
  5.6 0.0 copy-done.3
  5.6 0.0 copy-done.4
  5.6 0.0 copy-done.5
  5.6 0.0 copy-done.6
  5.6 0.0 copy-done.7
  5.6 0.0 copy-done.8
  5.7 0.0 copy-start
  5.7 0.0 copy-start.1
  5.7 0.7 %weights.1 = (f32[16,8,640]{2,1,0:T(8,128)S(1)}, f32[16,8,640]{2,1,0:T(8,128)S(1)}, f32[16,8,640]{2,1,0:T(8,128)S(1)}, f32[16,8,640]{2,1,0:T(8,128)S(1)}, f32[16...) custom-call(f32[16,8,640]{2,1,0:T(8,128)S(1)} %pad_maximum_fusion.waves, f32[16,4,640]{2,1,0:T(4,128)S(1)} %copy-done.2, ...), custom_call_target="tpu_custom_call" | custom-call | flops 4096000 | bytes 1638400 | tf_op jit(solution)/shard_map/weights/pallas_call | solution.py:523
  6.4 0.2 collective-permute-done.other
  6.6 0.0 copy-done
  6.6 0.0 copy-done.1
  6.6 1.8 %interior.1 = (f32[8,8,640]{2,1,0:T(8,128)S(1)}, f32[8,8,640]{2,1,0:T(8,128)S(1)}, f32[8,8,640]{2,1,0:T(8,128)S(1)}, f32[32,640]{1,0:T(8,128)S(1)}, f32[32,640]{1,0:T(8,128)S(1)}) custom-call(f32[16,8,640]{2,1,0:T(8,128)S(1)} %pad_maximum_fusion.waves, f32[16,8,640]{2,1,0:T(8,128)S(1)} %collective-permute-done.other, ...), custom_call_target="tpu_custom_call" | custom-call | flops 4096000 | bytes 1638400 | tf_op jit(solution)/shard_map/interior/pallas_call | solution.py:531
  8.4 0.0 collective-permute-done.1
  8.5 0.0 collective-permute-done.2
  8.5 0.4 %collective-permute-start.3 = (f32[8,8,640]{2,1,0:T(8,128)S(1)}, f32[8,8,640]{2,1,0:T(8,128)S(1)}, u32[]{:S(2)}, u32[]{:S(2)}) collective-permute-start(f32[8,8,640]{2,1,0:T(8,128)S(1)} %constant_dynamic-update-slice_fusion.edges), channel_id=1, source_target_pairs={{0,1},{1,0},{2,3},{3,2},{4,5},{5,4},{6,7},{7,6},{8,9},{9,8},{10,11... | collective-permute-start | bytes 491528 | tf_op jit(solution)/shard_map/ppermute | solution.py:536
  8.9 0.0 copy-start.9
  8.9 0.3 %halo.1 = (f32[8,8,640]{2,1,0:T(8,128)S(1)}, f32[8,8,640]{2,1,0:T(8,128)S(1)}) custom-call(f32[8,8,640]{2,1,0:T(8,128)S(1)} %constant_dynamic-update-slice_fusion.edges, f32[16,8,640]{2,1,0:T(8,128)S(1)} %get-tuple-element.46.axis_x, f32[16,8,640]{2,1,0:T(8,128)S(1)} %get-tuple-element.47.axis_y, f32[16,8,640]{2,1,0:T(8,128)S(1)} %get-tuple-element.48.axis_z, ...), custom_call_target="tpu_custom_call" | custom-call | flops 4096000 | bytes 1638400 | tf_op jit(solution)/shard_map/halo/pallas_call | solution.py:537
  9.3 0.7 %collective-permute-done.3.edges_other = f32[8,8,640]{2,1,0:T(8,128)S(1)} collective-permute-done((f32[8,8,640]{2,1,0:T(8,128)S(1)}, f32[8,8,640]{2,1,0:T(8,128)S(1)}, u32[]{:S(2)}, u32[]{:S(2)}) %collective-permute-start.3) | collective-permute-done | bytes 163872 | tf_op jit(solution)/shard_map/ppermute | solution.py:536
  10.0 0.0 copy-done.9
  10.0 0.0 copy-done.10
  10.0 0.7 %step.1 = (f32[8,8,640]{2,1,0:T(8,128)S(1)}, f32[32,640]{1,0:T(8,128)S(1)}, f32[24,640]{1,0:T(8,128)S(1)}, f32[24,640]{1,0:T(8,128)S(1)}, f32[8,640]{1,0:T(8,128)S(1)}, /*index=5*/f32[8,640]{1,0:T(8,128)S(1)}) custom-call(f32[8,8,640]{2,1,0:T(8,128)S(1)} %collective-permute-done.3.edges_other, f32[8,8,640]{2,1,0:T(8,128)S(1)} %get-tuple-element.63.h_edge, ...), custom_call_target="tpu_custom_call" | custom-call | flops 16384000 | bytes 1638400 | tf_op jit(solution)/shard_map/step/pallas_call | solution.py:556
  10.7 3.9 %collective-permute-start.4 = (f32[24,640]{1,0:T(8,128)S(1)}, f32[24,640]{1,0:T(8,128)S(1)}, u32[]{:S(2)}, u32[]{:S(2)}) collective-permute-start(f32[24,640]{1,0:T(8,128)S(1)} %get-tuple-element.72), channel_id=1, source_target_pairs={{0,14},{2,4},{4,2},{6,8},{8,6},{10,12},{12,10},{14,0},{1,15},{3,5}... | collective-permute-start | bytes 184328 | tf_op jit(solution)/shard_map/ppermute | solution.py:562
  14.6 0.9 %collective-permute-start.5 = (f32[24,640]{1,0:T(8,128)S(1)}, f32[24,640]{1,0:T(8,128)S(1)}, u32[]{:S(2)}, u32[]{:S(2)}) collective-permute-start(f32[24,640]{1,0:T(8,128)S(1)} %get-tuple-element.73), channel_id=1, source_target_pairs={{0,2},{2,0},{4,6},{6,4},{8,10},{10,8},{12,14},{14,12},{1,3},{3,1},... | collective-permute-start | bytes 184328 | tf_op jit(solution)/shard_map/ppermute | solution.py:562
  15.5 1.7 %collective-permute-start.6 = (f32[8,640]{1,0:T(8,128)S(1)}, f32[8,640]{1,0:T(8,128)S(1)}, u32[]{:S(2)}, u32[]{:S(2)}) collective-permute-start(f32[8,640]{1,0:T(8,128)S(1)} %get-tuple-element.77), channel_id=1, source_target_pairs={{0,12},{2,14},{4,8},{6,10},{8,4},{10,6},{12,0},{14,2},{1,13},{3,15... | collective-permute-start | bytes 61448 | tf_op jit(solution)/shard_map/ppermute | solution.py:562
  17.1 1.5 %collective-permute-start.7 = (f32[8,640]{1,0:T(8,128)S(1)}, f32[8,640]{1,0:T(8,128)S(1)}, u32[]{:S(2)}, u32[]{:S(2)}) collective-permute-start(f32[8,640]{1,0:T(8,128)S(1)} %get-tuple-element.78), channel_id=1, source_target_pairs={{0,4},{2,6},{4,0},{6,2},{8,12},{10,14},{12,8},{14,10},{1,5},{3,7},... | collective-permute-start | bytes 61448 | tf_op jit(solution)/shard_map/ppermute | solution.py:562
  18.6 0.0 copy-done.11
  18.6 0.0 copy-done.12
  18.6 1.2 %own.1 = (f32[16,4,640]{2,1,0:T(4,128)}, f32[16,4,640]{2,1,0:T(4,128)}, f32[64,640]{1,0:T(8,128)S(1)}) custom-call(f32[8,8,640]{2,1,0:T(8,128)S(1)} %get-tuple-element.54.inside, f32[8,8,640]{2,1,0:T(8,128)S(1)} %get-tuple-element.66.outside, f32[32,640]{1,0:T(8,128)S(1)} %get-tuple-element.67.packed, f32[32,640]{1,0:T(8,128)S(1)} %get-tuple-element.68.crossline, ...), custom_call_target="tpu_custom_call" | custom-call | flops 4096000 | bytes 1638400 | tf_op jit(solution)/shard_map/own/pallas_call | solution.py:564
  19.8 0.0 collective-permute-done.4.outer
  19.8 0.0 collective-permute-done.5.inner
  19.8 1.2 %fine.1 = (f32[8,4,640]{2,1,0:T(4,128)}, f32[4,4,640]{2,1,0:T(4,128)}, f32[16,640]{1,0:T(8,128)S(1)}) custom-call(f32[64,640]{1,0:T(8,128)S(1)} %get-tuple-element.71.mine, bf16[384,128]{1,0:T(8,128)(2,1)S(1)} %copy-done.1, bf16[384,128]{1,0:T(8,128)(2,1)S(1)} %copy-done, f32[24,640]{1,0:T(8,128)S(1)} %collective-permute-done.4.outer, ...), custom_call_target="tpu_custom_call" | custom-call | flops 819200 | bytes 1638400 | tf_op jit(solution)/shard_map/fine/pallas_call | solution.py:571
  21.0 0.1 collective-permute-done.6.outer
  21.1 0.0 collective-permute-done.7.inner
  21.1 0.6 %coarse.1 = (f32[2,4,640]{2,1,0:T(4,128)}, f32[2,4,640]{2,1,0:T(4,128)}) custom-call(f32[16,640]{1,0:T(8,128)S(1)} %get-tuple-element.79.begun, f32[8,640]{1,0:T(8,128)S(1)} %collective-permute-done.6.outer, f32[8,640]{1,0:T(8,128)S(1)} %collective-permute-done.7.inner), custom_call_target="tpu_custom_call" | custom-call | flops 819200 | bytes 1638400 | tf_op jit(solution)/shard_map/coarse/pallas_call | solution.py:575
  (6 shorter events, 0.0 us)
Async XLA Ops:
  1.7 3.9 %copy-start.2 = (f32[16,4,640]{2,1,0:T(4,128)S(1)}, f32[16,4,640]{2,1,0:T(4,128)}, u32[]{:S(2)}) copy-start(f32[16,4,640]{2,1,0:T(4,128)} %prior_p.1) | copy-start | bytes 491524
  1.7 3.8 %copy-start.3 = (f32[16,4,640]{2,1,0:T(4,128)S(1)}, f32[16,4,640]{2,1,0:T(4,128)}, u32[]{:S(2)}) copy-start(f32[16,4,640]{2,1,0:T(4,128)} %prior_q.1) | copy-start | bytes 491524
  1.8 3.8 %copy-start.4 = (bf16[16,4,640]{2,1,0:T(4,128)(2,1)S(1)}, bf16[16,4,640]{2,1,0:T(4,128)(2,1)}, u32[]{:S(2)}) copy-start(bf16[16,4,640]{2,1,0:T(4,128)(2,1)} %courant.1) | copy-start | bytes 245764
  1.8 3.8 %copy-start.5 = (bf16[16,4,640]{2,1,0:T(4,128)(2,1)S(1)}, bf16[16,4,640]{2,1,0:T(4,128)(2,1)}, u32[]{:S(2)}) copy-start(bf16[16,4,640]{2,1,0:T(4,128)(2,1)} %epsilon.1) | copy-start | bytes 245764
  1.8 3.8 %copy-start.6 = (bf16[16,4,640]{2,1,0:T(4,128)(2,1)S(1)}, bf16[16,4,640]{2,1,0:T(4,128)(2,1)}, u32[]{:S(2)}) copy-start(bf16[16,4,640]{2,1,0:T(4,128)(2,1)} %delta.1) | copy-start | bytes 245764
  1.8 3.8 %copy-start.7 = (bf16[16,4,640]{2,1,0:T(4,128)(2,1)S(1)}, bf16[16,4,640]{2,1,0:T(4,128)(2,1)}, u32[]{:S(2)}) copy-start(bf16[16,4,640]{2,1,0:T(4,128)(2,1)} %tilt.1) | copy-start | bytes 245764
  1.8 3.8 %copy-start.8 = (bf16[16,4,640]{2,1,0:T(4,128)(2,1)S(1)}, bf16[16,4,640]{2,1,0:T(4,128)(2,1)}, u32[]{:S(2)}) copy-start(bf16[16,4,640]{2,1,0:T(4,128)(2,1)} %azimuth.1) | copy-start | bytes 245764
  1.8 6.6 %collective-permute-start.1 = (f32[4,8,640]{2,1,0:T(8,128)S(1)}, f32[4,8,640]{2,1,0:T(8,128)S(1)}, u32[]{:S(2)}, u32[]{:S(2)}) collective-permute-start(f32[4,8,640]{2,1,0:T(8,128)S(1)} %get-tuple-element.57), channel_id=1, source_target_pairs={{0,2},{2,0},{4,6},{6,4},{8,10},{10,8},{12,14},{14,12},{1,3},{3,1},... | collective-permute-start | bytes 245768 | tf_op jit(solution)/shard_map/ppermute | solution.py:518
  4.8 3.6 %collective-permute-start.2 = (f32[4,8,640]{2,1,0:T(8,128)S(1)}, f32[4,8,640]{2,1,0:T(8,128)S(1)}, u32[]{:S(2)}, u32[]{:S(2)}) collective-permute-start(f32[4,8,640]{2,1,0:T(8,128)S(1)} %get-tuple-element.58), channel_id=1, source_target_pairs={{0,1},{1,0},{2,4},{3,5},{4,2},{5,3},{6,8},{7,9},{8,6},{9,7},{10,12... | collective-permute-start | bytes 245768 | tf_op jit(solution)/shard_map/ppermute | solution.py:517
  4.8 1.8 %collective-permute-start = (f32[16,8,640]{2,1,0:T(8,128)S(1)}, f32[16,8,640]{2,1,0:T(8,128)S(1)}, u32[]{:S(2)}, u32[]{:S(2)}) collective-permute-start(f32[16,8,640]{2,1,0:T(8,128)S(1)} %pad_maximum_fusion.waves), channel_id=1, source_target_pairs={{0,1},{1,0},{2,3},{3,2},{4,5},{5,4},{6,7},{7,6},{8,9},{9,8},{10,11... | collective-permute-start | bytes 983048 | tf_op jit(solution)/shard_map/ppermute | solution.py:519
  5.7 0.9 %copy-start = (bf16[384,128]{1,0:T(8,128)(2,1)S(1)}, bf16[384,128]{1,0:T(8,128)(2,1)}, u32[]{:S(2)}) copy-start(bf16[384,128]{1,0:T(8,128)(2,1)} %constant.33.clone.block_low) | copy-start | bytes 294916
  5.7 0.9 %copy-start.1 = (bf16[384,128]{1,0:T(8,128)(2,1)S(1)}, bf16[384,128]{1,0:T(8,128)(2,1)}, u32[]{:S(2)}) copy-start(bf16[384,128]{1,0:T(8,128)(2,1)} %constant.32.clone.block_high) | copy-start | bytes 294916
  8.5 1.5 %collective-permute-start.3 = (f32[8,8,640]{2,1,0:T(8,128)S(1)}, f32[8,8,640]{2,1,0:T(8,128)S(1)}, u32[]{:S(2)}, u32[]{:S(2)}) collective-permute-start(f32[8,8,640]{2,1,0:T(8,128)S(1)} %constant_dynamic-update-slice_fusion.edges), channel_id=1, source_target_pairs={{0,1},{1,0},{2,3},{3,2},{4,5},{5,4},{6,7},{7,6},{8,9},{9,8},{10,11... | collective-permute-start | bytes 491528 | tf_op jit(solution)/shard_map/ppermute | solution.py:536
  8.9 1.0 %copy-start.9 = (bf16[64,64]{1,0:T(8,128)(2,1)S(1)}, bf16[64,64]{1,0:T(8,128)(2,1)}, u32[]{:S(2)}) copy-start(bf16[64,64]{1,0:T(8,128)(2,1)} %constant.35.clone.inline_low) | copy-start | bytes 24580
  8.9 1.0 %copy-start.10 = (bf16[64,64]{1,0:T(8,128)(2,1)S(1)}, bf16[64,64]{1,0:T(8,128)(2,1)}, u32[]{:S(2)}) copy-start(bf16[64,64]{1,0:T(8,128)(2,1)} %constant.34.clone.inline_high) | copy-start | bytes 24580
  10.0 8.7 %copy-start.11 = (bf16[64,64]{1,0:T(8,128)(2,1)S(1)}, bf16[64,64]{1,0:T(8,128)(2,1)}, u32[]{:S(2)}) copy-start(bf16[64,64]{1,0:T(8,128)(2,1)} %constant.37.clone.own_low) | copy-start | bytes 24580
  10.0 8.7 %copy-start.12 = (bf16[64,64]{1,0:T(8,128)(2,1)S(1)}, bf16[64,64]{1,0:T(8,128)(2,1)}, u32[]{:S(2)}) copy-start(bf16[64,64]{1,0:T(8,128)(2,1)} %constant.36.clone.own_high) | copy-start | bytes 24580
  10.7 9.1 %collective-permute-start.4 = (f32[24,640]{1,0:T(8,128)S(1)}, f32[24,640]{1,0:T(8,128)S(1)}, u32[]{:S(2)}, u32[]{:S(2)}) collective-permute-start(f32[24,640]{1,0:T(8,128)S(1)} %get-tuple-element.72), channel_id=1, source_target_pairs={{0,14},{2,4},{4,2},{6,8},{8,6},{10,12},{12,10},{14,0},{1,15},{3,5}... | collective-permute-start | bytes 184328 | tf_op jit(solution)/shard_map/ppermute | solution.py:562
  14.6 5.2 %collective-permute-start.5 = (f32[24,640]{1,0:T(8,128)S(1)}, f32[24,640]{1,0:T(8,128)S(1)}, u32[]{:S(2)}, u32[]{:S(2)}) collective-permute-start(f32[24,640]{1,0:T(8,128)S(1)} %get-tuple-element.73), channel_id=1, source_target_pairs={{0,2},{2,0},{4,6},{6,4},{8,10},{10,8},{12,14},{14,12},{1,3},{3,1},... | collective-permute-start | bytes 184328 | tf_op jit(solution)/shard_map/ppermute | solution.py:562
  15.5 5.7 %collective-permute-start.6 = (f32[8,640]{1,0:T(8,128)S(1)}, f32[8,640]{1,0:T(8,128)S(1)}, u32[]{:S(2)}, u32[]{:S(2)}) collective-permute-start(f32[8,640]{1,0:T(8,128)S(1)} %get-tuple-element.77), channel_id=1, source_target_pairs={{0,12},{2,14},{4,8},{6,10},{8,4},{10,6},{12,0},{14,2},{1,13},{3,15... | collective-permute-start | bytes 61448 | tf_op jit(solution)/shard_map/ppermute | solution.py:562
  17.1 4.0 %collective-permute-start.7 = (f32[8,640]{1,0:T(8,128)S(1)}, f32[8,640]{1,0:T(8,128)S(1)}, u32[]{:S(2)}, u32[]{:S(2)}) collective-permute-start(f32[8,640]{1,0:T(8,128)S(1)} %get-tuple-element.78), channel_id=1, source_target_pairs={{0,4},{2,6},{4,0},{6,2},{8,12},{10,14},{12,8},{14,10},{1,5},{3,7},... | collective-permute-start | bytes 61448 | tf_op jit(solution)/shard_map/ppermute | solution.py:562

commit v24 on v23

--- a/solution.py
+++ b/solution.py
@@ -404,7 +404,15 @@
 
 
 def own_kernel(
-    inside, outside, packed, crossline, block_high, block_low, own_high, own_low, next_p, next_q, mine
+    packed, crossline, block_high, block_low, own_high, own_low, mine
+):
+    edge = crossline_of(packed[...], block_high[...], block_low[...])
+    ordered = jnp.concatenate([edge[:16], crossline[...], edge[16:]], axis=0)
+    mine[...] = dot3(own_high[...], own_low[...], *halves(ordered))
+
+
+def fine_kernel(
+    takes, mine, inside, outside, block_high, block_low, outer, inner, first, second, rest, next_p, next_q
 ):
     rows = next_p.shape[0]
     for x in range(rows):
@@ -414,12 +422,6 @@
             value = outside[x if x < 4 else x - rows + 8]
         next_p[x] = value[:4]
         next_q[x] = value[4:]
-    edge = crossline_of(packed[...], block_high[...], block_low[...])
-    ordered = jnp.concatenate([edge[:16], crossline[...], edge[16:]], axis=0)
-    mine[...] = dot3(own_high[...], own_low[...], *halves(ordered))
-
-
-def fine_kernel(takes, mine, block_high, block_low, outer, inner, first, second, rest):
     even = lax.axis_index("xy") % 2 == 0
     outer, inner = outer[...], inner[...]
     received = jnp.where(even, outer, inner), jnp.where(even, inner, outer)
@@ -561,16 +563,16 @@
     )(edges_other, h_edge, sum_edge, axis_x, axis_z, *gains, packed_inside, *block, *inline)
     received = [lax.ppermute(send, "xy", pair) for send, pair in zip(sends, pairs)]
     grid = jax.ShapeDtypeStruct(wave_p.shape, f32)
-    next_p, next_q, mine = kernel(own_kernel, [grid, grid, flat], 100, "own")(
-        inside, outside, packed, crossline, *block, *inline_own
+    mine = kernel(own_kernel, flat, 100, "own")(
+        packed, crossline, *block, *inline_own
     )
     takes = [factors[offset][0] for offset in offsets]
     counts = (rows // 2, rows // 4, rows // 8, rows // 8)
     outs = [jax.ShapeDtypeStruct((count, layers, width), f32) for count in counts]
     begun = jax.ShapeDtypeStruct((layers * (counts[2] + counts[3]), width), f32)
-    first, second, begun = kernel(
-        functools.partial(fine_kernel, takes[:2]), [*outs[:2], begun], 20, "fine"
-    )(mine, *block, *received[:2])
+    first, second, begun, next_p, next_q = kernel(
+        functools.partial(fine_kernel, takes[:2]), [*outs[:2], begun, grid, grid], 20, "fine"
+    )(mine, inside, outside, *block, *received[:2])
     begun, *received[2:] = lax.optimization_barrier((begun, *received[2:]))
     third, coarse = kernel(functools.partial(coarse_kernel, takes[2:]), outs[2:], 20, "coarse")(
         begun, *received[2:]

time: 21.9 us -> 21.9 us (level)
  Pallas kernels: 6.86 us -> 6.29 us
  waiting for transfers between devices: 0.99 us -> 1.54 us
    pallas_call x2, Pallas kernels: 2.4 us -> 1.83 us  [the longest x1 1.31 us: body(): kernel(functools.partial(fine_kernel, takes[:2]), [*outs[:2], begun, grid...]
    ppermute x4, waiting for transfers between devices: 0.1 us -> 0.65 us  [body(): lax.ppermute(send, 'xy', pair)]
  transfers between devices with their start and end apart: 8 -> 8, of which waited for: 3 -> 3; matrix products, arithmetic and copies ran while one was open for 0% -> 0% of each run, Pallas kernels for 25% -> 23%
where the time goes in v24:
time: 21.9 us; the launch traced here: 21.8 us
  starting transfers between devices  11.9 us (54%)
  Pallas kernels  6.29 us (29%)
  waiting for transfers between devices  1.54 us (7%)
  other arithmetic  1.08 us (5%)
  between operations  0.87 us (4%)
    ppermute x4, starting transfers between devices, body(): lax.ppermute(send, 'xy', pair)  7.95 us
    ppermute x1, starting transfers between devices, body(): inner = lax.ppermute(to_inner, 'xy', pairs[1])  3 us
    pallas_call x1, Pallas kernels, body(): kernel(interior_kernel, [edge, edge, inside, ready, ready], 100, 'interio...  1.83 us
    pallas_call x1, Pallas kernels, body(): kernel(functools.partial(fine_kernel, takes[:2]), [*outs[:2], begun, grid...  1.31 us
    concatenate x1, other arithmetic, body(): waves = lax.optimization_barrier(jnp.concatenate([wave_p, wave_q], axis=1))  1.07 us
    pallas_call x1, Pallas kernels, body(): kernel(weights_kernel, [stack] * 6, 100, 'weights')  0.71 us
    pallas_call x1, Pallas kernels, body(): kernel(functools.partial(step_kernel, size, gives), [edge, packed_edge] +...  0.7 us
    ppermute x1, waiting for transfers between devices, body(): edges_other = lax.ppermute(edges, 'gz', cores)  0.68 us
  transfers between devices with their start and end apart: 8, of which 3 were waited for; matrix products, arithmetic and copies ran while one was open for 0% of the time, Pallas kernels for 23%

profile of v24, /device:TPU:0, one launch (start us, length us, event | category | flops | bytes accessed | tf_op | source)
XLA Modules:
  0.0 21.8 jit_solution(8397596778936537770)
XLA Ops:
  0.6 1.1 %pad_maximum_fusion.waves = f32[16,8,640]{2,1,0:T(8,128)S(1)} fusion(f32[16,4,640]{2,1,0:T(4,128)} %param.16, f32[16,4,640]{2,1,0:T(4,128)} %param.15), kind=kLoop, calls=%fused_computation | loop fusion | flops 81920 | bytes 655360 | tf_op jit(solution)/shard_map/concatenate | solution.py:510
  1.7 0.0 copy-start.2
  1.7 0.0 copy-start.3
  1.8 0.0 copy-start.4
  1.8 0.0 copy-start.5
  1.8 0.0 copy-start.6
  1.8 0.0 copy-start.7
  1.8 0.0 copy-start.8
  1.8 3.0 %collective-permute-start.1 = (f32[4,8,640]{2,1,0:T(8,128)S(1)}, f32[4,8,640]{2,1,0:T(8,128)S(1)}, u32[]{:S(2)}, u32[]{:S(2)}) collective-permute-start(f32[4,8,640]{2,1,0:T(8,128)S(1)} %get-tuple-element.55), channel_id=1, source_target_pairs={{0,2},{2,0},{4,6},{6,4},{8,10},{10,8},{12,14},{14,12},{1,3},{3,1},... | collective-permute-start | bytes 245768 | tf_op jit(solution)/shard_map/ppermute | solution.py:520
  4.8 0.0 collective-permute-start.2
  4.8 0.5 %collective-permute-start = (f32[16,8,640]{2,1,0:T(8,128)S(1)}, f32[16,8,640]{2,1,0:T(8,128)S(1)}, u32[]{:S(2)}, u32[]{:S(2)}) collective-permute-start(f32[16,8,640]{2,1,0:T(8,128)S(1)} %pad_maximum_fusion.waves), channel_id=1, source_target_pairs={{0,1},{1,0},{2,3},{3,2},{4,5},{5,4},{6,7},{7,6},{8,9},{9,8},{10,11... | collective-permute-start | bytes 983048 | tf_op jit(solution)/shard_map/ppermute | solution.py:521
  5.3 0.2 %taps.1 = (bf16[512,256]{1,0:T(8,128)(2,1)S(1)}, bf16[512,256]{1,0:T(8,128)(2,1)S(1)}) custom-call(), custom_call_target="tpu_custom_call" | custom-call | flops 10240000000 | bytes 1638400 | tf_op jit(solution)/shard_map/taps/pallas_call | solution.py:524
  5.6 0.0 copy-done.2
  5.6 0.0 copy-done.3
  5.6 0.0 copy-done.4
  5.6 0.0 copy-done.5
  5.6 0.0 copy-done.6
  5.6 0.0 copy-done.7
  5.6 0.0 copy-done.8
  5.7 0.0 copy-start
  5.7 0.0 copy-start.1
  5.7 0.7 %weights.1 = (f32[16,8,640]{2,1,0:T(8,128)S(1)}, f32[16,8,640]{2,1,0:T(8,128)S(1)}, f32[16,8,640]{2,1,0:T(8,128)S(1)}, f32[16,8,640]{2,1,0:T(8,128)S(1)}, f32[16...) custom-call(f32[16,8,640]{2,1,0:T(8,128)S(1)} %pad_maximum_fusion.waves, f32[16,4,640]{2,1,0:T(4,128)S(1)} %copy-done.2, ...), custom_call_target="tpu_custom_call" | custom-call | flops 4096000 | bytes 1638400 | tf_op jit(solution)/shard_map/weights/pallas_call | solution.py:525
  6.4 0.2 collective-permute-done.other
  6.6 0.0 copy-done
  6.6 0.0 copy-done.1
  6.6 1.8 %interior.1 = (f32[8,8,640]{2,1,0:T(8,128)S(1)}, f32[8,8,640]{2,1,0:T(8,128)S(1)}, f32[8,8,640]{2,1,0:T(8,128)S(1)}, f32[32,640]{1,0:T(8,128)S(1)}, f32[32,640]{1,0:T(8,128)S(1)}) custom-call(f32[16,8,640]{2,1,0:T(8,128)S(1)} %pad_maximum_fusion.waves, f32[16,8,640]{2,1,0:T(8,128)S(1)} %collective-permute-done.other, ...), custom_call_target="tpu_custom_call" | custom-call | flops 4096000 | bytes 1638400 | tf_op jit(solution)/shard_map/interior/pallas_call | solution.py:533
  8.4 0.0 collective-permute-done.1
  8.5 0.0 collective-permute-done.2
  8.5 0.4 %collective-permute-start.3 = (f32[8,8,640]{2,1,0:T(8,128)S(1)}, f32[8,8,640]{2,1,0:T(8,128)S(1)}, u32[]{:S(2)}, u32[]{:S(2)}) collective-permute-start(f32[8,8,640]{2,1,0:T(8,128)S(1)} %constant_dynamic-update-slice_fusion.edges), channel_id=1, source_target_pairs={{0,1},{1,0},{2,3},{3,2},{4,5},{5,4},{6,7},{7,6},{8,9},{9,8},{10,11... | collective-permute-start | bytes 491528 | tf_op jit(solution)/shard_map/ppermute | solution.py:538
  8.9 0.0 copy-start.9
  8.9 0.3 %halo.1 = (f32[8,8,640]{2,1,0:T(8,128)S(1)}, f32[8,8,640]{2,1,0:T(8,128)S(1)}) custom-call(f32[8,8,640]{2,1,0:T(8,128)S(1)} %constant_dynamic-update-slice_fusion.edges, f32[16,8,640]{2,1,0:T(8,128)S(1)} %get-tuple-element.45.axis_x, f32[16,8,640]{2,1,0:T(8,128)S(1)} %get-tuple-element.46.axis_y, f32[16,8,640]{2,1,0:T(8,128)S(1)} %get-tuple-element.47.axis_z, ...), custom_call_target="tpu_custom_call" | custom-call | flops 4096000 | bytes 1638400 | tf_op jit(solution)/shard_map/halo/pallas_call | solution.py:539
  9.3 0.7 %collective-permute-done.3.edges_other = f32[8,8,640]{2,1,0:T(8,128)S(1)} collective-permute-done((f32[8,8,640]{2,1,0:T(8,128)S(1)}, f32[8,8,640]{2,1,0:T(8,128)S(1)}, u32[]{:S(2)}, u32[]{:S(2)}) %collective-permute-start.3) | collective-permute-done | bytes 163872 | tf_op jit(solution)/shard_map/ppermute | solution.py:538
  10.0 0.0 copy-done.9
  10.0 0.0 copy-done.10
  10.0 0.7 %step.1 = (f32[8,8,640]{2,1,0:T(8,128)S(1)}, f32[32,640]{1,0:T(8,128)S(1)}, f32[24,640]{1,0:T(8,128)S(1)}, f32[24,640]{1,0:T(8,128)S(1)}, f32[8,640]{1,0:T(8,128)S(1)}, /*index=5*/f32[8,640]{1,0:T(8,128)S(1)}) custom-call(f32[8,8,640]{2,1,0:T(8,128)S(1)} %collective-permute-done.3.edges_other, f32[8,8,640]{2,1,0:T(8,128)S(1)} %get-tuple-element.61.h_edge, ...), custom_call_target="tpu_custom_call" | custom-call | flops 16384000 | bytes 1638400 | tf_op jit(solution)/shard_map/step/pallas_call | solution.py:558
  10.7 3.9 %collective-permute-start.4 = (f32[24,640]{1,0:T(8,128)S(1)}, f32[24,640]{1,0:T(8,128)S(1)}, u32[]{:S(2)}, u32[]{:S(2)}) collective-permute-start(f32[24,640]{1,0:T(8,128)S(1)} %get-tuple-element.68), channel_id=1, source_target_pairs={{0,14},{2,4},{4,2},{6,8},{8,6},{10,12},{12,10},{14,0},{1,15},{3,5}... | collective-permute-start | bytes 184328 | tf_op jit(solution)/shard_map/ppermute | solution.py:564
  14.6 0.9 %collective-permute-start.5 = (f32[24,640]{1,0:T(8,128)S(1)}, f32[24,640]{1,0:T(8,128)S(1)}, u32[]{:S(2)}, u32[]{:S(2)}) collective-permute-start(f32[24,640]{1,0:T(8,128)S(1)} %get-tuple-element.69), channel_id=1, source_target_pairs={{0,2},{2,0},{4,6},{6,4},{8,10},{10,8},{12,14},{14,12},{1,3},{3,1},... | collective-permute-start | bytes 184328 | tf_op jit(solution)/shard_map/ppermute | solution.py:564
  15.5 1.7 %collective-permute-start.6 = (f32[8,640]{1,0:T(8,128)S(1)}, f32[8,640]{1,0:T(8,128)S(1)}, u32[]{:S(2)}, u32[]{:S(2)}) collective-permute-start(f32[8,640]{1,0:T(8,128)S(1)} %get-tuple-element.75), channel_id=1, source_target_pairs={{0,12},{2,14},{4,8},{6,10},{8,4},{10,6},{12,0},{14,2},{1,13},{3,15... | collective-permute-start | bytes 61448 | tf_op jit(solution)/shard_map/ppermute | solution.py:564
  17.1 1.5 %collective-permute-start.7 = (f32[8,640]{1,0:T(8,128)S(1)}, f32[8,640]{1,0:T(8,128)S(1)}, u32[]{:S(2)}, u32[]{:S(2)}) collective-permute-start(f32[8,640]{1,0:T(8,128)S(1)} %get-tuple-element.76), channel_id=1, source_target_pairs={{0,4},{2,6},{4,0},{6,2},{8,12},{10,14},{12,8},{14,10},{1,5},{3,7},... | collective-permute-start | bytes 61448 | tf_op jit(solution)/shard_map/ppermute | solution.py:564
  18.6 0.0 copy-done.11
  18.6 0.0 copy-done.12
  18.6 0.5 %own.1.mine = f32[64,640]{1,0:T(8,128)S(1)} custom-call(f32[32,640]{1,0:T(8,128)S(1)} %get-tuple-element.64.packed, f32[32,640]{1,0:T(8,128)S(1)} %get-tuple-element.65.crossline, bf16[384,128]{1,0:T(8,128)(2,1)S(1)} %copy-done.1, bf16[384,128]{1,0:T(8,128)(2,1)S(1)} %copy-done, bf16[64,64]{1,0:T(8,128)(2,1)S(1)} %copy-done.12, bf16[64,64]{1,0:T(8,128)(2,1)S(1)} %copy-done.11), custom_call_target="tpu_custom_call" | custom-call | flops 4096000 | bytes 1638400 | tf_op jit(solution)/shard_map/own/pallas_call | solution.py:566
  19.2 0.0 collective-permute-done.4.outer
  19.2 0.0 collective-permute-done.5.inner
  19.2 1.3 %fine.1 = (f32[8,4,640]{2,1,0:T(4,128)}, f32[4,4,640]{2,1,0:T(4,128)}, f32[16,640]{1,0:T(8,128)S(1)}, f32[16,4,640]{2,1,0:T(4,128)}, f32[16,4,640]{2,1,0:T(4,128)}) custom-call(f32[64,640]{1,0:T(8,128)S(1)} %own.1.mine, f32[8,8,640]{2,1,0:T(8,128)S(1)} %get-tuple-element.66.inside, f32[8,8,640]{2,1,0:T(8,128)S(1)} %get-tuple-element.67.outside, ...), custom_call_target="tpu_custom_call" | custom-call | flops 819200 | bytes 1638400 | tf_op jit(solution)/shard_map/fine/pallas_call | solution.py:573
  20.5 0.6 %collective-permute-done.6.outer = f32[8,640]{1,0:T(8,128)S(1)} collective-permute-done((f32[8,640]{1,0:T(8,128)S(1)}, f32[8,640]{1,0:T(8,128)S(1)}, u32[]{:S(2)}, u32[]{:S(2)}) %collective-permute-start.6) | collective-permute-done | bytes 20512 | tf_op jit(solution)/shard_map/ppermute | solution.py:564
  21.1 0.0 collective-permute-done.7.inner
  21.1 0.6 %coarse.1 = (f32[2,4,640]{2,1,0:T(4,128)}, f32[2,4,640]{2,1,0:T(4,128)}) custom-call(f32[16,640]{1,0:T(8,128)S(1)} %get-tuple-element.77.begun, f32[8,640]{1,0:T(8,128)S(1)} %collective-permute-done.6.outer, f32[8,640]{1,0:T(8,128)S(1)} %collective-permute-done.7.inner), custom_call_target="tpu_custom_call" | custom-call | flops 819200 | bytes 1638400 | tf_op jit(solution)/shard_map/coarse/pallas_call | solution.py:577
  (6 shorter events, 0.0 us)
Async XLA Ops:
  1.7 3.9 %copy-start.2 = (f32[16,4,640]{2,1,0:T(4,128)S(1)}, f32[16,4,640]{2,1,0:T(4,128)}, u32[]{:S(2)}) copy-start(f32[16,4,640]{2,1,0:T(4,128)} %prior_p.1) | copy-start | bytes 491524
  1.7 3.8 %copy-start.3 = (f32[16,4,640]{2,1,0:T(4,128)S(1)}, f32[16,4,640]{2,1,0:T(4,128)}, u32[]{:S(2)}) copy-start(f32[16,4,640]{2,1,0:T(4,128)} %prior_q.1) | copy-start | bytes 491524
  1.8 3.8 %copy-start.4 = (bf16[16,4,640]{2,1,0:T(4,128)(2,1)S(1)}, bf16[16,4,640]{2,1,0:T(4,128)(2,1)}, u32[]{:S(2)}) copy-start(bf16[16,4,640]{2,1,0:T(4,128)(2,1)} %courant.1) | copy-start | bytes 245764
  1.8 3.8 %copy-start.5 = (bf16[16,4,640]{2,1,0:T(4,128)(2,1)S(1)}, bf16[16,4,640]{2,1,0:T(4,128)(2,1)}, u32[]{:S(2)}) copy-start(bf16[16,4,640]{2,1,0:T(4,128)(2,1)} %epsilon.1) | copy-start | bytes 245764
  1.8 3.8 %copy-start.6 = (bf16[16,4,640]{2,1,0:T(4,128)(2,1)S(1)}, bf16[16,4,640]{2,1,0:T(4,128)(2,1)}, u32[]{:S(2)}) copy-start(bf16[16,4,640]{2,1,0:T(4,128)(2,1)} %delta.1) | copy-start | bytes 245764
  1.8 3.8 %copy-start.7 = (bf16[16,4,640]{2,1,0:T(4,128)(2,1)S(1)}, bf16[16,4,640]{2,1,0:T(4,128)(2,1)}, u32[]{:S(2)}) copy-start(bf16[16,4,640]{2,1,0:T(4,128)(2,1)} %tilt.1) | copy-start | bytes 245764
  1.8 3.8 %copy-start.8 = (bf16[16,4,640]{2,1,0:T(4,128)(2,1)S(1)}, bf16[16,4,640]{2,1,0:T(4,128)(2,1)}, u32[]{:S(2)}) copy-start(bf16[16,4,640]{2,1,0:T(4,128)(2,1)} %azimuth.1) | copy-start | bytes 245764
  1.8 6.6 %collective-permute-start.1 = (f32[4,8,640]{2,1,0:T(8,128)S(1)}, f32[4,8,640]{2,1,0:T(8,128)S(1)}, u32[]{:S(2)}, u32[]{:S(2)}) collective-permute-start(f32[4,8,640]{2,1,0:T(8,128)S(1)} %get-tuple-element.55), channel_id=1, source_target_pairs={{0,2},{2,0},{4,6},{6,4},{8,10},{10,8},{12,14},{14,12},{1,3},{3,1},... | collective-permute-start | bytes 245768 | tf_op jit(solution)/shard_map/ppermute | solution.py:520
  4.8 3.6 %collective-permute-start.2 = (f32[4,8,640]{2,1,0:T(8,128)S(1)}, f32[4,8,640]{2,1,0:T(8,128)S(1)}, u32[]{:S(2)}, u32[]{:S(2)}) collective-permute-start(f32[4,8,640]{2,1,0:T(8,128)S(1)} %get-tuple-element.56), channel_id=1, source_target_pairs={{0,1},{1,0},{2,4},{3,5},{4,2},{5,3},{6,8},{7,9},{8,6},{9,7},{10,12... | collective-permute-start | bytes 245768 | tf_op jit(solution)/shard_map/ppermute | solution.py:519
  4.8 1.8 %collective-permute-start = (f32[16,8,640]{2,1,0:T(8,128)S(1)}, f32[16,8,640]{2,1,0:T(8,128)S(1)}, u32[]{:S(2)}, u32[]{:S(2)}) collective-permute-start(f32[16,8,640]{2,1,0:T(8,128)S(1)} %pad_maximum_fusion.waves), channel_id=1, source_target_pairs={{0,1},{1,0},{2,3},{3,2},{4,5},{5,4},{6,7},{7,6},{8,9},{9,8},{10,11... | collective-permute-start | bytes 983048 | tf_op jit(solution)/shard_map/ppermute | solution.py:521
  5.7 0.9 %copy-start = (bf16[384,128]{1,0:T(8,128)(2,1)S(1)}, bf16[384,128]{1,0:T(8,128)(2,1)}, u32[]{:S(2)}) copy-start(bf16[384,128]{1,0:T(8,128)(2,1)} %constant.33.clone.block_low) | copy-start | bytes 294916
  5.7 0.9 %copy-start.1 = (bf16[384,128]{1,0:T(8,128)(2,1)S(1)}, bf16[384,128]{1,0:T(8,128)(2,1)}, u32[]{:S(2)}) copy-start(bf16[384,128]{1,0:T(8,128)(2,1)} %constant.32.clone.block_high) | copy-start | bytes 294916
  8.5 1.5 %collective-permute-start.3 = (f32[8,8,640]{2,1,0:T(8,128)S(1)}, f32[8,8,640]{2,1,0:T(8,128)S(1)}, u32[]{:S(2)}, u32[]{:S(2)}) collective-permute-start(f32[8,8,640]{2,1,0:T(8,128)S(1)} %constant_dynamic-update-slice_fusion.edges), channel_id=1, source_target_pairs={{0,1},{1,0},{2,3},{3,2},{4,5},{5,4},{6,7},{7,6},{8,9},{9,8},{10,11... | collective-permute-start | bytes 491528 | tf_op jit(solution)/shard_map/ppermute | solution.py:538
  8.9 1.0 %copy-start.9 = (bf16[64,64]{1,0:T(8,128)(2,1)S(1)}, bf16[64,64]{1,0:T(8,128)(2,1)}, u32[]{:S(2)}) copy-start(bf16[64,64]{1,0:T(8,128)(2,1)} %constant.35.clone.inline_low) | copy-start | bytes 24580
  8.9 1.0 %copy-start.10 = (bf16[64,64]{1,0:T(8,128)(2,1)S(1)}, bf16[64,64]{1,0:T(8,128)(2,1)}, u32[]{:S(2)}) copy-start(bf16[64,64]{1,0:T(8,128)(2,1)} %constant.34.clone.inline_high) | copy-start | bytes 24580
  10.0 8.7 %copy-start.11 = (bf16[64,64]{1,0:T(8,128)(2,1)S(1)}, bf16[64,64]{1,0:T(8,128)(2,1)}, u32[]{:S(2)}) copy-start(bf16[64,64]{1,0:T(8,128)(2,1)} %constant.37.clone.own_low) | copy-start | bytes 24580
  10.0 8.7 %copy-start.12 = (bf16[64,64]{1,0:T(8,128)(2,1)S(1)}, bf16[64,64]{1,0:T(8,128)(2,1)}, u32[]{:S(2)}) copy-start(bf16[64,64]{1,0:T(8,128)(2,1)} %constant.36.clone.own_high) | copy-start | bytes 24580
  10.7 8.5 %collective-permute-start.4 = (f32[24,640]{1,0:T(8,128)S(1)}, f32[24,640]{1,0:T(8,128)S(1)}, u32[]{:S(2)}, u32[]{:S(2)}) collective-permute-start(f32[24,640]{1,0:T(8,128)S(1)} %get-tuple-element.68), channel_id=1, source_target_pairs={{0,14},{2,4},{4,2},{6,8},{8,6},{10,12},{12,10},{14,0},{1,15},{3,5}... | collective-permute-start | bytes 184328 | tf_op jit(solution)/shard_map/ppermute | solution.py:564
  14.6 4.6 %collective-permute-start.5 = (f32[24,640]{1,0:T(8,128)S(1)}, f32[24,640]{1,0:T(8,128)S(1)}, u32[]{:S(2)}, u32[]{:S(2)}) collective-permute-start(f32[24,640]{1,0:T(8,128)S(1)} %get-tuple-element.69), channel_id=1, source_target_pairs={{0,2},{2,0},{4,6},{6,4},{8,10},{10,8},{12,14},{14,12},{1,3},{3,1},... | collective-permute-start | bytes 184328 | tf_op jit(solution)/shard_map/ppermute | solution.py:564
  15.5 5.7 %collective-permute-start.6 = (f32[8,640]{1,0:T(8,128)S(1)}, f32[8,640]{1,0:T(8,128)S(1)}, u32[]{:S(2)}, u32[]{:S(2)}) collective-permute-start(f32[8,640]{1,0:T(8,128)S(1)} %get-tuple-element.75), channel_id=1, source_target_pairs={{0,12},{2,14},{4,8},{6,10},{8,4},{10,6},{12,0},{14,2},{1,13},{3,15... | collective-permute-start | bytes 61448 | tf_op jit(solution)/shard_map/ppermute | solution.py:564
  17.1 4.0 %collective-permute-start.7 = (f32[8,640]{1,0:T(8,128)S(1)}, f32[8,640]{1,0:T(8,128)S(1)}, u32[]{:S(2)}, u32[]{:S(2)}) collective-permute-start(f32[8,640]{1,0:T(8,128)S(1)} %get-tuple-element.76), channel_id=1, source_target_pairs={{0,4},{2,6},{4,0},{6,2},{8,12},{10,14},{12,8},{14,10},{1,5},{3,7},... | collective-permute-start | bytes 61448 | tf_op jit(solution)/shard_map/ppermute | solution.py:564
